TPU v7x, 32 devices: a whole 2x2x4 slice. The times are simulated.
32 devices in a mesh: alpha: 8 (over z, x), beta: 4 (over y, core).
Axes of the slice: x: 2, y: 2, z: 4, core: 2. Of those that a mesh axis runs over, the one named last changes fastest.
Arguments:
- coeffs: float32 [6144, 6144], P('alpha', 'beta'), may hold values from -6 to 6
- denominator: float32 [6144, 6144], P('alpha', 'beta'), may hold values from 1.5 to 6
- coupling: bfloat16 [6144, 4, 768], P('alpha'), may hold values from -0.15625 to 0.15625
- tile_cols: int32 [8, 4], replicated, may hold values from 0 to 7, as said below
- tile_count: int32 [8], replicated, may hold values from 1 to 4, as said below
Outputs:
- coeffs_out: float32 [6144, 6144], P('alpha', 'beta')
Inputs may be any that keep to these rules, and one draw needn't show every extreme that they name: `tile_cols`: in every row the 4 entries are distinct; only the first tile_count entries of a row name coupled tiles, the others are unused. `tile_count`: some tile row has exactly 4 coupled tiles.
All inputs are finite; a program needn't handle non-finite values.
Results may differ from a plain program's by a relative error of at most 0.0017.
Values may be sent and summed in bfloat16 or wider, within the bound.
No kernel may reach another device: no remote copies, remote signals or barrier semaphores. Data moves between devices by JAX's collectives and lax.ppermute only.
A program may use at most 128 MiB of HBM per device.

v0:
```python
import jax
import jax.numpy as jnp
from jax import lax
from jax.sharding import PartitionSpec as P

STEPS = 2


def sigma_part(coeffs, coupling, tile_cols, tile_count):
    rows_dev = coeffs.shape[0]
    tile = coupling.shape[2]
    first_row = lax.axis_index("alpha") * rows_dev
    block_row = first_row // tile
    row_columns = lax.dynamic_index_in_dim(tile_cols, block_row, 0, keepdims=False)
    filled = lax.dynamic_index_in_dim(tile_count, block_row, 0, keepdims=False)
    coeff_half = coeffs.astype(jnp.bfloat16)
    initial = jnp.zeros((rows_dev, coeffs.shape[1]), jnp.float32)
    gathered = lax.all_gather(coeff_half, "alpha", axis=0, tiled=True)

    def add_slot(slot, running):
        column = lax.dynamic_index_in_dim(row_columns, slot, 0, keepdims=False)
        column_block = lax.dynamic_slice_in_dim(gathered, column * tile, tile, 0)
        weights = lax.dynamic_index_in_dim(coupling, slot, 1, keepdims=False)
        return running + jnp.dot(weights, column_block, preferred_element_type=jnp.float32)

    return lax.fori_loop(jnp.int32(0), filled, add_slot, initial)


def mirror_exchanges(sigma):
    rows_dev = sigma.shape[0]
    alpha_devices = lax.axis_size("alpha")
    beta_devices = lax.axis_size("beta")
    share = rows_dev // alpha_devices
    halves = jnp.stack([sigma[:, :rows_dev].T, sigma[:, rows_dev:].T])
    segmented = halves.reshape(2, alpha_devices, share, rows_dev)
    first_hop = lax.all_to_all(segmented, "alpha", split_axis=1, concat_axis=2, tiled=True)
    second_input = first_hop.reshape(2, beta_devices, 2 * share, rows_dev)
    second_hop = lax.all_to_all(second_input, "beta", split_axis=1, concat_axis=0, tiled=True)
    third_input = second_hop.reshape(2 * beta_devices, 2 * share, rows_dev)
    third_hop = lax.all_to_all(third_input, "alpha", split_axis=0, concat_axis=1, tiled=True)
    arranged = third_hop.reshape(alpha_devices, 2, share, rows_dev).transpose(0, 2, 1, 3)
    return arranged.reshape(rows_dev, 2 * rows_dev)


def body(coeffs, denominator, coupling, tile_cols, tile_count):
    current = coeffs
    for step_index in range(STEPS):
        sigma = sigma_part(current, coupling, tile_cols, tile_count)
        mirrored = mirror_exchanges(sigma)
        current = current - (sigma + mirrored) / denominator
    return current


def solution(mesh):
    placed = (P("alpha", "beta"), P("alpha", "beta"), P("alpha", None, None), P(), P())
    return jax.shard_map(
        body, mesh=mesh, in_specs=placed, out_specs=P("alpha", "beta"), check_vma=False
    )
```

profile of v0, /device:TPU:25, one launch (start us, length us, event | category | flops | bytes accessed | tf_op | source)
XLA Modules:
  0.0 1415.1 jit_solution(15100356796464970455)
XLA Ops:
  6.5 4.0 convert_element_type.6
  10.6 0.0 all-gather.3.cloned.1.call-update
  10.6 0.0 all-gather.5.cloned.1.call-start
  10.7 0.0 copy-done.2
  10.7 0.6 dynamic_slice.30
  11.3 0.0 copy-done
  11.4 0.2 dynamic-slice_reduce_fusion
  11.5 5.1 copy.24
  16.6 357.8 %all-gather.3.cloned.1.call-done = bf16[6144,1536]{1,0:T(8,128)(2,1)} async-done(((bf16[768,1536]{1,0:T(8,128)(2,1)}), bf16[6144,1536]{1,0:T(8,128)(2,1)}) %all-gather.3.cloned.1.call-update) | async-done | bytes 18874384 | tf_op jit(solution)/shard_map/all_gather | solution.py:18
  374.4 2.7 broadcast.3.clone
  377.1 10.0 while.20
  377.8 0.6 dynamic_slice.53
  379.0 7.5 convolution_add_fusion.4
  387.2 6.0 copy.25
  393.2 2.7 fusion.10
  395.9 0.4 pad_maximum_fusion
  396.3 0.4 copy.27
  396.7 132.7 %all_to_all.66 = f32[2,8,96,768]{3,2,0,1:T(8,128)S(1)} all-to-all(f32[2,8,96,768]{3,2,0,1:T(8,128)S(1)} %copy.27), channel_id=1, replica_groups=mesh['alpha'=8,'beta'=4] {'alpha'}, dimensions={1} | all-to-all | bytes 9437184 | tf_op jit(solution)/shard_map/all_to_all | solution.py:36
  529.4 0.4 copy.28
  529.9 0.3 copy.29
  530.2 56.3 %all_to_all.67 = f32[2,4,192,768]{3,2,0,1:T(8,128)S(1)} all-to-all(f32[2,4,192,768]{3,2,0,1:T(8,128)S(1)} %copy.29), channel_id=1, replica_groups=mesh['alpha'=8,'beta'=4] {'beta'}, dimensions={1} | all-to-all | bytes 9437184 | tf_op jit(solution)/shard_map/all_to_all | solution.py:38
  586.5 107.3 %all_to_all.68 = f32[8,192,768]{2,1,0:T(8,128)S(1)} all-to-all(f32[8,192,768]{2,1,0:T(8,128)S(1)} %bitcast.68), channel_id=1, replica_groups=mesh['alpha'=8,'beta'=4] {'alpha'}, dimensions={0} | all-to-all | bytes 9437184 | tf_op jit(solution)/shard_map/all_to_all | solution.py:40
  693.8 3.6 copy.30
  697.4 0.0 slice-start.1
  697.4 0.0 slice-start.7
  697.4 2.5 copy.38
  699.9 0.0 slice-done.6
  700.0 6.5 fusion.8
  706.4 0.0 all-gather.5.cloned.1.call-update
  706.5 363.8 %all-gather.5.cloned.1.call-done = bf16[6144,1536]{1,0:T(8,128)(2,1)} async-done(((bf16[768,1536]{1,0:T(8,128)(2,1)}), bf16[6144,1536]{1,0:T(8,128)(2,1)}) %all-gather.5.cloned.1.call-update) | async-done | bytes 18874384 | tf_op jit(solution)/shard_map/all_gather | solution.py:18
  1070.2 2.8 broadcast.3
  1073.0 10.2 while.21
  1073.8 0.6 dynamic_slice.56
  1075.0 7.6 convolution_add_fusion.5
  1083.2 6.1 copy.32
  1089.3 2.7 fusion.9
  1092.0 0.4 pad_maximum_fusion.1
  1092.4 0.4 copy.34
  1092.8 132.7 %all_to_all.69 = f32[2,8,96,768]{3,2,0,1:T(8,128)S(1)} all-to-all(f32[2,8,96,768]{3,2,0,1:T(8,128)S(1)} %copy.34), channel_id=1, replica_groups=mesh['alpha'=8,'beta'=4] {'alpha'}, dimensions={1} | all-to-all | bytes 9437184 | tf_op jit(solution)/shard_map/all_to_all | solution.py:36
  1225.5 0.4 copy.35
  1225.9 0.3 copy.36
  1226.2 56.3 %all_to_all.70 = f32[2,4,192,768]{3,2,0,1:T(8,128)S(1)} all-to-all(f32[2,4,192,768]{3,2,0,1:T(8,128)S(1)} %copy.36), channel_id=1, replica_groups=mesh['alpha'=8,'beta'=4] {'beta'}, dimensions={1} | all-to-all | bytes 9437184 | tf_op jit(solution)/shard_map/all_to_all | solution.py:38
  1282.5 108.0 %all_to_all.71 = f32[8,192,768]{2,1,0:T(8,128)} all-to-all(f32[8,192,768]{2,1,0:T(8,128)S(1)} %bitcast.72), channel_id=1, replica_groups=mesh['alpha'=8,'beta'=4] {'alpha'}, dimensions={0} | all-to-all | bytes 9437184 | tf_op jit(solution)/shard_map/all_to_all | solution.py:40
  1390.5 8.3 copy.37
  1398.8 2.8 copy.39
  1401.7 0.7 slice-done.3
  1402.4 5.9 divide_subtract_fusion
  1408.3 0.0 copy-done.1
  (30 shorter events, 0.0 us)
Async XLA Ops:
  6.5 4.8 copy-start
  6.5 4.2 copy-start.2
  6.5 367.9 %all-gather.3.cloned.1.call-start = ((), (), s32[]{:S(2)}) async-start(), calls=%async_computation.6 | async-start | bytes 21233664 | tf_op jit(solution)/shard_map/all_gather | solution.py:18
  10.6 1059.6 %all-gather.5.cloned.1.call-start = ((), (), s32[]{:S(2)}) async-start(), calls=%async_computation.7 | async-start | bytes 21233664 | tf_op jit(solution)/shard_map/all_gather | solution.py:18
  693.8 6.2 slice-start
  693.8 6.2 slice-start.6
  697.4 2.5 slice-start.1
  697.4 2.5 slice-start.7
  1282.5 119.1 %slice-start.4 = ((s8[4718592]{0:T(1024)(128)(4,1)}), s8[4194304]{0:T(1024)(128)(4,1)S(1)}, s32[]{:S(2)}) async-start(s8[4718592]{0:T(1024)(128)(4,1)} %bitcast.57), calls=%async_computation.12 | async-start | bytes 8388608
  1282.5 119.1 %slice-start.8 = ((s8[4718592]{0:T(1024)(128)(4,1)}), s8[4194304]{0:T(1024)(128)(4,1)S(1)}, s32[]{:S(2)}) async-start(s8[4718592]{0:T(1024)(128)(4,1)} %bitcast.61), calls=%async_computation.16 | async-start | bytes 8388608
  1282.5 119.1 %slice-start.10 = ((s8[4718592]{0:T(1024)(128)(4,1)}), s8[4194304]{0:T(1024)(128)(4,1)S(1)}, s32[]{:S(2)}) async-start(s8[4718592]{0:T(1024)(128)(4,1)} %bitcast.64), calls=%async_computation.18 | async-start | bytes 8388608
  1390.5 11.2 slice-start.2
  1390.5 11.2 slice-start.5
  1390.5 11.2 slice-start.9
  1390.5 11.2 slice-start.11
  1398.8 3.6 slice-start.3
  1402.4 5.9 copy-start.1
Sparse Core Ops, SparseCore 0:
  10.7 363.6 all-gather.2
  706.6 363.6 all-gather.4
where the time goes:
time: 1420 us
  waiting for transfers between devices  722 us (51%)
  blocking collectives  593 us (42%)
  local copies, waits for them, and re-layouts  50.3 us (4%)
  other arithmetic  17.2 us (1%)
  matrix products  15.1 us (1%)
    all_gather x2, waiting for transfers between devices, sigma_part(): gathered = lax.all_gather(coeff_half, 'alpha', axis=0, tiled=True)  722 us
    all_to_all x2, blocking collectives, mirror_exchanges(): lax.all_to_all(segmented, 'alpha', split_axis=1, concat_axis=2, tiled=True)  265 us
    all_to_all x2, blocking collectives, mirror_exchanges(): lax.all_to_all(third_input, 'alpha', split_axis=0, concat_axis=1, tiled=T...  215 us
    all_to_all x2, blocking collectives, mirror_exchanges(): lax.all_to_all(second_input, 'beta', split_axis=1, concat_axis=0, tiled=T...  113 us
  transfers between devices with their start and end apart: 2, of which 2 were waited for; matrix products, arithmetic and copies ran while one was open for 0% of the time, Pallas kernels for 0%

commit v1 on v0

v1 whole, which is shorter than its diff:
```python
import jax
import jax.numpy as jnp
from jax import lax
from jax.experimental import pallas as pl
from jax.experimental.pallas import tpu as pltpu
from jax.sharding import PartitionSpec as P

STEPS = 2
COUPLING_MAX = 0.15625
DENOMINATOR_MIN = 1.5
HALF_TOP = 60000.0
AXES = ("alpha", "beta")
ROW_CHUNKS = 2


class Grid:
    def __init__(self, alpha_devices, beta_devices):
        self.bands = beta_devices
        self.lanes = alpha_devices // beta_devices
        self.per_lane = beta_devices // self.lanes

    def index(self, band, lane, beta):
        return (band * self.lanes + lane) * self.bands + beta

    def send(self, value, where):
        pairs = []
        for band in range(self.bands):
            for lane in range(self.lanes):
                for beta in range(self.bands):
                    target = where(band, lane, beta)
                    if target is not None:
                        pairs.append((self.index(band, lane, beta), self.index(*target)))
        if all(source == target for source, target in pairs):
            return value
        return lax.ppermute(value, AXES, pairs)


def gather_couplings(grid, coupling, band, beta):
    rows, slots, _ = coupling.shape
    bands = grid.bands
    chunk = rows // bands
    own = lax.dynamic_slice_in_dim(coupling, beta * chunk, chunk, 0)
    gathered = []
    for slot in range(slots):
        upward, downward = [own[:, slot]], [own[:, slot]]
        for _ in range(bands - 1):
            upward.append(grid.send(upward[-1], lambda z, x, b: (z + 1, x, b) if z + 1 < bands else None))
            downward.append(grid.send(downward[-1], lambda z, x, b: (z - 1, x, b) if z > 0 else None))
        line = [upward[0]] + [jnp.where(band >= hop, upward[hop], downward[bands - hop]) for hop in range(1, bands)]
        pieces = {0: jnp.stack(line)}
        bit = bands // 2
        while bit:
            received = {
                key ^ bit: grid.send(piece, lambda z, x, b, bit=bit: (z, x, b ^ bit)) for key, piece in pieces.items()
            }
            pieces.update(received)
            bit //= 2
        pieces = [pieces[key] for key in range(bands)]
        if chunk % 16:
            whole = jnp.take(jnp.stack(pieces), beta ^ jnp.arange(bands), axis=0)
            pieces = [whole.transpose(1, 0, 2, 3).reshape(bands, rows, whole.shape[3])]
        gathered.append(pieces)
    return gathered


def to_columns(grid, half, band, lane, beta):
    rows, cols = half.shape
    bands, lanes = grid.bands, grid.lanes
    strip = cols // bands
    part = rows // ROW_CHUNKS
    whole = jnp.zeros((bands, lanes, rows, strip), half.dtype)
    for chunk in range(ROW_CHUNKS):
        block = half[chunk * part : (chunk + 1) * part]
        first = []
        for key in range(bands):
            piece = lax.dynamic_slice(block, (0, (beta ^ key) * strip), (part, strip))
            first.append(grid.send(piece, lambda z, x, b: (z, x, b ^ key)))
        first = jnp.stack(first)
        for key in range(bands):
            piece = lax.dynamic_index_in_dim(first, band ^ key ^ beta, 0, keepdims=False)
            piece = grid.send(piece, lambda z, x, b: (z ^ key, x, b))
            for turn in range(lanes):
                other = grid.send(piece, lambda z, x, b: (z, (x + turn) % lanes, b))
                place = (band ^ key, (lane - turn) % lanes, chunk * part, 0)
                whole = lax.dynamic_update_slice(whole, other[None, None], place)
    return whole.reshape(bands * lanes * rows, strip)


def product_kernel(slots, pieces, hop_ref, column_ref, count_ref, offset_ref, *refs):
    block = pl.program_id(0)
    coeff_ref, out_ref = refs[slots * pieces], refs[slots * pieces + 1]
    chunk, tile = refs[0].shape[1:]
    for piece in range(pieces):
        place = pl.ds(pl.multiple_of(offset_ref[piece], chunk), chunk)
        for slot in range(slots):

            def product():
                first = pl.multiple_of(column_ref[block * slots + slot] * tile, tile)
                return jnp.dot(
                    refs[slot * pieces + piece][0], coeff_ref[pl.ds(first, tile), :], preferred_element_type=jnp.float32
                )

            if slot == 0:
                out_ref[0, place, :] = product()
            else:

                @pl.when(slot < count_ref[block])
                def _():
                    out_ref[0, place, :] += product()


def products(couplings, columns, hops, tile_columns, counts, offsets):
    slots, pieces = len(couplings), len(couplings[0])
    bands, chunk, tile = couplings[0][0].shape
    strip = columns.shape[1]
    spec = pl.BlockSpec((1, chunk, tile), lambda i, hop, *_: (hop[i], 0, 0))
    return pl.pallas_call(
        lambda *refs: product_kernel(slots, pieces, *refs),
        grid_spec=pltpu.PrefetchScalarGridSpec(
            num_scalar_prefetch=4,
            grid=(bands,),
            in_specs=[spec] * (slots * pieces) + [pl.BlockSpec(columns.shape, lambda i, *_: (0, 0))],
            out_specs=pl.BlockSpec((1, pieces * chunk, strip), lambda i, *_: (i, 0, 0)),
        ),
        out_shape=jax.ShapeDtypeStruct((bands, pieces * chunk, strip), jnp.float32),
        compiler_params=pltpu.CompilerParams(vmem_limit_bytes=48 << 20),
        cost_estimate=pl.CostEstimate(
            flops=2 * bands * slots * pieces * chunk * tile * strip,
            bytes_accessed=2 * bands * slots * pieces * chunk * tile,
            transcendentals=0,
        ),
    )(hops, tile_columns, counts, offsets, *[piece for slot in couplings for piece in slot], columns)


def bring_home(grid, sigma, scale, band, lane, beta):
    bands, rows, strip = sigma.shape
    lanes, per_lane = grid.lanes, grid.per_lane
    scaled = (sigma * scale).astype(jnp.float16)
    mirrored = scaled.transpose(0, 2, 1)
    direct = jnp.zeros((rows, bands * strip), jnp.float16)
    mirror = jnp.zeros((rows, bands * strip), jnp.float16)
    for key in range(bands):
        piece = lax.dynamic_index_in_dim(scaled, beta ^ key, 0, keepdims=False)
        piece = grid.send(piece, lambda z, x, b: (b ^ key, x, z))
        direct = lax.dynamic_update_slice(direct, piece, (0, (band ^ key) * strip))
    for key in range(bands):
        target = (lane * per_lane + beta % per_lane) ^ key
        piece = lax.dynamic_index_in_dim(mirrored, target, 0, keepdims=False)
        piece = grid.send(piece, lambda z, x, b: (z, b // per_lane, (x * per_lane + b % per_lane) ^ key))
        source = beta ^ key
        mirror = lax.dynamic_update_slice(mirror, piece, ((source % per_lane) * strip, (source // per_lane) * rows))
    return direct, mirror


def body(coeffs, denominator, coupling, tile_cols, tile_count):
    rows = coeffs.shape[0]
    _, slots, tile = coupling.shape
    grid = Grid(lax.axis_size("alpha"), lax.axis_size("beta"))
    alpha, beta = lax.axis_index("alpha"), lax.axis_index("beta")
    band, lane = alpha // grid.lanes, alpha % grid.lanes
    every = jnp.arange(grid.bands, dtype=jnp.int32)
    tile_rows = (every * grid.lanes + lane) * rows // tile
    tile_columns = jnp.take(tile_cols, tile_rows, axis=0).reshape(-1)
    counts = jnp.take(tile_count, tile_rows)
    hops = (band - every) % grid.bands
    couplings = gather_couplings(grid, coupling, band, beta)
    pieces = len(couplings[0])
    offsets = (beta ^ every) * (rows // grid.bands) if pieces > 1 else jnp.zeros((1,), jnp.int32)

    growth = slots * tile * COUPLING_MAX
    largest = jnp.maximum(lax.pmax(jnp.max(jnp.abs(coeffs)), AXES), 1e-30)
    current = coeffs
    for step_index in range(STEPS):
        scale = HALF_TOP / (growth * largest)
        largest = largest * (1 + 2 * growth / DENOMINATOR_MIN)
        columns = to_columns(grid, current.astype(jnp.bfloat16), band, lane, beta)
        sigma = products(couplings, columns, hops, tile_columns, counts, offsets)
        direct, mirror = bring_home(grid, sigma, scale, band, lane, beta)
        total = (direct.astype(jnp.float32) + mirror.astype(jnp.float32)) / scale
        current = current - total / denominator
    return current


def solution(mesh):
    placed = (P("alpha", "beta"), P("alpha", "beta"), P("alpha", None, None), P(), P())
    return jax.shard_map(
        body, mesh=mesh, in_specs=placed, out_specs=P("alpha", "beta"), check_vma=False
    )
```

time: 1420 us -> 674 us (0.47)
  the two profiles are of different devices: /device:TPU:25 before, /device:TPU:3 now
where the time goes in v1:
time: 674 us; the launch traced here: 666 us
  starting transfers between devices  269 us (40%)
  waiting for transfers between devices  191 us (28%)
  local copies, waits for them, and re-layouts  103 us (15%)
  blocking collectives  40.8 us (6%)
  other arithmetic  32.1 us (5%)
  Pallas kernels  27.7 us (4%)
    ppermute x92, starting transfers between devices, send(): return lax.ppermute(value, AXES, pairs)  269 us
    ppermute x92, waiting for transfers between devices, send(): return lax.ppermute(value, AXES, pairs)  191 us
    dynamic_update_slice x8, local copies, waits for them, and re-layouts, bring_home(): lax.dynamic_update_slice(mirror, piece, (source % per_lane * strip, sourc...  52.7 us
    pmax x1, blocking collectives, body(): largest = jnp.maximum(lax.pmax(jnp.max(jnp.abs(coeffs)), AXES), 1e-30)  40.8 us
    pallas_call x2, Pallas kernels, products(): pl.pallas_call(lambda *refs: product_kernel(slots, pieces, *refs), grid_s...  27.7 us
    ppermute x8, local copies, waits for them, and re-layouts, send(): return lax.ppermute(value, AXES, pairs)  14.2 us
  transfers between devices with their start and end apart: 92, of which 30 were waited for; matrix products, arithmetic and copies ran while one was open for 14% of the time, Pallas kernels for 0%

profile of v1, /device:TPU:3, one launch (start us, length us, event | category | flops | bytes accessed | tf_op | source)
XLA Modules:
  0.0 665.8 jit_solution(16587672355784615587)
XLA Ops:
  0.0 5.1 fusion.3
  12.4 4.7 constant_dynamic-slice_fusion.15
  19.2 4.7 collective-permute-start.27
  31.8 40.8 %pmax.7 = f32[]{:T(128)} all-reduce(f32[]{:T(128)} %get-tuple-element.6), channel_id=1, replica_groups=mesh['alpha'=8,'beta'=4] {'alpha','beta'}, use_global_device_ids=true, to_apply=%region_1.2 | all-reduce | flops 1 | bytes 8 | tf_op jit(solution)/shard_map/pmax | solution.py:171
  84.7 4.6 collective-permute-start.31
  129.3 14.8 %collective-permute-done.32 = bf16[192,768]{1,0:T(8,128)(2,1)S(1)} collective-permute-done((bf16[192,768]{1,0:T(8,128)(2,1)S(1)}, bf16[192,768]{1,0:T(8,128)(2,1)S(1)}, u32[]{:S(2)}, u32[]{:S(2)}) %collective-permute-start.32) | collective-permute-done | bytes 294944 | tf_op jit(solution)/shard_map/ppermute | solution.py:35
  151.8 5.1 collective-permute-done.30
  161.2 4.2 collective-permute-done.21
  185.3 6.1 collective-permute-done.50
  193.1 9.0 %collective-permute-done.54 = bf16[384,384]{1,0:T(8,128)(2,1)S(1)} collective-permute-done((bf16[384,384]{1,0:T(8,128)(2,1)S(1)}, bf16[384,384]{1,0:T(8,128)(2,1)S(1)}, u32[]{:S(2)}, u32[]{:S(2)}) %collective-permute-start.54) | collective-permute-done | bytes 294944 | tf_op jit(solution)/shard_map/ppermute | solution.py:35
  208.0 16.2 %collective-permute-start.33 = (bf16[4,192,768]{2,1,0:T(8,128)(2,1)S(1)}, bf16[4,192,768]{2,1,0:T(8,128)(2,1)S(1)}, u32[]{:S(2)}, u32[]{:S(2)}) collective-permute-start(bf16[4,192,768]{2,1,0:T(8,128)(2,1)S(1)} %pad_maximum_fusion.3.refs_16_), channel_id=1, source_target_pairs={{0,1},{1,0},{2,3},{3,2},{4,5},{5,4},{6,7},{7,6},{8,9},{9,8},{10,11... | collective-permute-start | bytes 3538952 | tf_op jit(solution)/shard_map/ppermute | solution.py:35
  233.1 12.8 %collective-permute-start.6 = (bf16[4,192,768]{2,1,0:T(8,128)(2,1)S(1)}, bf16[4,192,768]{2,1,0:T(8,128)(2,1)S(1)}, u32[]{:S(2)}, u32[]{:S(2)}) collective-permute-start(bf16[4,192,768]{2,1,0:T(8,128)(2,1)S(1)} %pad_maximum_fusion.refs_4_), channel_id=1, source_target_pairs={{0,1},{1,0},{2,3},{3,2},{4,5},{5,4},{6,7},{7,6},{8,9},{9,8},{10,11... | collective-permute-start | bytes 3538952 | tf_op jit(solution)/shard_map/ppermute | solution.py:35
  246.0 9.9 %collective-permute-done.16.refs_10_ = bf16[4,192,768]{2,1,0:T(8,128)(2,1)S(1)} collective-permute-done((bf16[4,192,768]{2,1,0:T(8,128)(2,1)S(1)}, bf16[4,192,768]{2,1,0:T(8,128)(2,1)S(1)}, u32[]{:S(2)}, u32[]{:S(2)}) %collective-permute-start.16) | collective-permute-done | bytes 1179680 | tf_op jit(solution)/shard_map/ppermute | solution.py:35
  255.9 13.1 %collective-permute-start.26 = (bf16[4,192,768]{2,1,0:T(8,128)(2,1)S(1)}, bf16[4,192,768]{2,1,0:T(8,128)(2,1)S(1)}, u32[]{:S(2)}, u32[]{:S(2)}) collective-permute-start(bf16[4,192,768]{2,1,0:T(8,128)(2,1)S(1)} %collective-permute-done.25.refs_14_), channel_id=1, source_target_pairs={{0,1},{1,0},{2,3},{3,2},{4,5},{5,4},{6,7},{7,6},{8,9},{9,8},{10,11... | collective-permute-start | bytes 3538952 | tf_op jit(solution)/shard_map/ppermute | solution.py:35
  269.1 12.1 %collective-permute-done.7.refs_6_ = bf16[4,192,768]{2,1,0:T(8,128)(2,1)S(1)} collective-permute-done((bf16[4,192,768]{2,1,0:T(8,128)(2,1)S(1)}, bf16[4,192,768]{2,1,0:T(8,128)(2,1)S(1)}, u32[]{:S(2)}, u32[]{:S(2)}) %collective-permute-start.7) | collective-permute-done | bytes 1179680 | tf_op jit(solution)/shard_map/ppermute | solution.py:35
  281.1 6.8 %collective-permute-start.8 = (bf16[4,192,768]{2,1,0:T(8,128)(2,1)S(1)}, bf16[4,192,768]{2,1,0:T(8,128)(2,1)S(1)}, u32[]{:S(2)}, u32[]{:S(2)}) collective-permute-start(bf16[4,192,768]{2,1,0:T(8,128)(2,1)S(1)} %collective-permute-done.7.refs_6_), channel_id=1, source_target_pairs={{0,1},{1,0},{2,3},{3,2},{4,5},{5,4},{6,7},{7,6},{8,9},{9,8},{10,11... | collective-permute-start | bytes 3538952 | tf_op jit(solution)/shard_map/ppermute | solution.py:35
  291.5 13.8 %shard_map.55 = f32[4,768,384]{2,1,0:T(8,128)} custom-call(s32[4]{0:T(128)S(1)} %get-tuple-element.71.refs_0_, s32[16]{0:T(128)S(1)} %select_n.460.refs_1_, s32[4]{0:T(128)S(1)} %get-tuple-element.72.refs_2_, s32[4]{0:T(128)S(1)} %xor_multiply_fusion.refs_3_, bf16[4,192,768]{2,1,0:T(8,128)(2,1)S(1)} %pad_maximum_fusion.refs_4_, ...), custom_call_target="tpu_custom_call" | custom-call | flops 7247757312 | bytes 18874368 | tf_op jit(solution)/shard_map/pallas_call | solution.py:117
  310.4 5.5 collective-permute-start.60
  321.2 9.4 %collective-permute-done.60 = f16[384,768]{0,1:T(8,128)(2,1)S(1)} collective-permute-done((f16[384,768]{0,1:T(8,128)(2,1)S(1)}, f16[384,768]{0,1:T(8,128)(2,1)S(1)}, u32[]{:S(2)}, u32[]{:S(2)}) %collective-permute-start.60) | collective-permute-done | bytes 589856 | tf_op jit(solution)/shard_map/ppermute | solution.py:35
  332.4 21.6 %collective-permute-done.61 = f16[384,768]{0,1:T(8,128)(2,1)S(1)} collective-permute-done((f16[384,768]{0,1:T(8,128)(2,1)S(1)}, f16[384,768]{0,1:T(8,128)(2,1)S(1)}, u32[]{:S(2)}, u32[]{:S(2)}) %collective-permute-start.61) | collective-permute-done | bytes 589856 | tf_op jit(solution)/shard_map/ppermute | solution.py:35
  354.1 12.6 %collective-permute-done.62 = f16[384,768]{0,1:T(8,128)(2,1)S(1)} collective-permute-done((f16[384,768]{0,1:T(8,128)(2,1)S(1)}, f16[384,768]{0,1:T(8,128)(2,1)S(1)}, u32[]{:S(2)}, u32[]{:S(2)}) %collective-permute-start.62) | collective-permute-done | bytes 589856 | tf_op jit(solution)/shard_map/ppermute | solution.py:35
  367.6 15.9 %collective-permute-start.59 = (f16[768,384]{1,0:T(8,128)(2,1)}, f16[768,384]{1,0:T(8,128)(2,1)}, u32[]{:S(2)}, u32[]{:S(2)}) collective-permute-start(f16[768,384]{1,0:T(8,128)(2,1)} %get-tuple-element.21), channel_id=1, source_target_pairs={{0,24},{1,16},{2,8},{3,0},{4,28},{5,20},{6,12},{7,4},{8,25},{9,17}... | collective-permute-start | bytes 1769480 | tf_op jit(solution)/shard_map/ppermute | solution.py:35
  387.2 6.7 %dynamic_update_slice.164 = f16[768,1536]{1,0:T(8,128)(2,1)} dynamic-update-slice(f16[768,1536]{1,0:T(8,128)(2,1)} %broadcast.166.clone.1, f16[384,768]{1,0:T(8,128)(2,1)S(1)} %copy-done.21, s32[]{:T(128)S(6)} %select_n.504, s32[]{:T(128)S(6)} %select_n.506) | dynamic-update-slice | bytes 1179652 | tf_op jit(solution)/shard_map/dynamic_update_slice | solution.py:151
  396.1 7.1 %dynamic_update_slice.165 = f16[768,1536]{1,0:T(8,128)(2,1)} dynamic-update-slice(f16[768,1536]{1,0:T(8,128)(2,1)} %dynamic_update_slice.164, f16[384,768]{1,0:T(8,128)(2,1)} %copy.19, s32[]{:T(128)S(6)} %select_n.509, s32[]{:T(128)S(6)} %select_n.511) | dynamic-update-slice | bytes 1179652 | tf_op jit(solution)/shard_map/dynamic_update_slice | solution.py:151
  405.5 6.3 dynamic_update_slice.166
  414.0 6.4 dynamic_update_slice.167
  425.5 7.1 %fusion.2 = bf16[768,1536]{1,0:T(8,128)(2,1)S(1)} fusion(f32[768,1536]{1,0:T(8,128)} %param.5, f32[768,1536]{1,0:T(8,128)} %param.6, f32[]{:T(128)S(6)} %div.82, f16[768,1536]{1,0:T(8,128)(2,1)} %dynamic_update_slice.167, f16[768,1536]{1,0:T(8,128)(2,1)S(1)} %constant_dynamic-update-slice_fusion.4), kind=kLoop, calls=%fused_computation.141 | loop fusion | flops 8257536 | bytes 16515076 | tf_op jit(solution)/shard_map/convert_element_type | solution.py:176
  442.1 8.0 %collective-permute-done.66 = bf16[384,384]{1,0:T(8,128)(2,1)} collective-permute-done((bf16[384,384]{1,0:T(8,128)(2,1)}, bf16[384,384]{1,0:T(8,128)(2,1)}, u32[]{:S(2)}, u32[]{:S(2)}) %collective-permute-start.66) | collective-permute-done | bytes 294944 | tf_op jit(solution)/shard_map/ppermute | solution.py:35
  455.4 6.6 collective-permute-done.76
  464.0 4.6 collective-permute-start.80
  468.8 11.6 %collective-permute-start.82 = (bf16[384,384]{1,0:T(8,128)(2,1)S(1)}, bf16[384,384]{1,0:T(8,128)(2,1)S(1)}, u32[]{:S(2)}, u32[]{:S(2)}) collective-permute-start(bf16[384,384]{1,0:T(8,128)(2,1)S(1)} %get-tuple-element.31), channel_id=1, source_target_pairs={{0,24},{1,25},{2,26},{3,27},{4,28},{5,29},{6,30},{7,31},{8,16},{9,... | collective-permute-start | bytes 884744 | tf_op jit(solution)/shard_map/ppermute | solution.py:35
  482.3 16.7 %collective-permute-done.80 = bf16[384,384]{1,0:T(8,128)(2,1)S(1)} collective-permute-done((bf16[384,384]{1,0:T(8,128)(2,1)S(1)}, bf16[384,384]{1,0:T(8,128)(2,1)S(1)}, u32[]{:S(2)}, u32[]{:S(2)}) %collective-permute-start.80) | collective-permute-done | bytes 294944 | tf_op jit(solution)/shard_map/ppermute | solution.py:35
  502.7 4.4 collective-permute-done.79
  507.1 6.2 collective-permute-done.81
  513.5 6.2 collective-permute-done.83
  521.9 13.9 %shard_map.56 = f32[4,768,384]{2,1,0:T(8,128)} custom-call(s32[4]{0:T(128)S(1)} %get-tuple-element.71.refs_0_, s32[16]{0:T(128)S(1)} %select_n.460.refs_1_, s32[4]{0:T(128)S(1)} %get-tuple-element.72.refs_2_, s32[4]{0:T(128)S(1)} %xor_multiply_fusion.refs_3_, bf16[4,192,768]{2,1,0:T(8,128)(2,1)S(1)} %pad_maximum_fusion.refs_4_, ...), custom_call_target="tpu_custom_call" | custom-call | flops 7247757312 | bytes 18874368 | tf_op jit(solution)/shard_map/pallas_call | solution.py:117
  541.0 6.4 collective-permute-start.88
  550.6 10.0 %collective-permute-start.84 = (f16[768,384]{1,0:T(8,128)(2,1)}, f16[768,384]{1,0:T(8,128)(2,1)}, u32[]{:S(2)}, u32[]{:S(2)}) collective-permute-start(f16[768,384]{1,0:T(8,128)(2,1)} %get-tuple-element.18), channel_id=1, source_target_pairs={{0,0},{1,8},{2,16},{3,24},{4,4},{5,12},{6,20},{7,28},{8,1},{9,9},{... | collective-permute-start | bytes 1769480 | tf_op jit(solution)/shard_map/ppermute | solution.py:35
  560.7 7.9 %collective-permute-start.85 = (f16[768,384]{1,0:T(8,128)(2,1)}, f16[768,384]{1,0:T(8,128)(2,1)}, u32[]{:S(2)}, u32[]{:S(2)}) collective-permute-start(f16[768,384]{1,0:T(8,128)(2,1)} %get-tuple-element.17), channel_id=1, source_target_pairs={{0,8},{1,0},{2,24},{3,16},{4,12},{5,4},{6,28},{7,20},{8,9},{9,1},{... | collective-permute-start | bytes 1769480 | tf_op jit(solution)/shard_map/ppermute | solution.py:35
  568.6 8.7 %collective-permute-done.89 = f16[384,768]{0,1:T(8,128)(2,1)S(1)} collective-permute-done((f16[384,768]{0,1:T(8,128)(2,1)S(1)}, f16[384,768]{0,1:T(8,128)(2,1)S(1)}, u32[]{:S(2)}, u32[]{:S(2)}) %collective-permute-start.89) | collective-permute-done | bytes 589856 | tf_op jit(solution)/shard_map/ppermute | solution.py:35
  577.3 7.2 %collective-permute-start.86 = (f16[768,384]{1,0:T(8,128)(2,1)}, f16[768,384]{1,0:T(8,128)(2,1)}, u32[]{:S(2)}, u32[]{:S(2)}) collective-permute-start(f16[768,384]{1,0:T(8,128)(2,1)} %get-tuple-element.16), channel_id=1, source_target_pairs={{0,16},{1,24},{2,0},{3,8},{4,20},{5,28},{6,4},{7,12},{8,17},{9,25}... | collective-permute-start | bytes 1769480 | tf_op jit(solution)/shard_map/ppermute | solution.py:35
  584.6 5.4 collective-permute-done.90
  590.8 31.3 %collective-permute-start.87 = (f16[768,384]{1,0:T(8,128)(2,1)}, f16[768,384]{1,0:T(8,128)(2,1)}, u32[]{:S(2)}, u32[]{:S(2)}) collective-permute-start(f16[768,384]{1,0:T(8,128)(2,1)} %get-tuple-element.11), channel_id=1, source_target_pairs={{0,24},{1,16},{2,8},{3,0},{4,28},{5,20},{6,12},{7,4},{8,25},{9,17}... | collective-permute-start | bytes 1769480 | tf_op jit(solution)/shard_map/ppermute | solution.py:35
  622.8 7.5 %dynamic_update_slice.188 = f16[768,1536]{1,0:T(8,128)(2,1)S(1)} dynamic-update-slice(f16[768,1536]{1,0:T(8,128)(2,1)S(1)} %broadcast.166.clone, f16[384,768]{1,0:T(8,128)(2,1)S(1)} %copy.22, s32[]{:T(128)S(6)} %select_n.504, s32[]{:T(128)S(6)} %select_n.506) | dynamic-update-slice | bytes 1179652 | tf_op jit(solution)/shard_map/dynamic_update_slice | solution.py:151
  631.9 8.0 %dynamic_update_slice.189 = f16[768,1536]{1,0:T(8,128)(2,1)S(1)} dynamic-update-slice(f16[768,1536]{1,0:T(8,128)(2,1)S(1)} %dynamic_update_slice.188, f16[384,768]{1,0:T(8,128)(2,1)S(1)} %copy.23, s32[]{:T(128)S(6)} %select_n.509, s32[]{:T(128)S(6)} %select_n.511) | dynamic-update-slice | bytes 1179652 | tf_op jit(solution)/shard_map/dynamic_update_slice | solution.py:151
  641.5 5.2 dynamic_update_slice.190
  648.3 5.5 dynamic_update_slice.191
  659.2 6.1 divide_subtract_fusion
  (328 shorter events, 192.9 us)
Async XLA Ops:
  9.8 18.8 %collective-permute-start.47 = (bf16[384,384]{1,0:T(8,128)(2,1)}, bf16[384,384]{1,0:T(8,128)(2,1)}, u32[]{:S(2)}, u32[]{:S(2)}) collective-permute-start(bf16[384,384]{1,0:T(8,128)(2,1)} %get-tuple-element.53), channel_id=1, source_target_pairs={{0,2},{1,3},{2,0},{3,1},{4,6},{5,7},{6,4},{7,5},{8,10},{9,11},{10,... | collective-permute-start | bytes 884744 | tf_op jit(solution)/shard_map/ppermute | solution.py:35
  17.9 59.0 %collective-permute-start.28 = (bf16[192,768]{1,0:T(8,128)(2,1)S(1)}, bf16[192,768]{1,0:T(8,128)(2,1)}, u32[]{:S(2)}, u32[]{:S(2)}) collective-permute-start(bf16[192,768]{1,0:T(8,128)(2,1)S(1)} %bitcast.216), channel_id=1, source_target_pairs={{8,0},{9,1},{10,2},{11,3},{12,4},{13,5},{14,6},{15,7},{16,8},{17,9... | collective-permute-start | bytes 884744 | tf_op jit(solution)/shard_map/ppermute | solution.py:35
  19.2 61.7 %collective-permute-start.27 = (bf16[192,768]{1,0:T(8,128)(2,1)S(1)}, bf16[192,768]{1,0:T(8,128)(2,1)}, u32[]{:S(2)}, u32[]{:S(2)}) collective-permute-start(bf16[192,768]{1,0:T(8,128)(2,1)S(1)} %bitcast.217), channel_id=1, source_target_pairs={{0,8},{1,9},{2,10},{3,11},{4,12},{5,13},{6,14},{7,15},{8,16},{9,17... | collective-permute-start | bytes 884744 | tf_op jit(solution)/shard_map/ppermute | solution.py:35
  23.9 51.7 %collective-permute-start.48 = (bf16[384,384]{1,0:T(8,128)(2,1)}, bf16[384,384]{1,0:T(8,128)(2,1)}, u32[]{:S(2)}, u32[]{:S(2)}) collective-permute-start(bf16[384,384]{1,0:T(8,128)(2,1)} %get-tuple-element.52), channel_id=1, source_target_pairs={{0,3},{1,2},{2,1},{3,0},{4,7},{5,6},{6,5},{7,4},{8,11},{9,10},{10,... | collective-permute-start | bytes 884744 | tf_op jit(solution)/shard_map/ppermute | solution.py:35
  25.4 58.0 %collective-permute-start.19 = (bf16[192,768]{1,0:T(8,128)(2,1)S(1)}, bf16[192,768]{1,0:T(8,128)(2,1)S(1)}, u32[]{:S(2)}, u32[]{:S(2)}) collective-permute-start(bf16[192,768]{1,0:T(8,128)(2,1)S(1)} %bitcast.219), channel_id=1, source_target_pairs={{8,0},{9,1},{10,2},{11,3},{12,4},{13,5},{14,6},{15,7},{16,8},{17,9... | collective-permute-start | bytes 884744 | tf_op jit(solution)/shard_map/ppermute | solution.py:35
  28.5 56.2 %collective-permute-start.18 = (bf16[192,768]{1,0:T(8,128)(2,1)S(1)}, bf16[192,768]{1,0:T(8,128)(2,1)S(1)}, u32[]{:S(2)}, u32[]{:S(2)}) collective-permute-start(bf16[192,768]{1,0:T(8,128)(2,1)S(1)} %bitcast.220), channel_id=1, source_target_pairs={{0,8},{1,9},{2,10},{3,11},{4,12},{5,13},{6,14},{7,15},{8,16},{9,17... | collective-permute-start | bytes 884744 | tf_op jit(solution)/shard_map/ppermute | solution.py:35
  112.5 62.7 %collective-permute-start.42 = (bf16[384,384]{1,0:T(8,128)(2,1)S(1)}, bf16[384,384]{1,0:T(8,128)(2,1)S(1)}, u32[]{:S(2)}, u32[]{:S(2)}) collective-permute-start(bf16[384,384]{1,0:T(8,128)(2,1)S(1)} %get-tuple-element.57), channel_id=1, source_target_pairs={{0,16},{1,17},{2,18},{3,19},{4,20},{5,21},{6,22},{7,23},{8,24},{9,... | collective-permute-start | bytes 884744 | tf_op jit(solution)/shard_map/ppermute | solution.py:35
  115.3 62.3 %collective-permute-start.44 = (bf16[384,384]{1,0:T(8,128)(2,1)S(1)}, bf16[384,384]{1,0:T(8,128)(2,1)S(1)}, u32[]{:S(2)}, u32[]{:S(2)}) collective-permute-start(bf16[384,384]{1,0:T(8,128)(2,1)S(1)} %get-tuple-element.55), channel_id=1, source_target_pairs={{0,24},{1,25},{2,26},{3,27},{4,28},{5,29},{6,30},{7,31},{8,16},{9,... | collective-permute-start | bytes 884744 | tf_op jit(solution)/shard_map/ppermute | solution.py:35
  118.8 61.3 %collective-permute-start.49 = (bf16[384,384]{1,0:T(8,128)(2,1)S(1)}, bf16[384,384]{1,0:T(8,128)(2,1)S(1)}, u32[]{:S(2)}, u32[]{:S(2)}) collective-permute-start(bf16[384,384]{1,0:T(8,128)(2,1)S(1)} %get-tuple-element.48), channel_id=1, source_target_pairs={{0,4},{1,5},{2,6},{3,7},{4,0},{5,1},{6,2},{7,3},{8,12},{9,13},{10,... | collective-permute-start | bytes 884744 | tf_op jit(solution)/shard_map/ppermute | solution.py:35
  119.5 24.6 %collective-permute-start.32 = (bf16[192,768]{1,0:T(8,128)(2,1)S(1)}, bf16[192,768]{1,0:T(8,128)(2,1)S(1)}, u32[]{:S(2)}, u32[]{:S(2)}) collective-permute-start(bf16[192,768]{1,0:T(8,128)(2,1)S(1)} %collective-permute-done.31), channel_id=1, source_target_pairs={{0,8},{1,9},{2,10},{3,11},{4,12},{5,13},{6,14},{7,15},{8,16},{9,17... | collective-permute-start | bytes 884744 | tf_op jit(solution)/shard_map/ppermute | solution.py:35
  125.1 25.3 %collective-permute-start.23 = (bf16[192,768]{1,0:T(8,128)(2,1)S(1)}, bf16[192,768]{1,0:T(8,128)(2,1)S(1)}, u32[]{:S(2)}, u32[]{:S(2)}) collective-permute-start(bf16[192,768]{1,0:T(8,128)(2,1)S(1)} %collective-permute-done.22), channel_id=1, source_target_pairs={{0,8},{1,9},{2,10},{3,11},{4,12},{5,13},{6,14},{7,15},{8,16},{9,17... | collective-permute-start | bytes 884744 | tf_op jit(solution)/shard_map/ppermute | solution.py:35
  182.3 46.9 %collective-permute-start.34 = (bf16[4,192,768]{2,1,0:T(8,128)(2,1)S(1)}, bf16[4,192,768]{2,1,0:T(8,128)(2,1)S(1)}, u32[]{:S(2)}, u32[]{:S(2)}) collective-permute-start(bf16[4,192,768]{2,1,0:T(8,128)(2,1)S(1)} %pad_maximum_fusion.3.refs_16_), channel_id=1, source_target_pairs={{0,2},{1,3},{2,0},{3,1},{4,6},{5,7},{6,4},{7,5},{8,10},{9,11},{10,... | collective-permute-start | bytes 3538952 | tf_op jit(solution)/shard_map/ppermute | solution.py:35
  185.2 47.6 %collective-permute-start.25 = (bf16[4,192,768]{2,1,0:T(8,128)(2,1)S(1)}, bf16[4,192,768]{2,1,0:T(8,128)(2,1)S(1)}, u32[]{:S(2)}, u32[]{:S(2)}) collective-permute-start(bf16[4,192,768]{2,1,0:T(8,128)(2,1)S(1)} %pad_maximum_fusion.2.refs_12_), channel_id=1, source_target_pairs={{0,2},{1,3},{2,0},{3,1},{4,6},{5,7},{6,4},{7,5},{8,10},{9,11},{10,... | collective-permute-start | bytes 3538952 | tf_op jit(solution)/shard_map/ppermute | solution.py:35
  203.5 20.7 %collective-permute-start.53 = (bf16[384,384]{1,0:T(8,128)(2,1)S(1)}, bf16[384,384]{1,0:T(8,128)(2,1)S(1)}, u32[]{:S(2)}, u32[]{:S(2)}) collective-permute-start(bf16[384,384]{1,0:T(8,128)(2,1)S(1)} %collective-permute-done.52), channel_id=1, source_target_pairs={{0,4},{1,5},{2,6},{3,7},{4,0},{5,1},{6,2},{7,3},{8,12},{9,13},{10,... | collective-permute-start | bytes 884744 | tf_op jit(solution)/shard_map/ppermute | solution.py:35
  203.6 23.8 %collective-permute-start.55 = (bf16[384,384]{1,0:T(8,128)(2,1)S(1)}, bf16[384,384]{1,0:T(8,128)(2,1)S(1)}, u32[]{:S(2)}, u32[]{:S(2)}) collective-permute-start(bf16[384,384]{1,0:T(8,128)(2,1)S(1)} %collective-permute-done.54), channel_id=1, source_target_pairs={{0,4},{1,5},{2,6},{3,7},{4,0},{5,1},{6,2},{7,3},{8,12},{9,13},{10,... | collective-permute-start | bytes 884744 | tf_op jit(solution)/shard_map/ppermute | solution.py:35
  208.0 25.1 %collective-permute-start.33 = (bf16[4,192,768]{2,1,0:T(8,128)(2,1)S(1)}, bf16[4,192,768]{2,1,0:T(8,128)(2,1)S(1)}, u32[]{:S(2)}, u32[]{:S(2)}) collective-permute-start(bf16[4,192,768]{2,1,0:T(8,128)(2,1)S(1)} %pad_maximum_fusion.3.refs_16_), channel_id=1, source_target_pairs={{0,1},{1,0},{2,3},{3,2},{4,5},{5,4},{6,7},{7,6},{8,9},{9,8},{10,11... | collective-permute-start | bytes 3538952 | tf_op jit(solution)/shard_map/ppermute | solution.py:35
  224.2 21.7 %collective-permute-start.24 = (bf16[4,192,768]{2,1,0:T(8,128)(2,1)S(1)}, bf16[4,192,768]{2,1,0:T(8,128)(2,1)S(1)}, u32[]{:S(2)}, u32[]{:S(2)}) collective-permute-start(bf16[4,192,768]{2,1,0:T(8,128)(2,1)S(1)} %pad_maximum_fusion.2.refs_12_), channel_id=1, source_target_pairs={{0,1},{1,0},{2,3},{3,2},{4,5},{5,4},{6,7},{7,6},{8,9},{9,8},{10,11... | collective-permute-start | bytes 3538952 | tf_op jit(solution)/shard_map/ppermute | solution.py:35
  227.4 28.5 %collective-permute-start.16 = (bf16[4,192,768]{2,1,0:T(8,128)(2,1)S(1)}, bf16[4,192,768]{2,1,0:T(8,128)(2,1)S(1)}, u32[]{:S(2)}, u32[]{:S(2)}) collective-permute-start(bf16[4,192,768]{2,1,0:T(8,128)(2,1)S(1)} %pad_maximum_fusion.1.refs_8_), channel_id=1, source_target_pairs={{0,2},{1,3},{2,0},{3,1},{4,6},{5,7},{6,4},{7,5},{8,10},{9,11},{10,... | collective-permute-start | bytes 3538952 | tf_op jit(solution)/shard_map/ppermute | solution.py:35
  229.3 39.7 %collective-permute-start.15 = (bf16[4,192,768]{2,1,0:T(8,128)(2,1)S(1)}, bf16[4,192,768]{2,1,0:T(8,128)(2,1)S(1)}, u32[]{:S(2)}, u32[]{:S(2)}) collective-permute-start(bf16[4,192,768]{2,1,0:T(8,128)(2,1)S(1)} %pad_maximum_fusion.1.refs_8_), channel_id=1, source_target_pairs={{0,1},{1,0},{2,3},{3,2},{4,5},{5,4},{6,7},{7,6},{8,9},{9,8},{10,11... | collective-permute-start | bytes 3538952 | tf_op jit(solution)/shard_map/ppermute | solution.py:35
  232.7 48.4 %collective-permute-start.7 = (bf16[4,192,768]{2,1,0:T(8,128)(2,1)S(1)}, bf16[4,192,768]{2,1,0:T(8,128)(2,1)S(1)}, u32[]{:S(2)}, u32[]{:S(2)}) collective-permute-start(bf16[4,192,768]{2,1,0:T(8,128)(2,1)S(1)} %pad_maximum_fusion.refs_4_), channel_id=1, source_target_pairs={{0,2},{1,3},{2,0},{3,1},{4,6},{5,7},{6,4},{7,5},{8,10},{9,11},{10,... | collective-permute-start | bytes 3538952 | tf_op jit(solution)/shard_map/ppermute | solution.py:35
  233.1 55.1 %collective-permute-start.6 = (bf16[4,192,768]{2,1,0:T(8,128)(2,1)S(1)}, bf16[4,192,768]{2,1,0:T(8,128)(2,1)S(1)}, u32[]{:S(2)}, u32[]{:S(2)}) collective-permute-start(bf16[4,192,768]{2,1,0:T(8,128)(2,1)S(1)} %pad_maximum_fusion.refs_4_), channel_id=1, source_target_pairs={{0,1},{1,0},{2,3},{3,2},{4,5},{5,4},{6,7},{7,6},{8,9},{9,8},{10,11... | collective-permute-start | bytes 3538952 | tf_op jit(solution)/shard_map/ppermute | solution.py:35
  245.9 42.4 %collective-permute-start.35 = (bf16[4,192,768]{2,1,0:T(8,128)(2,1)S(1)}, bf16[4,192,768]{2,1,0:T(8,128)(2,1)S(1)}, u32[]{:S(2)}, u32[]{:S(2)}) collective-permute-start(bf16[4,192,768]{2,1,0:T(8,128)(2,1)S(1)} %collective-permute-done.34.refs_18_), channel_id=1, source_target_pairs={{0,1},{1,0},{2,3},{3,2},{4,5},{5,4},{6,7},{7,6},{8,9},{9,8},{10,11... | collective-permute-start | bytes 3538952 | tf_op jit(solution)/shard_map/ppermute | solution.py:35
  255.9 32.4 %collective-permute-start.26 = (bf16[4,192,768]{2,1,0:T(8,128)(2,1)S(1)}, bf16[4,192,768]{2,1,0:T(8,128)(2,1)S(1)}, u32[]{:S(2)}, u32[]{:S(2)}) collective-permute-start(bf16[4,192,768]{2,1,0:T(8,128)(2,1)S(1)} %collective-permute-done.25.refs_14_), channel_id=1, source_target_pairs={{0,1},{1,0},{2,3},{3,2},{4,5},{5,4},{6,7},{7,6},{8,9},{9,8},{10,11... | collective-permute-start | bytes 3538952 | tf_op jit(solution)/shard_map/ppermute | solution.py:35
  269.0 19.3 %collective-permute-start.17 = (bf16[4,192,768]{2,1,0:T(8,128)(2,1)S(1)}, bf16[4,192,768]{2,1,0:T(8,128)(2,1)S(1)}, u32[]{:S(2)}, u32[]{:S(2)}) collective-permute-start(bf16[4,192,768]{2,1,0:T(8,128)(2,1)S(1)} %collective-permute-done.16.refs_10_), channel_id=1, source_target_pairs={{0,1},{1,0},{2,3},{3,2},{4,5},{5,4},{6,7},{7,6},{8,9},{9,8},{10,11... | collective-permute-start | bytes 3538952 | tf_op jit(solution)/shard_map/ppermute | solution.py:35
  310.4 20.1 %collective-permute-start.60 = (f16[384,768]{0,1:T(8,128)(2,1)S(1)}, f16[384,768]{0,1:T(8,128)(2,1)S(1)}, u32[]{:S(2)}, u32[]{:S(2)}) collective-permute-start(f16[384,768]{0,1:T(8,128)(2,1)S(1)} %get-tuple-element.25), channel_id=1, source_target_pairs={{0,0},{1,1},{2,4},{3,5},{4,2},{5,3},{6,6},{7,7},{8,8},{9,9},{10,12... | collective-permute-start | bytes 1769480 | tf_op jit(solution)/shard_map/ppermute | solution.py:35
  316.0 38.1 %collective-permute-start.61 = (f16[384,768]{0,1:T(8,128)(2,1)S(1)}, f16[384,768]{0,1:T(8,128)(2,1)S(1)}, u32[]{:S(2)}, u32[]{:S(2)}) collective-permute-start(f16[384,768]{0,1:T(8,128)(2,1)S(1)} %get-tuple-element.24), channel_id=1, source_target_pairs={{0,1},{1,0},{2,5},{3,4},{4,3},{5,2},{6,7},{7,6},{8,9},{9,8},{10,13... | collective-permute-start | bytes 1769480 | tf_op jit(solution)/shard_map/ppermute | solution.py:35
  316.1 50.6 %collective-permute-start.62 = (f16[384,768]{0,1:T(8,128)(2,1)S(1)}, f16[384,768]{0,1:T(8,128)(2,1)S(1)}, u32[]{:S(2)}, u32[]{:S(2)}) collective-permute-start(f16[384,768]{0,1:T(8,128)(2,1)S(1)} %get-tuple-element.23), channel_id=1, source_target_pairs={{0,2},{1,3},{2,6},{3,7},{4,0},{5,1},{6,4},{7,5},{8,10},{9,11},{10,... | collective-permute-start | bytes 1769480 | tf_op jit(solution)/shard_map/ppermute | solution.py:35
  316.1 95.6 %collective-permute-start.63 = (f16[384,768]{0,1:T(8,128)(2,1)}, f16[384,768]{0,1:T(8,128)(2,1)}, u32[]{:S(2)}, u32[]{:S(2)}) collective-permute-start(f16[384,768]{0,1:T(8,128)(2,1)} %get-tuple-element.22), channel_id=1, source_target_pairs={{0,3},{1,2},{2,7},{3,6},{4,1},{5,0},{6,5},{7,4},{8,11},{9,10},{10,... | collective-permute-start | bytes 1769480 | tf_op jit(solution)/shard_map/ppermute | solution.py:35
  319.3 101.1 %collective-permute-start.56 = (f16[768,384]{1,0:T(8,128)(2,1)}, f16[768,384]{1,0:T(8,128)(2,1)}, u32[]{:S(2)}, u32[]{:S(2)}) collective-permute-start(f16[768,384]{1,0:T(8,128)(2,1)} %get-tuple-element.28), channel_id=1, source_target_pairs={{0,0},{1,8},{2,16},{3,24},{4,4},{5,12},{6,20},{7,28},{8,1},{9,9},{... | collective-permute-start | bytes 1769480 | tf_op jit(solution)/shard_map/ppermute | solution.py:35
  330.6 91.2 %collective-permute-start.57 = (f16[768,384]{1,0:T(8,128)(2,1)}, f16[768,384]{1,0:T(8,128)(2,1)}, u32[]{:S(2)}, u32[]{:S(2)}) collective-permute-start(f16[768,384]{1,0:T(8,128)(2,1)} %get-tuple-element.27), channel_id=1, source_target_pairs={{0,8},{1,0},{2,24},{3,16},{4,12},{5,4},{6,28},{7,20},{8,9},{9,1},{... | collective-permute-start | bytes 1769480 | tf_op jit(solution)/shard_map/ppermute | solution.py:35
  354.1 69.0 %collective-permute-start.58 = (f16[768,384]{1,0:T(8,128)(2,1)}, f16[768,384]{1,0:T(8,128)(2,1)}, u32[]{:S(2)}, u32[]{:S(2)}) collective-permute-start(f16[768,384]{1,0:T(8,128)(2,1)} %get-tuple-element.26), channel_id=1, source_target_pairs={{0,16},{1,24},{2,0},{3,8},{4,20},{5,28},{6,4},{7,12},{8,17},{9,25}... | collective-permute-start | bytes 1769480 | tf_op jit(solution)/shard_map/ppermute | solution.py:35
  367.6 56.7 %collective-permute-start.59 = (f16[768,384]{1,0:T(8,128)(2,1)}, f16[768,384]{1,0:T(8,128)(2,1)}, u32[]{:S(2)}, u32[]{:S(2)}) collective-permute-start(f16[768,384]{1,0:T(8,128)(2,1)} %get-tuple-element.21), channel_id=1, source_target_pairs={{0,24},{1,16},{2,8},{3,0},{4,28},{5,20},{6,12},{7,4},{8,25},{9,17}... | collective-permute-start | bytes 1769480 | tf_op jit(solution)/shard_map/ppermute | solution.py:35
  437.1 24.9 %collective-permute-start.76 = (bf16[384,384]{1,0:T(8,128)(2,1)}, bf16[384,384]{1,0:T(8,128)(2,1)}, u32[]{:S(2)}, u32[]{:S(2)}) collective-permute-start(bf16[384,384]{1,0:T(8,128)(2,1)} %get-tuple-element.36), channel_id=1, source_target_pairs={{0,3},{1,2},{2,1},{3,0},{4,7},{5,6},{6,5},{7,4},{8,11},{9,10},{10,... | collective-permute-start | bytes 884744 | tf_op jit(solution)/shard_map/ppermute | solution.py:35
  454.8 25.9 %collective-permute-start.72 = (bf16[384,384]{1,0:T(8,128)(2,1)S(1)}, bf16[384,384]{1,0:T(8,128)(2,1)S(1)}, u32[]{:S(2)}, u32[]{:S(2)}) collective-permute-start(bf16[384,384]{1,0:T(8,128)(2,1)S(1)} %get-tuple-element.39), channel_id=1, source_target_pairs={{0,24},{1,25},{2,26},{3,27},{4,28},{5,29},{6,30},{7,31},{8,16},{9,... | collective-permute-start | bytes 884744 | tf_op jit(solution)/shard_map/ppermute | solution.py:35
  464.0 35.0 %collective-permute-start.80 = (bf16[384,384]{1,0:T(8,128)(2,1)S(1)}, bf16[384,384]{1,0:T(8,128)(2,1)S(1)}, u32[]{:S(2)}, u32[]{:S(2)}) collective-permute-start(bf16[384,384]{1,0:T(8,128)(2,1)S(1)} %get-tuple-element.33), channel_id=1, source_target_pairs={{0,16},{1,17},{2,18},{3,19},{4,20},{5,21},{6,22},{7,23},{8,24},{9,... | collective-permute-start | bytes 884744 | tf_op jit(solution)/shard_map/ppermute | solution.py:35
  468.8 32.0 %collective-permute-start.82 = (bf16[384,384]{1,0:T(8,128)(2,1)S(1)}, bf16[384,384]{1,0:T(8,128)(2,1)S(1)}, u32[]{:S(2)}, u32[]{:S(2)}) collective-permute-start(bf16[384,384]{1,0:T(8,128)(2,1)S(1)} %get-tuple-element.31), channel_id=1, source_target_pairs={{0,24},{1,25},{2,26},{3,27},{4,28},{5,29},{6,30},{7,31},{8,16},{9,... | collective-permute-start | bytes 884744 | tf_op jit(solution)/shard_map/ppermute | solution.py:35
  480.4 20.4 %collective-permute-start.71 = (bf16[384,384]{1,0:T(8,128)(2,1)S(1)}, bf16[384,384]{1,0:T(8,128)(2,1)S(1)}, u32[]{:S(2)}, u32[]{:S(2)}) collective-permute-start(bf16[384,384]{1,0:T(8,128)(2,1)S(1)} %collective-permute-done.70), channel_id=1, source_target_pairs={{0,4},{1,5},{2,6},{3,7},{4,0},{5,1},{6,2},{7,3},{8,12},{9,13},{10,... | collective-permute-start | bytes 884744 | tf_op jit(solution)/shard_map/ppermute | solution.py:35
  480.7 21.8 %collective-permute-start.77 = (bf16[384,384]{1,0:T(8,128)(2,1)S(1)}, bf16[384,384]{1,0:T(8,128)(2,1)S(1)}, u32[]{:S(2)}, u32[]{:S(2)}) collective-permute-start(bf16[384,384]{1,0:T(8,128)(2,1)S(1)} %get-tuple-element.32), channel_id=1, source_target_pairs={{0,4},{1,5},{2,6},{3,7},{4,0},{5,1},{6,2},{7,3},{8,12},{9,13},{10,... | collective-permute-start | bytes 884744 | tf_op jit(solution)/shard_map/ppermute | solution.py:35
  482.2 20.2 %collective-permute-start.73 = (bf16[384,384]{1,0:T(8,128)(2,1)S(1)}, bf16[384,384]{1,0:T(8,128)(2,1)S(1)}, u32[]{:S(2)}, u32[]{:S(2)}) collective-permute-start(bf16[384,384]{1,0:T(8,128)(2,1)S(1)} %collective-permute-done.72), channel_id=1, source_target_pairs={{0,4},{1,5},{2,6},{3,7},{4,0},{5,1},{6,2},{7,3},{8,12},{9,13},{10,... | collective-permute-start | bytes 884744 | tf_op jit(solution)/shard_map/ppermute | solution.py:35
  500.8 18.9 %collective-permute-start.83 = (bf16[384,384]{1,0:T(8,128)(2,1)S(1)}, bf16[384,384]{1,0:T(8,128)(2,1)S(1)}, u32[]{:S(2)}, u32[]{:S(2)}) collective-permute-start(bf16[384,384]{1,0:T(8,128)(2,1)S(1)} %collective-permute-done.82), channel_id=1, source_target_pairs={{0,4},{1,5},{2,6},{3,7},{4,0},{5,1},{6,2},{7,3},{8,12},{9,13},{10,... | collective-permute-start | bytes 884744 | tf_op jit(solution)/shard_map/ppermute | solution.py:35
  541.0 19.7 %collective-permute-start.88 = (f16[384,768]{0,1:T(8,128)(2,1)S(1)}, f16[384,768]{0,1:T(8,128)(2,1)S(1)}, u32[]{:S(2)}, u32[]{:S(2)}) collective-permute-start(f16[384,768]{0,1:T(8,128)(2,1)S(1)} %get-tuple-element.15), channel_id=1, source_target_pairs={{0,0},{1,1},{2,4},{3,5},{4,2},{5,3},{6,6},{7,7},{8,8},{9,9},{10,12... | collective-permute-start | bytes 1769480 | tf_op jit(solution)/shard_map/ppermute | solution.py:35
  547.4 30.0 %collective-permute-start.89 = (f16[384,768]{0,1:T(8,128)(2,1)S(1)}, f16[384,768]{0,1:T(8,128)(2,1)S(1)}, u32[]{:S(2)}, u32[]{:S(2)}) collective-permute-start(f16[384,768]{0,1:T(8,128)(2,1)S(1)} %get-tuple-element.14), channel_id=1, source_target_pairs={{0,1},{1,0},{2,5},{3,4},{4,3},{5,2},{6,7},{7,6},{8,9},{9,8},{10,13... | collective-permute-start | bytes 1769480 | tf_op jit(solution)/shard_map/ppermute | solution.py:35
  549.0 41.0 %collective-permute-start.90 = (f16[384,768]{0,1:T(8,128)(2,1)S(1)}, f16[384,768]{0,1:T(8,128)(2,1)S(1)}, u32[]{:S(2)}, u32[]{:S(2)}) collective-permute-start(f16[384,768]{0,1:T(8,128)(2,1)S(1)} %get-tuple-element.13), channel_id=1, source_target_pairs={{0,2},{1,3},{2,6},{3,7},{4,0},{5,1},{6,4},{7,5},{8,10},{9,11},{10,... | collective-permute-start | bytes 1769480 | tf_op jit(solution)/shard_map/ppermute | solution.py:35
  549.0 97.8 %collective-permute-start.91 = (f16[384,768]{0,1:T(8,128)(2,1)}, f16[384,768]{0,1:T(8,128)(2,1)}, u32[]{:S(2)}, u32[]{:S(2)}) collective-permute-start(f16[384,768]{0,1:T(8,128)(2,1)} %get-tuple-element.12), channel_id=1, source_target_pairs={{0,3},{1,2},{2,7},{3,6},{4,1},{5,0},{6,5},{7,4},{8,11},{9,10},{10,... | collective-permute-start | bytes 1769480 | tf_op jit(solution)/shard_map/ppermute | solution.py:35
  550.6 103.2 %collective-permute-start.84 = (f16[768,384]{1,0:T(8,128)(2,1)}, f16[768,384]{1,0:T(8,128)(2,1)}, u32[]{:S(2)}, u32[]{:S(2)}) collective-permute-start(f16[768,384]{1,0:T(8,128)(2,1)} %get-tuple-element.18), channel_id=1, source_target_pairs={{0,0},{1,8},{2,16},{3,24},{4,4},{5,12},{6,20},{7,28},{8,1},{9,9},{... | collective-permute-start | bytes 1769480 | tf_op jit(solution)/shard_map/ppermute | solution.py:35
  560.7 94.8 %collective-permute-start.85 = (f16[768,384]{1,0:T(8,128)(2,1)}, f16[768,384]{1,0:T(8,128)(2,1)}, u32[]{:S(2)}, u32[]{:S(2)}) collective-permute-start(f16[768,384]{1,0:T(8,128)(2,1)} %get-tuple-element.17), channel_id=1, source_target_pairs={{0,8},{1,0},{2,24},{3,16},{4,12},{5,4},{6,28},{7,20},{8,9},{9,1},{... | collective-permute-start | bytes 1769480 | tf_op jit(solution)/shard_map/ppermute | solution.py:35
  577.3 79.3 %collective-permute-start.86 = (f16[768,384]{1,0:T(8,128)(2,1)}, f16[768,384]{1,0:T(8,128)(2,1)}, u32[]{:S(2)}, u32[]{:S(2)}) collective-permute-start(f16[768,384]{1,0:T(8,128)(2,1)} %get-tuple-element.16), channel_id=1, source_target_pairs={{0,16},{1,24},{2,0},{3,8},{4,20},{5,28},{6,4},{7,12},{8,17},{9,25}... | collective-permute-start | bytes 1769480 | tf_op jit(solution)/shard_map/ppermute | solution.py:35
  590.8 67.1 %collective-permute-start.87 = (f16[768,384]{1,0:T(8,128)(2,1)}, f16[768,384]{1,0:T(8,128)(2,1)}, u32[]{:S(2)}, u32[]{:S(2)}) collective-permute-start(f16[768,384]{1,0:T(8,128)(2,1)} %get-tuple-element.11), channel_id=1, source_target_pairs={{0,24},{1,16},{2,8},{3,0},{4,28},{5,20},{6,12},{7,4},{8,25},{9,17}... | collective-permute-start | bytes 1769480 | tf_op jit(solution)/shard_map/ppermute | solution.py:35
  (81 other events, 1331.2 us)

commit v2 on v1

v2 whole, which is shorter than its diff:
```python
import jax
import jax.numpy as jnp
from jax import lax
from jax.experimental import pallas as pl
from jax.experimental.pallas import tpu as pltpu
from jax.sharding import PartitionSpec as P

STEPS = 2
COUPLING_MAX = 0.15625
DENOMINATOR_MIN = 1.5
HALF_TOP = 60000.0
AXES = ("alpha", "beta")
ROW_CHUNKS = 3


class Grid:
    def __init__(self, alpha_devices, beta_devices):
        self.bands = beta_devices
        self.lanes = alpha_devices // beta_devices
        self.majors = beta_devices // 2
        self.per_lane = self.majors // self.lanes
        self.places = [
            (band, lane, major, minor)
            for band in range(self.bands)
            for lane in range(self.lanes)
            for major in range(self.majors)
            for minor in range(2)
        ]

    def index(self, band, lane, major, minor):
        return ((band * self.lanes + lane) * self.majors + major) * 2 + minor

    def send(self, value, where):
        pairs = [(self.index(*place), self.index(*where(*place))) for place in self.places]
        if all(source == target for source, target in pairs):
            return value
        return lax.ppermute(value, AXES, pairs)


def largest_anywhere(grid, value):
    devices = len(grid.places)
    largest = jnp.full((8, 128), value)
    bit = 1
    while bit < devices:
        pairs = [(device, device ^ bit) for device in range(devices)]
        largest = jnp.maximum(largest, lax.ppermute(largest, AXES, pairs))
        bit *= 2
    return largest[0, 0]


def gather_bands(grid, own, band):
    held = own[None]
    order = [[z] for z in range(grid.bands)]
    width = 2
    while width <= grid.bands:
        half = width // 2
        moving = held
        origin = list(range(grid.bands))
        kept, kept_origin = None, [None] * grid.bands
        for hop in range(half):
            partner = list(range(grid.bands))
            for base in range(0, grid.bands, width):
                low, high = base + half - 1, base + half
                if hop == 0:
                    pairs = [(low, high)]
                else:
                    pairs = [(low - hop + 1, low - hop), (high + hop - 1, high + hop)]
                for one, other in pairs:
                    partner[one], partner[other] = other, one
            moving = grid.send(moving, lambda z, x, m, n: (partner[z], x, m, n))
            origin = [origin[partner[z]] for z in range(grid.bands)]
            takes = [(half - 1 - z % width if z % width < half else z % width - half) == hop for z in range(grid.bands)]
            kept = moving if kept is None else jnp.where(jnp.array(takes)[band], moving, kept)
            kept_origin = [origin[z] if takes[z] else kept_origin[z] for z in range(grid.bands)]
        held = jnp.concatenate([held, kept])
        order = [order[z] + order[kept_origin[z]] for z in range(grid.bands)]
        width *= 2
    return held, order


def gather_couplings(grid, coupling, band, major, minor):
    rows, slots, _ = coupling.shape
    majors = grid.majors
    chunk = rows // (2 * majors)
    own = lax.dynamic_slice_in_dim(coupling, (minor * majors + major) * chunk, chunk, 0)
    gathered = []
    for slot in range(slots):
        line, order = gather_bands(grid, own[:, slot], band)
        pieces = {0: line}
        bit = majors // 2
        while bit:
            received = {
                key ^ bit: grid.send(piece, lambda z, x, m, n: (z, x, m ^ bit, n)) for key, piece in pieces.items()
            }
            pieces.update(received)
            bit //= 2
        pieces = [pieces[key] for key in range(majors)]
        if chunk % 16:
            whole = jnp.take(jnp.stack(pieces), major ^ jnp.arange(majors), axis=0)
            pieces = [whole.transpose(1, 0, 2, 3).reshape(grid.bands, rows // 2, whole.shape[3])]
        gathered.append(pieces)
    return gathered, jnp.array(order, jnp.int32)[band]


def to_columns(grid, half, band, lane, major, minor):
    rows, cols = half.shape
    bands, lanes, majors = grid.bands, grid.lanes, grid.majors
    strip = cols // majors
    part = rows // ROW_CHUNKS
    whole = jnp.zeros((bands, lanes, rows, strip), half.dtype)
    for chunk in range(ROW_CHUNKS):
        block = half[chunk * part : (chunk + 1) * part]
        first = []
        for key in range(majors):
            piece = lax.dynamic_slice(block, (0, (major ^ key) * strip), (part, strip))
            first.append(grid.send(piece, lambda z, x, m, n: (z, x, m ^ key, n)))
        first = jnp.stack(first)
        second = []
        for key in range(majors):
            piece = lax.dynamic_index_in_dim(first, (band // 2) ^ key ^ major, 0, keepdims=False)
            second.append(grid.send(piece, lambda z, x, m, n: ((z // 2 ^ key) * 2 + n, x, m, z % 2)))
        second = jnp.stack(second)
        for turn in range(lanes):
            third = grid.send(second, lambda z, x, m, n: (z, (x + turn) % lanes, m, n))
            for flip in range(2):
                fourth = third if flip == 0 else grid.send(third, lambda z, x, m, n: (z, x, m, 1 - n))
                for key in range(majors):
                    place = ((band // 2 ^ key) * 2 + (minor ^ flip), (lane - turn) % lanes, chunk * part, 0)
                    whole = lax.dynamic_update_slice(whole, fourth[key][None, None], place)
    return whole.reshape(bands * lanes * rows, strip)


def product_kernel(slots, pieces, order_ref, column_ref, count_ref, offset_ref, *refs):
    band = order_ref[pl.program_id(0)]
    coeff_ref, out_ref, mirror_ref = refs[slots * pieces :]
    chunk, tile = refs[0].shape[1:]

    def product(slot):
        first = pl.multiple_of(column_ref[band * slots + slot] * tile, tile)
        left = jnp.concatenate([refs[slot * pieces + piece][0] for piece in range(pieces)], axis=0)
        return jnp.dot(left, coeff_ref[pl.ds(first, tile), :], preferred_element_type=jnp.float32)

    def store(value, add):
        for piece in range(pieces):
            place = pl.ds(pl.multiple_of(offset_ref[piece], chunk), chunk)
            part = value[piece * chunk : (piece + 1) * chunk]
            out_ref[0, place, :] = out_ref[0, place, :] + part if add else part

    store(product(0), False)
    for slot in range(1, slots):

        @pl.when(slot < count_ref[band])
        def _():
            store(product(slot), True)

    mirror_ref[0] = out_ref[0].T


def products(couplings, columns, order, tile_columns, counts, offsets):
    slots, pieces = len(couplings), len(couplings[0])
    bands, chunk, tile = couplings[0][0].shape
    strip = columns.shape[1]
    rows = pieces * chunk
    spec = pl.BlockSpec((1, chunk, tile), lambda i, *_: (i, 0, 0))
    return pl.pallas_call(
        lambda *refs: product_kernel(slots, pieces, *refs),
        grid_spec=pltpu.PrefetchScalarGridSpec(
            num_scalar_prefetch=4,
            grid=(bands,),
            in_specs=[spec] * (slots * pieces) + [pl.BlockSpec(columns.shape, lambda i, *_: (0, 0))],
            out_specs=[
                pl.BlockSpec((1, rows, strip), lambda i, order, *_: (order[i], 0, 0)),
                pl.BlockSpec((1, strip, rows), lambda i, order, *_: (order[i], 0, 0)),
            ],
        ),
        out_shape=[
            jax.ShapeDtypeStruct((bands, rows, strip), jnp.float32),
            jax.ShapeDtypeStruct((bands, strip, rows), jnp.float32),
        ],
        compiler_params=pltpu.CompilerParams(vmem_limit_bytes=50 << 20),
        cost_estimate=pl.CostEstimate(
            flops=2 * bands * slots * rows * tile * strip,
            bytes_accessed=2 * bands * slots * rows * tile,
            transcendentals=0,
        ),
    )(order, tile_columns, counts, offsets, *[piece for slot in couplings for piece in slot], columns)


def bring_home(grid, sigma, mirrored, scale, band, lane, major, minor):
    bands, part, strip = sigma.shape
    rows, per_lane = 2 * part, grid.per_lane
    beta = major * 2 + minor
    direct = jnp.zeros((rows, grid.majors * strip), jnp.float16)
    mirror = jnp.zeros((rows, grid.majors * strip), jnp.float16)
    for key in range(bands):
        piece = lax.dynamic_index_in_dim(sigma, beta ^ key, 0, keepdims=False)
        piece = (piece * scale).astype(jnp.float16)
        piece = grid.send(piece, lambda z, x, m, n: ((m * 2 + n) ^ key, x, z // 2, z % 2))
        source = band ^ key
        direct = lax.dynamic_update_slice(direct, piece, ((source % 2) * part, (source // 2) * strip))

    def target(x, m, n):
        return (x * per_lane + m % per_lane) * 2 + n

    for key in range(bands):
        piece = lax.dynamic_index_in_dim(mirrored, target(lane, major, minor) ^ key, 0, keepdims=False)
        piece = (piece * scale).astype(jnp.float16)
        piece = grid.send(
            piece,
            lambda z, x, m, n: (z, m // per_lane, (target(x, m, n) ^ key) // 2, (target(x, m, n) ^ key) % 2),
        )
        source = beta ^ key
        place = (source // 2 % per_lane * strip, source // 2 // per_lane * rows + source % 2 * part)
        mirror = lax.dynamic_update_slice(mirror, piece, place)
    return direct, mirror


def body(coeffs, denominator, coupling, tile_cols, tile_count):
    rows = coeffs.shape[0]
    _, slots, tile = coupling.shape
    grid = Grid(lax.axis_size("alpha"), lax.axis_size("beta"))
    alpha, beta = lax.axis_index("alpha"), lax.axis_index("beta")
    band, lane = alpha // grid.lanes, alpha % grid.lanes
    major, minor = beta // 2, beta % 2
    every = jnp.arange(grid.bands, dtype=jnp.int32)
    tile_rows = (every * grid.lanes + lane) * rows // tile
    tile_columns = jnp.take(tile_cols, tile_rows, axis=0).reshape(-1)
    counts = jnp.take(tile_count, tile_rows)
    couplings, order = gather_couplings(grid, coupling, band, major, minor)
    pieces = len(couplings[0])
    offsets = (major ^ jnp.arange(pieces, dtype=jnp.int32)) * (rows // 2 // pieces)
    if pieces == 1:
        offsets = jnp.zeros((1,), jnp.int32)

    growth = slots * tile * COUPLING_MAX
    largest = jnp.maximum(largest_anywhere(grid, jnp.max(jnp.abs(coeffs))), 1e-30)
    current = coeffs
    for step_index in range(STEPS):
        scale = HALF_TOP / (growth * largest)
        largest = largest * (1 + 2 * growth / DENOMINATOR_MIN)
        columns = to_columns(grid, current.astype(jnp.bfloat16), band, lane, major, minor)
        sigma, mirrored = products(couplings, columns, order, tile_columns, counts, offsets)
        direct, mirror = bring_home(grid, sigma, mirrored, scale, band, lane, major, minor)
        total = (direct.astype(jnp.float32) + mirror.astype(jnp.float32)) / scale
        current = current - total / denominator
    return current


def solution(mesh):
    placed = (P("alpha", "beta"), P("alpha", "beta"), P("alpha", None, None), P(), P())
    return jax.shard_map(
        body, mesh=mesh, in_specs=placed, out_specs=P("alpha", "beta"), check_vma=False
    )
```

time: 674 us -> 649 us (0.963)
  the two profiles are of different devices: /device:TPU:3 before, /device:TPU:25 now
where the time goes in v2:
time: 649 us; the launch traced here: 637 us
  waiting for transfers between devices  311 us (48%)
  starting transfers between devices  151 us (23%)
  local copies, waits for them, and re-layouts  108 us (17%)
  other arithmetic  38.2 us (6%)
  Pallas kernels  25.5 us (4%)
    ppermute x68, waiting for transfers between devices, send(): return lax.ppermute(value, AXES, pairs)  294 us
    ppermute x68, starting transfers between devices, send(): return lax.ppermute(value, AXES, pairs)  148 us
    dynamic_update_slice x8, local copies, waits for them, and re-layouts, bring_home(): lax.dynamic_update_slice(direct, piece, (source % 2 * part, source // 2 *...  58.2 us
    pallas_call x2, Pallas kernels, products(): pl.pallas_call(lambda *refs: product_kernel(slots, pieces, *refs), grid_s...  25.5 us
    dynamic_update_slice x48, local copies, waits for them, and re-layouts, to_columns(): whole = lax.dynamic_update_slice(whole, fourth[key][None, None], place)  23.6 us
    ppermute x5, waiting for transfers between devices, largest_anywhere(): largest = jnp.maximum(largest, lax.ppermute(largest, AXES, pairs))  17 us
  transfers between devices with their start and end apart: 73, of which 31 were waited for; matrix products, arithmetic and copies ran while one was open for 18% of the time, Pallas kernels for 0%

profile of v2, /device:TPU:25, one launch (start us, length us, event | category | flops | bytes accessed | tf_op | source)
XLA Modules:
  0.0 636.6 jit_solution(4174270824884751450)
XLA Ops:
  0.0 5.1 fusion.79
  14.1 5.0 constant_dynamic-slice_fusion.9
  24.0 11.8 %collective-permute-done.35 = f32[8,128]{1,0:T(8,128)S(1)} collective-permute-done((f32[8,128]{1,0:T(8,128)S(1)}, f32[8,128]{1,0:T(8,128)S(1)}, u32[]{:S(2)}, u32[]{:S(2)}) %collective-permute-start.35) | collective-permute-done | bytes 4128 | tf_op jit(solution)/shard_map/ppermute | solution.py:46
  55.2 9.8 %collective-permute-done = bf16[1,192,768]{2,1,0:T(8,128)(2,1)S(1)} collective-permute-done((bf16[1,192,768]{2,1,0:T(8,128)(2,1)S(1)}, bf16[1,192,768]{2,1,0:T(8,128)(2,1)S(1)}, u32[]{:S(2)}, u32[]{:S(2)}) %collective-permute-start) | collective-permute-done | bytes 294944 | tf_op jit(solution)/shard_map/ppermute | solution.py:37
  65.7 11.7 %collective-permute-start.24 = (bf16[256,768]{1,0:T(8,128)(2,1)S(1)}, bf16[256,768]{1,0:T(8,128)(2,1)S(1)}, u32[]{:S(2)}, u32[]{:S(2)}) collective-permute-start(bf16[256,768]{1,0:T(8,128)(2,1)S(1)} %get-tuple-element.57), channel_id=1, source_target_pairs={{0,16},{1,24},{2,18},{3,26},{4,20},{5,28},{6,22},{7,30},{8,17},{9,... | collective-permute-start | bytes 1179656 | tf_op jit(solution)/shard_map/ppermute | solution.py:37
  82.8 7.8 %collective-permute-start.30 = (bf16[256,768]{1,0:T(8,128)(2,1)}, bf16[256,768]{1,0:T(8,128)(2,1)S(1)}, u32[]{:S(2)}, u32[]{:S(2)}) collective-permute-start(bf16[256,768]{1,0:T(8,128)(2,1)} %get-tuple-element.53), channel_id=1, source_target_pairs={{0,16},{1,24},{2,18},{3,26},{4,20},{5,28},{6,22},{7,30},{8,17},{9,... | collective-permute-start | bytes 1179656 | tf_op jit(solution)/shard_map/ppermute | solution.py:37
  91.6 19.7 %collective-permute-done.24 = bf16[256,768]{1,0:T(8,128)(2,1)S(1)} collective-permute-done((bf16[256,768]{1,0:T(8,128)(2,1)S(1)}, bf16[256,768]{1,0:T(8,128)(2,1)S(1)}, u32[]{:S(2)}, u32[]{:S(2)}) %collective-permute-start.24) | collective-permute-done | bytes 393248 | tf_op jit(solution)/shard_map/ppermute | solution.py:37
  113.0 12.6 %collective-permute-start.14 = (bf16[2,192,768]{2,1,0:T(8,128)(2,1)S(1)}, bf16[2,192,768]{2,1,0:T(8,128)(2,1)S(1)}, u32[]{:S(2)}, u32[]{:S(2)}) collective-permute-start(bf16[2,192,768]{2,1,0:T(8,128)(2,1)S(1)} %collective-permute-done.13), channel_id=1, source_target_pairs={{0,8},{1,9},{2,10},{3,11},{4,12},{5,13},{6,14},{7,15},{8,0},{9,1},... | collective-permute-start | bytes 1769480 | tf_op jit(solution)/shard_map/ppermute | solution.py:37
  127.2 5.2 collective-permute-done.30
  132.4 11.4 %collective-permute-start.10 = (bf16[2,192,768]{2,1,0:T(8,128)(2,1)}, bf16[2,192,768]{2,1,0:T(8,128)(2,1)S(1)}, u32[]{:S(2)}, u32[]{:S(2)}) collective-permute-start(bf16[2,192,768]{2,1,0:T(8,128)(2,1)} %collective-permute-done.9), channel_id=1, source_target_pairs={{0,8},{1,9},{2,10},{3,11},{4,12},{5,13},{6,14},{7,15},{8,0},{9,1},... | collective-permute-start | bytes 1769480 | tf_op jit(solution)/shard_map/ppermute | solution.py:37
  149.0 10.7 %collective-permute-start.25 = (bf16[2,256,768]{2,1,0:T(8,128)(2,1)}, bf16[2,256,768]{2,1,0:T(8,128)(2,1)S(1)}, u32[]{:S(2)}, u32[]{:S(2)}) collective-permute-start(bf16[2,256,768]{2,1,0:T(8,128)(2,1)} %pad_maximum_fusion.5), channel_id=1, source_target_pairs={{0,1},{1,0},{2,3},{3,2},{4,5},{5,4},{6,7},{7,6},{8,9},{9,8},{10,11... | collective-permute-start | bytes 2359304 | tf_op jit(solution)/shard_map/ppermute | solution.py:37
  159.7 4.5 collective-permute-start.2
  171.3 9.6 %collective-permute-done.2 = bf16[2,192,768]{2,1,0:T(8,128)(2,1)S(1)} collective-permute-done((bf16[2,192,768]{2,1,0:T(8,128)(2,1)S(1)}, bf16[2,192,768]{2,1,0:T(8,128)(2,1)S(1)}, u32[]{:S(2)}, u32[]{:S(2)}) %collective-permute-start.2) | collective-permute-done | bytes 589856 | tf_op jit(solution)/shard_map/ppermute | solution.py:37
  194.4 9.7 %collective-permute-done.32 = bf16[2,256,768]{2,1,0:T(8,128)(2,1)S(1)} collective-permute-done((bf16[2,256,768]{2,1,0:T(8,128)(2,1)S(1)}, bf16[2,256,768]{2,1,0:T(8,128)(2,1)S(1)}, u32[]{:S(2)}, u32[]{:S(2)}) %collective-permute-start.32) | collective-permute-done | bytes 786464 | tf_op jit(solution)/shard_map/ppermute | solution.py:37
  208.1 7.2 %collective-permute-done.15.refs_11_ = bf16[4,192,768]{2,1,0:T(8,128)(2,1)S(1)} collective-permute-done((bf16[4,192,768]{2,1,0:T(8,128)(2,1)S(1)}, bf16[4,192,768]{2,1,0:T(8,128)(2,1)S(1)}, u32[]{:S(2)}, u32[]{:S(2)}) %collective-permute-start.15) | collective-permute-done | bytes 1179680 | tf_op jit(solution)/shard_map/ppermute | solution.py:37
  215.3 25.3 %collective-permute-done.11.refs_9_ = bf16[4,192,768]{2,1,0:T(8,128)(2,1)S(1)} collective-permute-done((bf16[4,192,768]{2,1,0:T(8,128)(2,1)S(1)}, bf16[4,192,768]{2,1,0:T(8,128)(2,1)S(1)}, u32[]{:S(2)}, u32[]{:S(2)}) %collective-permute-start.11) | collective-permute-done | bytes 1179680 | tf_op jit(solution)/shard_map/ppermute | solution.py:37
  240.5 25.3 %collective-permute-done.7.refs_7_ = bf16[4,192,768]{2,1,0:T(8,128)(2,1)S(1)} collective-permute-done((bf16[4,192,768]{2,1,0:T(8,128)(2,1)S(1)}, bf16[4,192,768]{2,1,0:T(8,128)(2,1)S(1)}, u32[]{:S(2)}, u32[]{:S(2)}) %collective-permute-start.7) | collective-permute-done | bytes 1179680 | tf_op jit(solution)/shard_map/ppermute | solution.py:37
  265.8 25.3 %collective-permute-done.3.refs_5_ = bf16[4,192,768]{2,1,0:T(8,128)(2,1)S(1)} collective-permute-done((bf16[4,192,768]{2,1,0:T(8,128)(2,1)S(1)}, bf16[4,192,768]{2,1,0:T(8,128)(2,1)S(1)}, u32[]{:S(2)}, u32[]{:S(2)}) %collective-permute-start.3) | collective-permute-done | bytes 1179680 | tf_op jit(solution)/shard_map/ppermute | solution.py:37
  291.1 12.8 %shard_map.100 = (f32[4,384,768]{2,1,0:T(8,128)}, f32[4,768,384]{2,1,0:T(8,128)}) custom-call(s32[4]{0:T(128)S(1)} %fusion.77.refs_0_, s32[16]{0:T(128)S(1)} %select_n.626.refs_1_, s32[4]{0:T(128)S(1)} %broadcast_select_fusion.5.refs_2_, s32[2]{0:T(128)S(1)} %xor_multiply_fusion.refs_3_, bf16[4,192,768]{2,1,0:T(8,128)(2,1)S(1)} %pad_maximum_fusion.refs_4_, ...), custom_call_target="tpu_custom_call" | custom-call | flops 7247757312 | bytes 9437184 | tf_op jit(solution)/shard_map/pallas_call | solution.py:165
  307.8 5.3 collective-permute-start.39
  315.0 4.0 fusion.7
  319.0 5.9 collective-permute-start.43
  328.8 21.7 %collective-permute-done.39 = f16[384,768]{1,0:T(8,128)(2,1)} collective-permute-done((f16[384,768]{1,0:T(8,128)(2,1)}, f16[384,768]{1,0:T(8,128)(2,1)}, u32[]{:S(2)}, u32[]{:S(2)}) %collective-permute-start.39) | collective-permute-done | bytes 589856 | tf_op jit(solution)/shard_map/ppermute | solution.py:37
  350.4 14.8 %collective-permute-done.40 = f16[384,768]{1,0:T(8,128)(2,1)} collective-permute-done((f16[384,768]{1,0:T(8,128)(2,1)}, f16[384,768]{1,0:T(8,128)(2,1)}, u32[]{:S(2)}, u32[]{:S(2)}) %collective-permute-start.40) | collective-permute-done | bytes 589856 | tf_op jit(solution)/shard_map/ppermute | solution.py:37
  365.8 7.8 %dynamic_update_slice.224 = f16[768,1536]{1,0:T(8,128)(2,1)S(1)} dynamic-update-slice(f16[768,1536]{1,0:T(8,128)(2,1)S(1)} %broadcast.199.clone.2, f16[384,768]{1,0:T(8,128)(2,1)} %collective-permute-done.39, s32[]{:T(128)S(6)} %select_n.654, s32[]{:T(128)S(6)} %select_n.655) | dynamic-update-slice | bytes 1179652 | tf_op jit(solution)/shard_map/dynamic_update_slice | solution.py:200
  373.6 7.9 %dynamic_update_slice.225 = f16[768,1536]{1,0:T(8,128)(2,1)S(1)} dynamic-update-slice(f16[768,1536]{1,0:T(8,128)(2,1)S(1)} %dynamic_update_slice.224, f16[384,768]{1,0:T(8,128)(2,1)} %collective-permute-done.40, s32[]{:T(128)S(6)} %select_n.658, s32[]{:T(128)S(6)} %select_n.660) | dynamic-update-slice | bytes 1179652 | tf_op jit(solution)/shard_map/dynamic_update_slice | solution.py:200
  381.5 7.9 %dynamic_update_slice.226 = f16[768,1536]{1,0:T(8,128)(2,1)S(1)} dynamic-update-slice(f16[768,1536]{1,0:T(8,128)(2,1)S(1)} %dynamic_update_slice.225, f16[384,768]{1,0:T(8,128)(2,1)} %collective-permute-done.41, s32[]{:T(128)S(6)} %select_n.663, s32[]{:T(128)S(6)} %select_n.665) | dynamic-update-slice | bytes 1179652 | tf_op jit(solution)/shard_map/dynamic_update_slice | solution.py:200
  394.5 8.3 %dynamic_update_slice.227 = f16[768,1536]{1,0:T(8,128)(2,1)S(1)} dynamic-update-slice(f16[768,1536]{1,0:T(8,128)(2,1)S(1)} %dynamic_update_slice.226, f16[384,768]{1,0:T(8,128)(2,1)} %collective-permute-done.42, s32[]{:T(128)S(6)} %select_n.668, s32[]{:T(128)S(6)} %select_n.670) | dynamic-update-slice | bytes 1179652 | tf_op jit(solution)/shard_map/dynamic_update_slice | solution.py:200
  411.6 7.3 %collective-permute-done.47 = bf16[256,768]{1,0:T(8,128)(2,1)S(1)} collective-permute-done((bf16[256,768]{1,0:T(8,128)(2,1)S(1)}, bf16[256,768]{1,0:T(8,128)(2,1)S(1)}, u32[]{:S(2)}, u32[]{:S(2)}) %collective-permute-start.47) | collective-permute-done | bytes 393248 | tf_op jit(solution)/shard_map/ppermute | solution.py:37
  419.9 5.2 collective-permute-start.49
  428.4 5.2 collective-permute-start.55
  437.1 4.8 collective-permute-start.61
  441.9 5.8 collective-permute-done.49
  448.6 18.4 %collective-permute-done.55 = bf16[256,768]{1,0:T(8,128)(2,1)S(1)} collective-permute-done((bf16[256,768]{1,0:T(8,128)(2,1)S(1)}, bf16[256,768]{1,0:T(8,128)(2,1)S(1)}, u32[]{:S(2)}, u32[]{:S(2)}) %collective-permute-start.55) | collective-permute-done | bytes 393248 | tf_op jit(solution)/shard_map/ppermute | solution.py:37
  467.2 8.3 %collective-permute-done.61 = bf16[256,768]{1,0:T(8,128)(2,1)S(1)} collective-permute-done((bf16[256,768]{1,0:T(8,128)(2,1)S(1)}, bf16[256,768]{1,0:T(8,128)(2,1)S(1)}, u32[]{:S(2)}, u32[]{:S(2)}) %collective-permute-start.61) | collective-permute-done | bytes 393248 | tf_op jit(solution)/shard_map/ppermute | solution.py:37
  475.8 4.3 broadcast.207
  482.2 4.6 collective-permute-done.57
  486.8 15.0 %collective-permute-done.63 = bf16[2,256,768]{2,1,0:T(8,128)(2,1)S(1)} collective-permute-done((bf16[2,256,768]{2,1,0:T(8,128)(2,1)S(1)}, bf16[2,256,768]{2,1,0:T(8,128)(2,1)S(1)}, u32[]{:S(2)}, u32[]{:S(2)}) %collective-permute-start.63) | collective-permute-done | bytes 786464 | tf_op jit(solution)/shard_map/ppermute | solution.py:37
  523.0 12.7 %shard_map.101 = (f32[4,384,768]{2,1,0:T(8,128)}, f32[4,768,384]{2,1,0:T(8,128)}) custom-call(s32[4]{0:T(128)S(1)} %fusion.77.refs_0_, s32[16]{0:T(128)S(1)} %select_n.626.refs_1_, s32[4]{0:T(128)S(1)} %broadcast_select_fusion.5.refs_2_, s32[2]{0:T(128)S(1)} %xor_multiply_fusion.refs_3_, bf16[4,192,768]{2,1,0:T(8,128)(2,1)S(1)} %pad_maximum_fusion.refs_4_, ...), custom_call_target="tpu_custom_call" | custom-call | flops 7247757312 | bytes 9437184 | tf_op jit(solution)/shard_map/pallas_call | solution.py:165
  538.7 16.0 %collective-permute-start.65 = (f16[384,768]{1,0:T(8,128)(2,1)S(1)}, f16[384,768]{1,0:T(8,128)(2,1)S(1)}, u32[]{:S(2)}, u32[]{:S(2)}) collective-permute-start(f16[384,768]{1,0:T(8,128)(2,1)S(1)} %get-tuple-element.16), channel_id=1, source_target_pairs={{0,0},{1,8},{2,16},{3,24},{4,4},{5,12},{6,20},{7,28},{8,1},{9,9},{... | collective-permute-start | bytes 1769480 | tf_op jit(solution)/shard_map/ppermute | solution.py:37
  559.9 27.5 %collective-permute-done.65 = f16[384,768]{1,0:T(8,128)(2,1)S(1)} collective-permute-done((f16[384,768]{1,0:T(8,128)(2,1)S(1)}, f16[384,768]{1,0:T(8,128)(2,1)S(1)}, u32[]{:S(2)}, u32[]{:S(2)}) %collective-permute-start.65) | collective-permute-done | bytes 589856 | tf_op jit(solution)/shard_map/ppermute | solution.py:37
  587.4 12.6 %collective-permute-done.66 = f16[384,768]{1,0:T(8,128)(2,1)S(1)} collective-permute-done((f16[384,768]{1,0:T(8,128)(2,1)S(1)}, f16[384,768]{1,0:T(8,128)(2,1)S(1)}, u32[]{:S(2)}, u32[]{:S(2)}) %collective-permute-start.66) | collective-permute-done | bytes 589856 | tf_op jit(solution)/shard_map/ppermute | solution.py:37
  599.9 5.2 collective-permute-done.67
  605.3 5.2 dynamic_update_slice.256
  610.5 5.5 dynamic_update_slice.257
  616.0 7.5 %dynamic_update_slice.258 = f16[768,1536]{1,0:T(8,128)(2,1)S(1)} dynamic-update-slice(f16[768,1536]{1,0:T(8,128)(2,1)S(1)} %dynamic_update_slice.257, f16[384,768]{1,0:T(8,128)(2,1)S(1)} %collective-permute-done.67, s32[]{:T(128)S(6)} %select_n.663, s32[]{:T(128)S(6)} %select_n.665) | dynamic-update-slice | bytes 1179652 | tf_op jit(solution)/shard_map/dynamic_update_slice | solution.py:200
  623.6 8.0 %dynamic_update_slice.259 = f16[768,1536]{1,0:T(8,128)(2,1)S(1)} dynamic-update-slice(f16[768,1536]{1,0:T(8,128)(2,1)S(1)} %dynamic_update_slice.258, f16[384,768]{1,0:T(8,128)(2,1)S(1)} %collective-permute-done.68, s32[]{:T(128)S(6)} %select_n.668, s32[]{:T(128)S(6)} %select_n.670) | dynamic-update-slice | bytes 1179652 | tf_op jit(solution)/shard_map/dynamic_update_slice | solution.py:200
  632.6 4.0 divide_subtract_fusion
  (265 shorter events, 137.4 us)
Async XLA Ops:
  8.5 38.9 %collective-permute-start.16 = (bf16[256,768]{1,0:T(8,128)(2,1)}, bf16[256,768]{1,0:T(8,128)(2,1)}, u32[]{:S(2)}, u32[]{:S(2)}) collective-permute-start(bf16[256,768]{1,0:T(8,128)(2,1)} %get-tuple-element.63), channel_id=1, source_target_pairs={{0,2},{1,3},{2,0},{3,1},{4,6},{5,7},{6,4},{7,5},{8,10},{9,11},{10,... | collective-permute-start | bytes 1179656 | tf_op jit(solution)/shard_map/ppermute | solution.py:37
  11.8 37.2 %collective-permute-start.22 = (bf16[256,768]{1,0:T(8,128)(2,1)}, bf16[256,768]{1,0:T(8,128)(2,1)}, u32[]{:S(2)}, u32[]{:S(2)}) collective-permute-start(bf16[256,768]{1,0:T(8,128)(2,1)} %get-tuple-element.59), channel_id=1, source_target_pairs={{0,2},{1,3},{2,0},{3,1},{4,6},{5,7},{6,4},{7,5},{8,10},{9,11},{10,... | collective-permute-start | bytes 1179656 | tf_op jit(solution)/shard_map/ppermute | solution.py:37
  12.8 52.9 %collective-permute-start.28 = (bf16[256,768]{1,0:T(8,128)(2,1)}, bf16[256,768]{1,0:T(8,128)(2,1)}, u32[]{:S(2)}, u32[]{:S(2)}) collective-permute-start(bf16[256,768]{1,0:T(8,128)(2,1)} %get-tuple-element.55), channel_id=1, source_target_pairs={{0,2},{1,3},{2,0},{3,1},{4,6},{5,7},{6,4},{7,5},{8,10},{9,11},{10,... | collective-permute-start | bytes 1179656 | tf_op jit(solution)/shard_map/ppermute | solution.py:37
  19.1 26.8 %collective-permute-start.12 = (bf16[1,192,768]{2,1,0:T(8,128)(2,1)S(1)}, bf16[1,192,768]{2,1,0:T(8,128)(2,1)S(1)}, u32[]{:S(2)}, u32[]{:S(2)}) collective-permute-start(bf16[1,192,768]{2,1,0:T(8,128)(2,1)S(1)} %bitcast.281), channel_id=1, source_target_pairs={{0,8},{1,9},{2,10},{3,11},{4,12},{5,13},{6,14},{7,15},{8,0},{9,1},... | collective-permute-start | bytes 884744 | tf_op jit(solution)/shard_map/ppermute | solution.py:37
  49.0 28.5 %collective-permute-start.17 = (bf16[256,768]{1,0:T(8,128)(2,1)S(1)}, bf16[256,768]{1,0:T(8,128)(2,1)S(1)}, u32[]{:S(2)}, u32[]{:S(2)}) collective-permute-start(bf16[256,768]{1,0:T(8,128)(2,1)S(1)} %get-tuple-element.62), channel_id=1, source_target_pairs={{0,0},{1,8},{2,2},{3,10},{4,4},{5,12},{6,6},{7,14},{8,1},{9,9},{10... | collective-permute-start | bytes 1179656 | tf_op jit(solution)/shard_map/ppermute | solution.py:37
  51.1 30.0 %collective-permute-start.18 = (bf16[256,768]{1,0:T(8,128)(2,1)S(1)}, bf16[256,768]{1,0:T(8,128)(2,1)S(1)}, u32[]{:S(2)}, u32[]{:S(2)}) collective-permute-start(bf16[256,768]{1,0:T(8,128)(2,1)S(1)} %get-tuple-element.61), channel_id=1, source_target_pairs={{0,16},{1,24},{2,18},{3,26},{4,20},{5,28},{6,22},{7,30},{8,17},{9,... | collective-permute-start | bytes 1179656 | tf_op jit(solution)/shard_map/ppermute | solution.py:37
  54.5 28.3 %collective-permute-start.23 = (bf16[256,768]{1,0:T(8,128)(2,1)S(1)}, bf16[256,768]{1,0:T(8,128)(2,1)S(1)}, u32[]{:S(2)}, u32[]{:S(2)}) collective-permute-start(bf16[256,768]{1,0:T(8,128)(2,1)S(1)} %get-tuple-element.58), channel_id=1, source_target_pairs={{0,0},{1,8},{2,2},{3,10},{4,4},{5,12},{6,6},{7,14},{8,1},{9,9},{10... | collective-permute-start | bytes 1179656 | tf_op jit(solution)/shard_map/ppermute | solution.py:37
  65.0 48.0 %collective-permute-start.13 = (bf16[2,192,768]{2,1,0:T(8,128)(2,1)S(1)}, bf16[2,192,768]{2,1,0:T(8,128)(2,1)S(1)}, u32[]{:S(2)}, u32[]{:S(2)}) collective-permute-start(bf16[2,192,768]{2,1,0:T(8,128)(2,1)S(1)} %pad_maximum_fusion.13), channel_id=1, source_target_pairs={{0,0},{1,1},{2,2},{3,3},{4,4},{5,5},{6,6},{7,7},{8,16},{9,17},{10,... | collective-permute-start | bytes 1769480 | tf_op jit(solution)/shard_map/ppermute | solution.py:37
  65.7 45.6 %collective-permute-start.24 = (bf16[256,768]{1,0:T(8,128)(2,1)S(1)}, bf16[256,768]{1,0:T(8,128)(2,1)S(1)}, u32[]{:S(2)}, u32[]{:S(2)}) collective-permute-start(bf16[256,768]{1,0:T(8,128)(2,1)S(1)} %get-tuple-element.57), channel_id=1, source_target_pairs={{0,16},{1,24},{2,18},{3,26},{4,20},{5,28},{6,22},{7,30},{8,17},{9,... | collective-permute-start | bytes 1179656 | tf_op jit(solution)/shard_map/ppermute | solution.py:37
  77.5 54.9 %collective-permute-start.9 = (bf16[2,192,768]{2,1,0:T(8,128)(2,1)S(1)}, bf16[2,192,768]{2,1,0:T(8,128)(2,1)}, u32[]{:S(2)}, u32[]{:S(2)}) collective-permute-start(bf16[2,192,768]{2,1,0:T(8,128)(2,1)S(1)} %pad_maximum_fusion.12), channel_id=1, source_target_pairs={{0,0},{1,1},{2,2},{3,3},{4,4},{5,5},{6,6},{7,7},{8,16},{9,17},{10,... | collective-permute-start | bytes 1769480 | tf_op jit(solution)/shard_map/ppermute | solution.py:37
  81.2 45.1 %collective-permute-start.29 = (bf16[256,768]{1,0:T(8,128)(2,1)}, bf16[256,768]{1,0:T(8,128)(2,1)S(1)}, u32[]{:S(2)}, u32[]{:S(2)}) collective-permute-start(bf16[256,768]{1,0:T(8,128)(2,1)} %get-tuple-element.54), channel_id=1, source_target_pairs={{0,0},{1,8},{2,2},{3,10},{4,4},{5,12},{6,6},{7,14},{8,1},{9,9},{10... | collective-permute-start | bytes 1179656 | tf_op jit(solution)/shard_map/ppermute | solution.py:37
  82.8 49.6 %collective-permute-start.30 = (bf16[256,768]{1,0:T(8,128)(2,1)}, bf16[256,768]{1,0:T(8,128)(2,1)S(1)}, u32[]{:S(2)}, u32[]{:S(2)}) collective-permute-start(bf16[256,768]{1,0:T(8,128)(2,1)} %get-tuple-element.53), channel_id=1, source_target_pairs={{0,16},{1,24},{2,18},{3,26},{4,20},{5,28},{6,22},{7,30},{8,17},{9,... | collective-permute-start | bytes 1179656 | tf_op jit(solution)/shard_map/ppermute | solution.py:37
  111.3 32.6 %collective-permute-start.5 = (bf16[2,192,768]{2,1,0:T(8,128)(2,1)S(1)}, bf16[2,192,768]{2,1,0:T(8,128)(2,1)S(1)}, u32[]{:S(2)}, u32[]{:S(2)}) collective-permute-start(bf16[2,192,768]{2,1,0:T(8,128)(2,1)S(1)} %pad_maximum_fusion.11), channel_id=1, source_target_pairs={{0,0},{1,1},{2,2},{3,3},{4,4},{5,5},{6,6},{7,7},{8,16},{9,17},{10,... | collective-permute-start | bytes 1769480 | tf_op jit(solution)/shard_map/ppermute | solution.py:37
  113.0 32.2 %collective-permute-start.14 = (bf16[2,192,768]{2,1,0:T(8,128)(2,1)S(1)}, bf16[2,192,768]{2,1,0:T(8,128)(2,1)S(1)}, u32[]{:S(2)}, u32[]{:S(2)}) collective-permute-start(bf16[2,192,768]{2,1,0:T(8,128)(2,1)S(1)} %collective-permute-done.13), channel_id=1, source_target_pairs={{0,8},{1,9},{2,10},{3,11},{4,12},{5,13},{6,14},{7,15},{8,0},{9,1},... | collective-permute-start | bytes 1769480 | tf_op jit(solution)/shard_map/ppermute | solution.py:37
  132.4 52.0 %collective-permute-start.19 = (bf16[2,256,768]{2,1,0:T(8,128)(2,1)}, bf16[2,256,768]{2,1,0:T(8,128)(2,1)S(1)}, u32[]{:S(2)}, u32[]{:S(2)}) collective-permute-start(bf16[2,256,768]{2,1,0:T(8,128)(2,1)} %pad_maximum_fusion.4), channel_id=1, source_target_pairs={{0,1},{1,0},{2,3},{3,2},{4,5},{5,4},{6,7},{7,6},{8,9},{9,8},{10,11... | collective-permute-start | bytes 2359304 | tf_op jit(solution)/shard_map/ppermute | solution.py:37
  132.4 27.3 %collective-permute-start.10 = (bf16[2,192,768]{2,1,0:T(8,128)(2,1)}, bf16[2,192,768]{2,1,0:T(8,128)(2,1)S(1)}, u32[]{:S(2)}, u32[]{:S(2)}) collective-permute-start(bf16[2,192,768]{2,1,0:T(8,128)(2,1)} %collective-permute-done.9), channel_id=1, source_target_pairs={{0,8},{1,9},{2,10},{3,11},{4,12},{5,13},{6,14},{7,15},{8,0},{9,1},... | collective-permute-start | bytes 1769480 | tf_op jit(solution)/shard_map/ppermute | solution.py:37
  143.9 41.8 %collective-permute-start.20 = (bf16[2,256,768]{2,1,0:T(8,128)(2,1)}, bf16[2,256,768]{2,1,0:T(8,128)(2,1)S(1)}, u32[]{:S(2)}, u32[]{:S(2)}) collective-permute-start(bf16[2,256,768]{2,1,0:T(8,128)(2,1)} %pad_maximum_fusion.4), channel_id=1, source_target_pairs={{0,4},{1,5},{2,6},{3,7},{4,0},{5,1},{6,2},{7,3},{8,12},{9,13},{10,... | collective-permute-start | bytes 2359304 | tf_op jit(solution)/shard_map/ppermute | solution.py:37
  149.0 40.4 %collective-permute-start.25 = (bf16[2,256,768]{2,1,0:T(8,128)(2,1)}, bf16[2,256,768]{2,1,0:T(8,128)(2,1)S(1)}, u32[]{:S(2)}, u32[]{:S(2)}) collective-permute-start(bf16[2,256,768]{2,1,0:T(8,128)(2,1)} %pad_maximum_fusion.5), channel_id=1, source_target_pairs={{0,1},{1,0},{2,3},{3,2},{4,5},{5,4},{6,7},{7,6},{8,9},{9,8},{10,11... | collective-permute-start | bytes 2359304 | tf_op jit(solution)/shard_map/ppermute | solution.py:37
  188.0 27.3 %collective-permute-start.15 = (bf16[4,192,768]{2,1,0:T(8,128)(2,1)S(1)}, bf16[4,192,768]{2,1,0:T(8,128)(2,1)S(1)}, u32[]{:S(2)}, u32[]{:S(2)}) collective-permute-start(bf16[4,192,768]{2,1,0:T(8,128)(2,1)S(1)} %pad_maximum_fusion.3.refs_10_), channel_id=1, source_target_pairs={{0,2},{1,3},{2,0},{3,1},{4,6},{5,7},{6,4},{7,5},{8,10},{9,11},{10,... | collective-permute-start | bytes 3538952 | tf_op jit(solution)/shard_map/ppermute | solution.py:37
  189.4 51.1 %collective-permute-start.11 = (bf16[4,192,768]{2,1,0:T(8,128)(2,1)S(1)}, bf16[4,192,768]{2,1,0:T(8,128)(2,1)S(1)}, u32[]{:S(2)}, u32[]{:S(2)}) collective-permute-start(bf16[4,192,768]{2,1,0:T(8,128)(2,1)S(1)} %pad_maximum_fusion.2.refs_8_), channel_id=1, source_target_pairs={{0,2},{1,3},{2,0},{3,1},{4,6},{5,7},{6,4},{7,5},{8,10},{9,11},{10,... | collective-permute-start | bytes 3538952 | tf_op jit(solution)/shard_map/ppermute | solution.py:37
  192.7 73.2 %collective-permute-start.7 = (bf16[4,192,768]{2,1,0:T(8,128)(2,1)S(1)}, bf16[4,192,768]{2,1,0:T(8,128)(2,1)S(1)}, u32[]{:S(2)}, u32[]{:S(2)}) collective-permute-start(bf16[4,192,768]{2,1,0:T(8,128)(2,1)S(1)} %pad_maximum_fusion.1.refs_6_), channel_id=1, source_target_pairs={{0,2},{1,3},{2,0},{3,1},{4,6},{5,7},{6,4},{7,5},{8,10},{9,11},{10,... | collective-permute-start | bytes 3538952 | tf_op jit(solution)/shard_map/ppermute | solution.py:37
  194.1 97.0 %collective-permute-start.3 = (bf16[4,192,768]{2,1,0:T(8,128)(2,1)S(1)}, bf16[4,192,768]{2,1,0:T(8,128)(2,1)S(1)}, u32[]{:S(2)}, u32[]{:S(2)}) collective-permute-start(bf16[4,192,768]{2,1,0:T(8,128)(2,1)S(1)} %pad_maximum_fusion.refs_4_), channel_id=1, source_target_pairs={{0,2},{1,3},{2,0},{3,1},{4,6},{5,7},{6,4},{7,5},{8,10},{9,11},{10,... | collective-permute-start | bytes 3538952 | tf_op jit(solution)/shard_map/ppermute | solution.py:37
  307.8 42.6 %collective-permute-start.39 = (f16[384,768]{1,0:T(8,128)(2,1)}, f16[384,768]{1,0:T(8,128)(2,1)}, u32[]{:S(2)}, u32[]{:S(2)}) collective-permute-start(f16[384,768]{1,0:T(8,128)(2,1)} %get-tuple-element.24), channel_id=1, source_target_pairs={{0,0},{1,8},{2,16},{3,24},{4,4},{5,12},{6,20},{7,28},{8,1},{9,9},{... | collective-permute-start | bytes 1769480 | tf_op jit(solution)/shard_map/ppermute | solution.py:37
  313.1 52.2 %collective-permute-start.40 = (f16[384,768]{1,0:T(8,128)(2,1)}, f16[384,768]{1,0:T(8,128)(2,1)}, u32[]{:S(2)}, u32[]{:S(2)}) collective-permute-start(f16[384,768]{1,0:T(8,128)(2,1)} %get-tuple-element.23), channel_id=1, source_target_pairs={{0,8},{1,0},{2,24},{3,16},{4,12},{5,4},{6,28},{7,20},{8,9},{9,1},{... | collective-permute-start | bytes 1769480 | tf_op jit(solution)/shard_map/ppermute | solution.py:37
  315.0 50.3 %collective-permute-start.41 = (f16[384,768]{1,0:T(8,128)(2,1)}, f16[384,768]{1,0:T(8,128)(2,1)}, u32[]{:S(2)}, u32[]{:S(2)}) collective-permute-start(f16[384,768]{1,0:T(8,128)(2,1)} %get-tuple-element.22), channel_id=1, source_target_pairs={{0,16},{1,24},{2,0},{3,8},{4,20},{5,28},{6,4},{7,12},{8,17},{9,25}... | collective-permute-start | bytes 1769480 | tf_op jit(solution)/shard_map/ppermute | solution.py:37
  319.0 70.4 %collective-permute-start.43 = (f16[768,384]{1,0:T(8,128)(2,1)}, f16[768,384]{1,0:T(8,128)(2,1)}, u32[]{:S(2)}, u32[]{:S(2)}) collective-permute-start(f16[768,384]{1,0:T(8,128)(2,1)} %get-tuple-element.28), channel_id=1, source_target_pairs={{0,0},{1,1},{2,4},{3,5},{4,2},{5,3},{6,6},{7,7},{8,8},{9,9},{10,12... | collective-permute-start | bytes 1769480 | tf_op jit(solution)/shard_map/ppermute | solution.py:37
  325.0 65.8 %collective-permute-start.44 = (f16[768,384]{1,0:T(8,128)(2,1)}, f16[768,384]{1,0:T(8,128)(2,1)}, u32[]{:S(2)}, u32[]{:S(2)}) collective-permute-start(f16[768,384]{1,0:T(8,128)(2,1)} %get-tuple-element.27), channel_id=1, source_target_pairs={{0,1},{1,0},{2,5},{3,4},{4,3},{5,2},{6,7},{7,6},{8,9},{9,8},{10,13... | collective-permute-start | bytes 1769480 | tf_op jit(solution)/shard_map/ppermute | solution.py:37
  350.4 41.6 %collective-permute-start.45 = (f16[768,384]{1,0:T(8,128)(2,1)}, f16[768,384]{1,0:T(8,128)(2,1)}, u32[]{:S(2)}, u32[]{:S(2)}) collective-permute-start(f16[768,384]{1,0:T(8,128)(2,1)} %get-tuple-element.26), channel_id=1, source_target_pairs={{0,2},{1,3},{2,6},{3,7},{4,0},{5,1},{6,4},{7,5},{8,10},{9,11},{10,... | collective-permute-start | bytes 1769480 | tf_op jit(solution)/shard_map/ppermute | solution.py:37
  365.3 28.0 %collective-permute-start.46 = (f16[768,384]{1,0:T(8,128)(2,1)}, f16[768,384]{1,0:T(8,128)(2,1)}, u32[]{:S(2)}, u32[]{:S(2)}) collective-permute-start(f16[768,384]{1,0:T(8,128)(2,1)} %get-tuple-element.25), channel_id=1, source_target_pairs={{0,3},{1,2},{2,7},{3,6},{4,1},{5,0},{6,5},{7,4},{8,11},{9,10},{10,... | collective-permute-start | bytes 1769480 | tf_op jit(solution)/shard_map/ppermute | solution.py:37
  365.3 29.2 %collective-permute-start.42 = (f16[384,768]{1,0:T(8,128)(2,1)}, f16[384,768]{1,0:T(8,128)(2,1)}, u32[]{:S(2)}, u32[]{:S(2)}) collective-permute-start(f16[384,768]{1,0:T(8,128)(2,1)} %get-tuple-element.21), channel_id=1, source_target_pairs={{0,24},{1,16},{2,8},{3,0},{4,28},{5,20},{6,12},{7,4},{8,25},{9,17}... | collective-permute-start | bytes 1769480 | tf_op jit(solution)/shard_map/ppermute | solution.py:37
  419.9 27.7 %collective-permute-start.49 = (bf16[256,768]{1,0:T(8,128)(2,1)S(1)}, bf16[256,768]{1,0:T(8,128)(2,1)S(1)}, u32[]{:S(2)}, u32[]{:S(2)}) collective-permute-start(bf16[256,768]{1,0:T(8,128)(2,1)S(1)} %get-tuple-element.49), channel_id=1, source_target_pairs={{0,16},{1,24},{2,18},{3,26},{4,20},{5,28},{6,22},{7,30},{8,17},{9,... | collective-permute-start | bytes 1179656 | tf_op jit(solution)/shard_map/ppermute | solution.py:37
  428.4 38.7 %collective-permute-start.55 = (bf16[256,768]{1,0:T(8,128)(2,1)S(1)}, bf16[256,768]{1,0:T(8,128)(2,1)S(1)}, u32[]{:S(2)}, u32[]{:S(2)}) collective-permute-start(bf16[256,768]{1,0:T(8,128)(2,1)S(1)} %get-tuple-element.45), channel_id=1, source_target_pairs={{0,16},{1,24},{2,18},{3,26},{4,20},{5,28},{6,22},{7,30},{8,17},{9,... | collective-permute-start | bytes 1179656 | tf_op jit(solution)/shard_map/ppermute | solution.py:37
  436.1 31.1 %collective-permute-start.60 = (bf16[256,768]{1,0:T(8,128)(2,1)S(1)}, bf16[256,768]{1,0:T(8,128)(2,1)S(1)}, u32[]{:S(2)}, u32[]{:S(2)}) collective-permute-start(bf16[256,768]{1,0:T(8,128)(2,1)S(1)} %get-tuple-element.42), channel_id=1, source_target_pairs={{0,0},{1,8},{2,2},{3,10},{4,4},{5,12},{6,6},{7,14},{8,1},{9,9},{10... | collective-permute-start | bytes 1179656 | tf_op jit(solution)/shard_map/ppermute | solution.py:37
  437.1 38.4 %collective-permute-start.61 = (bf16[256,768]{1,0:T(8,128)(2,1)S(1)}, bf16[256,768]{1,0:T(8,128)(2,1)S(1)}, u32[]{:S(2)}, u32[]{:S(2)}) collective-permute-start(bf16[256,768]{1,0:T(8,128)(2,1)S(1)} %get-tuple-element.41), channel_id=1, source_target_pairs={{0,16},{1,24},{2,18},{3,26},{4,20},{5,28},{6,22},{7,30},{8,17},{9,... | collective-permute-start | bytes 1179656 | tf_op jit(solution)/shard_map/ppermute | solution.py:37
  448.6 33.1 %collective-permute-start.50 = (bf16[2,256,768]{2,1,0:T(8,128)(2,1)}, bf16[2,256,768]{2,1,0:T(8,128)(2,1)}, u32[]{:S(2)}, u32[]{:S(2)}) collective-permute-start(bf16[2,256,768]{2,1,0:T(8,128)(2,1)} %pad_maximum_fusion.7), channel_id=1, source_target_pairs={{0,1},{1,0},{2,3},{3,2},{4,5},{5,4},{6,7},{7,6},{8,9},{9,8},{10,11... | collective-permute-start | bytes 2359304 | tf_op jit(solution)/shard_map/ppermute | solution.py:37
  448.6 33.6 %collective-permute-start.51 = (bf16[2,256,768]{2,1,0:T(8,128)(2,1)}, bf16[2,256,768]{2,1,0:T(8,128)(2,1)}, u32[]{:S(2)}, u32[]{:S(2)}) collective-permute-start(bf16[2,256,768]{2,1,0:T(8,128)(2,1)} %pad_maximum_fusion.7), channel_id=1, source_target_pairs={{0,4},{1,5},{2,6},{3,7},{4,0},{5,1},{6,2},{7,3},{8,12},{9,13},{10,... | collective-permute-start | bytes 2359304 | tf_op jit(solution)/shard_map/ppermute | solution.py:37
  475.7 42.6 %collective-permute-start.62 = (bf16[2,256,768]{2,1,0:T(8,128)(2,1)S(1)}, bf16[2,256,768]{2,1,0:T(8,128)(2,1)S(1)}, u32[]{:S(2)}, u32[]{:S(2)}) collective-permute-start(bf16[2,256,768]{2,1,0:T(8,128)(2,1)S(1)} %pad_maximum_fusion.9), channel_id=1, source_target_pairs={{0,1},{1,0},{2,3},{3,2},{4,5},{5,4},{6,7},{7,6},{8,9},{9,8},{10,11... | collective-permute-start | bytes 2359304 | tf_op jit(solution)/shard_map/ppermute | solution.py:37
  481.7 30.3 %collective-permute-start.56 = (bf16[2,256,768]{2,1,0:T(8,128)(2,1)S(1)}, bf16[2,256,768]{2,1,0:T(8,128)(2,1)S(1)}, u32[]{:S(2)}, u32[]{:S(2)}) collective-permute-start(bf16[2,256,768]{2,1,0:T(8,128)(2,1)S(1)} %pad_maximum_fusion.8), channel_id=1, source_target_pairs={{0,1},{1,0},{2,3},{3,2},{4,5},{5,4},{6,7},{7,6},{8,9},{9,8},{10,11... | collective-permute-start | bytes 2359304 | tf_op jit(solution)/shard_map/ppermute | solution.py:37
  482.2 26.7 %collective-permute-start.52 = (bf16[2,256,768]{2,1,0:T(8,128)(2,1)}, bf16[2,256,768]{2,1,0:T(8,128)(2,1)S(1)}, u32[]{:S(2)}, u32[]{:S(2)}) collective-permute-start(bf16[2,256,768]{2,1,0:T(8,128)(2,1)} %collective-permute-done.51), channel_id=1, source_target_pairs={{0,1},{1,0},{2,3},{3,2},{4,5},{5,4},{6,7},{7,6},{8,9},{9,8},{10,11... | collective-permute-start | bytes 2359304 | tf_op jit(solution)/shard_map/ppermute | solution.py:37
  486.8 28.4 %collective-permute-start.58 = (bf16[2,256,768]{2,1,0:T(8,128)(2,1)S(1)}, bf16[2,256,768]{2,1,0:T(8,128)(2,1)S(1)}, u32[]{:S(2)}, u32[]{:S(2)}) collective-permute-start(bf16[2,256,768]{2,1,0:T(8,128)(2,1)S(1)} %collective-permute-done.57), channel_id=1, source_target_pairs={{0,1},{1,0},{2,3},{3,2},{4,5},{5,4},{6,7},{7,6},{8,9},{9,8},{10,11... | collective-permute-start | bytes 2359304 | tf_op jit(solution)/shard_map/ppermute | solution.py:37
  538.7 48.7 %collective-permute-start.65 = (f16[384,768]{1,0:T(8,128)(2,1)S(1)}, f16[384,768]{1,0:T(8,128)(2,1)S(1)}, u32[]{:S(2)}, u32[]{:S(2)}) collective-permute-start(f16[384,768]{1,0:T(8,128)(2,1)S(1)} %get-tuple-element.16), channel_id=1, source_target_pairs={{0,0},{1,8},{2,16},{3,24},{4,4},{5,12},{6,20},{7,28},{8,1},{9,9},{... | collective-permute-start | bytes 1769480 | tf_op jit(solution)/shard_map/ppermute | solution.py:37
  554.7 45.2 %collective-permute-start.66 = (f16[384,768]{1,0:T(8,128)(2,1)S(1)}, f16[384,768]{1,0:T(8,128)(2,1)S(1)}, u32[]{:S(2)}, u32[]{:S(2)}) collective-permute-start(f16[384,768]{1,0:T(8,128)(2,1)S(1)} %get-tuple-element.15), channel_id=1, source_target_pairs={{0,8},{1,0},{2,24},{3,16},{4,12},{5,4},{6,28},{7,20},{8,9},{9,1},{... | collective-permute-start | bytes 1769480 | tf_op jit(solution)/shard_map/ppermute | solution.py:37
  554.8 50.3 %collective-permute-start.67 = (f16[384,768]{1,0:T(8,128)(2,1)S(1)}, f16[384,768]{1,0:T(8,128)(2,1)S(1)}, u32[]{:S(2)}, u32[]{:S(2)}) collective-permute-start(f16[384,768]{1,0:T(8,128)(2,1)S(1)} %get-tuple-element.14), channel_id=1, source_target_pairs={{0,16},{1,24},{2,0},{3,8},{4,20},{5,28},{6,4},{7,12},{8,17},{9,25}... | collective-permute-start | bytes 1769480 | tf_op jit(solution)/shard_map/ppermute | solution.py:37
  554.9 68.7 %collective-permute-start.68 = (f16[384,768]{1,0:T(8,128)(2,1)S(1)}, f16[384,768]{1,0:T(8,128)(2,1)S(1)}, u32[]{:S(2)}, u32[]{:S(2)}) collective-permute-start(f16[384,768]{1,0:T(8,128)(2,1)S(1)} %get-tuple-element.13), channel_id=1, source_target_pairs={{0,24},{1,16},{2,8},{3,0},{4,28},{5,20},{6,12},{7,4},{8,25},{9,17}... | collective-permute-start | bytes 1769480 | tf_op jit(solution)/shard_map/ppermute | solution.py:37
  559.2 72.4 %collective-permute-start.69 = (f16[768,384]{1,0:T(8,128)(2,1)S(1)}, f16[768,384]{1,0:T(8,128)(2,1)S(1)}, u32[]{:S(2)}, u32[]{:S(2)}) collective-permute-start(f16[768,384]{1,0:T(8,128)(2,1)S(1)} %get-tuple-element.20), channel_id=1, source_target_pairs={{0,0},{1,1},{2,4},{3,5},{4,2},{5,3},{6,6},{7,7},{8,8},{9,9},{10,12... | collective-permute-start | bytes 1769480 | tf_op jit(solution)/shard_map/ppermute | solution.py:37
  587.4 44.6 %collective-permute-start.70 = (f16[768,384]{1,0:T(8,128)(2,1)S(1)}, f16[768,384]{1,0:T(8,128)(2,1)S(1)}, u32[]{:S(2)}, u32[]{:S(2)}) collective-permute-start(f16[768,384]{1,0:T(8,128)(2,1)S(1)} %get-tuple-element.19), channel_id=1, source_target_pairs={{0,1},{1,0},{2,5},{3,4},{4,3},{5,2},{6,7},{7,6},{8,9},{9,8},{10,13... | collective-permute-start | bytes 1769480 | tf_op jit(solution)/shard_map/ppermute | solution.py:37
  599.9 32.2 %collective-permute-start.71 = (f16[768,384]{1,0:T(8,128)(2,1)S(1)}, f16[768,384]{1,0:T(8,128)(2,1)S(1)}, u32[]{:S(2)}, u32[]{:S(2)}) collective-permute-start(f16[768,384]{1,0:T(8,128)(2,1)S(1)} %get-tuple-element.18), channel_id=1, source_target_pairs={{0,2},{1,3},{2,6},{3,7},{4,0},{5,1},{6,4},{7,5},{8,10},{9,11},{10,... | collective-permute-start | bytes 1769480 | tf_op jit(solution)/shard_map/ppermute | solution.py:37
  605.1 27.3 %collective-permute-start.72 = (f16[768,384]{1,0:T(8,128)(2,1)S(1)}, f16[768,384]{1,0:T(8,128)(2,1)S(1)}, u32[]{:S(2)}, u32[]{:S(2)}) collective-permute-start(f16[768,384]{1,0:T(8,128)(2,1)S(1)} %get-tuple-element.17), channel_id=1, source_target_pairs={{0,3},{1,2},{2,7},{3,6},{4,1},{5,0},{6,5},{7,4},{8,11},{9,10},{10,... | collective-permute-start | bytes 1769480 | tf_op jit(solution)/shard_map/ppermute | solution.py:37
  (40 other events, 809.5 us)

commit v3 on v2

v3 whole, which is shorter than its diff:
```python
import jax
import jax.numpy as jnp
from jax import lax
from jax.experimental import pallas as pl
from jax.experimental.pallas import tpu as pltpu
from jax.sharding import PartitionSpec as P

STEPS = 2
COUPLING_MAX = 0.15625
DENOMINATOR_MIN = 1.5
HALF_TOP = 60000.0
AXES = ("alpha", "beta")
ROW_CHUNKS = 4


class Grid:
    def __init__(self, alpha_devices, beta_devices):
        self.bands = beta_devices
        self.lanes = alpha_devices // beta_devices
        self.majors = beta_devices // 2
        self.per_lane = self.majors // self.lanes
        self.places = [
            (band, lane, major, minor)
            for band in range(self.bands)
            for lane in range(self.lanes)
            for major in range(self.majors)
            for minor in range(2)
        ]

    def index(self, band, lane, major, minor):
        return ((band * self.lanes + lane) * self.majors + major) * 2 + minor

    def send(self, value, where):
        pairs = [(self.index(*place), self.index(*where(*place))) for place in self.places]
        if all(source == target for source, target in pairs):
            return value
        return lax.ppermute(value, AXES, pairs)


def after(value, *earlier):
    return lax.optimization_barrier((value, *earlier))[0]


def largest_anywhere(grid, value, gates):
    devices = len(grid.places)
    largest = jnp.full((8, 128), value)
    bit = 1
    while bit < devices:
        pairs = [(device, device ^ bit) for device in range(devices)]
        largest = after(largest, gates[min(bit.bit_length(), len(gates)) - 1])
        largest = jnp.maximum(largest, lax.ppermute(largest, AXES, pairs))
        bit *= 2
    return largest[0, 0]


def gather_bands(grid, own, band, gate):
    held = own[None] if gate is None else after(own[None], gate)
    swaps = []
    order = [[z] for z in range(grid.bands)]
    width = 2
    while width <= grid.bands:
        half = width // 2
        moving = held
        origin = list(range(grid.bands))
        kept, kept_origin = None, [None] * grid.bands
        for hop in range(half):
            partner = list(range(grid.bands))
            for base in range(0, grid.bands, width):
                low, high = base + half - 1, base + half
                if hop == 0:
                    pairs = [(low, high)]
                else:
                    pairs = [(low - hop + 1, low - hop), (high + hop - 1, high + hop)]
                for one, other in pairs:
                    partner[one], partner[other] = other, one
            moving = grid.send(moving, lambda z, x, m, n: (partner[z], x, m, n))
            if hop == 0:
                swaps.append(moving)
            origin = [origin[partner[z]] for z in range(grid.bands)]
            takes = [(half - 1 - z % width if z % width < half else z % width - half) == hop for z in range(grid.bands)]
            kept = moving if kept is None else jnp.where(jnp.array(takes)[band], moving, kept)
            kept_origin = [origin[z] if takes[z] else kept_origin[z] for z in range(grid.bands)]
        held = jnp.concatenate([held, kept])
        order = [order[z] + order[kept_origin[z]] for z in range(grid.bands)]
        width *= 2
    return held, order, swaps


def gather_couplings(grid, coupling, band, major, minor):
    rows, slots, _ = coupling.shape
    majors = grid.majors
    chunk = rows // (2 * majors)
    own = lax.dynamic_slice_in_dim(coupling, (minor * majors + major) * chunk, chunk, 0)
    gathered, swaps, gate = [], [], None
    for slot in range(slots):
        line, order, swapped = gather_bands(grid, own[:, slot], band, gate)
        gate = swapped[0]
        swaps.append(swapped[-1])
        pieces = {0: line}
        bit = majors // 2
        while bit:
            received = {
                key ^ bit: grid.send(piece, lambda z, x, m, n: (z, x, m ^ bit, n)) for key, piece in pieces.items()
            }
            pieces.update(received)
            bit //= 2
        pieces = [pieces[key] for key in range(majors)]
        if chunk % 16:
            whole = jnp.take(jnp.stack(pieces), major ^ jnp.arange(majors), axis=0)
            pieces = [whole.transpose(1, 0, 2, 3).reshape(grid.bands, rows // 2, whole.shape[3])]
        gathered.append(pieces)
    return gathered, jnp.array(order, jnp.int32)[band], swaps


def to_columns(grid, half, band, lane, major, minor, gate):
    rows, cols = half.shape
    lanes, majors = grid.lanes, grid.majors
    strip = cols // majors
    part = rows // ROW_CHUNKS
    parts, places = [], []
    for chunk in range(ROW_CHUNKS):
        block = half[chunk * part : (chunk + 1) * part]
        first = []
        for key in range(majors):
            piece = lax.dynamic_slice(block, (0, (major ^ key) * strip), (part, strip))
            first.append(grid.send(piece, lambda z, x, m, n: (z, x, m ^ key, n)))
        first = jnp.stack(first)
        if gate is not None:
            first = after(first, gate)
        second = []
        for key in range(majors):
            piece = lax.dynamic_index_in_dim(first, (band // 2) ^ key ^ major, 0, keepdims=False)
            second.append(grid.send(piece, lambda z, x, m, n: ((z // 2 ^ key) * 2 + n, x, m, z % 2)))
        second = jnp.stack(second)
        for turn in range(lanes):
            third = grid.send(second, lambda z, x, m, n: (z, (x + turn) % lanes, m, n))
            for flip in range(2):
                parts.append(third if flip == 0 else grid.send(third, lambda z, x, m, n: (z, x, m, 1 - n)))
                for key in range(majors):
                    alpha = ((band // 2 ^ key) * 2 + (minor ^ flip)) * lanes + (lane - turn) % lanes
                    places.append(alpha * rows + chunk * part)
    return parts, jnp.stack(places)


def product_kernel(slots, pieces, order_ref, entry_ref, column_ref, count_ref, offset_ref, place_ref, scale_ref, *refs):
    couplings, parts = refs[: slots * pieces], refs[slots * pieces : -4]
    out_ref, mirror_ref, coeff_ref, sems = refs[-4:]
    band = order_ref[pl.program_id(0)]
    chunk, tile = couplings[0].shape[1:]
    majors, part, _ = parts[0].shape

    @pl.when(pl.program_id(0) == 0)
    def _():
        copies = []
        for i in range(len(parts) * majors):
            place = pl.ds(pl.multiple_of(place_ref[i], part), part)
            source = parts[i // majors].at[i % majors]
            copies.append(pltpu.make_async_copy(source, coeff_ref.at[place], sems.at[i]))
        for copy in copies:
            copy.start()
        for copy in copies:
            copy.wait()

    def product(slot):
        first = pl.multiple_of(column_ref[band * slots + slot] * tile, tile)
        left = jnp.concatenate([couplings[slot * pieces + piece][0] for piece in range(pieces)], axis=0)
        return jnp.dot(left, coeff_ref[pl.ds(first, tile), :], preferred_element_type=jnp.float32) * scale_ref[0]

    def store(value, add):
        for piece in range(pieces):
            place = pl.ds(pl.multiple_of(offset_ref[piece], chunk), chunk)
            part = value[piece * chunk : (piece + 1) * chunk]
            out_ref[0, place, :] = out_ref[0, place, :] + part if add else part

    store(product(0), False)
    for slot in range(1, slots):

        @pl.when(slot < count_ref[band])
        def _():
            store(product(slot), True)

    mirror_ref[0] = out_ref[0].T


def products(couplings, parts, order, entries, tile_columns, counts, offsets, places, scale):
    slots, pieces = len(couplings), len(couplings[0])
    _, chunk, tile = couplings[0][0].shape
    majors, part, strip = parts[0].shape
    rows, calls = pieces * chunk, order.shape[0]
    spec = pl.BlockSpec((1, chunk, tile), lambda i, order, entry, *_: (entry[i], 0, 0))
    return pl.pallas_call(
        lambda *refs: product_kernel(slots, pieces, *refs),
        grid_spec=pltpu.PrefetchScalarGridSpec(
            num_scalar_prefetch=7,
            grid=(calls,),
            in_specs=[spec] * (slots * pieces) + [pl.BlockSpec(memory_space=pl.ANY)] * len(parts),
            out_specs=[
                pl.BlockSpec((1, rows, strip), lambda i, *_: (i, 0, 0)),
                pl.BlockSpec((1, strip, rows), lambda i, *_: (i, 0, 0)),
            ],
            scratch_shapes=[
                pltpu.VMEM((len(parts) * majors * part, strip), jnp.bfloat16),
                pltpu.SemaphoreType.DMA((len(parts) * majors,)),
            ],
        ),
        out_shape=[
            jax.ShapeDtypeStruct((calls, rows, strip), jnp.float32),
            jax.ShapeDtypeStruct((calls, strip, rows), jnp.float32),
        ],
        compiler_params=pltpu.CompilerParams(vmem_limit_bytes=40 << 20),
        cost_estimate=pl.CostEstimate(
            flops=2 * calls * slots * rows * tile * strip,
            bytes_accessed=2 * (calls * slots * rows * tile + len(parts) * majors * part * strip),
            transcendentals=0,
        ),
    )(
        order,
        entries,
        tile_columns,
        counts,
        offsets,
        places,
        scale[None],
        *[piece for slot in couplings for piece in slot],
        *parts,
    )


def bring_home(grid, halves, band, lane, major, minor):
    bands, per_lane = grid.bands, grid.per_lane
    run, part, strip = halves[0][0].shape
    rows = 2 * part
    beta = major * 2 + minor
    direct = jnp.zeros((rows, grid.majors * strip), jnp.float16)
    mirror = jnp.zeros((rows, grid.majors * strip), jnp.float16)
    for key in range(bands):
        piece = halves[key // run][0][key % run].astype(jnp.float16)
        piece = grid.send(piece, lambda z, x, m, n: ((m * 2 + n) ^ key, x, z // 2, z % 2))
        source = band ^ key
        direct = lax.dynamic_update_slice(direct, piece, (source % 2 * part, source // 2 * strip))

    def target(x, m, n):
        return (x * per_lane + m % per_lane) * 2 + n

    for key in range(bands):
        entry = target(lane, major, minor) ^ key ^ beta
        piece = [lax.dynamic_index_in_dim(half[1], entry % run, 0, keepdims=False) for half in halves]
        piece = jnp.where(entry // run == 0, *piece).astype(jnp.float16)
        piece = grid.send(
            piece,
            lambda z, x, m, n: (z, m // per_lane, (target(x, m, n) ^ key) // 2, (target(x, m, n) ^ key) % 2),
        )
        source = beta ^ key
        place = (source // 2 % per_lane * strip, (source // 2 // per_lane * 2 + source % 2) * part)
        mirror = lax.dynamic_update_slice(mirror, piece, place)
    return direct, mirror


def body(coeffs, denominator, coupling, tile_cols, tile_count):
    rows = coeffs.shape[0]
    _, slots, tile = coupling.shape
    grid = Grid(lax.axis_size("alpha"), lax.axis_size("beta"))
    alpha, beta = lax.axis_index("alpha"), lax.axis_index("beta")
    band, lane = alpha // grid.lanes, alpha % grid.lanes
    major, minor = beta // 2, beta % 2
    every = jnp.arange(grid.bands, dtype=jnp.int32)
    tile_rows = (every * grid.lanes + lane) * rows // tile
    tile_columns = jnp.take(tile_cols, tile_rows, axis=0).reshape(-1)
    counts = jnp.take(tile_count, tile_rows)
    half = coeffs.astype(jnp.bfloat16)
    couplings, order, swaps = gather_couplings(grid, coupling, band, major, minor)
    pieces = len(couplings[0])
    offsets = (major ^ jnp.arange(pieces, dtype=jnp.int32)) * (rows // 2 // pieces)
    if pieces == 1:
        offsets = jnp.zeros((1,), jnp.int32)
    wanted = beta ^ every
    entries = jnp.argmax(order[None, :] == wanted[:, None], axis=1).astype(jnp.int32)

    growth = slots * tile * COUPLING_MAX
    largest = jnp.maximum(largest_anywhere(grid, jnp.max(jnp.abs(coeffs)), swaps), 1e-30)
    current = coeffs
    gate = swaps[-1]
    for step_index in range(STEPS):
        scale = HALF_TOP / (growth * largest)
        largest = largest * (1 + 2 * growth / DENOMINATOR_MIN)
        parts, places = to_columns(grid, half, band, lane, major, minor, gate)
        gate = None
        runs = [slice(0, grid.bands // 2), slice(grid.bands // 2, grid.bands)]
        halves = [
            products(couplings, parts, wanted[run], entries[run], tile_columns, counts, offsets, places, scale)
            for run in runs
        ]
        direct, mirror = bring_home(grid, halves, band, lane, major, minor)
        total = (direct.astype(jnp.float32) + mirror.astype(jnp.float32)) / scale
        current = current - total / denominator
        half = current.astype(jnp.bfloat16)
    return current


def solution(mesh):
    placed = (P("alpha", "beta"), P("alpha", "beta"), P("alpha", None, None), P(), P())
    return jax.shard_map(
        body, mesh=mesh, in_specs=placed, out_specs=P("alpha", "beta"), check_vma=False
    )
```

time: 649 us -> 620 us (0.955)
  the two profiles are of different devices: /device:TPU:25 before, /device:TPU:17 now
where the time goes in v3:
time: 620 us; the launch traced here: 613 us
  waiting for transfers between devices  257 us (41%)
  starting transfers between devices  171 us (28%)
  local copies, waits for them, and re-layouts  102 us (16%)
  other arithmetic  42.6 us (7%)
  Pallas kernels  37.2 us (6%)
    ppermute x80, waiting for transfers between devices, send(): return lax.ppermute(value, AXES, pairs)  242 us
    ppermute x80, starting transfers between devices, send(): return lax.ppermute(value, AXES, pairs)  154 us
    dynamic_update_slice x8, local copies, waits for them, and re-layouts, bring_home(): lax.dynamic_update_slice(direct, piece, (source % 2 * part, source // 2 *...  60.7 us
    pallas_call x4, Pallas kernels, products(): pl.pallas_call(lambda *refs: product_kernel(slots, pieces, *refs), grid_s...  37.2 us
    ppermute x5, starting transfers between devices, largest_anywhere(): largest = jnp.maximum(largest, lax.ppermute(largest, AXES, pairs))  17.2 us
    ppermute x5, waiting for transfers between devices, largest_anywhere(): largest = jnp.maximum(largest, lax.ppermute(largest, AXES, pairs))  15.4 us
    unnamed x151, local copies, waits for them, and re-layouts  15 us
  transfers between devices with their start and end apart: 85, of which 33 were waited for; matrix products, arithmetic and copies ran while one was open for 17% of the time, Pallas kernels for 3%

profile of v3, /device:TPU:17, one launch (start us, length us, event | category | flops | bytes accessed | tf_op | source)
XLA Modules:
  0.0 613.0 jit_solution(17120534848443989341)
XLA Ops:
  0.0 5.8 constant_dynamic-slice_fusion.11
  8.5 5.4 collective-permute-done
  25.2 4.7 collective-permute-start.6
  54.5 10.4 %collective-permute-start.13 = (bf16[2,192,768]{2,1,0:T(8,128)(2,1)}, bf16[2,192,768]{2,1,0:T(8,128)(2,1)S(1)}, u32[]{:S(2)}, u32[]{:S(2)}) collective-permute-start(bf16[2,192,768]{2,1,0:T(8,128)(2,1)} %collective-permute-done.1), channel_id=1, source_target_pairs={{0,8},{1,9},{2,10},{3,11},{4,12},{5,13},{6,14},{7,15},{8,0},{9,1},... | collective-permute-start | bytes 1769480 | tf_op jit(solution)/shard_map/ppermute | solution.py:37
  67.7 5.7 collective-permute-start.15
  84.9 4.5 collective-permute-start.34
  95.5 11.3 %collective-permute-done.11 = f32[8,128]{1,0:T(8,128)S(1)} collective-permute-done((f32[8,128]{1,0:T(8,128)S(1)}, f32[8,128]{1,0:T(8,128)S(1)}, u32[]{:S(2)}, u32[]{:S(2)}) %collective-permute-start.11) | collective-permute-done | bytes 4128 | tf_op jit(solution)/shard_map/ppermute | solution.py:51
  107.7 4.5 collective-permute-start.28
  116.8 13.2 %collective-permute-start.22 = (bf16[192,768]{1,0:T(8,128)(2,1)S(1)}, bf16[192,768]{1,0:T(8,128)(2,1)S(1)}, u32[]{:S(2)}, u32[]{:S(2)}) collective-permute-start(bf16[192,768]{1,0:T(8,128)(2,1)S(1)} %get-tuple-element.105), channel_id=1, source_target_pairs={{0,0},{1,8},{2,2},{3,10},{4,4},{5,12},{6,6},{7,14},{8,1},{9,9},{10... | collective-permute-start | bytes 884744 | tf_op jit(solution)/shard_map/ppermute | solution.py:37
  129.9 8.5 %collective-permute-done.28 = bf16[192,768]{1,0:T(8,128)(2,1)S(1)} collective-permute-done((bf16[192,768]{1,0:T(8,128)(2,1)S(1)}, bf16[192,768]{1,0:T(8,128)(2,1)S(1)}, u32[]{:S(2)}, u32[]{:S(2)}) %collective-permute-start.28) | collective-permute-done | bytes 294944 | tf_op jit(solution)/shard_map/ppermute | solution.py:37
  138.6 12.0 %collective-permute-start.12 = (f32[8,128]{1,0:T(8,128)S(1)}, f32[8,128]{1,0:T(8,128)S(1)}, u32[]{:S(2)}, u32[]{:S(2)}) collective-permute-start(f32[8,128]{1,0:T(8,128)S(1)} %max.22), channel_id=1, source_target_pairs={{0,16},{1,17},{2,18},{3,19},{4,20},{5,21},{6,22},{7,23},{8,24},{9,... | collective-permute-start | bytes 12296 | tf_op jit(solution)/shard_map/ppermute | solution.py:51
  160.8 6.5 %collective-permute-done.43.refs_29_ = bf16[2,192,768]{2,1,0:T(8,128)(2,1)} collective-permute-done((bf16[2,192,768]{2,1,0:T(8,128)(2,1)S(1)}, bf16[2,192,768]{2,1,0:T(8,128)(2,1)}, u32[]{:S(2)}, u32[]{:S(2)}) %collective-permute-start.43) | collective-permute-done | bytes 589856 | tf_op jit(solution)/shard_map/ppermute | solution.py:37
  168.8 11.2 %collective-permute-done.37.refs_25_ = bf16[2,192,768]{2,1,0:T(8,128)(2,1)S(1)} collective-permute-done((bf16[2,192,768]{2,1,0:T(8,128)(2,1)S(1)}, bf16[2,192,768]{2,1,0:T(8,128)(2,1)S(1)}, u32[]{:S(2)}, u32[]{:S(2)}) %collective-permute-start.37) | collective-permute-done | bytes 589856 | tf_op jit(solution)/shard_map/ppermute | solution.py:37
  182.3 10.4 %collective-permute-done.31.refs_21_ = bf16[2,192,768]{2,1,0:T(8,128)(2,1)S(1)} collective-permute-done((bf16[2,192,768]{2,1,0:T(8,128)(2,1)S(1)}, bf16[2,192,768]{2,1,0:T(8,128)(2,1)S(1)}, u32[]{:S(2)}, u32[]{:S(2)}) %collective-permute-start.31) | collective-permute-done | bytes 589856 | tf_op jit(solution)/shard_map/ppermute | solution.py:37
  205.7 15.1 %collective-permute-done.16.refs_10_ = bf16[4,192,768]{2,1,0:T(8,128)(2,1)} collective-permute-done((bf16[4,192,768]{2,1,0:T(8,128)(2,1)S(1)}, bf16[4,192,768]{2,1,0:T(8,128)(2,1)}, u32[]{:S(2)}, u32[]{:S(2)}) %collective-permute-start.16) | collective-permute-done | bytes 1179680 | tf_op jit(solution)/shard_map/ppermute | solution.py:37
  226.6 19.5 %collective-permute-done.18.refs_12_ = bf16[4,192,768]{2,1,0:T(8,128)(2,1)} collective-permute-done((bf16[4,192,768]{2,1,0:T(8,128)(2,1)}, bf16[4,192,768]{2,1,0:T(8,128)(2,1)}, u32[]{:S(2)}, u32[]{:S(2)}) %collective-permute-start.18) | collective-permute-done | bytes 1179680 | tf_op jit(solution)/shard_map/ppermute | solution.py:37
  246.0 19.3 %collective-permute-done.20.refs_14_ = bf16[4,192,768]{2,1,0:T(8,128)(2,1)} collective-permute-done((bf16[4,192,768]{2,1,0:T(8,128)(2,1)}, bf16[4,192,768]{2,1,0:T(8,128)(2,1)}, u32[]{:S(2)}, u32[]{:S(2)}) %collective-permute-start.20) | collective-permute-done | bytes 1179680 | tf_op jit(solution)/shard_map/ppermute | solution.py:37
  277.7 9.6 %shard_map.100 = (f32[2,384,768]{2,1,0:T(8,128)}, f32[2,768,384]{2,1,0:T(8,128)}) custom-call(s32[2]{0:T(128)S(1)} %copy-done.36, s32[2]{0:T(128)S(1)} %get-tuple-element.109.refs_1_, s32[16]{0:T(128)S(1)} %select_n.679.refs_2_, s32[4]{0:T(128)S(1)} %broadcast_select_fusion.5.refs_3_, s32[2]{0:T(128)S(1)} %get-tuple-element.113.refs_4_, ...), custom_call_target="tpu_custom_call" | custom-call | flops 3623878656 | bytes 14155776 | tf_op jit(solution)/shard_map/pallas_call | solution.py:191
  289.6 5.0 collective-permute-start.45
  294.8 9.6 %shard_map.101 = (f32[2,384,768]{2,1,0:T(8,128)}, f32[2,768,384]{2,1,0:T(8,128)}) custom-call(s32[2]{0:T(128)S(1)} %copy-done.35, s32[2]{0:T(128)S(1)} %get-tuple-element.110.refs_1_, s32[16]{0:T(128)S(1)} %select_n.679.refs_2_, s32[4]{0:T(128)S(1)} %copy-done.33, s32[2]{0:T(128)S(1)} %get-tuple-element.113.refs_4_, s32[32]{0:T(128)S(1)} %stack.308.refs_5_, ...), custom_call_target="tpu_custom_call" | custom-call | flops 3623878656 | bytes 14155776 | tf_op jit(solution)/shard_map/pallas_call | solution.py:191
  309.3 6.0 collective-permute-start.49
  315.8 14.3 %collective-permute-done.45 = f16[384,768]{1,0:T(8,128)(2,1)} collective-permute-done((f16[384,768]{1,0:T(8,128)(2,1)S(1)}, f16[384,768]{1,0:T(8,128)(2,1)}, u32[]{:S(2)}, u32[]{:S(2)}) %collective-permute-start.45) | collective-permute-done | bytes 589856 | tf_op jit(solution)/shard_map/ppermute | solution.py:37
  330.2 11.6 %collective-permute-done.46 = f16[384,768]{1,0:T(8,128)(2,1)} collective-permute-done((f16[384,768]{1,0:T(8,128)(2,1)S(1)}, f16[384,768]{1,0:T(8,128)(2,1)}, u32[]{:S(2)}, u32[]{:S(2)}) %collective-permute-start.46) | collective-permute-done | bytes 589856 | tf_op jit(solution)/shard_map/ppermute | solution.py:37
  341.8 9.0 %collective-permute-start.48 = (f16[384,768]{1,0:T(8,128)(2,1)}, f16[384,768]{1,0:T(8,128)(2,1)}, u32[]{:S(2)}, u32[]{:S(2)}) collective-permute-start(f16[384,768]{1,0:T(8,128)(2,1)} %get-tuple-element.73), channel_id=1, source_target_pairs={{0,24},{1,16},{2,8},{3,0},{4,28},{5,20},{6,12},{7,4},{8,25},{9,17}... | collective-permute-start | bytes 1769480 | tf_op jit(solution)/shard_map/ppermute | solution.py:37
  351.0 8.4 %dynamic_update_slice.56 = f16[768,1536]{1,0:T(8,128)(2,1)S(1)} dynamic-update-slice(f16[768,1536]{1,0:T(8,128)(2,1)S(1)} %broadcast.200.clone.2, f16[384,768]{1,0:T(8,128)(2,1)} %collective-permute-done.45, s32[]{:T(128)S(6)} %select_n.700, s32[]{:T(128)S(6)} %select_n.701) | dynamic-update-slice | bytes 1179652 | tf_op jit(solution)/shard_map/dynamic_update_slice | solution.py:240
  359.4 7.6 %dynamic_update_slice.57 = f16[768,1536]{1,0:T(8,128)(2,1)S(1)} dynamic-update-slice(f16[768,1536]{1,0:T(8,128)(2,1)S(1)} %dynamic_update_slice.56, f16[384,768]{1,0:T(8,128)(2,1)} %collective-permute-done.46, s32[]{:T(128)S(6)} %select_n.703, s32[]{:T(128)S(6)} %select_n.705) | dynamic-update-slice | bytes 1179652 | tf_op jit(solution)/shard_map/dynamic_update_slice | solution.py:240
  367.0 8.3 %dynamic_update_slice.58 = f16[768,1536]{1,0:T(8,128)(2,1)S(1)} dynamic-update-slice(f16[768,1536]{1,0:T(8,128)(2,1)S(1)} %dynamic_update_slice.57, f16[384,768]{1,0:T(8,128)(2,1)} %collective-permute-done.47, s32[]{:T(128)S(6)} %select_n.707, s32[]{:T(128)S(6)} %select_n.709) | dynamic-update-slice | bytes 1179652 | tf_op jit(solution)/shard_map/dynamic_update_slice | solution.py:240
  380.6 4.1 collective-permute-done.48
  384.7 7.8 %dynamic_update_slice.59 = f16[768,1536]{1,0:T(8,128)(2,1)S(1)} dynamic-update-slice(f16[768,1536]{1,0:T(8,128)(2,1)S(1)} %dynamic_update_slice.58, f16[384,768]{1,0:T(8,128)(2,1)} %collective-permute-done.48, s32[]{:T(128)S(6)} %select_n.711, s32[]{:T(128)S(6)} %select_n.713) | dynamic-update-slice | bytes 1179652 | tf_op jit(solution)/shard_map/dynamic_update_slice | solution.py:240
  399.3 6.0 collective-permute-done.71
  405.4 4.5 collective-permute-start.72
  411.7 4.5 collective-permute-start.66
  418.5 4.5 collective-permute-start.60
  423.0 6.1 %collective-permute-done.73 = bf16[192,768]{1,0:T(8,128)(2,1)S(1)} collective-permute-done((bf16[192,768]{1,0:T(8,128)(2,1)S(1)}, bf16[192,768]{1,0:T(8,128)(2,1)S(1)}, u32[]{:S(2)}, u32[]{:S(2)}) %collective-permute-start.73) | collective-permute-done | bytes 294944 | tf_op jit(solution)/shard_map/ppermute | solution.py:37
  432.3 4.3 collective-permute-done.67
  441.3 13.9 %collective-permute-done.61 = bf16[192,768]{1,0:T(8,128)(2,1)S(1)} collective-permute-done((bf16[192,768]{1,0:T(8,128)(2,1)S(1)}, bf16[192,768]{1,0:T(8,128)(2,1)S(1)}, u32[]{:S(2)}, u32[]{:S(2)}) %collective-permute-start.61) | collective-permute-done | bytes 294944 | tf_op jit(solution)/shard_map/ppermute | solution.py:37
  462.6 7.7 %collective-permute-done.69.refs_25_ = bf16[2,192,768]{2,1,0:T(8,128)(2,1)S(1)} collective-permute-done((bf16[2,192,768]{2,1,0:T(8,128)(2,1)S(1)}, bf16[2,192,768]{2,1,0:T(8,128)(2,1)S(1)}, u32[]{:S(2)}, u32[]{:S(2)}) %collective-permute-start.69) | collective-permute-done | bytes 589856 | tf_op jit(solution)/shard_map/ppermute | solution.py:37
  471.3 11.6 %collective-permute-done.63.refs_21_ = bf16[2,192,768]{2,1,0:T(8,128)(2,1)S(1)} collective-permute-done((bf16[2,192,768]{2,1,0:T(8,128)(2,1)S(1)}, bf16[2,192,768]{2,1,0:T(8,128)(2,1)S(1)}, u32[]{:S(2)}, u32[]{:S(2)}) %collective-permute-start.63) | collective-permute-done | bytes 589856 | tf_op jit(solution)/shard_map/ppermute | solution.py:37
  484.0 11.6 %collective-permute-done.57.refs_17_ = bf16[2,192,768]{2,1,0:T(8,128)(2,1)S(1)} collective-permute-done((bf16[2,192,768]{2,1,0:T(8,128)(2,1)S(1)}, bf16[2,192,768]{2,1,0:T(8,128)(2,1)S(1)}, u32[]{:S(2)}, u32[]{:S(2)}) %collective-permute-start.57) | collective-permute-done | bytes 589856 | tf_op jit(solution)/shard_map/ppermute | solution.py:37
  497.9 9.0 %shard_map.102 = (f32[2,384,768]{2,1,0:T(8,128)}, f32[2,768,384]{2,1,0:T(8,128)}) custom-call(s32[2]{0:T(128)S(1)} %copy-done.37, s32[2]{0:T(128)S(1)} %copy-done.41, s32[16]{0:T(128)S(1)} %select_n.679.refs_2_, s32[4]{0:T(128)S(1)} %copy-done.34, s32[2]{0:T(128)S(1)} %get-tuple-element.113.refs_4_, s32[32]{0:T(128)S(1)} %stack.308.refs_5_, ...), custom_call_target="tpu_custom_call" | custom-call | flops 3623878656 | bytes 14155776 | tf_op jit(solution)/shard_map/pallas_call | solution.py:191
  515.8 9.0 %shard_map.103 = (f32[2,384,768]{2,1,0:T(8,128)}, f32[2,768,384]{2,1,0:T(8,128)}) custom-call(s32[2]{0:T(128)S(1)} %copy-done.35, s32[2]{0:T(128)S(1)} %copy-done.39, s32[16]{0:T(128)S(1)} %select_n.679.refs_2_, s32[4]{0:T(128)S(1)} %copy-done.34, s32[2]{0:T(128)S(1)} %get-tuple-element.113.refs_4_, s32[32]{0:T(128)S(1)} %stack.308.refs_5_, ...), custom_call_target="tpu_custom_call" | custom-call | flops 3623878656 | bytes 14155776 | tf_op jit(solution)/shard_map/pallas_call | solution.py:191
  529.5 20.0 %collective-permute-done.77 = f16[384,768]{1,0:T(8,128)(2,1)S(1)} collective-permute-done((f16[384,768]{1,0:T(8,128)(2,1)}, f16[384,768]{1,0:T(8,128)(2,1)S(1)}, u32[]{:S(2)}, u32[]{:S(2)}) %collective-permute-start.77) | collective-permute-done | bytes 589856 | tf_op jit(solution)/shard_map/ppermute | solution.py:37
  550.0 12.2 %collective-permute-done.78 = f16[384,768]{1,0:T(8,128)(2,1)} collective-permute-done((f16[384,768]{1,0:T(8,128)(2,1)}, f16[384,768]{1,0:T(8,128)(2,1)}, u32[]{:S(2)}, u32[]{:S(2)}) %collective-permute-start.78) | collective-permute-done | bytes 589856 | tf_op jit(solution)/shard_map/ppermute | solution.py:37
  563.6 15.4 %collective-permute-start.84 = (f16[768,384]{1,0:T(8,128)(2,1)S(1)}, f16[768,384]{1,0:T(8,128)(2,1)S(1)}, u32[]{:S(2)}, u32[]{:S(2)}) collective-permute-start(f16[768,384]{1,0:T(8,128)(2,1)S(1)} %get-tuple-element.47), channel_id=1, source_target_pairs={{0,3},{1,2},{2,7},{3,6},{4,1},{5,0},{6,5},{7,4},{8,11},{9,10},{10,... | collective-permute-start | bytes 1769480 | tf_op jit(solution)/shard_map/ppermute | solution.py:37
  579.1 5.5 dynamic_update_slice.64
  584.7 7.6 %dynamic_update_slice.65 = f16[768,1536]{1,0:T(8,128)(2,1)S(1)} dynamic-update-slice(f16[768,1536]{1,0:T(8,128)(2,1)S(1)} %dynamic_update_slice.64, f16[384,768]{1,0:T(8,128)(2,1)} %collective-permute-done.78, s32[]{:T(128)S(6)} %select_n.703, s32[]{:T(128)S(6)} %select_n.705) | dynamic-update-slice | bytes 1179652 | tf_op jit(solution)/shard_map/dynamic_update_slice | solution.py:240
  592.3 8.0 %dynamic_update_slice.66 = f16[768,1536]{1,0:T(8,128)(2,1)S(1)} dynamic-update-slice(f16[768,1536]{1,0:T(8,128)(2,1)S(1)} %dynamic_update_slice.65, f16[384,768]{1,0:T(8,128)(2,1)S(1)} %collective-permute-done.79, s32[]{:T(128)S(6)} %select_n.707, s32[]{:T(128)S(6)} %select_n.709) | dynamic-update-slice | bytes 1179652 | tf_op jit(solution)/shard_map/dynamic_update_slice | solution.py:240
  600.3 7.5 %dynamic_update_slice.67 = f16[768,1536]{1,0:T(8,128)(2,1)S(1)} dynamic-update-slice(f16[768,1536]{1,0:T(8,128)(2,1)S(1)} %dynamic_update_slice.66, f16[384,768]{1,0:T(8,128)(2,1)S(1)} %collective-permute-done.80, s32[]{:T(128)S(6)} %select_n.711, s32[]{:T(128)S(6)} %select_n.713) | dynamic-update-slice | bytes 1179652 | tf_op jit(solution)/shard_map/dynamic_update_slice | solution.py:240
  (378 shorter events, 171.9 us)
Async XLA Ops:
  18.5 28.0 %collective-permute-start.39 = (bf16[192,768]{1,0:T(8,128)(2,1)}, bf16[192,768]{1,0:T(8,128)(2,1)}, u32[]{:S(2)}, u32[]{:S(2)}) collective-permute-start(bf16[192,768]{1,0:T(8,128)(2,1)} %get-tuple-element.96), channel_id=1, source_target_pairs={{0,2},{1,3},{2,0},{3,1},{4,6},{5,7},{6,4},{7,5},{8,10},{9,11},{10,... | collective-permute-start | bytes 884744 | tf_op jit(solution)/shard_map/ppermute | solution.py:37
  30.7 23.8 %collective-permute-start.33 = (bf16[192,768]{1,0:T(8,128)(2,1)}, bf16[192,768]{1,0:T(8,128)(2,1)}, u32[]{:S(2)}, u32[]{:S(2)}) collective-permute-start(bf16[192,768]{1,0:T(8,128)(2,1)} %get-tuple-element.100), channel_id=1, source_target_pairs={{0,2},{1,3},{2,0},{3,1},{4,6},{5,7},{6,4},{7,5},{8,10},{9,11},{10,... | collective-permute-start | bytes 884744 | tf_op jit(solution)/shard_map/ppermute | solution.py:37
  31.6 33.3 %collective-permute-start.27 = (bf16[192,768]{1,0:T(8,128)(2,1)}, bf16[192,768]{1,0:T(8,128)(2,1)}, u32[]{:S(2)}, u32[]{:S(2)}) collective-permute-start(bf16[192,768]{1,0:T(8,128)(2,1)} %get-tuple-element.104), channel_id=1, source_target_pairs={{0,2},{1,3},{2,0},{3,1},{4,6},{5,7},{6,4},{7,5},{8,10},{9,11},{10,... | collective-permute-start | bytes 884744 | tf_op jit(solution)/shard_map/ppermute | solution.py:37
  46.5 28.0 %collective-permute-start.7 = (bf16[2,192,768]{2,1,0:T(8,128)(2,1)}, bf16[2,192,768]{2,1,0:T(8,128)(2,1)}, u32[]{:S(2)}, u32[]{:S(2)}) collective-permute-start(bf16[2,192,768]{2,1,0:T(8,128)(2,1)} %pad_maximum_fusion.6), channel_id=1, source_target_pairs={{0,0},{1,1},{2,2},{3,3},{4,4},{5,5},{6,6},{7,7},{8,16},{9,17},{10,... | collective-permute-start | bytes 1769480 | tf_op jit(solution)/shard_map/ppermute | solution.py:37
  50.1 29.3 %collective-permute-start.10 = (bf16[2,192,768]{2,1,0:T(8,128)(2,1)}, bf16[2,192,768]{2,1,0:T(8,128)(2,1)}, u32[]{:S(2)}, u32[]{:S(2)}) collective-permute-start(bf16[2,192,768]{2,1,0:T(8,128)(2,1)} %pad_maximum_fusion.7), channel_id=1, source_target_pairs={{0,0},{1,1},{2,2},{3,3},{4,4},{5,5},{6,6},{7,7},{8,16},{9,17},{10,... | collective-permute-start | bytes 1769480 | tf_op jit(solution)/shard_map/ppermute | solution.py:37
  54.3 27.0 %collective-permute-start.21 = (bf16[192,768]{1,0:T(8,128)(2,1)S(1)}, bf16[192,768]{1,0:T(8,128)(2,1)S(1)}, u32[]{:S(2)}, u32[]{:S(2)}) collective-permute-start(bf16[192,768]{1,0:T(8,128)(2,1)S(1)} %get-tuple-element.108), channel_id=1, source_target_pairs={{0,2},{1,3},{2,0},{3,1},{4,6},{5,7},{6,4},{7,5},{8,10},{9,11},{10,... | collective-permute-start | bytes 884744 | tf_op jit(solution)/shard_map/ppermute | solution.py:37
  54.5 35.0 %collective-permute-start.13 = (bf16[2,192,768]{2,1,0:T(8,128)(2,1)}, bf16[2,192,768]{2,1,0:T(8,128)(2,1)S(1)}, u32[]{:S(2)}, u32[]{:S(2)}) collective-permute-start(bf16[2,192,768]{2,1,0:T(8,128)(2,1)} %collective-permute-done.1), channel_id=1, source_target_pairs={{0,8},{1,9},{2,10},{3,11},{4,12},{5,13},{6,14},{7,15},{8,0},{9,1},... | collective-permute-start | bytes 1769480 | tf_op jit(solution)/shard_map/ppermute | solution.py:37
  67.7 25.6 %collective-permute-start.15 = (bf16[2,192,768]{2,1,0:T(8,128)(2,1)}, bf16[2,192,768]{2,1,0:T(8,128)(2,1)S(1)}, u32[]{:S(2)}, u32[]{:S(2)}) collective-permute-start(bf16[2,192,768]{2,1,0:T(8,128)(2,1)} %collective-permute-done.4), channel_id=1, source_target_pairs={{0,8},{1,9},{2,10},{3,11},{4,12},{5,13},{6,14},{7,15},{8,0},{9,1},... | collective-permute-start | bytes 1769480 | tf_op jit(solution)/shard_map/ppermute | solution.py:37
  79.4 28.3 %collective-permute-start.40 = (bf16[192,768]{1,0:T(8,128)(2,1)S(1)}, bf16[192,768]{1,0:T(8,128)(2,1)S(1)}, u32[]{:S(2)}, u32[]{:S(2)}) collective-permute-start(bf16[192,768]{1,0:T(8,128)(2,1)S(1)} %get-tuple-element.93), channel_id=1, source_target_pairs={{0,0},{1,8},{2,2},{3,10},{4,4},{5,12},{6,6},{7,14},{8,1},{9,9},{10... | collective-permute-start | bytes 884744 | tf_op jit(solution)/shard_map/ppermute | solution.py:37
  81.4 30.9 %collective-permute-start.41 = (bf16[192,768]{1,0:T(8,128)(2,1)S(1)}, bf16[192,768]{1,0:T(8,128)(2,1)S(1)}, u32[]{:S(2)}, u32[]{:S(2)}) collective-permute-start(bf16[192,768]{1,0:T(8,128)(2,1)S(1)} %get-tuple-element.94), channel_id=1, source_target_pairs={{0,16},{1,24},{2,18},{3,26},{4,20},{5,28},{6,22},{7,30},{8,17},{9,... | collective-permute-start | bytes 884744 | tf_op jit(solution)/shard_map/ppermute | solution.py:37
  84.9 29.1 %collective-permute-start.34 = (bf16[192,768]{1,0:T(8,128)(2,1)S(1)}, bf16[192,768]{1,0:T(8,128)(2,1)S(1)}, u32[]{:S(2)}, u32[]{:S(2)}) collective-permute-start(bf16[192,768]{1,0:T(8,128)(2,1)S(1)} %get-tuple-element.97), channel_id=1, source_target_pairs={{0,0},{1,8},{2,2},{3,10},{4,4},{5,12},{6,6},{7,14},{8,1},{9,9},{10... | collective-permute-start | bytes 884744 | tf_op jit(solution)/shard_map/ppermute | solution.py:37
  93.4 62.4 %collective-permute-start.17 = (bf16[2,192,768]{2,1,0:T(8,128)(2,1)}, bf16[2,192,768]{2,1,0:T(8,128)(2,1)S(1)}, u32[]{:S(2)}, u32[]{:S(2)}) collective-permute-start(bf16[2,192,768]{2,1,0:T(8,128)(2,1)} %collective-permute-done.7), channel_id=1, source_target_pairs={{0,8},{1,9},{2,10},{3,11},{4,12},{5,13},{6,14},{7,15},{8,0},{9,1},... | collective-permute-start | bytes 1769480 | tf_op jit(solution)/shard_map/ppermute | solution.py:37
  107.7 30.7 %collective-permute-start.28 = (bf16[192,768]{1,0:T(8,128)(2,1)S(1)}, bf16[192,768]{1,0:T(8,128)(2,1)S(1)}, u32[]{:S(2)}, u32[]{:S(2)}) collective-permute-start(bf16[192,768]{1,0:T(8,128)(2,1)S(1)} %get-tuple-element.101), channel_id=1, source_target_pairs={{0,0},{1,8},{2,2},{3,10},{4,4},{5,12},{6,6},{7,14},{8,1},{9,9},{10... | collective-permute-start | bytes 884744 | tf_op jit(solution)/shard_map/ppermute | solution.py:37
  112.2 44.3 %collective-permute-start.19 = (bf16[2,192,768]{2,1,0:T(8,128)(2,1)}, bf16[2,192,768]{2,1,0:T(8,128)(2,1)S(1)}, u32[]{:S(2)}, u32[]{:S(2)}) collective-permute-start(bf16[2,192,768]{2,1,0:T(8,128)(2,1)} %collective-permute-done.10), channel_id=1, source_target_pairs={{0,8},{1,9},{2,10},{3,11},{4,12},{5,13},{6,14},{7,15},{8,0},{9,1},... | collective-permute-start | bytes 1769480 | tf_op jit(solution)/shard_map/ppermute | solution.py:37
  114.0 24.5 %collective-permute-start.29 = (bf16[192,768]{1,0:T(8,128)(2,1)S(1)}, bf16[192,768]{1,0:T(8,128)(2,1)S(1)}, u32[]{:S(2)}, u32[]{:S(2)}) collective-permute-start(bf16[192,768]{1,0:T(8,128)(2,1)S(1)} %get-tuple-element.102), channel_id=1, source_target_pairs={{0,16},{1,24},{2,18},{3,26},{4,20},{5,28},{6,22},{7,30},{8,17},{9,... | collective-permute-start | bytes 884744 | tf_op jit(solution)/shard_map/ppermute | solution.py:37
  116.8 38.7 %collective-permute-start.22 = (bf16[192,768]{1,0:T(8,128)(2,1)S(1)}, bf16[192,768]{1,0:T(8,128)(2,1)S(1)}, u32[]{:S(2)}, u32[]{:S(2)}) collective-permute-start(bf16[192,768]{1,0:T(8,128)(2,1)S(1)} %get-tuple-element.105), channel_id=1, source_target_pairs={{0,0},{1,8},{2,2},{3,10},{4,4},{5,12},{6,6},{7,14},{8,1},{9,9},{10... | collective-permute-start | bytes 884744 | tf_op jit(solution)/shard_map/ppermute | solution.py:37
  155.5 24.5 %collective-permute-start.37 = (bf16[2,192,768]{2,1,0:T(8,128)(2,1)S(1)}, bf16[2,192,768]{2,1,0:T(8,128)(2,1)S(1)}, u32[]{:S(2)}, u32[]{:S(2)}) collective-permute-start(bf16[2,192,768]{2,1,0:T(8,128)(2,1)S(1)} %pad_maximum_fusion.13.refs_23_), channel_id=1, source_target_pairs={{0,4},{1,5},{2,6},{3,7},{4,0},{5,1},{6,2},{7,3},{8,12},{9,13},{10,... | collective-permute-start | bytes 1769480 | tf_op jit(solution)/shard_map/ppermute | solution.py:37
  155.8 24.2 %collective-permute-start.36 = (bf16[2,192,768]{2,1,0:T(8,128)(2,1)S(1)}, bf16[2,192,768]{2,1,0:T(8,128)(2,1)S(1)}, u32[]{:S(2)}, u32[]{:S(2)}) collective-permute-start(bf16[2,192,768]{2,1,0:T(8,128)(2,1)S(1)} %pad_maximum_fusion.13.refs_23_), channel_id=1, source_target_pairs={{0,1},{1,0},{2,3},{3,2},{4,5},{5,4},{6,7},{7,6},{8,9},{9,8},{10,11... | collective-permute-start | bytes 1769480 | tf_op jit(solution)/shard_map/ppermute | solution.py:37
  156.5 36.2 %collective-permute-start.31 = (bf16[2,192,768]{2,1,0:T(8,128)(2,1)S(1)}, bf16[2,192,768]{2,1,0:T(8,128)(2,1)S(1)}, u32[]{:S(2)}, u32[]{:S(2)}) collective-permute-start(bf16[2,192,768]{2,1,0:T(8,128)(2,1)S(1)} %pad_maximum_fusion.11.refs_19_), channel_id=1, source_target_pairs={{0,4},{1,5},{2,6},{3,7},{4,0},{5,1},{6,2},{7,3},{8,12},{9,13},{10,... | collective-permute-start | bytes 1769480 | tf_op jit(solution)/shard_map/ppermute | solution.py:37
  167.3 38.4 %collective-permute-start.14 = (bf16[4,192,768]{2,1,0:T(8,128)(2,1)S(1)}, bf16[4,192,768]{2,1,0:T(8,128)(2,1)S(1)}, u32[]{:S(2)}, u32[]{:S(2)}) collective-permute-start(bf16[4,192,768]{2,1,0:T(8,128)(2,1)S(1)} %pad_maximum_fusion.refs_7_), channel_id=1, source_target_pairs={{0,2},{1,3},{2,0},{3,1},{4,6},{5,7},{6,4},{7,5},{8,10},{9,11},{10,... | collective-permute-start | bytes 3538952 | tf_op jit(solution)/shard_map/ppermute | solution.py:37
  168.7 52.1 %collective-permute-start.16 = (bf16[4,192,768]{2,1,0:T(8,128)(2,1)S(1)}, bf16[4,192,768]{2,1,0:T(8,128)(2,1)}, u32[]{:S(2)}, u32[]{:S(2)}) collective-permute-start(bf16[4,192,768]{2,1,0:T(8,128)(2,1)S(1)} %pad_maximum_fusion.1.refs_9_), channel_id=1, source_target_pairs={{0,2},{1,3},{2,0},{3,1},{4,6},{5,7},{6,4},{7,5},{8,10},{9,11},{10,... | collective-permute-start | bytes 3538952 | tf_op jit(solution)/shard_map/ppermute | solution.py:37
  197.4 23.4 %collective-permute-start.44 = (bf16[2,192,768]{2,1,0:T(8,128)(2,1)}, bf16[2,192,768]{2,1,0:T(8,128)(2,1)}, u32[]{:S(2)}, u32[]{:S(2)}) collective-permute-start(bf16[2,192,768]{2,1,0:T(8,128)(2,1)} %collective-permute-done.43.refs_29_), channel_id=1, source_target_pairs={{0,1},{1,0},{2,3},{3,2},{4,5},{5,4},{6,7},{7,6},{8,9},{9,8},{10,11... | collective-permute-start | bytes 1769480 | tf_op jit(solution)/shard_map/ppermute | solution.py:37
  201.3 44.8 %collective-permute-start.18 = (bf16[4,192,768]{2,1,0:T(8,128)(2,1)}, bf16[4,192,768]{2,1,0:T(8,128)(2,1)}, u32[]{:S(2)}, u32[]{:S(2)}) collective-permute-start(bf16[4,192,768]{2,1,0:T(8,128)(2,1)} %pad_maximum_fusion.2.refs_11_), channel_id=1, source_target_pairs={{0,2},{1,3},{2,0},{3,1},{4,6},{5,7},{6,4},{7,5},{8,10},{9,11},{10,... | collective-permute-start | bytes 3538952 | tf_op jit(solution)/shard_map/ppermute | solution.py:37
  203.5 61.8 %collective-permute-start.20 = (bf16[4,192,768]{2,1,0:T(8,128)(2,1)}, bf16[4,192,768]{2,1,0:T(8,128)(2,1)}, u32[]{:S(2)}, u32[]{:S(2)}) collective-permute-start(bf16[4,192,768]{2,1,0:T(8,128)(2,1)} %pad_maximum_fusion.3.refs_13_), channel_id=1, source_target_pairs={{0,2},{1,3},{2,0},{3,1},{4,6},{5,7},{6,4},{7,5},{8,10},{9,11},{10,... | collective-permute-start | bytes 3538952 | tf_op jit(solution)/shard_map/ppermute | solution.py:37
  289.6 40.6 %collective-permute-start.45 = (f16[384,768]{1,0:T(8,128)(2,1)S(1)}, f16[384,768]{1,0:T(8,128)(2,1)}, u32[]{:S(2)}, u32[]{:S(2)}) collective-permute-start(f16[384,768]{1,0:T(8,128)(2,1)S(1)} %get-tuple-element.76), channel_id=1, source_target_pairs={{0,0},{1,8},{2,16},{3,24},{4,4},{5,12},{6,20},{7,28},{8,1},{9,9},{... | collective-permute-start | bytes 1769480 | tf_op jit(solution)/shard_map/ppermute | solution.py:37
  294.6 47.2 %collective-permute-start.46 = (f16[384,768]{1,0:T(8,128)(2,1)S(1)}, f16[384,768]{1,0:T(8,128)(2,1)}, u32[]{:S(2)}, u32[]{:S(2)}) collective-permute-start(f16[384,768]{1,0:T(8,128)(2,1)S(1)} %get-tuple-element.75), channel_id=1, source_target_pairs={{0,8},{1,0},{2,24},{3,16},{4,12},{5,4},{6,28},{7,20},{8,9},{9,1},{... | collective-permute-start | bytes 1769480 | tf_op jit(solution)/shard_map/ppermute | solution.py:37
  307.4 34.4 %collective-permute-start.47 = (f16[384,768]{1,0:T(8,128)(2,1)S(1)}, f16[384,768]{1,0:T(8,128)(2,1)}, u32[]{:S(2)}, u32[]{:S(2)}) collective-permute-start(f16[384,768]{1,0:T(8,128)(2,1)S(1)} %get-tuple-element.74), channel_id=1, source_target_pairs={{0,16},{1,24},{2,0},{3,8},{4,20},{5,28},{6,4},{7,12},{8,17},{9,25}... | collective-permute-start | bytes 1769480 | tf_op jit(solution)/shard_map/ppermute | solution.py:37
  309.3 66.1 %collective-permute-start.49 = (f16[768,384]{1,0:T(8,128)(2,1)}, f16[768,384]{1,0:T(8,128)(2,1)}, u32[]{:S(2)}, u32[]{:S(2)}) collective-permute-start(f16[768,384]{1,0:T(8,128)(2,1)} %get-tuple-element.54), channel_id=1, source_target_pairs={{0,0},{1,1},{2,4},{3,5},{4,2},{5,3},{6,6},{7,7},{8,8},{9,9},{10,12... | collective-permute-start | bytes 1769480 | tf_op jit(solution)/shard_map/ppermute | solution.py:37
  315.2 61.6 %collective-permute-start.50 = (f16[768,384]{1,0:T(8,128)(2,1)}, f16[768,384]{1,0:T(8,128)(2,1)}, u32[]{:S(2)}, u32[]{:S(2)}) collective-permute-start(f16[768,384]{1,0:T(8,128)(2,1)} %get-tuple-element.53), channel_id=1, source_target_pairs={{0,1},{1,0},{2,5},{3,4},{4,3},{5,2},{6,7},{7,6},{8,9},{9,8},{10,13... | collective-permute-start | bytes 1769480 | tf_op jit(solution)/shard_map/ppermute | solution.py:37
  330.2 47.9 %collective-permute-start.51 = (f16[768,384]{1,0:T(8,128)(2,1)}, f16[768,384]{1,0:T(8,128)(2,1)}, u32[]{:S(2)}, u32[]{:S(2)}) collective-permute-start(f16[768,384]{1,0:T(8,128)(2,1)} %get-tuple-element.52), channel_id=1, source_target_pairs={{0,2},{1,3},{2,6},{3,7},{4,0},{5,1},{6,4},{7,5},{8,10},{9,11},{10,... | collective-permute-start | bytes 1769480 | tf_op jit(solution)/shard_map/ppermute | solution.py:37
  341.8 37.6 %collective-permute-start.52 = (f16[768,384]{1,0:T(8,128)(2,1)}, f16[768,384]{1,0:T(8,128)(2,1)}, u32[]{:S(2)}, u32[]{:S(2)}) collective-permute-start(f16[768,384]{1,0:T(8,128)(2,1)} %get-tuple-element.51), channel_id=1, source_target_pairs={{0,3},{1,2},{2,7},{3,6},{4,1},{5,0},{6,5},{7,4},{8,11},{9,10},{10,... | collective-permute-start | bytes 1769480 | tf_op jit(solution)/shard_map/ppermute | solution.py:37
  341.8 42.9 %collective-permute-start.48 = (f16[384,768]{1,0:T(8,128)(2,1)}, f16[384,768]{1,0:T(8,128)(2,1)}, u32[]{:S(2)}, u32[]{:S(2)}) collective-permute-start(f16[384,768]{1,0:T(8,128)(2,1)} %get-tuple-element.73), channel_id=1, source_target_pairs={{0,24},{1,16},{2,8},{3,0},{4,28},{5,20},{6,12},{7,4},{8,25},{9,17}... | collective-permute-start | bytes 1769480 | tf_op jit(solution)/shard_map/ppermute | solution.py:37
  429.2 33.2 %collective-permute-start.75 = (bf16[2,192,768]{2,1,0:T(8,128)(2,1)S(1)}, bf16[2,192,768]{2,1,0:T(8,128)(2,1)S(1)}, u32[]{:S(2)}, u32[]{:S(2)}) collective-permute-start(bf16[2,192,768]{2,1,0:T(8,128)(2,1)S(1)} %pad_maximum_fusion.19.refs_27_), channel_id=1, source_target_pairs={{0,4},{1,5},{2,6},{3,7},{4,0},{5,1},{6,2},{7,3},{8,12},{9,13},{10,... | collective-permute-start | bytes 1769480 | tf_op jit(solution)/shard_map/ppermute | solution.py:37
  429.3 33.2 %collective-permute-start.74 = (bf16[2,192,768]{2,1,0:T(8,128)(2,1)S(1)}, bf16[2,192,768]{2,1,0:T(8,128)(2,1)S(1)}, u32[]{:S(2)}, u32[]{:S(2)}) collective-permute-start(bf16[2,192,768]{2,1,0:T(8,128)(2,1)S(1)} %pad_maximum_fusion.19.refs_27_), channel_id=1, source_target_pairs={{0,1},{1,0},{2,3},{3,2},{4,5},{5,4},{6,7},{7,6},{8,9},{9,8},{10,11... | collective-permute-start | bytes 1769480 | tf_op jit(solution)/shard_map/ppermute | solution.py:37
  432.1 23.2 %collective-permute-start.61 = (bf16[192,768]{1,0:T(8,128)(2,1)S(1)}, bf16[192,768]{1,0:T(8,128)(2,1)S(1)}, u32[]{:S(2)}, u32[]{:S(2)}) collective-permute-start(bf16[192,768]{1,0:T(8,128)(2,1)S(1)} %get-tuple-element.86), channel_id=1, source_target_pairs={{0,16},{1,24},{2,18},{3,26},{4,20},{5,28},{6,22},{7,30},{8,17},{9,... | collective-permute-start | bytes 884744 | tf_op jit(solution)/shard_map/ppermute | solution.py:37
  460.9 22.0 %collective-permute-start.63 = (bf16[2,192,768]{2,1,0:T(8,128)(2,1)S(1)}, bf16[2,192,768]{2,1,0:T(8,128)(2,1)S(1)}, u32[]{:S(2)}, u32[]{:S(2)}) collective-permute-start(bf16[2,192,768]{2,1,0:T(8,128)(2,1)S(1)} %pad_maximum_fusion.17.refs_19_), channel_id=1, source_target_pairs={{0,4},{1,5},{2,6},{3,7},{4,0},{5,1},{6,2},{7,3},{8,12},{9,13},{10,... | collective-permute-start | bytes 1769480 | tf_op jit(solution)/shard_map/ppermute | solution.py:37
  462.4 21.6 %collective-permute-start.62 = (bf16[2,192,768]{2,1,0:T(8,128)(2,1)S(1)}, bf16[2,192,768]{2,1,0:T(8,128)(2,1)S(1)}, u32[]{:S(2)}, u32[]{:S(2)}) collective-permute-start(bf16[2,192,768]{2,1,0:T(8,128)(2,1)S(1)} %pad_maximum_fusion.17.refs_19_), channel_id=1, source_target_pairs={{0,1},{1,0},{2,3},{3,2},{4,5},{5,4},{6,7},{7,6},{8,9},{9,8},{10,11... | collective-permute-start | bytes 1769480 | tf_op jit(solution)/shard_map/ppermute | solution.py:37
  462.5 33.1 %collective-permute-start.57 = (bf16[2,192,768]{2,1,0:T(8,128)(2,1)S(1)}, bf16[2,192,768]{2,1,0:T(8,128)(2,1)S(1)}, u32[]{:S(2)}, u32[]{:S(2)}) collective-permute-start(bf16[2,192,768]{2,1,0:T(8,128)(2,1)S(1)} %pad_maximum_fusion.16.refs_15_), channel_id=1, source_target_pairs={{0,4},{1,5},{2,6},{3,7},{4,0},{5,1},{6,2},{7,3},{8,12},{9,13},{10,... | collective-permute-start | bytes 1769480 | tf_op jit(solution)/shard_map/ppermute | solution.py:37
  470.3 26.0 %collective-permute-start.56 = (bf16[2,192,768]{2,1,0:T(8,128)(2,1)S(1)}, bf16[2,192,768]{2,1,0:T(8,128)(2,1)S(1)}, u32[]{:S(2)}, u32[]{:S(2)}) collective-permute-start(bf16[2,192,768]{2,1,0:T(8,128)(2,1)S(1)} %pad_maximum_fusion.16.refs_15_), channel_id=1, source_target_pairs={{0,1},{1,0},{2,3},{3,2},{4,5},{5,4},{6,7},{7,6},{8,9},{9,8},{10,11... | collective-permute-start | bytes 1769480 | tf_op jit(solution)/shard_map/ppermute | solution.py:37
  471.3 25.0 %collective-permute-start.76 = (bf16[2,192,768]{2,1,0:T(8,128)(2,1)S(1)}, bf16[2,192,768]{2,1,0:T(8,128)(2,1)S(1)}, u32[]{:S(2)}, u32[]{:S(2)}) collective-permute-start(bf16[2,192,768]{2,1,0:T(8,128)(2,1)S(1)} %collective-permute-done.75.refs_29_), channel_id=1, source_target_pairs={{0,1},{1,0},{2,3},{3,2},{4,5},{5,4},{6,7},{7,6},{8,9},{9,8},{10,11... | collective-permute-start | bytes 1769480 | tf_op jit(solution)/shard_map/ppermute | solution.py:37
  510.0 39.5 %collective-permute-start.77 = (f16[384,768]{1,0:T(8,128)(2,1)}, f16[384,768]{1,0:T(8,128)(2,1)S(1)}, u32[]{:S(2)}, u32[]{:S(2)}) collective-permute-start(f16[384,768]{1,0:T(8,128)(2,1)} %get-tuple-element.72), channel_id=1, source_target_pairs={{0,0},{1,8},{2,16},{3,24},{4,4},{5,12},{6,20},{7,28},{8,1},{9,9},{... | collective-permute-start | bytes 1769480 | tf_op jit(solution)/shard_map/ppermute | solution.py:37
  511.9 50.3 %collective-permute-start.78 = (f16[384,768]{1,0:T(8,128)(2,1)}, f16[384,768]{1,0:T(8,128)(2,1)}, u32[]{:S(2)}, u32[]{:S(2)}) collective-permute-start(f16[384,768]{1,0:T(8,128)(2,1)} %get-tuple-element.71), channel_id=1, source_target_pairs={{0,8},{1,0},{2,24},{3,16},{4,12},{5,4},{6,28},{7,20},{8,9},{9,1},{... | collective-permute-start | bytes 1769480 | tf_op jit(solution)/shard_map/ppermute | solution.py:37
  527.1 36.5 %collective-permute-start.79 = (f16[384,768]{1,0:T(8,128)(2,1)S(1)}, f16[384,768]{1,0:T(8,128)(2,1)S(1)}, u32[]{:S(2)}, u32[]{:S(2)}) collective-permute-start(f16[384,768]{1,0:T(8,128)(2,1)S(1)} %get-tuple-element.70), channel_id=1, source_target_pairs={{0,16},{1,24},{2,0},{3,8},{4,20},{5,28},{6,4},{7,12},{8,17},{9,25}... | collective-permute-start | bytes 1769480 | tf_op jit(solution)/shard_map/ppermute | solution.py:37
  527.1 73.2 %collective-permute-start.80 = (f16[384,768]{1,0:T(8,128)(2,1)S(1)}, f16[384,768]{1,0:T(8,128)(2,1)S(1)}, u32[]{:S(2)}, u32[]{:S(2)}) collective-permute-start(f16[384,768]{1,0:T(8,128)(2,1)S(1)} %get-tuple-element.69), channel_id=1, source_target_pairs={{0,24},{1,16},{2,8},{3,0},{4,28},{5,20},{6,12},{7,4},{8,25},{9,17}... | collective-permute-start | bytes 1769480 | tf_op jit(solution)/shard_map/ppermute | solution.py:37
  528.8 79.0 %collective-permute-start.81 = (f16[768,384]{1,0:T(8,128)(2,1)S(1)}, f16[768,384]{1,0:T(8,128)(2,1)S(1)}, u32[]{:S(2)}, u32[]{:S(2)}) collective-permute-start(f16[768,384]{1,0:T(8,128)(2,1)S(1)} %get-tuple-element.50), channel_id=1, source_target_pairs={{0,0},{1,1},{2,4},{3,5},{4,2},{5,3},{6,6},{7,7},{8,8},{9,9},{10,12... | collective-permute-start | bytes 1769480 | tf_op jit(solution)/shard_map/ppermute | solution.py:37
  549.5 58.7 %collective-permute-start.82 = (f16[768,384]{1,0:T(8,128)(2,1)S(1)}, f16[768,384]{1,0:T(8,128)(2,1)S(1)}, u32[]{:S(2)}, u32[]{:S(2)}) collective-permute-start(f16[768,384]{1,0:T(8,128)(2,1)S(1)} %get-tuple-element.49), channel_id=1, source_target_pairs={{0,1},{1,0},{2,5},{3,4},{4,3},{5,2},{6,7},{7,6},{8,9},{9,8},{10,13... | collective-permute-start | bytes 1769480 | tf_op jit(solution)/shard_map/ppermute | solution.py:37
  562.2 46.1 %collective-permute-start.83 = (f16[768,384]{1,0:T(8,128)(2,1)S(1)}, f16[768,384]{1,0:T(8,128)(2,1)S(1)}, u32[]{:S(2)}, u32[]{:S(2)}) collective-permute-start(f16[768,384]{1,0:T(8,128)(2,1)S(1)} %get-tuple-element.48), channel_id=1, source_target_pairs={{0,2},{1,3},{2,6},{3,7},{4,0},{5,1},{6,4},{7,5},{8,10},{9,11},{10,... | collective-permute-start | bytes 1769480 | tf_op jit(solution)/shard_map/ppermute | solution.py:37
  563.6 44.9 %collective-permute-start.84 = (f16[768,384]{1,0:T(8,128)(2,1)S(1)}, f16[768,384]{1,0:T(8,128)(2,1)S(1)}, u32[]{:S(2)}, u32[]{:S(2)}) collective-permute-start(f16[768,384]{1,0:T(8,128)(2,1)S(1)} %get-tuple-element.47), channel_id=1, source_target_pairs={{0,3},{1,2},{2,7},{3,6},{4,1},{5,0},{6,5},{7,4},{8,11},{9,10},{10,... | collective-permute-start | bytes 1769480 | tf_op jit(solution)/shard_map/ppermute | solution.py:37
  (110 other events, 1906.3 us)

commit v4 on v3

--- a/solution.py
+++ b/solution.py
@@ -10,7 +10,7 @@
 DENOMINATOR_MIN = 1.5
 HALF_TOP = 60000.0
 AXES = ("alpha", "beta")
-ROW_CHUNKS = 4
+ROW_CHUNKS = 3
 
 
 class Grid:
@@ -30,31 +30,31 @@
     def index(self, band, lane, major, minor):
         return ((band * self.lanes + lane) * self.majors + major) * 2 + minor
 
-    def send(self, value, where):
-        pairs = [(self.index(*place), self.index(*where(*place))) for place in self.places]
-        if all(source == target for source, target in pairs):
+    def send(self, value, where, idle=None):
+        stays = [where(*place) == place for place in self.places]
+        if all(stays):
             return value
-        return lax.ppermute(value, AXES, pairs)
+        pairs = []
+        for place, stay in zip(self.places, stays):
+            target = idle(*place) if stay else where(*place)
+            pairs.append((self.index(*place), self.index(*target)))
+        received = lax.ppermute(value, AXES, pairs)
+        if any(stays):
+            device = lax.axis_index("alpha") * self.bands + lax.axis_index("beta")
+            received = jnp.where(jnp.array(stays)[device], value, received)
+        return received
 
 
 def after(value, *earlier):
     return lax.optimization_barrier((value, *earlier))[0]
 
 
-def largest_anywhere(grid, value, gates):
-    devices = len(grid.places)
-    largest = jnp.full((8, 128), value)
-    bit = 1
-    while bit < devices:
-        pairs = [(device, device ^ bit) for device in range(devices)]
-        largest = after(largest, gates[min(bit.bit_length(), len(gates)) - 1])
-        largest = jnp.maximum(largest, lax.ppermute(largest, AXES, pairs))
-        bit *= 2
-    return largest[0, 0]
-
-
-def gather_bands(grid, own, band, gate):
-    held = own[None] if gate is None else after(own[None], gate)
+def other_minor(z, x, m, n):
+    return (z, x, m, 1 - n)
+
+
+def gather_bands(grid, own, band, busy=None):
+    held = own[None]
     swaps = []
     order = [[z] for z in range(grid.bands)]
     width = 2
@@ -73,46 +73,81 @@
                     pairs = [(low - hop + 1, low - hop), (high + hop - 1, high + hop)]
                 for one, other in pairs:
                     partner[one], partner[other] = other, one
-            moving = grid.send(moving, lambda z, x, m, n: (partner[z], x, m, n))
+            pairs = [
+                (grid.index(z, x, m, n), grid.index(partner[z], x, m, 1 - n if partner[z] == z else n))
+                for z, x, m, n in grid.places
+            ]
+            moving = lax.ppermute(moving, AXES, pairs)
             if hop == 0:
                 swaps.append(moving)
             origin = [origin[partner[z]] for z in range(grid.bands)]
             takes = [(half - 1 - z % width if z % width < half else z % width - half) == hop for z in range(grid.bands)]
             kept = moving if kept is None else jnp.where(jnp.array(takes)[band], moving, kept)
             kept_origin = [origin[z] if takes[z] else kept_origin[z] for z in range(grid.bands)]
-        held = jnp.concatenate([held, kept])
+        if busy is None:
+            held = jnp.concatenate([held, kept])
+        else:
+            mine = jnp.any(busy & (jnp.arange(grid.bands) // half == band // half))
+            held = jnp.where(mine, held, kept)
         order = [order[z] + order[kept_origin[z]] for z in range(grid.bands)]
         width *= 2
     return held, order, swaps
 
 
-def gather_couplings(grid, coupling, band, major, minor):
-    rows, slots, _ = coupling.shape
-    majors = grid.majors
-    chunk = rows // (2 * majors)
-    own = lax.dynamic_slice_in_dim(coupling, (minor * majors + major) * chunk, chunk, 0)
-    gathered, swaps, gate = [], [], None
-    for slot in range(slots):
-        line, order, swapped = gather_bands(grid, own[:, slot], band, gate)
+def spread_majors(grid, line):
+    pieces = {0: line}
+    bit = grid.majors // 2
+    while bit:
+        received = {key ^ bit: grid.send(piece, lambda z, x, m, n: (z, x, m ^ bit, n)) for key, piece in pieces.items()}
+        pieces.update(received)
+        bit //= 2
+    return [pieces[key] for key in range(grid.majors)]
+
+
+def spread_inputs(grid, coupling, half, extreme, busy, band, lane, major, minor):
+    rows, slots, tile = coupling.shape
+    chunk = rows // (2 * grid.majors)
+    first = (minor * grid.majors + major) * chunk
+    dense = slots if busy is None else slots // 2
+    groups = [(slot, 1) for slot in range(dense)]
+    if busy is not None:
+        groups.append((dense, slots - dense))
+    extreme = jnp.full((16, tile), extreme)
+    for where in (lambda z, x, m, n: (z, (x + 1) % grid.lanes, m, n), other_minor):
+        extreme = jnp.maximum(extreme, grid.send(extreme, where))
+    lines, swaps, gate = [], [], None
+    for number, (slot, count) in enumerate(groups):
+        source = coupling if gate is None else after(coupling, gate)
+        own = lax.dynamic_slice_in_dim(source, first, chunk, 0)[:, slot : slot + count].transpose(1, 0, 2)
+        if number == 1:
+            own = jnp.concatenate([own, extreme[None]], axis=1)
+        line, line_order, swapped = gather_bands(grid, own, band, None if slot < dense else busy)
         gate = swapped[0]
         swaps.append(swapped[-1])
-        pieces = {0: line}
-        bit = majors // 2
-        while bit:
-            received = {
-                key ^ bit: grid.send(piece, lambda z, x, m, n: (z, x, m ^ bit, n)) for key, piece in pieces.items()
-            }
-            pieces.update(received)
-            bit //= 2
-        pieces = [pieces[key] for key in range(majors)]
+        lines.append(line)
+        if slot < dense:
+            order = line_order
+    gathered = [spread_majors(grid, line) for line in lines]
+    rode = [piece[:, 0, chunk, 0] for piece in gathered[1]]
+    largest = jnp.max(jnp.stack(rode)).astype(jnp.float32)
+    gates = [swaps[1], gathered[0][-1], gathered[1][-1]]
+    parts, places = to_columns(grid, half, band, lane, major, minor, gates, True)
+    result = []
+    for (slot, count), pieces in zip(groups, gathered):
+        if slot >= dense:
+            pieces = [jnp.broadcast_to(piece, (grid.bands, *piece.shape[1:])) for piece in pieces]
         if chunk % 16:
-            whole = jnp.take(jnp.stack(pieces), major ^ jnp.arange(majors), axis=0)
-            pieces = [whole.transpose(1, 0, 2, 3).reshape(grid.bands, rows // 2, whole.shape[3])]
-        gathered.append(pieces)
-    return gathered, jnp.array(order, jnp.int32)[band], swaps
-
-
-def to_columns(grid, half, band, lane, major, minor, gate):
+            whole = jnp.take(jnp.stack(pieces), major ^ jnp.arange(grid.majors), axis=0)[:, :, :, :chunk]
+            pieces = [whole.transpose(1, 2, 0, 3, 4).reshape(grid.bands, count, rows // 2, tile)]
+        for i in range(count):
+            result.append([piece[:, i] for piece in pieces])
+    return result, jnp.array(order, jnp.int32)[band], largest, parts, places
+
+
+def to_columns(grid, half, band, lane, major, minor, gates, by_lane):
+    def idle(z, x, m, n):
+        return (z, (x + 1) % lanes, m, n) if by_lane else (z, x, m ^ 1, n)
+
     rows, cols = half.shape
     lanes, majors = grid.lanes, grid.majors
     strip = cols // majors
@@ -125,12 +160,12 @@
             piece = lax.dynamic_slice(block, (0, (major ^ key) * strip), (part, strip))
             first.append(grid.send(piece, lambda z, x, m, n: (z, x, m ^ key, n)))
         first = jnp.stack(first)
-        if gate is not None:
-            first = after(first, gate)
+        if gates:
+            first = after(first, gates[min(chunk, len(gates) - 1)])
         second = []
         for key in range(majors):
             piece = lax.dynamic_index_in_dim(first, (band // 2) ^ key ^ major, 0, keepdims=False)
-            second.append(grid.send(piece, lambda z, x, m, n: ((z // 2 ^ key) * 2 + n, x, m, z % 2)))
+            second.append(grid.send(piece, lambda z, x, m, n: ((z // 2 ^ key) * 2 + n, x, m, z % 2), idle))
         second = jnp.stack(second)
         for turn in range(lanes):
             third = grid.send(second, lambda z, x, m, n: (z, (x + turn) % lanes, m, n))
@@ -146,7 +181,8 @@
     couplings, parts = refs[: slots * pieces], refs[slots * pieces : -4]
     out_ref, mirror_ref, coeff_ref, sems = refs[-4:]
     band = order_ref[pl.program_id(0)]
-    chunk, tile = couplings[0].shape[1:]
+    chunk = out_ref.shape[1] // pieces
+    tile = couplings[0].shape[2]
     majors, part, _ = parts[0].shape
 
     @pl.when(pl.program_id(0) == 0)
@@ -163,7 +199,7 @@
 
     def product(slot):
         first = pl.multiple_of(column_ref[band * slots + slot] * tile, tile)
-        left = jnp.concatenate([couplings[slot * pieces + piece][0] for piece in range(pieces)], axis=0)
+        left = jnp.concatenate([couplings[slot * pieces + piece][0, :chunk] for piece in range(pieces)], axis=0)
         return jnp.dot(left, coeff_ref[pl.ds(first, tile), :], preferred_element_type=jnp.float32) * scale_ref[0]
 
     def store(value, add):
@@ -184,8 +220,9 @@
 
 def products(couplings, parts, order, entries, tile_columns, counts, offsets, places, scale):
     slots, pieces = len(couplings), len(couplings[0])
-    _, chunk, tile = couplings[0][0].shape
+    tile = couplings[0][0].shape[2]
     majors, part, strip = parts[0].shape
+    chunk = part * ROW_CHUNKS // 2 // pieces
     rows, calls = pieces * chunk, order.shape[0]
     spec = pl.BlockSpec((1, chunk, tile), lambda i, order, entry, *_: (entry[i], 0, 0))
     return pl.pallas_call(
@@ -193,7 +230,7 @@
         grid_spec=pltpu.PrefetchScalarGridSpec(
             num_scalar_prefetch=7,
             grid=(calls,),
-            in_specs=[spec] * (slots * pieces) + [pl.BlockSpec(memory_space=pl.ANY)] * len(parts),
+            in_specs=[spec] * (slots * pieces) + [pl.BlockSpec(memory_space=pltpu.HBM)] * len(parts),
             out_specs=[
                 pl.BlockSpec((1, rows, strip), lambda i, *_: (i, 0, 0)),
                 pl.BlockSpec((1, strip, rows), lambda i, *_: (i, 0, 0)),
@@ -231,13 +268,23 @@
     run, part, strip = halves[0][0].shape
     rows = 2 * part
     beta = major * 2 + minor
-    direct = jnp.zeros((rows, grid.majors * strip), jnp.float16)
     mirror = jnp.zeros((rows, grid.majors * strip), jnp.float16)
+    received = []
     for key in range(bands):
         piece = halves[key // run][0][key % run].astype(jnp.float16)
-        piece = grid.send(piece, lambda z, x, m, n: ((m * 2 + n) ^ key, x, z // 2, z % 2))
-        source = band ^ key
-        direct = lax.dynamic_update_slice(direct, piece, (source % 2 * part, source // 2 * strip))
+        received.append(
+            grid.send(
+                piece,
+                lambda z, x, m, n: ((m * 2 + n) ^ key, x, z // 2, z % 2),
+                lambda z, x, m, n: (z, (x + 1) % grid.lanes, m, n),
+            )
+        )
+    direct = jnp.zeros((rows, grid.majors * strip), jnp.float16)
+    for key in range(grid.majors):
+        one, other = received[2 * key : 2 * key + 2]
+        even = band % 2 == 0
+        pair = jnp.concatenate([jnp.where(even, one, other), jnp.where(even, other, one)])
+        direct = lax.dynamic_update_slice_in_dim(direct, pair, (band // 2 ^ key) * strip, 1)
 
     def target(x, m, n):
         return (x * per_lane + m % per_lane) * 2 + n
@@ -249,6 +296,7 @@
         piece = grid.send(
             piece,
             lambda z, x, m, n: (z, m // per_lane, (target(x, m, n) ^ key) // 2, (target(x, m, n) ^ key) % 2),
+            other_minor,
         )
         source = beta ^ key
         place = (source // 2 % per_lane * strip, (source // 2 // per_lane * 2 + source % 2) * part)
@@ -268,7 +316,20 @@
     tile_columns = jnp.take(tile_cols, tile_rows, axis=0).reshape(-1)
     counts = jnp.take(tile_count, tile_rows)
     half = coeffs.astype(jnp.bfloat16)
-    couplings, order, swaps = gather_couplings(grid, coupling, band, major, minor)
+    extreme = (jnp.maximum(jnp.max(jnp.abs(coeffs)), 1e-30) * 1.01).astype(jnp.bfloat16)
+    all_rows = (jnp.arange(grid.bands * grid.lanes) * rows // tile).reshape(grid.bands, grid.lanes)
+    many = jnp.take(tile_count, all_rows) > slots // 2
+    busy = jnp.take(many, lane, axis=1)
+
+    def one_busy(*values):
+        return spread_inputs(grid, *values, busy, band, lane, major, minor)
+
+    def any_busy(*values):
+        return spread_inputs(grid, *values, None, band, lane, major, minor)
+
+    couplings, order, largest, parts, places = lax.cond(
+        jnp.max(jnp.sum(many, axis=0)) <= 1, one_busy, any_busy, coupling, half, extreme
+    )
     pieces = len(couplings[0])
     offsets = (major ^ jnp.arange(pieces, dtype=jnp.int32)) * (rows // 2 // pieces)
     if pieces == 1:
@@ -277,14 +338,13 @@
     entries = jnp.argmax(order[None, :] == wanted[:, None], axis=1).astype(jnp.int32)
 
     growth = slots * tile * COUPLING_MAX
-    largest = jnp.maximum(largest_anywhere(grid, jnp.max(jnp.abs(coeffs)), swaps), 1e-30)
     current = coeffs
-    gate = swaps[-1]
     for step_index in range(STEPS):
         scale = HALF_TOP / (growth * largest)
         largest = largest * (1 + 2 * growth / DENOMINATOR_MIN)
-        parts, places = to_columns(grid, half, band, lane, major, minor, gate)
-        gate = None
+        if step_index:
+            half = current.astype(jnp.bfloat16)
+            parts, places = to_columns(grid, half, band, lane, major, minor, [], False)
         runs = [slice(0, grid.bands // 2), slice(grid.bands // 2, grid.bands)]
         halves = [
             products(couplings, parts, wanted[run], entries[run], tile_columns, counts, offsets, places, scale)
@@ -293,7 +353,6 @@
         direct, mirror = bring_home(grid, halves, band, lane, major, minor)
         total = (direct.astype(jnp.float32) + mirror.astype(jnp.float32)) / scale
         current = current - total / denominator
-        half = current.astype(jnp.bfloat16)
     return current
 
 

time: 620 us -> 561 us (0.905)
  the two profiles are of different devices: /device:TPU:17 before, /device:TPU:21 now
where the time goes in v4:
time: 561 us; the launch traced here: 551 us
  waiting for transfers between devices  338 us (60%)
  starting transfers between devices  75.2 us (13%)
  other arithmetic  50.7 us (9%)
  local copies, waits for them, and re-layouts  44.2 us (8%)
  Pallas kernels  37.5 us (7%)
    ppermute x57, waiting for transfers between devices, send(): received = lax.ppermute(value, AXES, pairs)  316 us
    ppermute x57, starting transfers between devices, send(): received = lax.ppermute(value, AXES, pairs)  65.8 us
    pallas_call x4, Pallas kernels, products(): pl.pallas_call(lambda *refs: product_kernel(slots, pieces, *refs), grid_s...  37.5 us
    ppermute x9, waiting for transfers between devices, gather_bands(): moving = lax.ppermute(moving, AXES, pairs)  22.6 us
  transfers between devices with their start and end apart: 66, of which 30 were waited for; matrix products, arithmetic and copies ran while one was open for 11% of the time, Pallas kernels for 0%

profile of v4, /device:TPU:21, one launch (start us, length us, event | category | flops | bytes accessed | tf_op | source)
XLA Modules:
  0.0 551.0 jit_solution(1827702322825985745)
XLA Ops:
  1.2 5.1 fusion.36
  9.7 225.7 %conditional.2 = (bf16[4,192,768]{2,1,0:T(8,128)(2,1)S(1)}, bf16[4,192,768]{2,1,0:T(8,128)(2,1)}, bf16[4,208,768]{2,1,0:T(8,128)(2,1)S(1)}, bf16[4,208,768]{2,1,...) conditional(s32[]{:T(128)} %convert_element_type.115, ...), branch_computations={%region_3.6_spmd, %region_6.11_spmd} | conditional | flops 10850435 | bytes 200986592
  11.6 5.1 copy.47
  21.2 4.1 collective-permute-done.36
  26.6 3.1 collective-permute-start.42
  29.7 7.1 %collective-permute-done.42 = bf16[1,1,208,768]{3,2,0,1:T(8,128)(2,1)S(1)} collective-permute-done((bf16[1,1,208,768]{3,2,0,1:T(8,128)(2,1)S(1)}, bf16[1,1,208,768]{3,2,0,1:T(8,128)(2,1)S(1)}, u32[]{:S(2)}, u32[]{:S(2)}) %collective-permute-start.42) | collective-permute-done | bytes 319520 | tf_op jit(solution)/shard_map/cond/branch_1_fun/ppermute | solution.py:80
  38.5 2.2 collective-permute-start.38
  42.0 2.1 dynamic-slice_bitcast_fusion.16
  44.3 8.4 %collective-permute-done.43 = bf16[2,1,208,768]{3,2,0,1:T(8,128)(2,1)} collective-permute-done((bf16[2,1,208,768]{3,2,0,1:T(8,128)(2,1)}, bf16[2,1,208,768]{3,2,0,1:T(8,128)(2,1)}, u32[]{:S(2)}, u32[]{:S(2)}) %collective-permute-start.43) | collective-permute-done | bytes 639008 | tf_op jit(solution)/shard_map/cond/branch_1_fun/ppermute | solution.py:80
  64.3 2.4 collective-permute-done.44
  72.5 6.2 %collective-permute-start.51 = (bf16[256,768]{1,0:T(8,128)(2,1)S(1)}, bf16[256,768]{1,0:T(8,128)(2,1)S(1)}, u32[]{:S(2)}, u32[]{:S(2)}) collective-permute-start(bf16[256,768]{1,0:T(8,128)(2,1)S(1)} %get-tuple-element.335), channel_id=1, source_target_pairs={{0,4},{1,8},{2,6},{3,10},{4,0},{5,12},{6,2},{7,14},{8,1},{9,13},{1... | collective-permute-start | bytes 1179656 | tf_op jit(solution)/shard_map/cond/branch_1_fun/ppermute | solution.py:41
  78.7 44.5 %collective-permute-done.56 = bf16[256,768]{1,0:T(8,128)(2,1)S(1)} collective-permute-done((bf16[256,768]{1,0:T(8,128)(2,1)S(1)}, bf16[256,768]{1,0:T(8,128)(2,1)S(1)}, u32[]{:S(2)}, u32[]{:S(2)}) %collective-permute-start.56) | collective-permute-done | bytes 393248 | tf_op jit(solution)/shard_map/cond/branch_1_fun/ppermute | solution.py:41
  123.3 1.9 broadcast_select_fusion.5
  126.2 4.7 collective-permute-start.52
  134.6 35.2 %collective-permute-done.52 = bf16[256,768]{1,0:T(8,128)(2,1)S(1)} collective-permute-done((bf16[256,768]{1,0:T(8,128)(2,1)S(1)}, bf16[256,768]{1,0:T(8,128)(2,1)S(1)}, u32[]{:S(2)}, u32[]{:S(2)}) %collective-permute-start.52) | collective-permute-done | bytes 393248 | tf_op jit(solution)/shard_map/cond/branch_1_fun/ppermute | solution.py:41
  170.2 2.8 collective-permute-start.64
  176.6 14.6 %collective-permute-done.64 = bf16[256,768]{1,0:T(8,128)(2,1)S(1)} collective-permute-done((bf16[256,768]{1,0:T(8,128)(2,1)S(1)}, bf16[256,768]{1,0:T(8,128)(2,1)S(1)}, u32[]{:S(2)}, u32[]{:S(2)}) %collective-permute-start.64) | collective-permute-done | bytes 393248 | tf_op jit(solution)/shard_map/cond/branch_1_fun/ppermute | solution.py:41
  193.2 2.1 select_select_fusion
  196.7 13.2 %collective-permute-done.49 = bf16[1,2,192,768]{3,2,1,0:T(8,128)(2,1)} collective-permute-done((bf16[1,2,192,768]{3,2,1,0:T(8,128)(2,1)}, bf16[1,2,192,768]{3,2,1,0:T(8,128)(2,1)}, u32[]{:S(2)}, u32[]{:S(2)}) %collective-permute-start.49) | collective-permute-done | bytes 589856 | tf_op jit(solution)/shard_map/cond/branch_1_fun/ppermute | solution.py:41
  210.4 12.1 %collective-permute-done.66 = bf16[2,256,768]{2,1,0:T(8,128)(2,1)} collective-permute-done((bf16[2,256,768]{2,1,0:T(8,128)(2,1)}, bf16[2,256,768]{2,1,0:T(8,128)(2,1)}, u32[]{:S(2)}, u32[]{:S(2)}) %collective-permute-start.66) | collective-permute-done | bytes 786464 | tf_op jit(solution)/shard_map/cond/branch_1_fun/ppermute | solution.py:41
  240.5 10.2 %shard_map.254 = (f32[2,384,768]{2,1,0:T(8,128)S(1)}, f32[2,768,384]{2,1,0:T(8,128)S(1)}) custom-call(s32[2]{0:T(128)S(1)} %get-tuple-element.387.refs_0_, s32[2]{0:T(128)S(1)} %get-tuple-element.385.refs_1_, s32[16]{0:T(128)S(1)} %select_n.937.refs_2_, s32[4]{0:T(128)S(1)} %broadcast_select_fusion.18.refs_3_, s32[2]{0:T(128)S(1)} %get-tuple-element.388.refs_4_, ...), custom_call_target="tpu_custom_call" | custom-call | flops 3623878656 | bytes 14155776 | tf_op jit(solution)/shard_map/pallas_call | solution.py:228
  252.1 8.7 %shard_map.253 = (f32[2,384,768]{2,1,0:T(8,128)S(1)}, f32[2,768,384]{2,1,0:T(8,128)S(1)}) custom-call(s32[2]{0:T(128)S(1)} %get-tuple-element.386.refs_0_, s32[2]{0:T(128)S(1)} %get-tuple-element.384.refs_1_, s32[16]{0:T(128)S(1)} %select_n.937.refs_2_, s32[4]{0:T(128)S(1)} %broadcast_select_fusion.18.refs_3_, s32[2]{0:T(128)S(1)} %get-tuple-element.388.refs_4_, ...), custom_call_target="tpu_custom_call" | custom-call | flops 3623878656 | bytes 14155776 | tf_op jit(solution)/shard_map/pallas_call | solution.py:228
  263.7 4.1 fusion.13
  268.2 2.6 collective-permute-start.73
  275.6 9.1 %collective-permute-done.72 = f16[768,384]{1,0:T(8,128)(2,1)S(1)} collective-permute-done((f16[768,384]{1,0:T(8,128)(2,1)S(1)}, f16[768,384]{1,0:T(8,128)(2,1)S(1)}, u32[]{:S(2)}, u32[]{:S(2)}) %collective-permute-start.72) | collective-permute-done | bytes 589856 | tf_op jit(solution)/shard_map/ppermute | solution.py:41
  285.8 22.1 %collective-permute-done.73 = f16[768,384]{1,0:T(8,128)(2,1)} collective-permute-done((f16[768,384]{1,0:T(8,128)(2,1)}, f16[768,384]{1,0:T(8,128)(2,1)}, u32[]{:S(2)}, u32[]{:S(2)}) %collective-permute-start.73) | collective-permute-done | bytes 589856 | tf_op jit(solution)/shard_map/ppermute | solution.py:41
  309.1 15.0 %collective-permute-start.75 = (f16[768,384]{1,0:T(8,128)(2,1)S(1)}, f16[768,384]{1,0:T(8,128)(2,1)S(1)}, u32[]{:S(2)}, u32[]{:S(2)}) collective-permute-start(f16[768,384]{1,0:T(8,128)(2,1)S(1)} %copy-done.52), channel_id=1, source_target_pairs={{0,3},{1,2},{2,7},{3,6},{4,1},{5,0},{6,5},{7,4},{8,11},{9,10},{10,... | collective-permute-start | bytes 1769480 | tf_op jit(solution)/shard_map/ppermute | solution.py:41
  324.1 2.8 broadcast_select_fusion.16
  330.3 16.9 %collective-permute-done.75 = f16[768,384]{1,0:T(8,128)(2,1)S(1)} collective-permute-done((f16[768,384]{1,0:T(8,128)(2,1)S(1)}, f16[768,384]{1,0:T(8,128)(2,1)S(1)}, u32[]{:S(2)}, u32[]{:S(2)}) %collective-permute-start.75) | collective-permute-done | bytes 589856 | tf_op jit(solution)/shard_map/ppermute | solution.py:41
  352.0 8.6 %collective-permute-done.88 = bf16[256,768]{1,0:T(8,128)(2,1)S(1)} collective-permute-done((bf16[256,768]{1,0:T(8,128)(2,1)}, bf16[256,768]{1,0:T(8,128)(2,1)S(1)}, u32[]{:S(2)}, u32[]{:S(2)}) %collective-permute-start.88) | collective-permute-done | bytes 393248 | tf_op jit(solution)/shard_map/ppermute | solution.py:41
  361.6 7.4 %collective-permute-done.82 = bf16[256,768]{1,0:T(8,128)(2,1)S(1)} collective-permute-done((bf16[256,768]{1,0:T(8,128)(2,1)S(1)}, bf16[256,768]{1,0:T(8,128)(2,1)S(1)}, u32[]{:S(2)}, u32[]{:S(2)}) %collective-permute-start.82) | collective-permute-done | bytes 393248 | tf_op jit(solution)/shard_map/ppermute | solution.py:41
  369.5 8.0 %collective-permute-done.76 = bf16[256,768]{1,0:T(8,128)(2,1)S(1)} collective-permute-done((bf16[256,768]{1,0:T(8,128)(2,1)S(1)}, bf16[256,768]{1,0:T(8,128)(2,1)S(1)}, u32[]{:S(2)}, u32[]{:S(2)}) %collective-permute-start.76) | collective-permute-done | bytes 393248 | tf_op jit(solution)/shard_map/ppermute | solution.py:41
  378.6 14.6 %collective-permute-done.90 = bf16[256,768]{1,0:T(8,128)(2,1)S(1)} collective-permute-done((bf16[256,768]{1,0:T(8,128)(2,1)S(1)}, bf16[256,768]{1,0:T(8,128)(2,1)S(1)}, u32[]{:S(2)}, u32[]{:S(2)}) %collective-permute-start.90) | collective-permute-done | bytes 393248 | tf_op jit(solution)/shard_map/ppermute | solution.py:41
  394.1 12.1 %collective-permute-done.84 = bf16[256,768]{1,0:T(8,128)(2,1)S(1)} collective-permute-done((bf16[256,768]{1,0:T(8,128)(2,1)S(1)}, bf16[256,768]{1,0:T(8,128)(2,1)S(1)}, u32[]{:S(2)}, u32[]{:S(2)}) %collective-permute-start.84) | collective-permute-done | bytes 393248 | tf_op jit(solution)/shard_map/ppermute | solution.py:41
  407.0 3.5 collective-permute-done.78
  411.1 2.0 collective-permute-done.92.refs_25_
  414.5 15.5 %collective-permute-done.86.refs_21_ = bf16[2,256,768]{2,1,0:T(8,128)(2,1)} collective-permute-done((bf16[2,256,768]{2,1,0:T(8,128)(2,1)S(1)}, bf16[2,256,768]{2,1,0:T(8,128)(2,1)}, u32[]{:S(2)}, u32[]{:S(2)}) %collective-permute-start.86) | collective-permute-done | bytes 786464 | tf_op jit(solution)/shard_map/ppermute | solution.py:41
  429.9 13.9 %collective-permute-done.80.refs_17_ = bf16[2,256,768]{2,1,0:T(8,128)(2,1)} collective-permute-done((bf16[2,256,768]{2,1,0:T(8,128)(2,1)S(1)}, bf16[2,256,768]{2,1,0:T(8,128)(2,1)}, u32[]{:S(2)}, u32[]{:S(2)}) %collective-permute-start.80) | collective-permute-done | bytes 786464 | tf_op jit(solution)/shard_map/ppermute | solution.py:41
  444.0 2.5 collective-permute-done.81.refs_18_
  447.6 10.2 %shard_map.256 = (f32[2,384,768]{2,1,0:T(8,128)S(1)}, f32[2,768,384]{2,1,0:T(8,128)S(1)}) custom-call(s32[2]{0:T(128)S(1)} %get-tuple-element.387.refs_0_, s32[2]{0:T(128)S(1)} %get-tuple-element.385.refs_1_, s32[16]{0:T(128)S(1)} %select_n.937.refs_2_, s32[4]{0:T(128)S(1)} %broadcast_select_fusion.18.refs_3_, s32[2]{0:T(128)S(1)} %get-tuple-element.388.refs_4_, ...), custom_call_target="tpu_custom_call" | custom-call | flops 3623878656 | bytes 14155776 | tf_op jit(solution)/shard_map/pallas_call | solution.py:228
  457.9 8.4 %shard_map.255 = (f32[2,384,768]{2,1,0:T(8,128)S(1)}, f32[2,768,384]{2,1,0:T(8,128)S(1)}) custom-call(s32[2]{0:T(128)S(1)} %get-tuple-element.386.refs_0_, s32[2]{0:T(128)S(1)} %get-tuple-element.384.refs_1_, s32[16]{0:T(128)S(1)} %select_n.937.refs_2_, s32[4]{0:T(128)S(1)} %broadcast_select_fusion.18.refs_3_, s32[2]{0:T(128)S(1)} %get-tuple-element.388.refs_4_, ...), custom_call_target="tpu_custom_call" | custom-call | flops 3623878656 | bytes 14155776 | tf_op jit(solution)/shard_map/pallas_call | solution.py:228
  467.5 2.4 collective-permute-start.99
  470.8 16.4 %collective-permute-done.98 = f16[768,384]{1,0:T(8,128)(2,1)S(1)} collective-permute-done((f16[768,384]{1,0:T(8,128)(2,1)S(1)}, f16[768,384]{1,0:T(8,128)(2,1)S(1)}, u32[]{:S(2)}, u32[]{:S(2)}) %collective-permute-start.98) | collective-permute-done | bytes 589856 | tf_op jit(solution)/shard_map/ppermute | solution.py:41
  488.1 19.8 %collective-permute-done.99 = f16[768,384]{1,0:T(8,128)(2,1)S(1)} collective-permute-done((f16[768,384]{1,0:T(8,128)(2,1)S(1)}, f16[768,384]{1,0:T(8,128)(2,1)S(1)}, u32[]{:S(2)}, u32[]{:S(2)}) %collective-permute-start.99) | collective-permute-done | bytes 589856 | tf_op jit(solution)/shard_map/ppermute | solution.py:41
  508.1 15.5 %collective-permute-start.101 = (f16[768,384]{1,0:T(8,128)(2,1)S(1)}, f16[768,384]{1,0:T(8,128)(2,1)S(1)}, u32[]{:S(2)}, u32[]{:S(2)}) collective-permute-start(f16[768,384]{1,0:T(8,128)(2,1)S(1)} %get-tuple-element.343), channel_id=1, source_target_pairs={{0,3},{1,2},{2,7},{3,6},{4,1},{5,0},{6,5},{7,4},{8,11},{9,10},{10,... | collective-permute-start | bytes 1769480 | tf_op jit(solution)/shard_map/ppermute | solution.py:41
  525.4 7.5 %collective-permute-done.97 = f16[384,768]{1,0:T(8,128)(2,1)S(1)} collective-permute-done((f16[384,768]{1,0:T(8,128)(2,1)S(1)}, f16[384,768]{1,0:T(8,128)(2,1)S(1)}, u32[]{:S(2)}, u32[]{:S(2)}) %collective-permute-start.97) | collective-permute-done | bytes 589856 | tf_op jit(solution)/shard_map/ppermute | solution.py:41
  533.6 12.7 %collective-permute-done.101 = f16[768,384]{1,0:T(8,128)(2,1)S(1)} collective-permute-done((f16[768,384]{1,0:T(8,128)(2,1)S(1)}, f16[768,384]{1,0:T(8,128)(2,1)S(1)}, u32[]{:S(2)}, u32[]{:S(2)}) %collective-permute-start.101) | collective-permute-done | bytes 589856 | tf_op jit(solution)/shard_map/ppermute | solution.py:41
  546.5 4.1 divide_subtract_fusion
  (327 shorter events, 93.0 us)
Async XLA Ops:
  38.5 22.6 %collective-permute-start.38 = (bf16[2,1,192,768]{3,2,0,1:T(8,128)(2,1)}, bf16[2,1,192,768]{3,2,0,1:T(8,128)(2,1)}, u32[]{:S(2)}, u32[]{:S(2)}) collective-permute-start(bf16[2,1,192,768]{3,2,0,1:T(8,128)(2,1)} %collective-permute-done.37), channel_id=1, source_target_pairs={{0,8},{1,9},{2,10},{3,11},{4,12},{5,13},{6,14},{7,15},{8,0},{9,1},... | collective-permute-start | bytes 1769480 | tf_op jit(solution)/shard_map/cond/branch_1_fun/ppermute | solution.py:80
  44.1 24.8 %collective-permute-start.62 = (bf16[256,768]{1,0:T(8,128)(2,1)}, bf16[256,768]{1,0:T(8,128)(2,1)}, u32[]{:S(2)}, u32[]{:S(2)}) collective-permute-start(bf16[256,768]{1,0:T(8,128)(2,1)} %get-tuple-element.330), channel_id=1, source_target_pairs={{0,2},{1,3},{2,0},{3,1},{4,6},{5,7},{6,4},{7,5},{8,10},{9,11},{10,... | collective-permute-start | bytes 1179656 | tf_op jit(solution)/shard_map/cond/branch_1_fun/ppermute | solution.py:41
  59.5 63.8 %collective-permute-start.46 = (bf16[1,2,192,768]{3,2,1,0:T(8,128)(2,1)S(1)}, bf16[1,2,192,768]{3,2,1,0:T(8,128)(2,1)S(1)}, u32[]{:S(2)}, u32[]{:S(2)}) collective-permute-start(bf16[1,2,192,768]{3,2,1,0:T(8,128)(2,1)S(1)} %dynamic-slice_bitcast_fusion.13), channel_id=1, source_target_pairs={{0,8},{1,9},{2,10},{3,11},{4,12},{5,13},{6,14},{7,15},{8,0},{9,1},... | collective-permute-start | bytes 1769480 | tf_op jit(solution)/shard_map/cond/branch_1_fun/ppermute | solution.py:80
  62.9 68.0 %collective-permute-start.39 = (bf16[4,1,192,768]{3,2,0,1:T(8,128)(2,1)S(1)}, bf16[4,1,192,768]{3,2,0,1:T(8,128)(2,1)}, u32[]{:S(2)}, u32[]{:S(2)}) collective-permute-start(bf16[4,1,192,768]{3,2,0,1:T(8,128)(2,1)S(1)} %get-tuple-element.325), channel_id=1, source_target_pairs={{0,2},{1,3},{2,0},{3,1},{4,6},{5,7},{6,4},{7,5},{8,10},{9,11},{10,... | collective-permute-start | bytes 3538952 | tf_op jit(solution)/shard_map/cond/branch_1_fun/ppermute | solution.py:41
  68.6 64.9 %collective-permute-start.45 = (bf16[4,1,208,768]{3,2,0,1:T(8,128)(2,1)S(1)}, bf16[4,1,208,768]{3,2,0,1:T(8,128)(2,1)}, u32[]{:S(2)}, u32[]{:S(2)}) collective-permute-start(bf16[4,1,208,768]{3,2,0,1:T(8,128)(2,1)S(1)} %get-tuple-element.323), channel_id=1, source_target_pairs={{0,2},{1,3},{2,0},{3,1},{4,6},{5,7},{6,4},{7,5},{8,10},{9,11},{10,... | collective-permute-start | bytes 3833864 | tf_op jit(solution)/shard_map/cond/branch_1_fun/ppermute | solution.py:41
  69.0 54.2 %collective-permute-start.56 = (bf16[256,768]{1,0:T(8,128)(2,1)S(1)}, bf16[256,768]{1,0:T(8,128)(2,1)S(1)}, u32[]{:S(2)}, u32[]{:S(2)}) collective-permute-start(bf16[256,768]{1,0:T(8,128)(2,1)S(1)} %get-tuple-element.334), channel_id=1, source_target_pairs={{0,2},{1,3},{2,0},{3,1},{4,6},{5,7},{6,4},{7,5},{8,10},{9,11},{10,... | collective-permute-start | bytes 1179656 | tf_op jit(solution)/shard_map/cond/branch_1_fun/ppermute | solution.py:41
  72.5 59.4 %collective-permute-start.51 = (bf16[256,768]{1,0:T(8,128)(2,1)S(1)}, bf16[256,768]{1,0:T(8,128)(2,1)S(1)}, u32[]{:S(2)}, u32[]{:S(2)}) collective-permute-start(bf16[256,768]{1,0:T(8,128)(2,1)S(1)} %get-tuple-element.335), channel_id=1, source_target_pairs={{0,4},{1,8},{2,6},{3,10},{4,0},{5,12},{6,2},{7,14},{8,1},{9,13},{1... | collective-permute-start | bytes 1179656 | tf_op jit(solution)/shard_map/cond/branch_1_fun/ppermute | solution.py:41
  125.2 45.0 %collective-permute-start.47 = (bf16[1,2,192,768]{3,2,1,0:T(8,128)(2,1)S(1)}, bf16[1,2,192,768]{3,2,1,0:T(8,128)(2,1)S(1)}, u32[]{:S(2)}, u32[]{:S(2)}) collective-permute-start(bf16[1,2,192,768]{3,2,1,0:T(8,128)(2,1)S(1)} %broadcast_select_fusion.5), channel_id=1, source_target_pairs={{0,1},{1,0},{2,3},{3,2},{4,5},{5,4},{6,7},{7,6},{8,16},{9,17},{10,... | collective-permute-start | bytes 1769480 | tf_op jit(solution)/shard_map/cond/branch_1_fun/ppermute | solution.py:80
  126.2 43.6 %collective-permute-start.52 = (bf16[256,768]{1,0:T(8,128)(2,1)S(1)}, bf16[256,768]{1,0:T(8,128)(2,1)S(1)}, u32[]{:S(2)}, u32[]{:S(2)}) collective-permute-start(bf16[256,768]{1,0:T(8,128)(2,1)S(1)} %get-tuple-element.336), channel_id=1, source_target_pairs={{0,16},{1,24},{2,18},{3,26},{4,20},{5,28},{6,22},{7,30},{8,17},{9,... | collective-permute-start | bytes 1179656 | tf_op jit(solution)/shard_map/cond/branch_1_fun/ppermute | solution.py:41
  131.0 39.3 %collective-permute-start.57 = (bf16[256,768]{1,0:T(8,128)(2,1)S(1)}, bf16[256,768]{1,0:T(8,128)(2,1)S(1)}, u32[]{:S(2)}, u32[]{:S(2)}) collective-permute-start(bf16[256,768]{1,0:T(8,128)(2,1)S(1)} %get-tuple-element.331), channel_id=1, source_target_pairs={{0,4},{1,8},{2,6},{3,10},{4,0},{5,12},{6,2},{7,14},{8,1},{9,13},{1... | collective-permute-start | bytes 1179656 | tf_op jit(solution)/shard_map/cond/branch_1_fun/ppermute | solution.py:41
  132.6 42.0 %collective-permute-start.58 = (bf16[256,768]{1,0:T(8,128)(2,1)S(1)}, bf16[256,768]{1,0:T(8,128)(2,1)S(1)}, u32[]{:S(2)}, u32[]{:S(2)}) collective-permute-start(bf16[256,768]{1,0:T(8,128)(2,1)S(1)} %get-tuple-element.332), channel_id=1, source_target_pairs={{0,16},{1,24},{2,18},{3,26},{4,20},{5,28},{6,22},{7,30},{8,17},{9,... | collective-permute-start | bytes 1179656 | tf_op jit(solution)/shard_map/cond/branch_1_fun/ppermute | solution.py:41
  133.6 42.0 %collective-permute-start.63 = (bf16[256,768]{1,0:T(8,128)(2,1)S(1)}, bf16[256,768]{1,0:T(8,128)(2,1)S(1)}, u32[]{:S(2)}, u32[]{:S(2)}) collective-permute-start(bf16[256,768]{1,0:T(8,128)(2,1)S(1)} %get-tuple-element.327), channel_id=1, source_target_pairs={{0,4},{1,8},{2,6},{3,10},{4,0},{5,12},{6,2},{7,14},{8,1},{9,13},{1... | collective-permute-start | bytes 1179656 | tf_op jit(solution)/shard_map/cond/branch_1_fun/ppermute | solution.py:41
  169.9 26.2 %collective-permute-start.54 = (bf16[2,256,768]{2,1,0:T(8,128)(2,1)S(1)}, bf16[2,256,768]{2,1,0:T(8,128)(2,1)}, u32[]{:S(2)}, u32[]{:S(2)}) collective-permute-start(bf16[2,256,768]{2,1,0:T(8,128)(2,1)S(1)} %pad_maximum_fusion.17), channel_id=1, source_target_pairs={{0,4},{1,5},{2,6},{3,7},{4,0},{5,1},{6,2},{7,3},{8,12},{9,13},{10,... | collective-permute-start | bytes 2359304 | tf_op jit(solution)/shard_map/cond/branch_1_fun/ppermute | solution.py:41
  170.2 23.0 %collective-permute-start.48 = (bf16[1,2,192,768]{3,2,1,0:T(8,128)(2,1)S(1)}, bf16[1,2,192,768]{3,2,1,0:T(8,128)(2,1)S(1)}, u32[]{:S(2)}, u32[]{:S(2)}) collective-permute-start(bf16[1,2,192,768]{3,2,1,0:T(8,128)(2,1)S(1)} %collective-permute-done.47), channel_id=1, source_target_pairs={{0,8},{1,9},{2,10},{3,11},{4,12},{5,13},{6,14},{7,15},{8,0},{9,1},... | collective-permute-start | bytes 1769480 | tf_op jit(solution)/shard_map/cond/branch_1_fun/ppermute | solution.py:80
  170.2 21.0 %collective-permute-start.64 = (bf16[256,768]{1,0:T(8,128)(2,1)S(1)}, bf16[256,768]{1,0:T(8,128)(2,1)S(1)}, u32[]{:S(2)}, u32[]{:S(2)}) collective-permute-start(bf16[256,768]{1,0:T(8,128)(2,1)S(1)} %get-tuple-element.328), channel_id=1, source_target_pairs={{0,16},{1,24},{2,18},{3,26},{4,20},{5,28},{6,22},{7,30},{8,17},{9,... | collective-permute-start | bytes 1179656 | tf_op jit(solution)/shard_map/cond/branch_1_fun/ppermute | solution.py:41
  174.6 21.6 %collective-permute-start.53 = (bf16[2,256,768]{2,1,0:T(8,128)(2,1)S(1)}, bf16[2,256,768]{2,1,0:T(8,128)(2,1)}, u32[]{:S(2)}, u32[]{:S(2)}) collective-permute-start(bf16[2,256,768]{2,1,0:T(8,128)(2,1)S(1)} %pad_maximum_fusion.17), channel_id=1, source_target_pairs={{0,1},{1,0},{2,3},{3,2},{4,5},{5,4},{6,7},{7,6},{8,9},{9,8},{10,11... | collective-permute-start | bytes 2359304 | tf_op jit(solution)/shard_map/cond/branch_1_fun/ppermute | solution.py:41
  175.5 34.3 %collective-permute-start.60 = (bf16[2,256,768]{2,1,0:T(8,128)(2,1)}, bf16[2,256,768]{2,1,0:T(8,128)(2,1)}, u32[]{:S(2)}, u32[]{:S(2)}) collective-permute-start(bf16[2,256,768]{2,1,0:T(8,128)(2,1)} %pad_maximum_fusion.19), channel_id=1, source_target_pairs={{0,4},{1,5},{2,6},{3,7},{4,0},{5,1},{6,2},{7,3},{8,12},{9,13},{10,... | collective-permute-start | bytes 2359304 | tf_op jit(solution)/shard_map/cond/branch_1_fun/ppermute | solution.py:41
  192.2 30.2 %collective-permute-start.66 = (bf16[2,256,768]{2,1,0:T(8,128)(2,1)}, bf16[2,256,768]{2,1,0:T(8,128)(2,1)}, u32[]{:S(2)}, u32[]{:S(2)}) collective-permute-start(bf16[2,256,768]{2,1,0:T(8,128)(2,1)} %pad_maximum_fusion.21), channel_id=1, source_target_pairs={{0,4},{1,5},{2,6},{3,7},{4,0},{5,1},{6,2},{7,3},{8,12},{9,13},{10,... | collective-permute-start | bytes 2359304 | tf_op jit(solution)/shard_map/cond/branch_1_fun/ppermute | solution.py:41
  196.1 34.6 %collective-permute-start.55 = (bf16[2,256,768]{2,1,0:T(8,128)(2,1)}, bf16[2,256,768]{2,1,0:T(8,128)(2,1)}, u32[]{:S(2)}, u32[]{:S(2)}) collective-permute-start(bf16[2,256,768]{2,1,0:T(8,128)(2,1)} %collective-permute-done.54), channel_id=1, source_target_pairs={{0,1},{1,0},{2,3},{3,2},{4,5},{5,4},{6,7},{7,6},{8,9},{9,8},{10,11... | collective-permute-start | bytes 2359304 | tf_op jit(solution)/shard_map/cond/branch_1_fun/ppermute | solution.py:41
  196.2 34.5 %collective-permute-start.59 = (bf16[2,256,768]{2,1,0:T(8,128)(2,1)}, bf16[2,256,768]{2,1,0:T(8,128)(2,1)}, u32[]{:S(2)}, u32[]{:S(2)}) collective-permute-start(bf16[2,256,768]{2,1,0:T(8,128)(2,1)} %pad_maximum_fusion.19), channel_id=1, source_target_pairs={{0,1},{1,0},{2,3},{3,2},{4,5},{5,4},{6,7},{7,6},{8,9},{9,8},{10,11... | collective-permute-start | bytes 2359304 | tf_op jit(solution)/shard_map/cond/branch_1_fun/ppermute | solution.py:41
  209.9 20.9 %collective-permute-start.65 = (bf16[2,256,768]{2,1,0:T(8,128)(2,1)}, bf16[2,256,768]{2,1,0:T(8,128)(2,1)}, u32[]{:S(2)}, u32[]{:S(2)}) collective-permute-start(bf16[2,256,768]{2,1,0:T(8,128)(2,1)} %pad_maximum_fusion.21), channel_id=1, source_target_pairs={{0,1},{1,0},{2,3},{3,2},{4,5},{5,4},{6,7},{7,6},{8,9},{9,8},{10,11... | collective-permute-start | bytes 2359304 | tf_op jit(solution)/shard_map/cond/branch_1_fun/ppermute | solution.py:41
  209.9 20.9 %collective-permute-start.61 = (bf16[2,256,768]{2,1,0:T(8,128)(2,1)}, bf16[2,256,768]{2,1,0:T(8,128)(2,1)}, u32[]{:S(2)}, u32[]{:S(2)}) collective-permute-start(bf16[2,256,768]{2,1,0:T(8,128)(2,1)} %collective-permute-done.60), channel_id=1, source_target_pairs={{0,1},{1,0},{2,3},{3,2},{4,5},{5,4},{6,7},{7,6},{8,9},{9,8},{10,11... | collective-permute-start | bytes 2359304 | tf_op jit(solution)/shard_map/cond/branch_1_fun/ppermute | solution.py:41
  268.2 39.7 %collective-permute-start.73 = (f16[768,384]{1,0:T(8,128)(2,1)}, f16[768,384]{1,0:T(8,128)(2,1)}, u32[]{:S(2)}, u32[]{:S(2)}) collective-permute-start(f16[768,384]{1,0:T(8,128)(2,1)} %get-tuple-element.349), channel_id=1, source_target_pairs={{0,1},{1,0},{2,5},{3,4},{4,3},{5,2},{6,7},{7,6},{8,9},{9,8},{10,13... | collective-permute-start | bytes 1769480 | tf_op jit(solution)/shard_map/ppermute | solution.py:41
  272.2 36.9 %collective-permute-start.68 = (f16[384,768]{1,0:T(8,128)(2,1)}, f16[384,768]{1,0:T(8,128)(2,1)}, u32[]{:S(2)}, u32[]{:S(2)}) collective-permute-start(f16[384,768]{1,0:T(8,128)(2,1)} %get-tuple-element.370), channel_id=1, source_target_pairs={{0,4},{1,8},{2,16},{3,24},{4,0},{5,12},{6,20},{7,28},{8,1},{9,13},... | collective-permute-start | bytes 1769480 | tf_op jit(solution)/shard_map/ppermute | solution.py:41
  272.2 52.0 %collective-permute-start.69 = (f16[384,768]{1,0:T(8,128)(2,1)}, f16[384,768]{1,0:T(8,128)(2,1)}, u32[]{:S(2)}, u32[]{:S(2)}) collective-permute-start(f16[384,768]{1,0:T(8,128)(2,1)} %get-tuple-element.371), channel_id=1, source_target_pairs={{0,8},{1,0},{2,24},{3,16},{4,12},{5,4},{6,28},{7,20},{8,9},{9,1},{... | collective-permute-start | bytes 1769480 | tf_op jit(solution)/shard_map/ppermute | solution.py:41
  274.4 53.3 %collective-permute-start.70 = (f16[384,768]{1,0:T(8,128)(2,1)}, f16[384,768]{1,0:T(8,128)(2,1)S(1)}, u32[]{:S(2)}, u32[]{:S(2)}) collective-permute-start(f16[384,768]{1,0:T(8,128)(2,1)} %get-tuple-element.368), channel_id=1, source_target_pairs={{0,16},{1,24},{2,0},{3,8},{4,20},{5,28},{6,4},{7,12},{8,17},{9,25}... | collective-permute-start | bytes 1769480 | tf_op jit(solution)/shard_map/ppermute | solution.py:41
  284.7 42.3 %collective-permute-start.74 = (f16[768,384]{1,0:T(8,128)(2,1)}, f16[768,384]{1,0:T(8,128)(2,1)S(1)}, u32[]{:S(2)}, u32[]{:S(2)}) collective-permute-start(f16[768,384]{1,0:T(8,128)(2,1)} %get-tuple-element.348), channel_id=1, source_target_pairs={{0,2},{1,3},{2,6},{3,7},{4,0},{5,1},{6,4},{7,5},{8,10},{9,11},{10,... | collective-permute-start | bytes 1769480 | tf_op jit(solution)/shard_map/ppermute | solution.py:41
  307.9 21.7 %collective-permute-start.71 = (f16[384,768]{1,0:T(8,128)(2,1)S(1)}, f16[384,768]{1,0:T(8,128)(2,1)S(1)}, u32[]{:S(2)}, u32[]{:S(2)}) collective-permute-start(f16[384,768]{1,0:T(8,128)(2,1)S(1)} %copy-done.51), channel_id=1, source_target_pairs={{0,24},{1,16},{2,8},{3,0},{4,28},{5,20},{6,12},{7,4},{8,25},{9,17}... | collective-permute-start | bytes 1769480 | tf_op jit(solution)/shard_map/ppermute | solution.py:41
  309.1 38.1 %collective-permute-start.75 = (f16[768,384]{1,0:T(8,128)(2,1)S(1)}, f16[768,384]{1,0:T(8,128)(2,1)S(1)}, u32[]{:S(2)}, u32[]{:S(2)}) collective-permute-start(f16[768,384]{1,0:T(8,128)(2,1)S(1)} %copy-done.52), channel_id=1, source_target_pairs={{0,3},{1,2},{2,7},{3,6},{4,1},{5,0},{6,5},{7,4},{8,11},{9,10},{10,... | collective-permute-start | bytes 1769480 | tf_op jit(solution)/shard_map/ppermute | solution.py:41
  351.9 25.6 %collective-permute-start.76 = (bf16[256,768]{1,0:T(8,128)(2,1)S(1)}, bf16[256,768]{1,0:T(8,128)(2,1)S(1)}, u32[]{:S(2)}, u32[]{:S(2)}) collective-permute-start(bf16[256,768]{1,0:T(8,128)(2,1)S(1)} %get-tuple-element.382), channel_id=1, source_target_pairs={{0,2},{1,3},{2,0},{3,1},{4,6},{5,7},{6,4},{7,5},{8,10},{9,11},{10,... | collective-permute-start | bytes 1179656 | tf_op jit(solution)/shard_map/ppermute | solution.py:41
  361.6 31.6 %collective-permute-start.90 = (bf16[256,768]{1,0:T(8,128)(2,1)S(1)}, bf16[256,768]{1,0:T(8,128)(2,1)S(1)}, u32[]{:S(2)}, u32[]{:S(2)}) collective-permute-start(bf16[256,768]{1,0:T(8,128)(2,1)S(1)} %get-tuple-element.373), channel_id=1, source_target_pairs={{0,16},{1,24},{2,18},{3,26},{4,20},{5,28},{6,22},{7,30},{8,17},{9,... | collective-permute-start | bytes 1179656 | tf_op jit(solution)/shard_map/ppermute | solution.py:41
  369.3 24.0 %collective-permute-start.83 = (bf16[256,768]{1,0:T(8,128)(2,1)S(1)}, bf16[256,768]{1,0:T(8,128)(2,1)S(1)}, u32[]{:S(2)}, u32[]{:S(2)}) collective-permute-start(bf16[256,768]{1,0:T(8,128)(2,1)S(1)} %get-tuple-element.376), channel_id=1, source_target_pairs={{0,2},{1,8},{2,0},{3,10},{4,6},{5,12},{6,4},{7,14},{8,1},{9,11},{1... | collective-permute-start | bytes 1179656 | tf_op jit(solution)/shard_map/ppermute | solution.py:41
  369.4 36.8 %collective-permute-start.84 = (bf16[256,768]{1,0:T(8,128)(2,1)S(1)}, bf16[256,768]{1,0:T(8,128)(2,1)S(1)}, u32[]{:S(2)}, u32[]{:S(2)}) collective-permute-start(bf16[256,768]{1,0:T(8,128)(2,1)S(1)} %get-tuple-element.377), channel_id=1, source_target_pairs={{0,16},{1,24},{2,18},{3,26},{4,20},{5,28},{6,22},{7,30},{8,17},{9,... | collective-permute-start | bytes 1179656 | tf_op jit(solution)/shard_map/ppermute | solution.py:41
  377.8 28.6 %collective-permute-start.77 = (bf16[256,768]{1,0:T(8,128)(2,1)S(1)}, bf16[256,768]{1,0:T(8,128)(2,1)S(1)}, u32[]{:S(2)}, u32[]{:S(2)}) collective-permute-start(bf16[256,768]{1,0:T(8,128)(2,1)S(1)} %get-tuple-element.380), channel_id=1, source_target_pairs={{0,2},{1,8},{2,0},{3,10},{4,6},{5,12},{6,4},{7,14},{8,1},{9,11},{1... | collective-permute-start | bytes 1179656 | tf_op jit(solution)/shard_map/ppermute | solution.py:41
  377.8 32.7 %collective-permute-start.78 = (bf16[256,768]{1,0:T(8,128)(2,1)S(1)}, bf16[256,768]{1,0:T(8,128)(2,1)S(1)}, u32[]{:S(2)}, u32[]{:S(2)}) collective-permute-start(bf16[256,768]{1,0:T(8,128)(2,1)S(1)} %get-tuple-element.381), channel_id=1, source_target_pairs={{0,16},{1,24},{2,18},{3,26},{4,20},{5,28},{6,22},{7,30},{8,17},{9,... | collective-permute-start | bytes 1179656 | tf_op jit(solution)/shard_map/ppermute | solution.py:41
  406.3 23.7 %collective-permute-start.86 = (bf16[2,256,768]{2,1,0:T(8,128)(2,1)S(1)}, bf16[2,256,768]{2,1,0:T(8,128)(2,1)}, u32[]{:S(2)}, u32[]{:S(2)}) collective-permute-start(bf16[2,256,768]{2,1,0:T(8,128)(2,1)S(1)} %pad_maximum_fusion.25.refs_19_), channel_id=1, source_target_pairs={{0,4},{1,5},{2,6},{3,7},{4,0},{5,1},{6,2},{7,3},{8,12},{9,13},{10,... | collective-permute-start | bytes 2359304 | tf_op jit(solution)/shard_map/ppermute | solution.py:41
  410.6 33.3 %collective-permute-start.80 = (bf16[2,256,768]{2,1,0:T(8,128)(2,1)S(1)}, bf16[2,256,768]{2,1,0:T(8,128)(2,1)}, u32[]{:S(2)}, u32[]{:S(2)}) collective-permute-start(bf16[2,256,768]{2,1,0:T(8,128)(2,1)S(1)} %pad_maximum_fusion.24.refs_15_), channel_id=1, source_target_pairs={{0,4},{1,5},{2,6},{3,7},{4,0},{5,1},{6,2},{7,3},{8,12},{9,13},{10,... | collective-permute-start | bytes 2359304 | tf_op jit(solution)/shard_map/ppermute | solution.py:41
  411.1 32.9 %collective-permute-start.85 = (bf16[2,256,768]{2,1,0:T(8,128)(2,1)S(1)}, bf16[2,256,768]{2,1,0:T(8,128)(2,1)}, u32[]{:S(2)}, u32[]{:S(2)}) collective-permute-start(bf16[2,256,768]{2,1,0:T(8,128)(2,1)S(1)} %pad_maximum_fusion.25.refs_19_), channel_id=1, source_target_pairs={{0,1},{1,0},{2,3},{3,2},{4,5},{5,4},{6,7},{7,6},{8,9},{9,8},{10,11... | collective-permute-start | bytes 2359304 | tf_op jit(solution)/shard_map/ppermute | solution.py:41
  413.1 30.9 %collective-permute-start.79 = (bf16[2,256,768]{2,1,0:T(8,128)(2,1)S(1)}, bf16[2,256,768]{2,1,0:T(8,128)(2,1)}, u32[]{:S(2)}, u32[]{:S(2)}) collective-permute-start(bf16[2,256,768]{2,1,0:T(8,128)(2,1)S(1)} %pad_maximum_fusion.24.refs_15_), channel_id=1, source_target_pairs={{0,1},{1,0},{2,3},{3,2},{4,5},{5,4},{6,7},{7,6},{8,9},{9,8},{10,11... | collective-permute-start | bytes 2359304 | tf_op jit(solution)/shard_map/ppermute | solution.py:41
  414.0 30.0 %collective-permute-start.93 = (bf16[2,256,768]{2,1,0:T(8,128)(2,1)S(1)}, bf16[2,256,768]{2,1,0:T(8,128)(2,1)}, u32[]{:S(2)}, u32[]{:S(2)}) collective-permute-start(bf16[2,256,768]{2,1,0:T(8,128)(2,1)S(1)} %collective-permute-done.92.refs_25_), channel_id=1, source_target_pairs={{0,1},{1,0},{2,3},{3,2},{4,5},{5,4},{6,7},{7,6},{8,9},{9,8},{10,11... | collective-permute-start | bytes 2359304 | tf_op jit(solution)/shard_map/ppermute | solution.py:41
  466.8 20.3 %collective-permute-start.98 = (f16[768,384]{1,0:T(8,128)(2,1)S(1)}, f16[768,384]{1,0:T(8,128)(2,1)S(1)}, u32[]{:S(2)}, u32[]{:S(2)}) collective-permute-start(f16[768,384]{1,0:T(8,128)(2,1)S(1)} %get-tuple-element.346), channel_id=1, source_target_pairs={{0,1},{1,0},{2,4},{3,5},{4,2},{5,3},{6,7},{7,6},{8,9},{9,8},{10,12... | collective-permute-start | bytes 1769480 | tf_op jit(solution)/shard_map/ppermute | solution.py:41
  467.5 40.4 %collective-permute-start.99 = (f16[768,384]{1,0:T(8,128)(2,1)S(1)}, f16[768,384]{1,0:T(8,128)(2,1)S(1)}, u32[]{:S(2)}, u32[]{:S(2)}) collective-permute-start(f16[768,384]{1,0:T(8,128)(2,1)S(1)} %get-tuple-element.345), channel_id=1, source_target_pairs={{0,1},{1,0},{2,5},{3,4},{4,3},{5,2},{6,7},{7,6},{8,9},{9,8},{10,13... | collective-permute-start | bytes 1769480 | tf_op jit(solution)/shard_map/ppermute | solution.py:41
  470.2 37.9 %collective-permute-start.94 = (f16[384,768]{1,0:T(8,128)(2,1)S(1)}, f16[384,768]{1,0:T(8,128)(2,1)S(1)}, u32[]{:S(2)}, u32[]{:S(2)}) collective-permute-start(f16[384,768]{1,0:T(8,128)(2,1)S(1)} %get-tuple-element.364), channel_id=1, source_target_pairs={{0,4},{1,8},{2,16},{3,24},{4,0},{5,12},{6,20},{7,28},{8,1},{9,13},... | collective-permute-start | bytes 1769480 | tf_op jit(solution)/shard_map/ppermute | solution.py:41
  470.3 53.3 %collective-permute-start.95 = (f16[384,768]{1,0:T(8,128)(2,1)S(1)}, f16[384,768]{1,0:T(8,128)(2,1)S(1)}, u32[]{:S(2)}, u32[]{:S(2)}) collective-permute-start(f16[384,768]{1,0:T(8,128)(2,1)S(1)} %get-tuple-element.365), channel_id=1, source_target_pairs={{0,8},{1,0},{2,24},{3,16},{4,12},{5,4},{6,28},{7,20},{8,9},{9,1},{... | collective-permute-start | bytes 1769480 | tf_op jit(solution)/shard_map/ppermute | solution.py:41
  470.7 54.7 %collective-permute-start.96 = (f16[384,768]{1,0:T(8,128)(2,1)S(1)}, f16[384,768]{1,0:T(8,128)(2,1)S(1)}, u32[]{:S(2)}, u32[]{:S(2)}) collective-permute-start(f16[384,768]{1,0:T(8,128)(2,1)S(1)} %get-tuple-element.362), channel_id=1, source_target_pairs={{0,16},{1,24},{2,0},{3,8},{4,20},{5,28},{6,4},{7,12},{8,17},{9,25}... | collective-permute-start | bytes 1769480 | tf_op jit(solution)/shard_map/ppermute | solution.py:41
  487.1 37.6 %collective-permute-start.100 = (f16[768,384]{1,0:T(8,128)(2,1)S(1)}, f16[768,384]{1,0:T(8,128)(2,1)S(1)}, u32[]{:S(2)}, u32[]{:S(2)}) collective-permute-start(f16[768,384]{1,0:T(8,128)(2,1)S(1)} %get-tuple-element.344), channel_id=1, source_target_pairs={{0,2},{1,3},{2,6},{3,7},{4,0},{5,1},{6,4},{7,5},{8,10},{9,11},{10,... | collective-permute-start | bytes 1769480 | tf_op jit(solution)/shard_map/ppermute | solution.py:41
  507.9 25.1 %collective-permute-start.97 = (f16[384,768]{1,0:T(8,128)(2,1)S(1)}, f16[384,768]{1,0:T(8,128)(2,1)S(1)}, u32[]{:S(2)}, u32[]{:S(2)}) collective-permute-start(f16[384,768]{1,0:T(8,128)(2,1)S(1)} %get-tuple-element.363), channel_id=1, source_target_pairs={{0,24},{1,16},{2,8},{3,0},{4,28},{5,20},{6,12},{7,4},{8,25},{9,17}... | collective-permute-start | bytes 1769480 | tf_op jit(solution)/shard_map/ppermute | solution.py:41
  508.1 38.2 %collective-permute-start.101 = (f16[768,384]{1,0:T(8,128)(2,1)S(1)}, f16[768,384]{1,0:T(8,128)(2,1)S(1)}, u32[]{:S(2)}, u32[]{:S(2)}) collective-permute-start(f16[768,384]{1,0:T(8,128)(2,1)S(1)} %get-tuple-element.343), channel_id=1, source_target_pairs={{0,3},{1,2},{2,7},{3,6},{4,1},{5,0},{6,5},{7,4},{8,11},{9,10},{10,... | collective-permute-start | bytes 1769480 | tf_op jit(solution)/shard_map/ppermute | solution.py:41
  (75 other events, 875.2 us)

commit v5 on v4

v5 whole, which is shorter than its diff:
```python
import jax
import jax.numpy as jnp
from jax import lax
from jax.experimental import pallas as pl
from jax.experimental.pallas import tpu as pltpu
from jax.sharding import PartitionSpec as P

STEPS = 2
COUPLING_MAX = 0.15625
DENOMINATOR_MIN = 1.5
HALF_TOP = 60000.0
AXES = ("alpha", "beta")
ROW_CHUNKS = 4


class Grid:
    def __init__(self, alpha_devices, beta_devices):
        self.bands = beta_devices
        self.lanes = alpha_devices // beta_devices
        self.majors = beta_devices // 2
        self.places = [
            (band, lane, major, minor)
            for band in range(self.bands)
            for lane in range(self.lanes)
            for major in range(self.majors)
            for minor in range(2)
        ]

    def index(self, band, lane, major, minor):
        return ((band * self.lanes + lane) * self.majors + major) * 2 + minor

    def send(self, value, where, idle=None):
        stays = [where(*place) == place for place in self.places]
        if all(stays):
            return value
        pairs = []
        for place, stay in zip(self.places, stays):
            target = idle(*place) if stay else where(*place)
            pairs.append((self.index(*place), self.index(*target)))
        received = lax.ppermute(value, AXES, pairs)
        if any(stays):
            device = lax.axis_index("alpha") * self.bands + lax.axis_index("beta")
            received = jnp.where(jnp.array(stays)[device], value, received)
        return received


def after(value, *earlier):
    earlier = [array for array in earlier if array is not None]
    return lax.optimization_barrier((value, *earlier))[0] if earlier else value


def bits(count):
    return [1 << i for i in reversed(range(count.bit_length() - 1))]


def ordered(entries, me):
    if len(entries) == 1:
        return entries
    half = len(entries) // 2
    near, far = ordered(entries[:half], me), ordered(entries[half:], me)
    low = (me & half) == 0
    pairs = list(zip(near, far))
    return [jnp.where(low, a, b) for a, b in pairs] + [jnp.where(low, b, a) for a, b in pairs]


def line_order(bands):
    order, half = [[z] for z in range(bands)], 1
    while half < bands:
        middle = [z // (2 * half) * 2 * half + half - (z // half % 2) for z in range(bands)]
        order, half = [order[z] + order[middle[z]] for z in range(bands)], 2 * half
    return order


def gather_bands(grid, own, band, busy=None):
    held = own[None]
    brought = []
    width = 2
    while width <= grid.bands:
        half = width // 2
        moving, kept = held, None
        for hop in range(half):
            partner = list(range(grid.bands))
            for base in range(0, grid.bands, width):
                low, high = base + half - 1, base + half
                if hop == 0:
                    pairs = [(low, high)]
                else:
                    pairs = [(low - hop + 1, low - hop), (high + hop - 1, high + hop)]
                for one, other in pairs:
                    partner[one], partner[other] = other, one
            pairs = [
                (grid.index(z, x, m, n), grid.index(partner[z], x, m, 1 - n if partner[z] == z else n))
                for z, x, m, n in grid.places
            ]
            moving = lax.ppermute(moving, AXES, pairs)
            if hop == 0:
                brought.append(moving)
            takes = [(half - 1 - z % width if z % width < half else z % width - half) == hop for z in range(grid.bands)]
            kept = moving if kept is None else jnp.where(jnp.array(takes)[band], moving, kept)
        if busy is None:
            held = jnp.concatenate([held, kept])
        else:
            mine = jnp.any(busy & (jnp.arange(grid.bands) // half == band // half))
            held = jnp.where(mine, held, kept)
        width *= 2
    return held, brought


def spread_majors(grid, line):
    pieces = {0: line}
    for bit in bits(grid.majors):
        received = {key ^ bit: grid.send(piece, lambda z, x, m, n: (z, x, m ^ bit, n)) for key, piece in pieces.items()}
        pieces.update(received)
    return [pieces[key] for key in range(grid.majors)]


def spread_inputs(grid, coupling, coeffs, busy, band, lane, major, minor):
    rows, slots, tile = coupling.shape
    chunk = rows // (2 * grid.majors)
    first = (minor * grid.majors + major) * chunk
    dense = slots if busy is None else slots // 2
    groups = [(slot, 1) for slot in range(dense)]
    if busy is not None:
        groups.append((dense, slots - dense))
    rider = 1
    lines, gates = [], [None]
    half, extreme = None, None
    for number, (slot, count) in enumerate(groups):
        source = after(coupling, gates[-1])
        own = [lax.dynamic_slice(source, (first, slot + i, 0), (chunk, 1, tile)) for i in range(count)]
        own = jnp.concatenate([one.reshape(1, chunk, tile) for one in own])
        if number == 0:
            values = after(coeffs, own)
            half = values.astype(jnp.bfloat16)
            extreme = (jnp.maximum(jnp.max(jnp.abs(values)), 1e-30) * 1.01).astype(jnp.bfloat16)
            extreme = jnp.full((16, tile), extreme)
        if number == rider:
            for where in (lambda z, x, m, n: (z, x, m, 1 - n), lambda z, x, m, n: (z, (x + 1) % grid.lanes, m, n)):
                extreme = jnp.maximum(extreme, grid.send(extreme, where))
            own = jnp.concatenate([own, jnp.broadcast_to(extreme, (count, *extreme.shape))], axis=1)
        line, brought = gather_bands(grid, own, band, None if slot < dense else busy)
        gates.append(brought[0])
        lines.append((line, brought))
    gathered = [spread_majors(grid, line) for line, _ in lines]
    rode = [piece[:, 0, chunk, 0] for piece in gathered[rider]]
    largest = jnp.max(jnp.stack(rode)).astype(jnp.float32)
    z_gates = [lines[0][0], lines[1][1][-1], gathered[0][-1], gathered[1][-1]]
    parts = to_columns(grid, half, band, lane, major, minor, z_gates, [ROW_CHUNKS], True)
    result = []
    for (slot, count), pieces in zip(groups, gathered):
        if slot >= dense:
            pieces = [jnp.broadcast_to(piece, (grid.bands, *piece.shape[1:])) for piece in pieces]
        if chunk % 16:
            whole = jnp.take(jnp.stack(pieces), major ^ jnp.arange(grid.majors), axis=0)[:, :, :, :chunk]
            pieces = [whole.transpose(1, 2, 0, 3, 4).reshape(grid.bands, count, rows // 2, tile)]
        result.append(pieces)
    if busy is None:
        late, result = result[dense // 2 :], result[: dense // 2]
        kept = rows // 2 // len(late[0])
        joined = [jnp.concatenate([one[:, :, :kept] for one in ones], axis=1) for ones in zip(*late)]
        result.append(joined)
    return result, largest, parts


def to_columns(grid, half, band, lane, major, minor, gates, batches, by_lane):
    rows = half.shape[0]
    lanes, majors = grid.lanes, grid.majors
    part, share = rows // ROW_CHUNKS, rows // majors

    def idle(z, x, m, n):
        return (z, (x + 1) % lanes, m, n) if by_lane else (z, x, m ^ 1, n)

    firsts, done = [], 0
    for batch in batches:
        block = half[done * part : (done + batch) * part]
        first = []
        for key in range(majors):
            piece = [
                lax.dynamic_slice_in_dim(block, (x * majors + (major ^ key)) * share, share, 1) for x in range(lanes)
            ]
            first.append(grid.send(jnp.concatenate(piece, 1), lambda z, x, m, n: (z, x, m ^ key, n)))
        firsts += [[one[i * part : (i + 1) * part] for one in first] for i in range(batch)]
        done += batch
    parts, earlier = [], [None] * majors
    for chunk, first in enumerate(firsts):
        first = jnp.stack(first)
        second = []
        for key in range(majors):
            piece = lax.dynamic_index_in_dim(first, (band // 2) ^ key ^ major, 0, keepdims=False)
            piece = after(piece, earlier[key], gates[min(chunk, len(gates) - 1)] if gates else None)
            piece = grid.send(piece, lambda z, x, m, n: ((z // 2 ^ key) * 2 + n, x, m, z % 2), idle)
            earlier[key] = piece
            second.append(piece)
        second = jnp.stack(second)
        for turn in range(lanes):
            third = grid.send(second, lambda z, x, m, n: (z, (x + turn) % lanes, m, n))
            parts += [third, grid.send(third, lambda z, x, m, n: (z, x, m, 1 - n))]
    return parts


def product_kernel(groups, pieces, lanes, base, id_ref, entry_ref, column_ref, count_ref, scale_ref, *refs):
    couplings, parts = refs[: len(groups) * pieces], refs[len(groups) * pieces : -4]
    out_ref, mirror_ref, coeff_ref, sems = refs[-4:]
    band, lane, major, minor = (id_ref[i] for i in range(4))
    chunk = out_ref.shape[1] // pieces
    tile = couplings[0].shape[3]
    majors, part, _ = parts[0].shape
    bands, rows = 2 * majors, part * ROW_CHUNKS
    wanted = (major * 2 + minor) ^ (base + pl.program_id(0))
    tile_row = (wanted * lanes + lane) * rows // tile

    @pl.when(pl.program_id(0) == 0)
    def _():
        copies = []
        for i, ref in enumerate(parts):
            turn, flip = i // 2 % lanes, i % 2
            for key in range(majors):
                alpha = (((band // 2) ^ key) * 2 + (minor ^ flip)) * lanes + lax.rem(lane + lanes - turn, lanes)
                first = pl.multiple_of(alpha * rows + i // (2 * lanes) * part, part)
                target = coeff_ref.at[pl.ds(first, part)]
                copies.append(pltpu.make_async_copy(ref.at[key], target, sems.at[i * majors + key]))
        for copy in copies:
            copy.start()
        for copy in copies:
            copy.wait()

    def product(number, i, slot):
        first = pl.multiple_of(column_ref[tile_row * sum(groups) + slot] * tile, tile)
        left = [couplings[number * pieces + piece][0, i, :chunk] for piece in range(pieces)]
        left = jnp.concatenate(left, axis=0)
        return jnp.dot(left, coeff_ref[pl.ds(first, tile), :], preferred_element_type=jnp.float32) * scale_ref[0]

    def store(value, add):
        for piece in range(pieces):
            first = (major ^ piece) * chunk if pieces > 1 else 0
            place = pl.ds(pl.multiple_of(first, chunk), chunk)
            rows_of = value[piece * chunk : (piece + 1) * chunk]
            out_ref[0, place, :] = out_ref[0, place, :] + rows_of if add else rows_of

    slot = 0
    for number, count in enumerate(groups):
        for i in range(count):
            if slot == 0:
                store(product(number, i, slot), False)
            else:
                pl.when(slot < count_ref[tile_row])(lambda: store(product(number, i, slot), True))
            slot += 1

    mirror_ref[0] = out_ref[0].T


def products(grid, couplings, parts, ids, entries, tile_cols, tile_count, scale, base):
    bands, lanes = grid.bands, grid.lanes
    groups, pieces = [group[0].shape[1] for group in couplings], len(couplings[0])
    tile = couplings[0][0].shape[3]
    majors, part, strip = parts[0].shape
    rows = part * ROW_CHUNKS // 2
    chunk = rows // pieces

    def spec(count):
        def block(i, ids, entries, *_):
            wanted = (ids[2] * 2 + ids[3]) ^ (base + i)
            return (entries[ids[0] * bands + wanted], 0, 0, 0)

        return pl.BlockSpec((1, count, chunk, tile), block)

    calls = bands // 2
    return pl.pallas_call(
        lambda *refs: product_kernel(groups, pieces, lanes, base, *refs),
        grid_spec=pltpu.PrefetchScalarGridSpec(
            num_scalar_prefetch=5,
            grid=(calls,),
            in_specs=[spec(count) for count in groups for _ in range(pieces)]
            + [pl.BlockSpec(memory_space=pltpu.HBM)] * len(parts),
            out_specs=[
                pl.BlockSpec((1, rows, strip), lambda i, *_: (i, 0, 0)),
                pl.BlockSpec((1, strip, rows), lambda i, *_: (i, 0, 0)),
            ],
            scratch_shapes=[
                pltpu.VMEM((len(parts) * majors * part, strip), jnp.bfloat16),
                pltpu.SemaphoreType.DMA((len(parts) * majors,)),
            ],
        ),
        out_shape=[
            jax.ShapeDtypeStruct((calls, rows, strip), jnp.float32),
            jax.ShapeDtypeStruct((calls, strip, rows), jnp.float32),
        ],
        compiler_params=pltpu.CompilerParams(vmem_limit_bytes=40 << 20),
        cost_estimate=pl.CostEstimate(
            flops=2 * calls * sum(groups) * rows * tile * strip,
            bytes_accessed=2 * (calls * sum(groups) * rows * tile + len(parts) * majors * part * strip),
            transcendentals=0,
        ),
    )(
        ids,
        entries,
        tile_cols.reshape(-1),
        tile_count,
        scale[None],
        *[piece for group in couplings for piece in group],
        *parts,
    )


def send_direct(grid, sigma, base):
    return [
        grid.send(
            sigma[i],
            lambda z, x, m, n: ((m * 2 + n) ^ (base + i), x, z // 2, z % 2),
            lambda z, x, m, n: (z, (x + 1) % grid.lanes, m, n),
        )
        for i in range(sigma.shape[0])
    ]


def bring_home(grid, run, ids, band, lane, major, minor):
    bands, lanes, majors = grid.bands, grid.lanes, grid.majors
    far, far_mirror = run(ids, bands // 2)
    far, far_mirror = far.astype(jnp.float16), far_mirror.astype(jnp.float16)
    received_far = send_direct(grid, far, bands // 2)
    entries = grid.send(far_mirror, lambda z, x, m, n: (z, x, m ^ (majors // 2), n))
    near, near_mirror = run(after(ids, far, far_mirror), 0)
    near, near_mirror = near.astype(jnp.float16), near_mirror.astype(jnp.float16)
    received = send_direct(grid, near, 0) + received_far

    entries = [near_mirror[i] for i in range(bands // 2)] + [entries[i] for i in range(bands // 2)]
    for bit in bits(majors)[1:]:
        moved = [j for j in range(bands) if j // 2 & bit]
        brought = grid.send(jnp.stack([entries[j] for j in moved]), lambda z, x, m, n: (z, x, m ^ bit, n))
        for i, j in enumerate(moved):
            entries[j] = brought[i]
    strip, part = entries[0].shape
    share = strip // lanes
    table = {}
    for turn in range(lanes):
        turned = [lax.dynamic_slice_in_dim(entry, (lane ^ turn) * share, share, 0) for entry in entries]
        turned = grid.send(jnp.stack(turned), lambda z, x, m, n: (z, x ^ turn, m, n))
        for j in range(bands):
            table[j, turn] = turned[j]
    moved = [(j, turn) for j in range(1, bands, 2) for turn in range(lanes)]
    brought = grid.send(jnp.stack([table[key] for key in moved]), lambda z, x, m, n: (z, x, m, 1 - n))
    for i, key in enumerate(moved):
        table[key] = brought[i]

    rows = 2 * part
    direct = jnp.zeros((rows, lanes * rows), jnp.float16)
    for key in range(majors):
        pair = jnp.concatenate(ordered(received[2 * key : 2 * key + 2], band % 2))
        for x in range(lanes):
            first = (x * majors + ((band // 2) ^ key)) * share
            direct = lax.dynamic_update_slice_in_dim(direct, pair[:, x * share : (x + 1) * share], first, 1)
    mirror = jnp.zeros((rows, lanes * rows), jnp.float16)
    for turn in range(lanes):
        for flip in range(2):
            block = jnp.concatenate(ordered([table[2 * key + flip, turn] for key in range(majors)], major))
            first = ((lane ^ turn) * 2 + (minor ^ flip)) * part
            mirror = lax.dynamic_update_slice_in_dim(mirror, block, first, 1)
    return direct, mirror


def body(coeffs, denominator, coupling, tile_cols, tile_count):
    rows = coeffs.shape[0]
    _, slots, tile = coupling.shape
    grid = Grid(lax.axis_size("alpha"), lax.axis_size("beta"))
    alpha, beta = lax.axis_index("alpha"), lax.axis_index("beta")
    band, lane = alpha // grid.lanes, alpha % grid.lanes
    major, minor = beta // 2, beta % 2
    ids = jnp.stack([band, lane, major, minor]).astype(jnp.int32)
    all_rows = (jnp.arange(grid.bands * grid.lanes) * rows // tile).reshape(grid.bands, grid.lanes)
    many = tile_count[all_rows] > slots // 2
    busy = jnp.take(many, lane, axis=1)

    def one_busy(*values):
        return spread_inputs(grid, *values, busy, band, lane, major, minor)

    def any_busy(*values):
        return spread_inputs(grid, *values, None, band, lane, major, minor)

    couplings, largest, parts = lax.cond(
        jnp.max(jnp.sum(many, axis=0)) <= 1, one_busy, any_busy, coupling, coeffs
    )
    entries = jnp.array([row.index(z) for row in line_order(grid.bands) for z in range(grid.bands)], jnp.int32)
    growth = slots * tile * COUPLING_MAX
    current = coeffs
    for step_index in range(STEPS):
        scale = HALF_TOP / (growth * largest)
        largest = largest * (1 + 2 * growth / DENOMINATOR_MIN)
        if step_index:
            half = current.astype(jnp.bfloat16)
            parts = to_columns(grid, half, band, lane, major, minor, [], [1, ROW_CHUNKS - 1], False)

        def run(ids, base):
            return products(grid, couplings, parts, ids, entries, tile_cols, tile_count, scale, base)

        direct, mirror = bring_home(grid, run, ids, band, lane, major, minor)
        total = (direct.astype(jnp.float32) + mirror.astype(jnp.float32)) / scale
        current = current - total / denominator
    return current


def solution(mesh):
    placed = (P("alpha", "beta"), P("alpha", "beta"), P("alpha", None, None), P(), P())
    return jax.shard_map(
        body, mesh=mesh, in_specs=placed, out_specs=P("alpha", "beta"), check_vma=False
    )
```

time: 561 us -> 507 us (0.904)
  the two profiles are of different devices: /device:TPU:21 before, /device:TPU:25 now
where the time goes in v5:
time: 507 us; the launch traced here: 497 us
  waiting for transfers between devices  269 us (53%)
  starting transfers between devices  93.2 us (18%)
  other arithmetic  58.3 us (11%)
  local copies, waits for them, and re-layouts  40.8 us (8%)
  Pallas kernels  31.4 us (6%)
    ppermute x62, waiting for transfers between devices, send(): received = lax.ppermute(value, AXES, pairs)  246 us
    ppermute x62, starting transfers between devices, send(): received = lax.ppermute(value, AXES, pairs)  73.3 us
    pallas_call x4, Pallas kernels, products(): pl.pallas_call(lambda *refs: product_kernel(groups, pieces, lanes, base,...  31.4 us
    ppermute x9, waiting for transfers between devices, gather_bands(): moving = lax.ppermute(moving, AXES, pairs)  22.4 us
    ppermute x9, starting transfers between devices, gather_bands(): moving = lax.ppermute(moving, AXES, pairs)  19.9 us
  transfers between devices with their start and end apart: 71, of which 30 were waited for; matrix products, arithmetic and copies ran while one was open for 13% of the time, Pallas kernels for 3%

profile of v5, /device:TPU:25, one launch (start us, length us, event | category | flops | bytes accessed | tf_op | source)
XLA Modules:
  0.0 496.9 jit_solution(6589674854677131166)
XLA Ops:
  3.1 170.1 %conditional.2 = (bf16[4,1,192,768]{3,2,1,0:T(8,128)(2,1)S(1)}, bf16[4,1,192,768]{3,2,1,0:T(8,128)(2,1)}, bf16[4,1,208,768]{3,2,1,0:T(8,128)(2,1)}, bf16[4,1,208...) conditional(s32[]{:T(128)} %convert_element_type.65, ...), branch_computations={%region_2.6_spmd, %region_6.12_spmd} | conditional | flops 26185744 | bytes 207965664
  3.3 5.1 %copy.32 = bf16[768,4,768]{2,0,1:T(8,128)(2,1)} copy(bf16[768,4,768]{2,1,0:T(4,128)(2,1)} %get-tuple-element.288) | data formatting | bytes 9437184 | tf_op jit(solution)/shard_map
  9.7 5.1 %fusion.84 = (bf16[768,1536]{1,0:T(8,128)(2,1)S(1)}, f32[]{:T(128)}) fusion(f32[768,1536]{1,0:T(8,128)} %get-tuple-element.146), kind=kLoop, calls=%fused_computation.339 | loop fusion | flops 3538943 | bytes 7077892 | tf_op jit(solution)/shard_map/cond/branch_1_fun/convert_element_type | solution.py:134
  30.5 2.3 collective-permute-done.45
  36.0 4.8 collective-permute-start.41
  40.8 7.7 %collective-permute-done.53 = bf16[768,768]{1,0:T(8,128)(2,1)} collective-permute-done((bf16[768,768]{1,0:T(8,128)(2,1)}, bf16[768,768]{1,0:T(8,128)(2,1)}, u32[]{:S(2)}, u32[]{:S(2)}) %collective-permute-start.53) | collective-permute-done | bytes 1179680 | tf_op jit(solution)/shard_map/cond/branch_1_fun/ppermute | solution.py:40
  50.3 4.1 collective-permute-start.47
  55.2 2.5 collective-permute-start.50
  57.6 5.8 %collective-permute-done.41 = bf16[2,1,192,768]{3,2,1,0:T(8,128)(2,1)S(1)} collective-permute-done((bf16[2,1,192,768]{3,2,1,0:T(8,128)(2,1)}, bf16[2,1,192,768]{3,2,1,0:T(8,128)(2,1)S(1)}, u32[]{:S(2)}, u32[]{:S(2)}) %collective-permute-start.41) | collective-permute-done | bytes 589856 | tf_op jit(solution)/shard_map/cond/branch_1_fun/ppermute | solution.py:95
  65.9 14.4 %collective-permute-done.47 = bf16[2,1,208,768]{3,2,1,0:T(8,128)(2,1)S(1)} collective-permute-done((bf16[2,1,208,768]{3,2,1,0:T(8,128)(2,1)S(1)}, bf16[2,1,208,768]{3,2,1,0:T(8,128)(2,1)S(1)}, u32[]{:S(2)}, u32[]{:S(2)}) %collective-permute-start.47) | collective-permute-done | bytes 639008 | tf_op jit(solution)/shard_map/cond/branch_1_fun/ppermute | solution.py:95
  87.2 3.9 collective-permute-start.51
  93.7 8.2 %collective-permute-done.60 = bf16[192,768]{1,0:T(8,128)(2,1)S(1)} collective-permute-done((bf16[192,768]{1,0:T(8,128)(2,1)S(1)}, bf16[192,768]{1,0:T(8,128)(2,1)S(1)}, u32[]{:S(2)}, u32[]{:S(2)}) %collective-permute-start.60) | collective-permute-done | bytes 294944 | tf_op jit(solution)/shard_map/cond/branch_1_fun/ppermute | solution.py:40
  102.0 2.8 collective-permute-start.65
  105.5 12.5 %collective-permute-done.48 = bf16[4,1,208,768]{3,2,1,0:T(8,128)(2,1)S(1)} collective-permute-done((bf16[4,1,208,768]{3,2,1,0:T(8,128)(2,1)}, bf16[4,1,208,768]{3,2,1,0:T(8,128)(2,1)S(1)}, u32[]{:S(2)}, u32[]{:S(2)}) %collective-permute-start.48) | collective-permute-done | bytes 1277984 | tf_op jit(solution)/shard_map/cond/branch_1_fun/ppermute | solution.py:40
  122.5 8.3 %collective-permute-start.61 = (bf16[2,192,768]{2,1,0:T(8,128)(2,1)S(1)}, bf16[2,192,768]{2,1,0:T(8,128)(2,1)S(1)}, u32[]{:S(2)}, u32[]{:S(2)}) collective-permute-start(bf16[2,192,768]{2,1,0:T(8,128)(2,1)S(1)} %pad_maximum_fusion.21), channel_id=1, source_target_pairs={{0,1},{1,0},{2,3},{3,2},{4,5},{5,4},{6,7},{7,6},{8,9},{9,8},{10,11... | collective-permute-start | bytes 1769480 | tf_op jit(solution)/shard_map/cond/branch_1_fun/ppermute | solution.py:40
  130.7 5.8 %collective-permute-done.69 = bf16[192,768]{1,0:T(8,128)(2,1)S(1)} collective-permute-done((bf16[192,768]{1,0:T(8,128)(2,1)S(1)}, bf16[192,768]{1,0:T(8,128)(2,1)S(1)}, u32[]{:S(2)}, u32[]{:S(2)}) %collective-permute-start.69) | collective-permute-done | bytes 294944 | tf_op jit(solution)/shard_map/cond/branch_1_fun/ppermute | solution.py:40
  141.5 12.1 %collective-permute-done.52 = bf16[1,2,192,768]{3,2,1,0:T(8,128)(2,1)S(1)} collective-permute-done((bf16[1,2,192,768]{3,2,1,0:T(8,128)(2,1)S(1)}, bf16[1,2,192,768]{3,2,1,0:T(8,128)(2,1)S(1)}, u32[]{:S(2)}, u32[]{:S(2)}) %collective-permute-start.52) | collective-permute-done | bytes 589856 | tf_op jit(solution)/shard_map/cond/branch_1_fun/ppermute | solution.py:40
  155.4 12.0 %collective-permute-done.72 = bf16[2,192,768]{2,1,0:T(8,128)(2,1)} collective-permute-done((bf16[2,192,768]{2,1,0:T(8,128)(2,1)}, bf16[2,192,768]{2,1,0:T(8,128)(2,1)}, u32[]{:S(2)}, u32[]{:S(2)}) %collective-permute-start.72) | collective-permute-done | bytes 589856 | tf_op jit(solution)/shard_map/cond/branch_1_fun/ppermute | solution.py:40
  175.4 8.4 %shard_map.253 = (f32[2,384,768]{2,1,0:T(8,128)S(1)}, f32[2,768,384]{2,1,0:T(8,128)S(1)}) custom-call(s32[4]{0:T(128)S(1)} %pad_add_fusion.refs_0_, s32[16]{0:T(128)S(1)} %copy-done.1, s32[32]{0:T(128)S(1)} %reshape.149.refs_2_, s32[8]{0:T(128)S(1)} %copy-done, f32[1]{0:T(128)} %get-tuple-element.206.refs_4_, ...), custom_call_target="tpu_custom_call" | custom-call | flops 3623878656 | bytes 14155776 | tf_op jit(solution)/shard_map/pallas_call | solution.py:268
  185.0 2.7 collective-permute-start.78
  190.1 9.2 %shard_map.254 = (f32[2,384,768]{2,1,0:T(8,128)S(1)}, f32[2,768,384]{2,1,0:T(8,128)S(1)}) custom-call(s32[4]{0:T(128)S(1)} %pad_add_fusion.refs_0_, s32[16]{0:T(128)S(1)} %copy-done.1, s32[32]{0:T(128)S(1)} %reshape.149.refs_2_, s32[8]{0:T(128)S(1)} %copy-done, f32[1]{0:T(128)} %get-tuple-element.206.refs_4_, ...), custom_call_target="tpu_custom_call" | custom-call | flops 3623878656 | bytes 14155776 | tf_op jit(solution)/shard_map/pallas_call | solution.py:268
  202.9 11.5 %collective-permute-done.78 = f16[2,768,384]{2,1,0:T(8,128)(2,1)} collective-permute-done((f16[2,768,384]{2,1,0:T(8,128)(2,1)}, f16[2,768,384]{2,1,0:T(8,128)(2,1)}, u32[]{:S(2)}, u32[]{:S(2)}) %collective-permute-start.78) | collective-permute-done | bytes 1179680 | tf_op jit(solution)/shard_map/ppermute | solution.py:40
  221.4 4.4 collective-permute-start.75
  228.4 17.6 %collective-permute-done.79 = f16[4,384,384]{2,1,0:T(8,128)(2,1)} collective-permute-done((f16[4,384,384]{2,1,0:T(8,128)(2,1)}, f16[4,384,384]{2,1,0:T(8,128)(2,1)}, u32[]{:S(2)}, u32[]{:S(2)}) %collective-permute-start.79) | collective-permute-done | bytes 1179680 | tf_op jit(solution)/shard_map/ppermute | solution.py:40
  249.4 12.4 %collective-permute-done.74 = f16[384,768]{1,0:T(8,128)(2,1)} collective-permute-done((f16[384,768]{1,0:T(8,128)(2,1)}, f16[384,768]{1,0:T(8,128)(2,1)}, u32[]{:S(2)}, u32[]{:S(2)}) %collective-permute-start.74) | collective-permute-done | bytes 589856 | tf_op jit(solution)/shard_map/ppermute | solution.py:40
  261.8 14.0 %collective-permute-done.75 = f16[384,768]{1,0:T(8,128)(2,1)} collective-permute-done((f16[384,768]{1,0:T(8,128)(2,1)}, f16[384,768]{1,0:T(8,128)(2,1)}, u32[]{:S(2)}, u32[]{:S(2)}) %collective-permute-start.75) | collective-permute-done | bytes 589856 | tf_op jit(solution)/shard_map/ppermute | solution.py:40
  275.9 2.3 broadcast_select_fusion.21
  278.7 2.5 collective-permute-done.77
  295.0 2.3 collective-permute-done.81
  300.1 9.8 %collective-permute-done.82 = bf16[192,768]{1,0:T(8,128)(2,1)S(1)} collective-permute-done((bf16[192,768]{1,0:T(8,128)(2,1)S(1)}, bf16[192,768]{1,0:T(8,128)(2,1)S(1)}, u32[]{:S(2)}, u32[]{:S(2)}) %collective-permute-start.82) | collective-permute-done | bytes 294944 | tf_op jit(solution)/shard_map/ppermute | solution.py:40
  312.0 11.3 %collective-permute-start.89 = (bf16[192,768]{1,0:T(8,128)(2,1)S(1)}, bf16[192,768]{1,0:T(8,128)(2,1)S(1)}, u32[]{:S(2)}, u32[]{:S(2)}) collective-permute-start(bf16[192,768]{1,0:T(8,128)(2,1)S(1)} %get-tuple-element.237), channel_id=1, source_target_pairs={{0,16},{1,24},{2,18},{3,26},{4,20},{5,28},{6,22},{7,30},{8,17},{9,... | collective-permute-start | bytes 884744 | tf_op jit(solution)/shard_map/ppermute | solution.py:40
  327.8 8.2 %collective-permute-done.89 = bf16[192,768]{1,0:T(8,128)(2,1)S(1)} collective-permute-done((bf16[192,768]{1,0:T(8,128)(2,1)S(1)}, bf16[192,768]{1,0:T(8,128)(2,1)S(1)}, u32[]{:S(2)}, u32[]{:S(2)}) %collective-permute-start.89) | collective-permute-done | bytes 294944 | tf_op jit(solution)/shard_map/ppermute | solution.py:40
  339.6 14.5 %collective-permute-done.94 = bf16[192,768]{1,0:T(8,128)(2,1)S(1)} collective-permute-done((bf16[192,768]{1,0:T(8,128)(2,1)S(1)}, bf16[192,768]{1,0:T(8,128)(2,1)S(1)}, u32[]{:S(2)}, u32[]{:S(2)}) %collective-permute-start.94) | collective-permute-done | bytes 294944 | tf_op jit(solution)/shard_map/ppermute | solution.py:40
  355.4 10.9 %collective-permute-done.99 = bf16[192,768]{1,0:T(8,128)(2,1)S(1)} collective-permute-done((bf16[192,768]{1,0:T(8,128)(2,1)S(1)}, bf16[192,768]{1,0:T(8,128)(2,1)S(1)}, u32[]{:S(2)}, u32[]{:S(2)}) %collective-permute-start.99) | collective-permute-done | bytes 294944 | tf_op jit(solution)/shard_map/ppermute | solution.py:40
  368.5 8.9 %collective-permute-done.96.refs_21_ = bf16[2,192,768]{2,1,0:T(8,128)(2,1)S(1)} collective-permute-done((bf16[2,192,768]{2,1,0:T(8,128)(2,1)S(1)}, bf16[2,192,768]{2,1,0:T(8,128)(2,1)S(1)}, u32[]{:S(2)}, u32[]{:S(2)}) %collective-permute-start.96) | collective-permute-done | bytes 589856 | tf_op jit(solution)/shard_map/ppermute | solution.py:40
  377.4 6.3 %collective-permute-done.101.refs_25_ = bf16[2,192,768]{2,1,0:T(8,128)(2,1)S(1)} collective-permute-done((bf16[2,192,768]{2,1,0:T(8,128)(2,1)S(1)}, bf16[2,192,768]{2,1,0:T(8,128)(2,1)S(1)}, u32[]{:S(2)}, u32[]{:S(2)}) %collective-permute-start.101) | collective-permute-done | bytes 589856 | tf_op jit(solution)/shard_map/ppermute | solution.py:40
  383.8 2.0 collective-permute-done.102.refs_26_
  385.8 6.4 %shard_map.255 = (f32[2,384,768]{2,1,0:T(8,128)S(1)}, f32[2,768,384]{2,1,0:T(8,128)S(1)}) custom-call(s32[4]{0:T(128)S(1)} %pad_add_fusion.refs_0_, s32[16]{0:T(128)S(1)} %copy-done.1, s32[32]{0:T(128)S(1)} %reshape.149.refs_2_, s32[8]{0:T(128)S(1)} %copy-done, f32[1]{0:T(128)} %get-tuple-element.235.refs_4_, ...), custom_call_target="tpu_custom_call" | custom-call | flops 3623878656 | bytes 14155776 | tf_op jit(solution)/shard_map/pallas_call | solution.py:268
  394.6 7.4 %shard_map.256 = (f32[2,384,768]{2,1,0:T(8,128)S(1)}, f32[2,768,384]{2,1,0:T(8,128)S(1)}) custom-call(s32[4]{0:T(128)S(1)} %pad_add_fusion.refs_0_, s32[16]{0:T(128)S(1)} %copy-done.1, s32[32]{0:T(128)S(1)} %reshape.149.refs_2_, s32[8]{0:T(128)S(1)} %copy-done, f32[1]{0:T(128)} %get-tuple-element.235.refs_4_, ...), custom_call_target="tpu_custom_call" | custom-call | flops 3623878656 | bytes 14155776 | tf_op jit(solution)/shard_map/pallas_call | solution.py:268
  402.6 18.5 %collective-permute-done.107 = f16[2,768,384]{2,1,0:T(8,128)(2,1)} collective-permute-done((f16[2,768,384]{2,1,0:T(8,128)(2,1)}, f16[2,768,384]{2,1,0:T(8,128)(2,1)}, u32[]{:S(2)}, u32[]{:S(2)}) %collective-permute-start.107) | collective-permute-done | bytes 1179680 | tf_op jit(solution)/shard_map/ppermute | solution.py:40
  424.3 10.3 %collective-permute-start.103 = (f16[384,768]{1,0:T(8,128)(2,1)S(1)}, f16[384,768]{1,0:T(8,128)(2,1)S(1)}, u32[]{:S(2)}, u32[]{:S(2)}) collective-permute-start(f16[384,768]{1,0:T(8,128)(2,1)S(1)} %get-tuple-element.360), channel_id=1, source_target_pairs={{0,4},{1,8},{2,16},{3,24},{4,0},{5,12},{6,20},{7,28},{8,1},{9,13},... | collective-permute-start | bytes 1769480 | tf_op jit(solution)/shard_map/ppermute | solution.py:40
  434.9 4.0 collective-permute-start.106
  438.9 11.0 %collective-permute-done.108 = f16[4,384,384]{2,1,0:T(8,128)(2,1)S(1)} collective-permute-done((f16[4,384,384]{2,1,0:T(8,128)(2,1)S(1)}, f16[4,384,384]{2,1,0:T(8,128)(2,1)S(1)}, u32[]{:S(2)}, u32[]{:S(2)}) %collective-permute-start.108) | collective-permute-done | bytes 1179680 | tf_op jit(solution)/shard_map/ppermute | solution.py:40
  450.6 1.9 collective-permute-start.109
  452.6 15.9 %collective-permute-done.103 = f16[384,768]{1,0:T(8,128)(2,1)S(1)} collective-permute-done((f16[384,768]{1,0:T(8,128)(2,1)S(1)}, f16[384,768]{1,0:T(8,128)(2,1)S(1)}, u32[]{:S(2)}, u32[]{:S(2)}) %collective-permute-start.103) | collective-permute-done | bytes 589856 | tf_op jit(solution)/shard_map/ppermute | solution.py:40
  468.4 12.8 %collective-permute-done.104 = f16[384,768]{1,0:T(8,128)(2,1)S(1)} collective-permute-done((f16[384,768]{1,0:T(8,128)(2,1)S(1)}, f16[384,768]{1,0:T(8,128)(2,1)S(1)}, u32[]{:S(2)}, u32[]{:S(2)}) %collective-permute-start.104) | collective-permute-done | bytes 589856 | tf_op jit(solution)/shard_map/ppermute | solution.py:40
  482.9 6.6 %collective-permute-done.106 = f16[384,768]{1,0:T(8,128)(2,1)S(1)} collective-permute-done((f16[384,768]{1,0:T(8,128)(2,1)S(1)}, f16[384,768]{1,0:T(8,128)(2,1)S(1)}, u32[]{:S(2)}, u32[]{:S(2)}) %collective-permute-start.106) | collective-permute-done | bytes 589856 | tf_op jit(solution)/shard_map/ppermute | solution.py:40
  493.0 3.7 divide_subtract_fusion
  (352 shorter events, 117.1 us)
Async XLA Ops:
  21.3 27.2 %collective-permute-start.53 = (bf16[768,768]{1,0:T(8,128)(2,1)}, bf16[768,768]{1,0:T(8,128)(2,1)}, u32[]{:S(2)}, u32[]{:S(2)}) collective-permute-start(bf16[768,768]{1,0:T(8,128)(2,1)} %pad_maximum_fusion.17), channel_id=1, source_target_pairs={{0,2},{1,3},{2,0},{3,1},{4,6},{5,7},{6,4},{7,5},{8,10},{9,11},{10,... | collective-permute-start | bytes 3538952 | tf_op jit(solution)/shard_map/cond/branch_1_fun/ppermute | solution.py:40
  32.8 17.5 %collective-permute-start.46 = (bf16[2,1,208,768]{3,2,1,0:T(8,128)(2,1)S(1)}, bf16[2,1,208,768]{3,2,1,0:T(8,128)(2,1)S(1)}, u32[]{:S(2)}, u32[]{:S(2)}) collective-permute-start(bf16[2,1,208,768]{3,2,1,0:T(8,128)(2,1)S(1)} %pad_maximum_fusion.18), channel_id=1, source_target_pairs={{0,1},{1,0},{2,3},{3,2},{4,5},{5,4},{6,7},{7,6},{8,16},{9,17},{10,... | collective-permute-start | bytes 1916936 | tf_op jit(solution)/shard_map/cond/branch_1_fun/ppermute | solution.py:95
  35.8 18.6 %collective-permute-start.49 = (bf16[1,2,192,768]{3,2,1,0:T(8,128)(2,1)S(1)}, bf16[1,2,192,768]{3,2,1,0:T(8,128)(2,1)S(1)}, u32[]{:S(2)}, u32[]{:S(2)}) collective-permute-start(bf16[1,2,192,768]{3,2,1,0:T(8,128)(2,1)S(1)} %maximum_bitcast_fusion.2), channel_id=1, source_target_pairs={{0,8},{1,9},{2,10},{3,11},{4,12},{5,13},{6,14},{7,15},{8,0},{9,1},... | collective-permute-start | bytes 1769480 | tf_op jit(solution)/shard_map/cond/branch_1_fun/ppermute | solution.py:95
  36.0 27.4 %collective-permute-start.41 = (bf16[2,1,192,768]{3,2,1,0:T(8,128)(2,1)}, bf16[2,1,192,768]{3,2,1,0:T(8,128)(2,1)S(1)}, u32[]{:S(2)}, u32[]{:S(2)}) collective-permute-start(bf16[2,1,192,768]{3,2,1,0:T(8,128)(2,1)} %collective-permute-done.40), channel_id=1, source_target_pairs={{0,8},{1,9},{2,10},{3,11},{4,12},{5,13},{6,14},{7,15},{8,0},{9,1},... | collective-permute-start | bytes 1769480 | tf_op jit(solution)/shard_map/cond/branch_1_fun/ppermute | solution.py:95
  50.3 29.9 %collective-permute-start.47 = (bf16[2,1,208,768]{3,2,1,0:T(8,128)(2,1)S(1)}, bf16[2,1,208,768]{3,2,1,0:T(8,128)(2,1)S(1)}, u32[]{:S(2)}, u32[]{:S(2)}) collective-permute-start(bf16[2,1,208,768]{3,2,1,0:T(8,128)(2,1)S(1)} %collective-permute-done.46), channel_id=1, source_target_pairs={{0,8},{1,9},{2,10},{3,11},{4,12},{5,13},{6,14},{7,15},{8,0},{9,1},... | collective-permute-start | bytes 1916936 | tf_op jit(solution)/shard_map/cond/branch_1_fun/ppermute | solution.py:95
  55.2 32.1 %collective-permute-start.50 = (bf16[1,2,192,768]{3,2,1,0:T(8,128)(2,1)S(1)}, bf16[1,2,192,768]{3,2,1,0:T(8,128)(2,1)S(1)}, u32[]{:S(2)}, u32[]{:S(2)}) collective-permute-start(bf16[1,2,192,768]{3,2,1,0:T(8,128)(2,1)S(1)} %broadcast_select_fusion.8), channel_id=1, source_target_pairs={{0,1},{1,0},{2,3},{3,2},{4,5},{5,4},{6,7},{7,6},{8,16},{9,17},{10,... | collective-permute-start | bytes 1769480 | tf_op jit(solution)/shard_map/cond/branch_1_fun/ppermute | solution.py:95
  64.3 27.5 %collective-permute-start.42 = (bf16[4,1,192,768]{3,2,1,0:T(8,128)(2,1)S(1)}, bf16[4,1,192,768]{3,2,1,0:T(8,128)(2,1)S(1)}, u32[]{:S(2)}, u32[]{:S(2)}) collective-permute-start(bf16[4,1,192,768]{3,2,1,0:T(8,128)(2,1)S(1)} %pad_maximum_fusion.16), channel_id=1, source_target_pairs={{0,2},{1,3},{2,0},{3,1},{4,6},{5,7},{6,4},{7,5},{8,10},{9,11},{10,... | collective-permute-start | bytes 3538952 | tf_op jit(solution)/shard_map/cond/branch_1_fun/ppermute | solution.py:40
  64.7 17.8 %collective-permute-start.54 = (bf16[192,768]{1,0:T(8,128)(2,1)S(1)}, bf16[192,768]{1,0:T(8,128)(2,1)S(1)}, u32[]{:S(2)}, u32[]{:S(2)}) collective-permute-start(bf16[192,768]{1,0:T(8,128)(2,1)S(1)} %get-tuple-element.153), channel_id=1, source_target_pairs={{0,4},{1,8},{2,6},{3,10},{4,0},{5,12},{6,2},{7,14},{8,1},{9,13},{1... | collective-permute-start | bytes 884744 | tf_op jit(solution)/shard_map/cond/branch_1_fun/ppermute | solution.py:40
  65.9 21.2 %collective-permute-start.55 = (bf16[192,768]{1,0:T(8,128)(2,1)S(1)}, bf16[192,768]{1,0:T(8,128)(2,1)S(1)}, u32[]{:S(2)}, u32[]{:S(2)}) collective-permute-start(bf16[192,768]{1,0:T(8,128)(2,1)S(1)} %get-tuple-element.154), channel_id=1, source_target_pairs={{0,16},{1,24},{2,18},{3,26},{4,20},{5,28},{6,22},{7,30},{8,17},{9,... | collective-permute-start | bytes 884744 | tf_op jit(solution)/shard_map/cond/branch_1_fun/ppermute | solution.py:40
  82.2 35.8 %collective-permute-start.48 = (bf16[4,1,208,768]{3,2,1,0:T(8,128)(2,1)}, bf16[4,1,208,768]{3,2,1,0:T(8,128)(2,1)S(1)}, u32[]{:S(2)}, u32[]{:S(2)}) collective-permute-start(bf16[4,1,208,768]{3,2,1,0:T(8,128)(2,1)} %pad_maximum_fusion.15), channel_id=1, source_target_pairs={{0,2},{1,3},{2,0},{3,1},{4,6},{5,7},{6,4},{7,5},{8,10},{9,11},{10,... | collective-permute-start | bytes 3833864 | tf_op jit(solution)/shard_map/cond/branch_1_fun/ppermute | solution.py:40
  87.2 31.1 %collective-permute-start.51 = (bf16[1,2,192,768]{3,2,1,0:T(8,128)(2,1)S(1)}, bf16[1,2,192,768]{3,2,1,0:T(8,128)(2,1)S(1)}, u32[]{:S(2)}, u32[]{:S(2)}) collective-permute-start(bf16[1,2,192,768]{3,2,1,0:T(8,128)(2,1)S(1)} %collective-permute-done.50), channel_id=1, source_target_pairs={{0,8},{1,9},{2,10},{3,11},{4,12},{5,13},{6,14},{7,15},{8,0},{9,1},... | collective-permute-start | bytes 1769480 | tf_op jit(solution)/shard_map/cond/branch_1_fun/ppermute | solution.py:95
  93.6 28.8 %collective-permute-start.57 = (bf16[2,192,768]{2,1,0:T(8,128)(2,1)S(1)}, bf16[2,192,768]{2,1,0:T(8,128)(2,1)S(1)}, u32[]{:S(2)}, u32[]{:S(2)}) collective-permute-start(bf16[2,192,768]{2,1,0:T(8,128)(2,1)S(1)} %pad_maximum_fusion.20), channel_id=1, source_target_pairs={{0,4},{1,5},{2,6},{3,7},{4,0},{5,1},{6,2},{7,3},{8,12},{9,13},{10,... | collective-permute-start | bytes 1769480 | tf_op jit(solution)/shard_map/cond/branch_1_fun/ppermute | solution.py:40
  101.9 37.2 %collective-permute-start.56 = (bf16[2,192,768]{2,1,0:T(8,128)(2,1)S(1)}, bf16[2,192,768]{2,1,0:T(8,128)(2,1)S(1)}, u32[]{:S(2)}, u32[]{:S(2)}) collective-permute-start(bf16[2,192,768]{2,1,0:T(8,128)(2,1)S(1)} %pad_maximum_fusion.20), channel_id=1, source_target_pairs={{0,1},{1,0},{2,3},{3,2},{4,5},{5,4},{6,7},{7,6},{8,9},{9,8},{10,11... | collective-permute-start | bytes 1769480 | tf_op jit(solution)/shard_map/cond/branch_1_fun/ppermute | solution.py:40
  102.0 19.4 %collective-permute-start.65 = (bf16[192,768]{1,0:T(8,128)(2,1)S(1)}, bf16[192,768]{1,0:T(8,128)(2,1)S(1)}, u32[]{:S(2)}, u32[]{:S(2)}) collective-permute-start(bf16[192,768]{1,0:T(8,128)(2,1)S(1)} %get-tuple-element.160), channel_id=1, source_target_pairs={{0,16},{1,24},{2,18},{3,26},{4,20},{5,28},{6,22},{7,30},{8,17},{9,... | collective-permute-start | bytes 884744 | tf_op jit(solution)/shard_map/cond/branch_1_fun/ppermute | solution.py:40
  118.0 21.7 %collective-permute-start.62 = (bf16[2,192,768]{2,1,0:T(8,128)(2,1)S(1)}, bf16[2,192,768]{2,1,0:T(8,128)(2,1)}, u32[]{:S(2)}, u32[]{:S(2)}) collective-permute-start(bf16[2,192,768]{2,1,0:T(8,128)(2,1)S(1)} %pad_maximum_fusion.21), channel_id=1, source_target_pairs={{0,4},{1,5},{2,6},{3,7},{4,0},{5,1},{6,2},{7,3},{8,12},{9,13},{10,... | collective-permute-start | bytes 1769480 | tf_op jit(solution)/shard_map/cond/branch_1_fun/ppermute | solution.py:40
  118.3 18.2 %collective-permute-start.69 = (bf16[192,768]{1,0:T(8,128)(2,1)S(1)}, bf16[192,768]{1,0:T(8,128)(2,1)S(1)}, u32[]{:S(2)}, u32[]{:S(2)}) collective-permute-start(bf16[192,768]{1,0:T(8,128)(2,1)S(1)} %get-tuple-element.162), channel_id=1, source_target_pairs={{0,4},{1,8},{2,6},{3,10},{4,0},{5,12},{6,2},{7,14},{8,1},{9,13},{1... | collective-permute-start | bytes 884744 | tf_op jit(solution)/shard_map/cond/branch_1_fun/ppermute | solution.py:40
  121.4 16.8 %collective-permute-start.70 = (bf16[192,768]{1,0:T(8,128)(2,1)S(1)}, bf16[192,768]{1,0:T(8,128)(2,1)S(1)}, u32[]{:S(2)}, u32[]{:S(2)}) collective-permute-start(bf16[192,768]{1,0:T(8,128)(2,1)S(1)} %get-tuple-element.163), channel_id=1, source_target_pairs={{0,16},{1,24},{2,18},{3,26},{4,20},{5,28},{6,22},{7,30},{8,17},{9,... | collective-permute-start | bytes 884744 | tf_op jit(solution)/shard_map/cond/branch_1_fun/ppermute | solution.py:40
  122.5 18.2 %collective-permute-start.61 = (bf16[2,192,768]{2,1,0:T(8,128)(2,1)S(1)}, bf16[2,192,768]{2,1,0:T(8,128)(2,1)S(1)}, u32[]{:S(2)}, u32[]{:S(2)}) collective-permute-start(bf16[2,192,768]{2,1,0:T(8,128)(2,1)S(1)} %pad_maximum_fusion.21), channel_id=1, source_target_pairs={{0,1},{1,0},{2,3},{3,2},{4,5},{5,4},{6,7},{7,6},{8,9},{9,8},{10,11... | collective-permute-start | bytes 1769480 | tf_op jit(solution)/shard_map/cond/branch_1_fun/ppermute | solution.py:40
  139.1 15.6 %collective-permute-start.67 = (bf16[2,192,768]{2,1,0:T(8,128)(2,1)}, bf16[2,192,768]{2,1,0:T(8,128)(2,1)}, u32[]{:S(2)}, u32[]{:S(2)}) collective-permute-start(bf16[2,192,768]{2,1,0:T(8,128)(2,1)} %pad_maximum_fusion.22), channel_id=1, source_target_pairs={{0,4},{1,5},{2,6},{3,7},{4,0},{5,1},{6,2},{7,3},{8,12},{9,13},{10,... | collective-permute-start | bytes 1769480 | tf_op jit(solution)/shard_map/cond/branch_1_fun/ppermute | solution.py:40
  139.8 27.6 %collective-permute-start.72 = (bf16[2,192,768]{2,1,0:T(8,128)(2,1)}, bf16[2,192,768]{2,1,0:T(8,128)(2,1)}, u32[]{:S(2)}, u32[]{:S(2)}) collective-permute-start(bf16[2,192,768]{2,1,0:T(8,128)(2,1)} %pad_maximum_fusion.23), channel_id=1, source_target_pairs={{0,4},{1,5},{2,6},{3,7},{4,0},{5,1},{6,2},{7,3},{8,12},{9,13},{10,... | collective-permute-start | bytes 1769480 | tf_op jit(solution)/shard_map/cond/branch_1_fun/ppermute | solution.py:40
  140.7 30.6 %collective-permute-start.63 = (bf16[2,192,768]{2,1,0:T(8,128)(2,1)}, bf16[2,192,768]{2,1,0:T(8,128)(2,1)}, u32[]{:S(2)}, u32[]{:S(2)}) collective-permute-start(bf16[2,192,768]{2,1,0:T(8,128)(2,1)} %collective-permute-done.62), channel_id=1, source_target_pairs={{0,1},{1,0},{2,3},{3,2},{4,5},{5,4},{6,7},{7,6},{8,9},{9,8},{10,11... | collective-permute-start | bytes 1769480 | tf_op jit(solution)/shard_map/cond/branch_1_fun/ppermute | solution.py:40
  141.0 30.3 %collective-permute-start.66 = (bf16[2,192,768]{2,1,0:T(8,128)(2,1)}, bf16[2,192,768]{2,1,0:T(8,128)(2,1)}, u32[]{:S(2)}, u32[]{:S(2)}) collective-permute-start(bf16[2,192,768]{2,1,0:T(8,128)(2,1)} %pad_maximum_fusion.22), channel_id=1, source_target_pairs={{0,1},{1,0},{2,3},{3,2},{4,5},{5,4},{6,7},{7,6},{8,9},{9,8},{10,11... | collective-permute-start | bytes 1769480 | tf_op jit(solution)/shard_map/cond/branch_1_fun/ppermute | solution.py:40
  153.6 17.7 %collective-permute-start.71 = (bf16[2,192,768]{2,1,0:T(8,128)(2,1)}, bf16[2,192,768]{2,1,0:T(8,128)(2,1)}, u32[]{:S(2)}, u32[]{:S(2)}) collective-permute-start(bf16[2,192,768]{2,1,0:T(8,128)(2,1)} %pad_maximum_fusion.23), channel_id=1, source_target_pairs={{0,1},{1,0},{2,3},{3,2},{4,5},{5,4},{6,7},{7,6},{8,9},{9,8},{10,11... | collective-permute-start | bytes 1769480 | tf_op jit(solution)/shard_map/cond/branch_1_fun/ppermute | solution.py:40
  154.8 16.6 %collective-permute-start.68 = (bf16[2,192,768]{2,1,0:T(8,128)(2,1)}, bf16[2,192,768]{2,1,0:T(8,128)(2,1)}, u32[]{:S(2)}, u32[]{:S(2)}) collective-permute-start(bf16[2,192,768]{2,1,0:T(8,128)(2,1)} %collective-permute-done.67), channel_id=1, source_target_pairs={{0,1},{1,0},{2,3},{3,2},{4,5},{5,4},{6,7},{7,6},{8,9},{9,8},{10,11... | collective-permute-start | bytes 1769480 | tf_op jit(solution)/shard_map/cond/branch_1_fun/ppermute | solution.py:40
  185.0 29.4 %collective-permute-start.78 = (f16[2,768,384]{2,1,0:T(8,128)(2,1)}, f16[2,768,384]{2,1,0:T(8,128)(2,1)}, u32[]{:S(2)}, u32[]{:S(2)}) collective-permute-start(f16[2,768,384]{2,1,0:T(8,128)(2,1)} %convert_element_type.67), channel_id=1, source_target_pairs={{0,2},{1,3},{2,0},{3,1},{4,6},{5,7},{6,4},{7,5},{8,10},{9,11},{10,... | collective-permute-start | bytes 3538952 | tf_op jit(solution)/shard_map/ppermute | solution.py:40
  218.8 27.3 %collective-permute-start.79 = (f16[4,384,384]{2,1,0:T(8,128)(2,1)}, f16[4,384,384]{2,1,0:T(8,128)(2,1)}, u32[]{:S(2)}, u32[]{:S(2)}) collective-permute-start(f16[4,384,384]{2,1,0:T(8,128)(2,1)} %pad_maximum_fusion.25), channel_id=1, source_target_pairs={{0,4},{1,5},{2,6},{3,7},{4,0},{5,1},{6,2},{7,3},{8,12},{9,13},{10,... | collective-permute-start | bytes 3538952 | tf_op jit(solution)/shard_map/ppermute | solution.py:40
  220.8 41.1 %collective-permute-start.74 = (f16[384,768]{1,0:T(8,128)(2,1)}, f16[384,768]{1,0:T(8,128)(2,1)}, u32[]{:S(2)}, u32[]{:S(2)}) collective-permute-start(f16[384,768]{1,0:T(8,128)(2,1)} %get-tuple-element.380), channel_id=1, source_target_pairs={{0,4},{1,8},{2,16},{3,24},{4,0},{5,12},{6,20},{7,28},{8,1},{9,13},... | collective-permute-start | bytes 1769480 | tf_op jit(solution)/shard_map/ppermute | solution.py:40
  221.4 54.5 %collective-permute-start.75 = (f16[384,768]{1,0:T(8,128)(2,1)}, f16[384,768]{1,0:T(8,128)(2,1)}, u32[]{:S(2)}, u32[]{:S(2)}) collective-permute-start(f16[384,768]{1,0:T(8,128)(2,1)} %get-tuple-element.381), channel_id=1, source_target_pairs={{0,8},{1,0},{2,24},{3,16},{4,12},{5,4},{6,28},{7,20},{8,9},{9,1},{... | collective-permute-start | bytes 1769480 | tf_op jit(solution)/shard_map/ppermute | solution.py:40
  227.0 51.7 %collective-permute-start.76 = (f16[384,768]{1,0:T(8,128)(2,1)}, f16[384,768]{1,0:T(8,128)(2,1)}, u32[]{:S(2)}, u32[]{:S(2)}) collective-permute-start(f16[384,768]{1,0:T(8,128)(2,1)} %get-tuple-element.379), channel_id=1, source_target_pairs={{0,16},{1,24},{2,0},{3,8},{4,20},{5,28},{6,4},{7,12},{8,17},{9,25}... | collective-permute-start | bytes 1769480 | tf_op jit(solution)/shard_map/ppermute | solution.py:40
  227.0 54.2 %collective-permute-start.77 = (f16[384,768]{1,0:T(8,128)(2,1)}, f16[384,768]{1,0:T(8,128)(2,1)}, u32[]{:S(2)}, u32[]{:S(2)}) collective-permute-start(f16[384,768]{1,0:T(8,128)(2,1)} %get-tuple-element.378), channel_id=1, source_target_pairs={{0,24},{1,16},{2,8},{3,0},{4,28},{5,20},{6,12},{7,4},{8,25},{9,17}... | collective-permute-start | bytes 1769480 | tf_op jit(solution)/shard_map/ppermute | solution.py:40
  247.9 36.5 %collective-permute-start.80 = (f16[4,384,384]{2,1,0:T(8,128)(2,1)S(1)}, f16[4,384,384]{2,1,0:T(8,128)(2,1)S(1)}, u32[]{:S(2)}, u32[]{:S(2)}) collective-permute-start(f16[4,384,384]{2,1,0:T(8,128)(2,1)S(1)} %pad_maximum_fusion.26), channel_id=1, source_target_pairs={{0,1},{1,0},{2,3},{3,2},{4,5},{5,4},{6,7},{7,6},{8,9},{9,8},{10,11... | collective-permute-start | bytes 3538952 | tf_op jit(solution)/shard_map/ppermute | solution.py:40
  292.5 18.0 %collective-permute-start.87 = (bf16[576,768]{1,0:T(8,128)(2,1)}, bf16[576,768]{1,0:T(8,128)(2,1)}, u32[]{:S(2)}, u32[]{:S(2)}) collective-permute-start(bf16[576,768]{1,0:T(8,128)(2,1)} %pad_maximum_fusion.29), channel_id=1, source_target_pairs={{0,2},{1,3},{2,0},{3,1},{4,6},{5,7},{6,4},{7,5},{8,10},{9,11},{10,... | collective-permute-start | bytes 2654216 | tf_op jit(solution)/shard_map/ppermute | solution.py:40
  312.0 24.0 %collective-permute-start.89 = (bf16[192,768]{1,0:T(8,128)(2,1)S(1)}, bf16[192,768]{1,0:T(8,128)(2,1)S(1)}, u32[]{:S(2)}, u32[]{:S(2)}) collective-permute-start(bf16[192,768]{1,0:T(8,128)(2,1)S(1)} %get-tuple-element.237), channel_id=1, source_target_pairs={{0,16},{1,24},{2,18},{3,26},{4,20},{5,28},{6,22},{7,30},{8,17},{9,... | collective-permute-start | bytes 884744 | tf_op jit(solution)/shard_map/ppermute | solution.py:40
  325.7 28.4 %collective-permute-start.85 = (bf16[2,192,768]{2,1,0:T(8,128)(2,1)S(1)}, bf16[2,192,768]{2,1,0:T(8,128)(2,1)S(1)}, u32[]{:S(2)}, u32[]{:S(2)}) collective-permute-start(bf16[2,192,768]{2,1,0:T(8,128)(2,1)S(1)} %pad_maximum_fusion.34.refs_11_), channel_id=1, source_target_pairs={{0,4},{1,5},{2,6},{3,7},{4,0},{5,1},{6,2},{7,3},{8,12},{9,13},{10,... | collective-permute-start | bytes 1769480 | tf_op jit(solution)/shard_map/ppermute | solution.py:40
  336.0 18.1 %collective-permute-start.94 = (bf16[192,768]{1,0:T(8,128)(2,1)S(1)}, bf16[192,768]{1,0:T(8,128)(2,1)S(1)}, u32[]{:S(2)}, u32[]{:S(2)}) collective-permute-start(bf16[192,768]{1,0:T(8,128)(2,1)S(1)} %get-tuple-element.239), channel_id=1, source_target_pairs={{0,16},{1,24},{2,18},{3,26},{4,20},{5,28},{6,22},{7,30},{8,17},{9,... | collective-permute-start | bytes 884744 | tf_op jit(solution)/shard_map/ppermute | solution.py:40
  336.8 17.4 %collective-permute-start.98 = (bf16[192,768]{1,0:T(8,128)(2,1)S(1)}, bf16[192,768]{1,0:T(8,128)(2,1)S(1)}, u32[]{:S(2)}, u32[]{:S(2)}) collective-permute-start(bf16[192,768]{1,0:T(8,128)(2,1)S(1)} %get-tuple-element.240), channel_id=1, source_target_pairs={{0,2},{1,8},{2,0},{3,10},{4,6},{5,12},{6,4},{7,14},{8,1},{9,11},{1... | collective-permute-start | bytes 884744 | tf_op jit(solution)/shard_map/ppermute | solution.py:40
  336.9 29.7 %collective-permute-start.84 = (bf16[2,192,768]{2,1,0:T(8,128)(2,1)S(1)}, bf16[2,192,768]{2,1,0:T(8,128)(2,1)S(1)}, u32[]{:S(2)}, u32[]{:S(2)}) collective-permute-start(bf16[2,192,768]{2,1,0:T(8,128)(2,1)S(1)} %pad_maximum_fusion.34.refs_11_), channel_id=1, source_target_pairs={{0,1},{1,0},{2,3},{3,2},{4,5},{5,4},{6,7},{7,6},{8,9},{9,8},{10,11... | collective-permute-start | bytes 1769480 | tf_op jit(solution)/shard_map/ppermute | solution.py:40
  337.9 30.0 %collective-permute-start.91 = (bf16[2,192,768]{2,1,0:T(8,128)(2,1)S(1)}, bf16[2,192,768]{2,1,0:T(8,128)(2,1)S(1)}, u32[]{:S(2)}, u32[]{:S(2)}) collective-permute-start(bf16[2,192,768]{2,1,0:T(8,128)(2,1)S(1)} %pad_maximum_fusion.35.refs_15_), channel_id=1, source_target_pairs={{0,4},{1,5},{2,6},{3,7},{4,0},{5,1},{6,2},{7,3},{8,12},{9,13},{10,... | collective-permute-start | bytes 1769480 | tf_op jit(solution)/shard_map/ppermute | solution.py:40
  366.7 17.0 %collective-permute-start.101 = (bf16[2,192,768]{2,1,0:T(8,128)(2,1)S(1)}, bf16[2,192,768]{2,1,0:T(8,128)(2,1)S(1)}, u32[]{:S(2)}, u32[]{:S(2)}) collective-permute-start(bf16[2,192,768]{2,1,0:T(8,128)(2,1)S(1)} %pad_maximum_fusion.37.refs_23_), channel_id=1, source_target_pairs={{0,4},{1,5},{2,6},{3,7},{4,0},{5,1},{6,2},{7,3},{8,12},{9,13},{10,... | collective-permute-start | bytes 1769480 | tf_op jit(solution)/shard_map/ppermute | solution.py:40
  367.9 15.8 %collective-permute-start.95 = (bf16[2,192,768]{2,1,0:T(8,128)(2,1)S(1)}, bf16[2,192,768]{2,1,0:T(8,128)(2,1)S(1)}, u32[]{:S(2)}, u32[]{:S(2)}) collective-permute-start(bf16[2,192,768]{2,1,0:T(8,128)(2,1)S(1)} %pad_maximum_fusion.36.refs_19_), channel_id=1, source_target_pairs={{0,1},{1,0},{2,3},{3,2},{4,5},{5,4},{6,7},{7,6},{8,9},{9,8},{10,11... | collective-permute-start | bytes 1769480 | tf_op jit(solution)/shard_map/ppermute | solution.py:40
  367.9 15.8 %collective-permute-start.92 = (bf16[2,192,768]{2,1,0:T(8,128)(2,1)S(1)}, bf16[2,192,768]{2,1,0:T(8,128)(2,1)S(1)}, u32[]{:S(2)}, u32[]{:S(2)}) collective-permute-start(bf16[2,192,768]{2,1,0:T(8,128)(2,1)S(1)} %collective-permute-done.91.refs_17_), channel_id=1, source_target_pairs={{0,1},{1,0},{2,3},{3,2},{4,5},{5,4},{6,7},{7,6},{8,9},{9,8},{10,11... | collective-permute-start | bytes 1769480 | tf_op jit(solution)/shard_map/ppermute | solution.py:40
  393.3 27.8 %collective-permute-start.107 = (f16[2,768,384]{2,1,0:T(8,128)(2,1)}, f16[2,768,384]{2,1,0:T(8,128)(2,1)}, u32[]{:S(2)}, u32[]{:S(2)}) collective-permute-start(f16[2,768,384]{2,1,0:T(8,128)(2,1)} %convert_element_type.74), channel_id=1, source_target_pairs={{0,2},{1,3},{2,0},{3,1},{4,6},{5,7},{6,4},{7,5},{8,10},{9,11},{10,... | collective-permute-start | bytes 3538952 | tf_op jit(solution)/shard_map/ppermute | solution.py:40
  423.4 26.6 %collective-permute-start.108 = (f16[4,384,384]{2,1,0:T(8,128)(2,1)S(1)}, f16[4,384,384]{2,1,0:T(8,128)(2,1)S(1)}, u32[]{:S(2)}, u32[]{:S(2)}) collective-permute-start(f16[4,384,384]{2,1,0:T(8,128)(2,1)S(1)} %pad_maximum_fusion.27), channel_id=1, source_target_pairs={{0,4},{1,5},{2,6},{3,7},{4,0},{5,1},{6,2},{7,3},{8,12},{9,13},{10,... | collective-permute-start | bytes 3538952 | tf_op jit(solution)/shard_map/ppermute | solution.py:40
  424.3 44.1 %collective-permute-start.103 = (f16[384,768]{1,0:T(8,128)(2,1)S(1)}, f16[384,768]{1,0:T(8,128)(2,1)S(1)}, u32[]{:S(2)}, u32[]{:S(2)}) collective-permute-start(f16[384,768]{1,0:T(8,128)(2,1)S(1)} %get-tuple-element.360), channel_id=1, source_target_pairs={{0,4},{1,8},{2,16},{3,24},{4,0},{5,12},{6,20},{7,28},{8,1},{9,13},... | collective-permute-start | bytes 1769480 | tf_op jit(solution)/shard_map/ppermute | solution.py:40
  434.6 46.6 %collective-permute-start.104 = (f16[384,768]{1,0:T(8,128)(2,1)S(1)}, f16[384,768]{1,0:T(8,128)(2,1)S(1)}, u32[]{:S(2)}, u32[]{:S(2)}) collective-permute-start(f16[384,768]{1,0:T(8,128)(2,1)S(1)} %get-tuple-element.361), channel_id=1, source_target_pairs={{0,8},{1,0},{2,24},{3,16},{4,12},{5,4},{6,28},{7,20},{8,9},{9,1},{... | collective-permute-start | bytes 1769480 | tf_op jit(solution)/shard_map/ppermute | solution.py:40
  434.9 48.0 %collective-permute-start.105 = (f16[384,768]{1,0:T(8,128)(2,1)S(1)}, f16[384,768]{1,0:T(8,128)(2,1)S(1)}, u32[]{:S(2)}, u32[]{:S(2)}) collective-permute-start(f16[384,768]{1,0:T(8,128)(2,1)S(1)} %get-tuple-element.359), channel_id=1, source_target_pairs={{0,16},{1,24},{2,0},{3,8},{4,20},{5,28},{6,4},{7,12},{8,17},{9,25}... | collective-permute-start | bytes 1769480 | tf_op jit(solution)/shard_map/ppermute | solution.py:40
  434.9 54.6 %collective-permute-start.106 = (f16[384,768]{1,0:T(8,128)(2,1)S(1)}, f16[384,768]{1,0:T(8,128)(2,1)S(1)}, u32[]{:S(2)}, u32[]{:S(2)}) collective-permute-start(f16[384,768]{1,0:T(8,128)(2,1)S(1)} %get-tuple-element.358), channel_id=1, source_target_pairs={{0,24},{1,16},{2,8},{3,0},{4,28},{5,20},{6,12},{7,4},{8,25},{9,17}... | collective-permute-start | bytes 1769480 | tf_op jit(solution)/shard_map/ppermute | solution.py:40
  450.6 40.0 %collective-permute-start.109 = (f16[4,384,384]{2,1,0:T(8,128)(2,1)S(1)}, f16[4,384,384]{2,1,0:T(8,128)(2,1)S(1)}, u32[]{:S(2)}, u32[]{:S(2)}) collective-permute-start(f16[4,384,384]{2,1,0:T(8,128)(2,1)S(1)} %pad_maximum_fusion.28), channel_id=1, source_target_pairs={{0,1},{1,0},{2,3},{3,2},{4,5},{5,4},{6,7},{7,6},{8,9},{9,8},{10,11... | collective-permute-start | bytes 3538952 | tf_op jit(solution)/shard_map/ppermute | solution.py:40
  (80 other events, 1333.2 us)

commit v6 on v5

--- a/solution.py
+++ b/solution.py
@@ -130,9 +130,9 @@
         own = [lax.dynamic_slice(source, (first, slot + i, 0), (chunk, 1, tile)) for i in range(count)]
         own = jnp.concatenate([one.reshape(1, chunk, tile) for one in own])
         if number == 0:
-            values = after(coeffs, own)
-            half = values.astype(jnp.bfloat16)
-            extreme = (jnp.maximum(jnp.max(jnp.abs(values)), 1e-30) * 1.01).astype(jnp.bfloat16)
+            half = after(coeffs, own).astype(jnp.bfloat16)
+            extreme = jnp.max(jnp.abs(lax.optimization_barrier(half))).astype(jnp.float32)
+            extreme = (jnp.maximum(extreme, 1e-30) * 1.01).astype(jnp.bfloat16)
             extreme = jnp.full((16, tile), extreme)
         if number == rider:
             for where in (lambda z, x, m, n: (z, x, m, 1 - n), lambda z, x, m, n: (z, (x + 1) % grid.lanes, m, n)):
@@ -206,7 +206,7 @@
     tile = couplings[0].shape[3]
     majors, part, _ = parts[0].shape
     bands, rows = 2 * majors, part * ROW_CHUNKS
-    wanted = (major * 2 + minor) ^ (base + pl.program_id(0))
+    wanted = (major * 2 + minor) ^ (2 * pl.program_id(0) + base)
     tile_row = (wanted * lanes + lane) * rows // tile
 
     @pl.when(pl.program_id(0) == 0)
@@ -259,7 +259,7 @@
 
     def spec(count):
         def block(i, ids, entries, *_):
-            wanted = (ids[2] * 2 + ids[3]) ^ (base + i)
+            wanted = (ids[2] * 2 + ids[3]) ^ (2 * i + base)
             return (entries[ids[0] * bands + wanted], 0, 0, 0)
 
         return pl.BlockSpec((1, count, chunk, tile), block)
@@ -302,45 +302,27 @@
     )
 
 
-def send_direct(grid, sigma, base):
-    return [
-        grid.send(
-            sigma[i],
-            lambda z, x, m, n: ((m * 2 + n) ^ (base + i), x, z // 2, z % 2),
-            lambda z, x, m, n: (z, (x + 1) % grid.lanes, m, n),
-        )
-        for i in range(sigma.shape[0])
-    ]
-
-
 def bring_home(grid, run, ids, band, lane, major, minor):
     bands, lanes, majors = grid.bands, grid.lanes, grid.majors
-    far, far_mirror = run(ids, bands // 2)
-    far, far_mirror = far.astype(jnp.float16), far_mirror.astype(jnp.float16)
-    received_far = send_direct(grid, far, bands // 2)
-    entries = grid.send(far_mirror, lambda z, x, m, n: (z, x, m ^ (majors // 2), n))
-    near, near_mirror = run(after(ids, far, far_mirror), 0)
-    near, near_mirror = near.astype(jnp.float16), near_mirror.astype(jnp.float16)
-    received = send_direct(grid, near, 0) + received_far
-
-    entries = [near_mirror[i] for i in range(bands // 2)] + [entries[i] for i in range(bands // 2)]
-    for bit in bits(majors)[1:]:
-        moved = [j for j in range(bands) if j // 2 & bit]
-        brought = grid.send(jnp.stack([entries[j] for j in moved]), lambda z, x, m, n: (z, x, m ^ bit, n))
-        for i, j in enumerate(moved):
-            entries[j] = brought[i]
-    strip, part = entries[0].shape
-    share = strip // lanes
-    table = {}
-    for turn in range(lanes):
-        turned = [lax.dynamic_slice_in_dim(entry, (lane ^ turn) * share, share, 0) for entry in entries]
-        turned = grid.send(jnp.stack(turned), lambda z, x, m, n: (z, x ^ turn, m, n))
-        for j in range(bands):
-            table[j, turn] = turned[j]
-    moved = [(j, turn) for j in range(1, bands, 2) for turn in range(lanes)]
-    brought = grid.send(jnp.stack([table[key] for key in moved]), lambda z, x, m, n: (z, x, m, 1 - n))
-    for i, key in enumerate(moved):
-        table[key] = brought[i]
+    received, table, gate = [None] * bands, {}, []
+    for base in range(2):
+        sigma, mirrored = run(after(ids, gate), base)
+        sigma, mirrored = sigma.astype(jnp.float16), mirrored.astype(jnp.float16)
+        gate = [sigma, mirrored]
+        if base:
+            sigma, mirrored = after((sigma, mirrored), received[0::2])
+        strip, part = mirrored.shape[1:]
+        share = strip // lanes
+        for i in range(majors):
+            key = 2 * i + base
+            received[key] = grid.send(
+                sigma[i],
+                lambda z, x, m, n: ((m * 2 + n) ^ key, x, z // 2, z % 2),
+                lambda z, x, m, n: (z, (x + 1) % lanes, m, n),
+            )
+            for turn in range(lanes):
+                piece = lax.dynamic_slice_in_dim(mirrored[i], (lane ^ turn) * share, share, 0)
+                table[key, turn] = grid.send(piece, lambda z, x, m, n: (z, x ^ turn, m ^ i, n ^ base))
 
     rows = 2 * part
     direct = jnp.zeros((rows, lanes * rows), jnp.float16)
@@ -387,7 +369,7 @@
         largest = largest * (1 + 2 * growth / DENOMINATOR_MIN)
         if step_index:
             half = current.astype(jnp.bfloat16)
-            parts = to_columns(grid, half, band, lane, major, minor, [], [1, ROW_CHUNKS - 1], False)
+            parts = to_columns(grid, half, band, lane, major, minor, [], [ROW_CHUNKS // 2] * 2, False)
 
         def run(ids, base):
             return products(grid, couplings, parts, ids, entries, tile_cols, tile_count, scale, base)

time: 507 us -> 478 us (0.943)
  waiting for transfers between devices: 269 us -> 246 us
  other arithmetic: 58.3 us -> 52.6 us
    ppermute x62 -> x70, waiting for transfers between devices: 246 us -> 223 us  [send(): received = lax.ppermute(value, AXES, pairs)]
    ppermute x62 -> x70, starting transfers between devices: 73.3 us -> 72.3 us  [send(): received = lax.ppermute(value, AXES, pairs)]
  transfers between devices with their start and end apart: 71 -> 79, of which waited for: 30 -> 29; matrix products, arithmetic and copies ran while one was open for 13% -> 13% of each run, Pallas kernels for 3% -> 3%
where the time goes in v6:
time: 478 us; the launch traced here: 469 us
  waiting for transfers between devices  246 us (51%)
  starting transfers between devices  93.1 us (19%)
  other arithmetic  52.6 us (11%)
  local copies, waits for them, and re-layouts  39.9 us (8%)
  Pallas kernels  33 us (7%)
    ppermute x70, waiting for transfers between devices, send(): received = lax.ppermute(value, AXES, pairs)  223 us
    ppermute x70, starting transfers between devices, send(): received = lax.ppermute(value, AXES, pairs)  72.3 us
    pallas_call x4, Pallas kernels, products(): pl.pallas_call(lambda *refs: product_kernel(groups, pieces, lanes, base,...  33 us
    ppermute x9, waiting for transfers between devices, gather_bands(): moving = lax.ppermute(moving, AXES, pairs)  22.5 us
    ppermute x9, starting transfers between devices, gather_bands(): moving = lax.ppermute(moving, AXES, pairs)  20.8 us
  transfers between devices with their start and end apart: 79, of which 29 were waited for; matrix products, arithmetic and copies ran while one was open for 13% of the time, Pallas kernels for 3%

profile of v6, /device:TPU:25, one launch (start us, length us, event | category | flops | bytes accessed | tf_op | source)
XLA Modules:
  0.0 469.1 jit_solution(362930123346736980)
XLA Ops:
  3.8 166.8 %conditional.2 = (bf16[4,1,192,768]{3,2,1,0:T(8,128)(2,1)S(1)}, bf16[4,1,192,768]{3,2,1,0:T(8,128)(2,1)}, bf16[4,1,208,768]{3,2,1,0:T(8,128)(2,1)}, bf16[4,1,208...) conditional(s32[]{:T(128)} %convert_element_type.71, ...), branch_computations={%region_2.6_spmd, %region_6.12_spmd} | conditional | flops 26185744 | bytes 215436768
  4.0 5.1 %copy.32 = bf16[768,4,768]{2,0,1:T(8,128)(2,1)} copy(bf16[768,4,768]{2,1,0:T(4,128)(2,1)} %get-tuple-element.296) | data formatting | bytes 9437184 | tf_op jit(solution)/shard_map
  10.4 2.6 convert_element_type.51
  29.6 2.2 collective-permute-done.45
  35.1 4.8 %collective-permute-start.41 = (bf16[2,1,192,768]{3,2,1,0:T(8,128)(2,1)}, bf16[2,1,192,768]{3,2,1,0:T(8,128)(2,1)S(1)}, u32[]{:S(2)}, u32[]{:S(2)}) collective-permute-start(bf16[2,1,192,768]{3,2,1,0:T(8,128)(2,1)} %collective-permute-done.40), channel_id=1, source_target_pairs={{0,8},{1,9},{2,10},{3,11},{4,12},{5,13},{6,14},{7,15},{8,0},{9,1},... | collective-permute-start | bytes 1769480 | tf_op jit(solution)/shard_map/cond/branch_1_fun/ppermute | solution.py:95
  39.9 7.7 %collective-permute-done.53 = bf16[768,768]{1,0:T(8,128)(2,1)} collective-permute-done((bf16[768,768]{1,0:T(8,128)(2,1)}, bf16[768,768]{1,0:T(8,128)(2,1)}, u32[]{:S(2)}, u32[]{:S(2)}) %collective-permute-start.53) | collective-permute-done | bytes 1179680 | tf_op jit(solution)/shard_map/cond/branch_1_fun/ppermute | solution.py:40
  49.4 4.0 collective-permute-start.47
  54.2 2.5 collective-permute-start.50
  56.7 5.8 %collective-permute-done.41 = bf16[2,1,192,768]{3,2,1,0:T(8,128)(2,1)S(1)} collective-permute-done((bf16[2,1,192,768]{3,2,1,0:T(8,128)(2,1)}, bf16[2,1,192,768]{3,2,1,0:T(8,128)(2,1)S(1)}, u32[]{:S(2)}, u32[]{:S(2)}) %collective-permute-start.41) | collective-permute-done | bytes 589856 | tf_op jit(solution)/shard_map/cond/branch_1_fun/ppermute | solution.py:95
  64.9 14.4 %collective-permute-done.47 = bf16[2,1,208,768]{3,2,1,0:T(8,128)(2,1)S(1)} collective-permute-done((bf16[2,1,208,768]{3,2,1,0:T(8,128)(2,1)S(1)}, bf16[2,1,208,768]{3,2,1,0:T(8,128)(2,1)S(1)}, u32[]{:S(2)}, u32[]{:S(2)}) %collective-permute-start.47) | collective-permute-done | bytes 639008 | tf_op jit(solution)/shard_map/cond/branch_1_fun/ppermute | solution.py:95
  85.5 4.8 %collective-permute-start.51 = (bf16[1,2,192,768]{3,2,1,0:T(8,128)(2,1)S(1)}, bf16[1,2,192,768]{3,2,1,0:T(8,128)(2,1)S(1)}, u32[]{:S(2)}, u32[]{:S(2)}) collective-permute-start(bf16[1,2,192,768]{3,2,1,0:T(8,128)(2,1)S(1)} %collective-permute-done.50), channel_id=1, source_target_pairs={{0,8},{1,9},{2,10},{3,11},{4,12},{5,13},{6,14},{7,15},{8,0},{9,1},... | collective-permute-start | bytes 1769480 | tf_op jit(solution)/shard_map/cond/branch_1_fun/ppermute | solution.py:95
  92.9 7.1 %collective-permute-done.60 = bf16[192,768]{1,0:T(8,128)(2,1)S(1)} collective-permute-done((bf16[192,768]{1,0:T(8,128)(2,1)S(1)}, bf16[192,768]{1,0:T(8,128)(2,1)S(1)}, u32[]{:S(2)}, u32[]{:S(2)}) %collective-permute-start.60) | collective-permute-done | bytes 294944 | tf_op jit(solution)/shard_map/cond/branch_1_fun/ppermute | solution.py:40
  100.1 2.2 collective-permute-start.65
  103.0 14.0 %collective-permute-done.48 = bf16[4,1,208,768]{3,2,1,0:T(8,128)(2,1)S(1)} collective-permute-done((bf16[4,1,208,768]{3,2,1,0:T(8,128)(2,1)S(1)}, bf16[4,1,208,768]{3,2,1,0:T(8,128)(2,1)S(1)}, u32[]{:S(2)}, u32[]{:S(2)}) %collective-permute-start.48) | collective-permute-done | bytes 1277984 | tf_op jit(solution)/shard_map/cond/branch_1_fun/ppermute | solution.py:40
  121.5 7.9 %collective-permute-start.61 = (bf16[2,192,768]{2,1,0:T(8,128)(2,1)S(1)}, bf16[2,192,768]{2,1,0:T(8,128)(2,1)S(1)}, u32[]{:S(2)}, u32[]{:S(2)}) collective-permute-start(bf16[2,192,768]{2,1,0:T(8,128)(2,1)S(1)} %pad_maximum_fusion.21), channel_id=1, source_target_pairs={{0,1},{1,0},{2,3},{3,2},{4,5},{5,4},{6,7},{7,6},{8,9},{9,8},{10,11... | collective-permute-start | bytes 1769480 | tf_op jit(solution)/shard_map/cond/branch_1_fun/ppermute | solution.py:40
  129.4 6.2 %collective-permute-done.69 = bf16[192,768]{1,0:T(8,128)(2,1)S(1)} collective-permute-done((bf16[192,768]{1,0:T(8,128)(2,1)S(1)}, bf16[192,768]{1,0:T(8,128)(2,1)S(1)}, u32[]{:S(2)}, u32[]{:S(2)}) %collective-permute-start.69) | collective-permute-done | bytes 294944 | tf_op jit(solution)/shard_map/cond/branch_1_fun/ppermute | solution.py:40
  140.5 10.4 %collective-permute-done.52 = bf16[1,2,192,768]{3,2,1,0:T(8,128)(2,1)S(1)} collective-permute-done((bf16[1,2,192,768]{3,2,1,0:T(8,128)(2,1)S(1)}, bf16[1,2,192,768]{3,2,1,0:T(8,128)(2,1)S(1)}, u32[]{:S(2)}, u32[]{:S(2)}) %collective-permute-start.52) | collective-permute-done | bytes 589856 | tf_op jit(solution)/shard_map/cond/branch_1_fun/ppermute | solution.py:40
  152.2 2.8 collective-permute-start.68
  155.0 9.7 %collective-permute-done.72 = bf16[2,192,768]{2,1,0:T(8,128)(2,1)} collective-permute-done((bf16[2,192,768]{2,1,0:T(8,128)(2,1)}, bf16[2,192,768]{2,1,0:T(8,128)(2,1)}, u32[]{:S(2)}, u32[]{:S(2)}) %collective-permute-start.72) | collective-permute-done | bytes 589856 | tf_op jit(solution)/shard_map/cond/branch_1_fun/ppermute | solution.py:40
  172.8 9.6 %shard_map.253 = (f32[2,384,768]{2,1,0:T(8,128)S(1)}, f32[2,768,384]{2,1,0:T(8,128)S(1)}) custom-call(s32[4]{0:T(128)S(1)} %pad_add_fusion.refs_0_, s32[16]{0:T(128)S(1)} %copy-done.2, s32[32]{0:T(128)S(1)} %reshape.105.refs_2_, s32[8]{0:T(128)S(1)} %copy-done, f32[1]{0:T(128)} %get-tuple-element.210.refs_4_, ...), custom_call_target="tpu_custom_call" | custom-call | flops 3623878656 | bytes 14155776 | tf_op jit(solution)/shard_map/pallas_call | solution.py:268
  188.2 3.0 collective-permute-start.82
  192.2 9.0 %shard_map.254 = (f32[2,384,768]{2,1,0:T(8,128)S(1)}, f32[2,768,384]{2,1,0:T(8,128)S(1)}) custom-call(s32[4]{0:T(128)S(1)} %pad_add_fusion.refs_0_, s32[16]{0:T(128)S(1)} %copy-done.2, s32[32]{0:T(128)S(1)} %reshape.105.refs_2_, s32[8]{0:T(128)S(1)} %copy-done, f32[1]{0:T(128)} %get-tuple-element.210.refs_4_, ...), custom_call_target="tpu_custom_call" | custom-call | flops 3623878656 | bytes 14155776 | tf_op jit(solution)/shard_map/pallas_call | solution.py:268
  202.6 2.8 convert_element_type.74
  208.1 8.5 %collective-permute-done.78 = f16[384,384]{1,0:T(8,128)(2,1)} collective-permute-done((f16[384,384]{1,0:T(8,128)(2,1)}, f16[384,384]{1,0:T(8,128)(2,1)}, u32[]{:S(2)}, u32[]{:S(2)}) %collective-permute-start.78) | collective-permute-done | bytes 294944 | tf_op jit(solution)/shard_map/ppermute | solution.py:40
  222.9 3.1 collective-permute-start.77
  226.0 2.9 collective-permute-start.76
  231.8 7.8 %collective-permute-done.84 = f16[384,384]{1,0:T(8,128)(2,1)S(1)} collective-permute-done((f16[384,384]{1,0:T(8,128)(2,1)S(1)}, f16[384,384]{1,0:T(8,128)(2,1)S(1)}, u32[]{:S(2)}, u32[]{:S(2)}) %collective-permute-start.84) | collective-permute-done | bytes 294944 | tf_op jit(solution)/shard_map/ppermute | solution.py:40
  239.6 5.6 %collective-permute-done.83 = f16[384,384]{1,0:T(8,128)(2,1)S(1)} collective-permute-done((f16[384,384]{1,0:T(8,128)(2,1)S(1)}, f16[384,384]{1,0:T(8,128)(2,1)S(1)}, u32[]{:S(2)}, u32[]{:S(2)}) %collective-permute-start.83) | collective-permute-done | bytes 294944 | tf_op jit(solution)/shard_map/ppermute | solution.py:40
  245.5 14.6 %collective-permute-done.76 = f16[384,768]{1,0:T(8,128)(2,1)S(1)} collective-permute-done((f16[384,768]{1,0:T(8,128)(2,1)S(1)}, f16[384,768]{1,0:T(8,128)(2,1)S(1)}, u32[]{:S(2)}, u32[]{:S(2)}) %collective-permute-start.76) | collective-permute-done | bytes 589856 | tf_op jit(solution)/shard_map/ppermute | solution.py:40
  271.4 7.5 %collective-permute-done.85 = bf16[384,768]{1,0:T(8,128)(2,1)} collective-permute-done((bf16[384,768]{1,0:T(8,128)(2,1)}, bf16[384,768]{1,0:T(8,128)(2,1)}, u32[]{:S(2)}, u32[]{:S(2)}) %collective-permute-start.85) | collective-permute-done | bytes 589856 | tf_op jit(solution)/shard_map/ppermute | solution.py:40
  283.1 5.5 %collective-permute-done.86 = bf16[192,768]{1,0:T(8,128)(2,1)S(1)} collective-permute-done((bf16[192,768]{1,0:T(8,128)(2,1)S(1)}, bf16[192,768]{1,0:T(8,128)(2,1)S(1)}, u32[]{:S(2)}, u32[]{:S(2)}) %collective-permute-start.86) | collective-permute-done | bytes 294944 | tf_op jit(solution)/shard_map/ppermute | solution.py:40
  289.6 9.4 %collective-permute-start.92 = (bf16[192,768]{1,0:T(8,128)(2,1)S(1)}, bf16[192,768]{1,0:T(8,128)(2,1)S(1)}, u32[]{:S(2)}, u32[]{:S(2)}) collective-permute-start(bf16[192,768]{1,0:T(8,128)(2,1)S(1)} %get-tuple-element.243), channel_id=1, source_target_pairs={{0,16},{1,24},{2,18},{3,26},{4,20},{5,28},{6,22},{7,30},{8,17},{9,... | collective-permute-start | bytes 884744 | tf_op jit(solution)/shard_map/ppermute | solution.py:40
  300.0 15.5 %collective-permute-done.92 = bf16[192,768]{1,0:T(8,128)(2,1)S(1)} collective-permute-done((bf16[192,768]{1,0:T(8,128)(2,1)S(1)}, bf16[192,768]{1,0:T(8,128)(2,1)S(1)}, u32[]{:S(2)}, u32[]{:S(2)}) %collective-permute-start.92) | collective-permute-done | bytes 294944 | tf_op jit(solution)/shard_map/ppermute | solution.py:40
  317.6 2.2 collective-permute-start.88
  320.4 11.0 %collective-permute-done.98 = bf16[192,768]{1,0:T(8,128)(2,1)S(1)} collective-permute-done((bf16[192,768]{1,0:T(8,128)(2,1)S(1)}, bf16[192,768]{1,0:T(8,128)(2,1)S(1)}, u32[]{:S(2)}, u32[]{:S(2)}) %collective-permute-start.98) | collective-permute-done | bytes 294944 | tf_op jit(solution)/shard_map/ppermute | solution.py:40
  332.2 11.5 %collective-permute-done.103 = bf16[192,768]{1,0:T(8,128)(2,1)S(1)} collective-permute-done((bf16[192,768]{1,0:T(8,128)(2,1)S(1)}, bf16[192,768]{1,0:T(8,128)(2,1)S(1)}, u32[]{:S(2)}, u32[]{:S(2)}) %collective-permute-start.103) | collective-permute-done | bytes 294944 | tf_op jit(solution)/shard_map/ppermute | solution.py:40
  346.1 12.9 %collective-permute-done.100.refs_21_ = bf16[2,192,768]{2,1,0:T(8,128)(2,1)S(1)} collective-permute-done((bf16[2,192,768]{2,1,0:T(8,128)(2,1)S(1)}, bf16[2,192,768]{2,1,0:T(8,128)(2,1)S(1)}, u32[]{:S(2)}, u32[]{:S(2)}) %collective-permute-start.100) | collective-permute-done | bytes 589856 | tf_op jit(solution)/shard_map/ppermute | solution.py:40
  359.6 10.6 %collective-permute-done.105.refs_25_ = bf16[2,192,768]{2,1,0:T(8,128)(2,1)S(1)} collective-permute-done((bf16[2,192,768]{2,1,0:T(8,128)(2,1)S(1)}, bf16[2,192,768]{2,1,0:T(8,128)(2,1)S(1)}, u32[]{:S(2)}, u32[]{:S(2)}) %collective-permute-start.105) | collective-permute-done | bytes 589856 | tf_op jit(solution)/shard_map/ppermute | solution.py:40
  372.2 7.6 %shard_map.255 = (f32[2,384,768]{2,1,0:T(8,128)S(1)}, f32[2,768,384]{2,1,0:T(8,128)S(1)}) custom-call(s32[4]{0:T(128)S(1)} %pad_add_fusion.refs_0_, s32[16]{0:T(128)S(1)} %copy-done.2, s32[32]{0:T(128)S(1)} %reshape.105.refs_2_, s32[8]{0:T(128)S(1)} %copy-done, f32[1]{0:T(128)} %get-tuple-element.241.refs_4_, ...), custom_call_target="tpu_custom_call" | custom-call | flops 3623878656 | bytes 14155776 | tf_op jit(solution)/shard_map/pallas_call | solution.py:268
  381.8 3.2 collective-permute-start.107
  389.3 6.8 %shard_map.256 = (f32[2,384,768]{2,1,0:T(8,128)S(1)}, f32[2,768,384]{2,1,0:T(8,128)S(1)}) custom-call(s32[4]{0:T(128)S(1)} %pad_add_fusion.refs_0_, s32[16]{0:T(128)S(1)} %copy-done.2, s32[32]{0:T(128)S(1)} %reshape.105.refs_2_, s32[8]{0:T(128)S(1)} %copy-done, f32[1]{0:T(128)} %get-tuple-element.241.refs_4_, ...), custom_call_target="tpu_custom_call" | custom-call | flops 3623878656 | bytes 14155776 | tf_op jit(solution)/shard_map/pallas_call | solution.py:268
  397.3 16.1 %collective-permute-done.111 = f16[384,384]{1,0:T(8,128)(2,1)} collective-permute-done((f16[384,384]{1,0:T(8,128)(2,1)}, f16[384,384]{1,0:T(8,128)(2,1)}, u32[]{:S(2)}, u32[]{:S(2)}) %collective-permute-start.111) | collective-permute-done | bytes 294944 | tf_op jit(solution)/shard_map/ppermute | solution.py:40
  417.7 8.0 %collective-permute-done.108 = f16[384,768]{1,0:T(8,128)(2,1)S(1)} collective-permute-done((f16[384,768]{1,0:T(8,128)(2,1)S(1)}, f16[384,768]{1,0:T(8,128)(2,1)S(1)}, u32[]{:S(2)}, u32[]{:S(2)}) %collective-permute-start.108) | collective-permute-done | bytes 589856 | tf_op jit(solution)/shard_map/ppermute | solution.py:40
  427.0 2.4 collective-permute-start.110
  433.6 8.3 %collective-permute-done.117 = f16[384,384]{1,0:T(8,128)(2,1)S(1)} collective-permute-done((f16[384,384]{1,0:T(8,128)(2,1)S(1)}, f16[384,384]{1,0:T(8,128)(2,1)S(1)}, u32[]{:S(2)}, u32[]{:S(2)}) %collective-permute-start.117) | collective-permute-done | bytes 294944 | tf_op jit(solution)/shard_map/ppermute | solution.py:40
  442.0 9.3 %collective-permute-done.116 = f16[384,384]{1,0:T(8,128)(2,1)S(1)} collective-permute-done((f16[384,384]{1,0:T(8,128)(2,1)S(1)}, f16[384,384]{1,0:T(8,128)(2,1)S(1)}, u32[]{:S(2)}, u32[]{:S(2)}) %collective-permute-start.116) | collective-permute-done | bytes 294944 | tf_op jit(solution)/shard_map/ppermute | solution.py:40
  451.6 10.5 %collective-permute-done.109 = f16[384,768]{1,0:T(8,128)(2,1)S(1)} collective-permute-done((f16[384,768]{1,0:T(8,128)(2,1)S(1)}, f16[384,768]{1,0:T(8,128)(2,1)S(1)}, u32[]{:S(2)}, u32[]{:S(2)}) %collective-permute-start.109) | collective-permute-done | bytes 589856 | tf_op jit(solution)/shard_map/ppermute | solution.py:40
  465.0 3.9 divide_subtract_fusion
  (370 shorter events, 121.1 us)
Async XLA Ops:
  20.4 27.2 %collective-permute-start.53 = (bf16[768,768]{1,0:T(8,128)(2,1)}, bf16[768,768]{1,0:T(8,128)(2,1)}, u32[]{:S(2)}, u32[]{:S(2)}) collective-permute-start(bf16[768,768]{1,0:T(8,128)(2,1)} %pad_maximum_fusion.17), channel_id=1, source_target_pairs={{0,2},{1,3},{2,0},{3,1},{4,6},{5,7},{6,4},{7,5},{8,10},{9,11},{10,... | collective-permute-start | bytes 3538952 | tf_op jit(solution)/shard_map/cond/branch_1_fun/ppermute | solution.py:40
  31.9 17.5 %collective-permute-start.46 = (bf16[2,1,208,768]{3,2,1,0:T(8,128)(2,1)S(1)}, bf16[2,1,208,768]{3,2,1,0:T(8,128)(2,1)S(1)}, u32[]{:S(2)}, u32[]{:S(2)}) collective-permute-start(bf16[2,1,208,768]{3,2,1,0:T(8,128)(2,1)S(1)} %pad_maximum_fusion.18), channel_id=1, source_target_pairs={{0,1},{1,0},{2,3},{3,2},{4,5},{5,4},{6,7},{7,6},{8,16},{9,17},{10,... | collective-permute-start | bytes 1916936 | tf_op jit(solution)/shard_map/cond/branch_1_fun/ppermute | solution.py:95
  34.9 18.6 %collective-permute-start.49 = (bf16[1,2,192,768]{3,2,1,0:T(8,128)(2,1)S(1)}, bf16[1,2,192,768]{3,2,1,0:T(8,128)(2,1)S(1)}, u32[]{:S(2)}, u32[]{:S(2)}) collective-permute-start(bf16[1,2,192,768]{3,2,1,0:T(8,128)(2,1)S(1)} %maximum_bitcast_fusion.2), channel_id=1, source_target_pairs={{0,8},{1,9},{2,10},{3,11},{4,12},{5,13},{6,14},{7,15},{8,0},{9,1},... | collective-permute-start | bytes 1769480 | tf_op jit(solution)/shard_map/cond/branch_1_fun/ppermute | solution.py:95
  35.1 27.4 %collective-permute-start.41 = (bf16[2,1,192,768]{3,2,1,0:T(8,128)(2,1)}, bf16[2,1,192,768]{3,2,1,0:T(8,128)(2,1)S(1)}, u32[]{:S(2)}, u32[]{:S(2)}) collective-permute-start(bf16[2,1,192,768]{3,2,1,0:T(8,128)(2,1)} %collective-permute-done.40), channel_id=1, source_target_pairs={{0,8},{1,9},{2,10},{3,11},{4,12},{5,13},{6,14},{7,15},{8,0},{9,1},... | collective-permute-start | bytes 1769480 | tf_op jit(solution)/shard_map/cond/branch_1_fun/ppermute | solution.py:95
  49.4 29.9 %collective-permute-start.47 = (bf16[2,1,208,768]{3,2,1,0:T(8,128)(2,1)S(1)}, bf16[2,1,208,768]{3,2,1,0:T(8,128)(2,1)S(1)}, u32[]{:S(2)}, u32[]{:S(2)}) collective-permute-start(bf16[2,1,208,768]{3,2,1,0:T(8,128)(2,1)S(1)} %collective-permute-done.46), channel_id=1, source_target_pairs={{0,8},{1,9},{2,10},{3,11},{4,12},{5,13},{6,14},{7,15},{8,0},{9,1},... | collective-permute-start | bytes 1916936 | tf_op jit(solution)/shard_map/cond/branch_1_fun/ppermute | solution.py:95
  54.2 31.2 %collective-permute-start.50 = (bf16[1,2,192,768]{3,2,1,0:T(8,128)(2,1)S(1)}, bf16[1,2,192,768]{3,2,1,0:T(8,128)(2,1)S(1)}, u32[]{:S(2)}, u32[]{:S(2)}) collective-permute-start(bf16[1,2,192,768]{3,2,1,0:T(8,128)(2,1)S(1)} %broadcast_select_fusion.8), channel_id=1, source_target_pairs={{0,1},{1,0},{2,3},{3,2},{4,5},{5,4},{6,7},{7,6},{8,16},{9,17},{10,... | collective-permute-start | bytes 1769480 | tf_op jit(solution)/shard_map/cond/branch_1_fun/ppermute | solution.py:95
  63.3 27.7 %collective-permute-start.42 = (bf16[4,1,192,768]{3,2,1,0:T(8,128)(2,1)S(1)}, bf16[4,1,192,768]{3,2,1,0:T(8,128)(2,1)S(1)}, u32[]{:S(2)}, u32[]{:S(2)}) collective-permute-start(bf16[4,1,192,768]{3,2,1,0:T(8,128)(2,1)S(1)} %pad_maximum_fusion.16), channel_id=1, source_target_pairs={{0,2},{1,3},{2,0},{3,1},{4,6},{5,7},{6,4},{7,5},{8,10},{9,11},{10,... | collective-permute-start | bytes 3538952 | tf_op jit(solution)/shard_map/cond/branch_1_fun/ppermute | solution.py:40
  63.7 17.0 %collective-permute-start.54 = (bf16[192,768]{1,0:T(8,128)(2,1)S(1)}, bf16[192,768]{1,0:T(8,128)(2,1)S(1)}, u32[]{:S(2)}, u32[]{:S(2)}) collective-permute-start(bf16[192,768]{1,0:T(8,128)(2,1)S(1)} %get-tuple-element.153), channel_id=1, source_target_pairs={{0,4},{1,8},{2,6},{3,10},{4,0},{5,12},{6,2},{7,14},{8,1},{9,13},{1... | collective-permute-start | bytes 884744 | tf_op jit(solution)/shard_map/cond/branch_1_fun/ppermute | solution.py:40
  64.9 20.4 %collective-permute-start.55 = (bf16[192,768]{1,0:T(8,128)(2,1)S(1)}, bf16[192,768]{1,0:T(8,128)(2,1)S(1)}, u32[]{:S(2)}, u32[]{:S(2)}) collective-permute-start(bf16[192,768]{1,0:T(8,128)(2,1)S(1)} %get-tuple-element.154), channel_id=1, source_target_pairs={{0,16},{1,24},{2,18},{3,26},{4,20},{5,28},{6,22},{7,30},{8,17},{9,... | collective-permute-start | bytes 884744 | tf_op jit(solution)/shard_map/cond/branch_1_fun/ppermute | solution.py:40
  80.3 36.7 %collective-permute-start.48 = (bf16[4,1,208,768]{3,2,1,0:T(8,128)(2,1)S(1)}, bf16[4,1,208,768]{3,2,1,0:T(8,128)(2,1)S(1)}, u32[]{:S(2)}, u32[]{:S(2)}) collective-permute-start(bf16[4,1,208,768]{3,2,1,0:T(8,128)(2,1)S(1)} %pad_maximum_fusion.15), channel_id=1, source_target_pairs={{0,2},{1,3},{2,0},{3,1},{4,6},{5,7},{6,4},{7,5},{8,10},{9,11},{10,... | collective-permute-start | bytes 3833864 | tf_op jit(solution)/shard_map/cond/branch_1_fun/ppermute | solution.py:40
  85.5 31.9 %collective-permute-start.51 = (bf16[1,2,192,768]{3,2,1,0:T(8,128)(2,1)S(1)}, bf16[1,2,192,768]{3,2,1,0:T(8,128)(2,1)S(1)}, u32[]{:S(2)}, u32[]{:S(2)}) collective-permute-start(bf16[1,2,192,768]{3,2,1,0:T(8,128)(2,1)S(1)} %collective-permute-done.50), channel_id=1, source_target_pairs={{0,8},{1,9},{2,10},{3,11},{4,12},{5,13},{6,14},{7,15},{8,0},{9,1},... | collective-permute-start | bytes 1769480 | tf_op jit(solution)/shard_map/cond/branch_1_fun/ppermute | solution.py:95
  92.8 28.7 %collective-permute-start.57 = (bf16[2,192,768]{2,1,0:T(8,128)(2,1)S(1)}, bf16[2,192,768]{2,1,0:T(8,128)(2,1)S(1)}, u32[]{:S(2)}, u32[]{:S(2)}) collective-permute-start(bf16[2,192,768]{2,1,0:T(8,128)(2,1)S(1)} %pad_maximum_fusion.20), channel_id=1, source_target_pairs={{0,4},{1,5},{2,6},{3,7},{4,0},{5,1},{6,2},{7,3},{8,12},{9,13},{10,... | collective-permute-start | bytes 1769480 | tf_op jit(solution)/shard_map/cond/branch_1_fun/ppermute | solution.py:40
  100.0 37.6 %collective-permute-start.56 = (bf16[2,192,768]{2,1,0:T(8,128)(2,1)S(1)}, bf16[2,192,768]{2,1,0:T(8,128)(2,1)S(1)}, u32[]{:S(2)}, u32[]{:S(2)}) collective-permute-start(bf16[2,192,768]{2,1,0:T(8,128)(2,1)S(1)} %pad_maximum_fusion.20), channel_id=1, source_target_pairs={{0,1},{1,0},{2,3},{3,2},{4,5},{5,4},{6,7},{7,6},{8,9},{9,8},{10,11... | collective-permute-start | bytes 1769480 | tf_op jit(solution)/shard_map/cond/branch_1_fun/ppermute | solution.py:40
  100.1 20.4 %collective-permute-start.65 = (bf16[192,768]{1,0:T(8,128)(2,1)S(1)}, bf16[192,768]{1,0:T(8,128)(2,1)S(1)}, u32[]{:S(2)}, u32[]{:S(2)}) collective-permute-start(bf16[192,768]{1,0:T(8,128)(2,1)S(1)} %get-tuple-element.160), channel_id=1, source_target_pairs={{0,16},{1,24},{2,18},{3,26},{4,20},{5,28},{6,22},{7,30},{8,17},{9,... | collective-permute-start | bytes 884744 | tf_op jit(solution)/shard_map/cond/branch_1_fun/ppermute | solution.py:40
  117.0 21.8 %collective-permute-start.62 = (bf16[2,192,768]{2,1,0:T(8,128)(2,1)S(1)}, bf16[2,192,768]{2,1,0:T(8,128)(2,1)}, u32[]{:S(2)}, u32[]{:S(2)}) collective-permute-start(bf16[2,192,768]{2,1,0:T(8,128)(2,1)S(1)} %pad_maximum_fusion.21), channel_id=1, source_target_pairs={{0,4},{1,5},{2,6},{3,7},{4,0},{5,1},{6,2},{7,3},{8,12},{9,13},{10,... | collective-permute-start | bytes 1769480 | tf_op jit(solution)/shard_map/cond/branch_1_fun/ppermute | solution.py:40
  117.3 18.3 %collective-permute-start.69 = (bf16[192,768]{1,0:T(8,128)(2,1)S(1)}, bf16[192,768]{1,0:T(8,128)(2,1)S(1)}, u32[]{:S(2)}, u32[]{:S(2)}) collective-permute-start(bf16[192,768]{1,0:T(8,128)(2,1)S(1)} %get-tuple-element.162), channel_id=1, source_target_pairs={{0,4},{1,8},{2,6},{3,10},{4,0},{5,12},{6,2},{7,14},{8,1},{9,13},{1... | collective-permute-start | bytes 884744 | tf_op jit(solution)/shard_map/cond/branch_1_fun/ppermute | solution.py:40
  120.5 15.8 %collective-permute-start.70 = (bf16[192,768]{1,0:T(8,128)(2,1)S(1)}, bf16[192,768]{1,0:T(8,128)(2,1)S(1)}, u32[]{:S(2)}, u32[]{:S(2)}) collective-permute-start(bf16[192,768]{1,0:T(8,128)(2,1)S(1)} %get-tuple-element.163), channel_id=1, source_target_pairs={{0,16},{1,24},{2,18},{3,26},{4,20},{5,28},{6,22},{7,30},{8,17},{9,... | collective-permute-start | bytes 884744 | tf_op jit(solution)/shard_map/cond/branch_1_fun/ppermute | solution.py:40
  121.5 17.6 %collective-permute-start.61 = (bf16[2,192,768]{2,1,0:T(8,128)(2,1)S(1)}, bf16[2,192,768]{2,1,0:T(8,128)(2,1)S(1)}, u32[]{:S(2)}, u32[]{:S(2)}) collective-permute-start(bf16[2,192,768]{2,1,0:T(8,128)(2,1)S(1)} %pad_maximum_fusion.21), channel_id=1, source_target_pairs={{0,1},{1,0},{2,3},{3,2},{4,5},{5,4},{6,7},{7,6},{8,9},{9,8},{10,11... | collective-permute-start | bytes 1769480 | tf_op jit(solution)/shard_map/cond/branch_1_fun/ppermute | solution.py:40
  138.8 25.8 %collective-permute-start.72 = (bf16[2,192,768]{2,1,0:T(8,128)(2,1)}, bf16[2,192,768]{2,1,0:T(8,128)(2,1)}, u32[]{:S(2)}, u32[]{:S(2)}) collective-permute-start(bf16[2,192,768]{2,1,0:T(8,128)(2,1)} %pad_maximum_fusion.23), channel_id=1, source_target_pairs={{0,4},{1,5},{2,6},{3,7},{4,0},{5,1},{6,2},{7,3},{8,12},{9,13},{10,... | collective-permute-start | bytes 1769480 | tf_op jit(solution)/shard_map/cond/branch_1_fun/ppermute | solution.py:40
  139.1 30.0 %collective-permute-start.63 = (bf16[2,192,768]{2,1,0:T(8,128)(2,1)}, bf16[2,192,768]{2,1,0:T(8,128)(2,1)}, u32[]{:S(2)}, u32[]{:S(2)}) collective-permute-start(bf16[2,192,768]{2,1,0:T(8,128)(2,1)} %collective-permute-done.62), channel_id=1, source_target_pairs={{0,1},{1,0},{2,3},{3,2},{4,5},{5,4},{6,7},{7,6},{8,9},{9,8},{10,11... | collective-permute-start | bytes 1769480 | tf_op jit(solution)/shard_map/cond/branch_1_fun/ppermute | solution.py:40
  140.4 28.6 %collective-permute-start.66 = (bf16[2,192,768]{2,1,0:T(8,128)(2,1)}, bf16[2,192,768]{2,1,0:T(8,128)(2,1)}, u32[]{:S(2)}, u32[]{:S(2)}) collective-permute-start(bf16[2,192,768]{2,1,0:T(8,128)(2,1)} %pad_maximum_fusion.22), channel_id=1, source_target_pairs={{0,1},{1,0},{2,3},{3,2},{4,5},{5,4},{6,7},{7,6},{8,9},{9,8},{10,11... | collective-permute-start | bytes 1769480 | tf_op jit(solution)/shard_map/cond/branch_1_fun/ppermute | solution.py:40
  150.9 18.1 %collective-permute-start.71 = (bf16[2,192,768]{2,1,0:T(8,128)(2,1)}, bf16[2,192,768]{2,1,0:T(8,128)(2,1)}, u32[]{:S(2)}, u32[]{:S(2)}) collective-permute-start(bf16[2,192,768]{2,1,0:T(8,128)(2,1)} %pad_maximum_fusion.23), channel_id=1, source_target_pairs={{0,1},{1,0},{2,3},{3,2},{4,5},{5,4},{6,7},{7,6},{8,9},{9,8},{10,11... | collective-permute-start | bytes 1769480 | tf_op jit(solution)/shard_map/cond/branch_1_fun/ppermute | solution.py:40
  152.2 16.9 %collective-permute-start.68 = (bf16[2,192,768]{2,1,0:T(8,128)(2,1)}, bf16[2,192,768]{2,1,0:T(8,128)(2,1)}, u32[]{:S(2)}, u32[]{:S(2)}) collective-permute-start(bf16[2,192,768]{2,1,0:T(8,128)(2,1)} %collective-permute-done.67), channel_id=1, source_target_pairs={{0,1},{1,0},{2,3},{3,2},{4,5},{5,4},{6,7},{7,6},{8,9},{9,8},{10,11... | collective-permute-start | bytes 1769480 | tf_op jit(solution)/shard_map/cond/branch_1_fun/ppermute | solution.py:40
  184.9 34.2 %collective-permute-start.74 = (f16[384,768]{1,0:T(8,128)(2,1)}, f16[384,768]{1,0:T(8,128)(2,1)}, u32[]{:S(2)}, u32[]{:S(2)}) collective-permute-start(f16[384,768]{1,0:T(8,128)(2,1)} %get-tuple-element.383), channel_id=1, source_target_pairs={{0,4},{1,8},{2,16},{3,24},{4,0},{5,12},{6,20},{7,28},{8,1},{9,13},... | collective-permute-start | bytes 1769480 | tf_op jit(solution)/shard_map/ppermute | solution.py:40
  184.9 36.1 %collective-permute-start.75 = (f16[384,768]{1,0:T(8,128)(2,1)}, f16[384,768]{1,0:T(8,128)(2,1)}, u32[]{:S(2)}, u32[]{:S(2)}) collective-permute-start(f16[384,768]{1,0:T(8,128)(2,1)} %get-tuple-element.382), channel_id=1, source_target_pairs={{0,16},{1,24},{2,0},{3,8},{4,20},{5,28},{6,4},{7,12},{8,17},{9,25}... | collective-permute-start | bytes 1769480 | tf_op jit(solution)/shard_map/ppermute | solution.py:40
  188.2 29.7 %collective-permute-start.82 = (f16[384,384]{1,0:T(8,128)(2,1)}, f16[384,384]{1,0:T(8,128)(2,1)}, u32[]{:S(2)}, u32[]{:S(2)}) collective-permute-start(f16[384,384]{1,0:T(8,128)(2,1)} %get-tuple-element.426), channel_id=1, source_target_pairs={{0,6},{1,7},{2,4},{3,5},{4,2},{5,3},{6,0},{7,1},{8,14},{9,15},{10,... | collective-permute-start | bytes 884744 | tf_op jit(solution)/shard_map/ppermute | solution.py:40
  192.0 25.9 %collective-permute-start.81 = (f16[384,384]{1,0:T(8,128)(2,1)}, f16[384,384]{1,0:T(8,128)(2,1)}, u32[]{:S(2)}, u32[]{:S(2)}) collective-permute-start(f16[384,384]{1,0:T(8,128)(2,1)} %dynamic-slice_bitcast_fusion.18), channel_id=1, source_target_pairs={{0,4},{1,5},{2,6},{3,7},{4,0},{5,1},{6,2},{7,3},{8,12},{9,13},{10,... | collective-permute-start | bytes 884744 | tf_op jit(solution)/shard_map/ppermute | solution.py:40
  192.2 24.4 %collective-permute-start.78 = (f16[384,384]{1,0:T(8,128)(2,1)}, f16[384,384]{1,0:T(8,128)(2,1)}, u32[]{:S(2)}, u32[]{:S(2)}) collective-permute-start(f16[384,384]{1,0:T(8,128)(2,1)} %get-tuple-element.427), channel_id=1, source_target_pairs={{0,2},{1,3},{2,0},{3,1},{4,6},{5,7},{6,4},{7,5},{8,10},{9,11},{10,... | collective-permute-start | bytes 884744 | tf_op jit(solution)/shard_map/ppermute | solution.py:40
  222.9 38.1 %collective-permute-start.77 = (f16[384,768]{1,0:T(8,128)(2,1)S(1)}, f16[384,768]{1,0:T(8,128)(2,1)S(1)}, u32[]{:S(2)}, u32[]{:S(2)}) collective-permute-start(f16[384,768]{1,0:T(8,128)(2,1)S(1)} %get-tuple-element.376), channel_id=1, source_target_pairs={{0,24},{1,16},{2,8},{3,0},{4,28},{5,20},{6,12},{7,4},{8,25},{9,17}... | collective-permute-start | bytes 1769480 | tf_op jit(solution)/shard_map/ppermute | solution.py:40
  226.0 34.1 %collective-permute-start.76 = (f16[384,768]{1,0:T(8,128)(2,1)S(1)}, f16[384,768]{1,0:T(8,128)(2,1)S(1)}, u32[]{:S(2)}, u32[]{:S(2)}) collective-permute-start(f16[384,768]{1,0:T(8,128)(2,1)S(1)} %get-tuple-element.377), channel_id=1, source_target_pairs={{0,8},{1,0},{2,24},{3,16},{4,12},{5,4},{6,28},{7,20},{8,9},{9,1},{... | collective-permute-start | bytes 1769480 | tf_op jit(solution)/shard_map/ppermute | solution.py:40
  268.7 20.6 %collective-permute-start.96 = (bf16[384,768]{1,0:T(8,128)(2,1)S(1)}, bf16[384,768]{1,0:T(8,128)(2,1)S(1)}, u32[]{:S(2)}, u32[]{:S(2)}) collective-permute-start(bf16[384,768]{1,0:T(8,128)(2,1)S(1)} %pad_maximum_fusion.32), channel_id=1, source_target_pairs={{0,2},{1,3},{2,0},{3,1},{4,6},{5,7},{6,4},{7,5},{8,10},{9,11},{10,... | collective-permute-start | bytes 1769480 | tf_op jit(solution)/shard_map/ppermute | solution.py:40
  289.6 25.9 %collective-permute-start.92 = (bf16[192,768]{1,0:T(8,128)(2,1)S(1)}, bf16[192,768]{1,0:T(8,128)(2,1)S(1)}, u32[]{:S(2)}, u32[]{:S(2)}) collective-permute-start(bf16[192,768]{1,0:T(8,128)(2,1)S(1)} %get-tuple-element.243), channel_id=1, source_target_pairs={{0,16},{1,24},{2,18},{3,26},{4,20},{5,28},{6,22},{7,30},{8,17},{9,... | collective-permute-start | bytes 884744 | tf_op jit(solution)/shard_map/ppermute | solution.py:40
  299.6 15.9 %collective-permute-start.97 = (bf16[192,768]{1,0:T(8,128)(2,1)S(1)}, bf16[192,768]{1,0:T(8,128)(2,1)S(1)}, u32[]{:S(2)}, u32[]{:S(2)}) collective-permute-start(bf16[192,768]{1,0:T(8,128)(2,1)S(1)} %get-tuple-element.244), channel_id=1, source_target_pairs={{0,2},{1,8},{2,0},{3,10},{4,6},{5,12},{6,4},{7,14},{8,1},{9,11},{1... | collective-permute-start | bytes 884744 | tf_op jit(solution)/shard_map/ppermute | solution.py:40
  315.5 15.9 %collective-permute-start.98 = (bf16[192,768]{1,0:T(8,128)(2,1)S(1)}, bf16[192,768]{1,0:T(8,128)(2,1)S(1)}, u32[]{:S(2)}, u32[]{:S(2)}) collective-permute-start(bf16[192,768]{1,0:T(8,128)(2,1)S(1)} %get-tuple-element.245), channel_id=1, source_target_pairs={{0,16},{1,24},{2,18},{3,26},{4,20},{5,28},{6,22},{7,30},{8,17},{9,... | collective-permute-start | bytes 884744 | tf_op jit(solution)/shard_map/ppermute | solution.py:40
  317.1 26.6 %collective-permute-start.89 = (bf16[2,192,768]{2,1,0:T(8,128)(2,1)S(1)}, bf16[2,192,768]{2,1,0:T(8,128)(2,1)S(1)}, u32[]{:S(2)}, u32[]{:S(2)}) collective-permute-start(bf16[2,192,768]{2,1,0:T(8,128)(2,1)S(1)} %pad_maximum_fusion.30.refs_11_), channel_id=1, source_target_pairs={{0,4},{1,5},{2,6},{3,7},{4,0},{5,1},{6,2},{7,3},{8,12},{9,13},{10,... | collective-permute-start | bytes 1769480 | tf_op jit(solution)/shard_map/ppermute | solution.py:40
  317.6 26.2 %collective-permute-start.88 = (bf16[2,192,768]{2,1,0:T(8,128)(2,1)S(1)}, bf16[2,192,768]{2,1,0:T(8,128)(2,1)S(1)}, u32[]{:S(2)}, u32[]{:S(2)}) collective-permute-start(bf16[2,192,768]{2,1,0:T(8,128)(2,1)S(1)} %pad_maximum_fusion.30.refs_11_), channel_id=1, source_target_pairs={{0,1},{1,0},{2,3},{3,2},{4,5},{5,4},{6,7},{7,6},{8,9},{9,8},{10,11... | collective-permute-start | bytes 1769480 | tf_op jit(solution)/shard_map/ppermute | solution.py:40
  319.8 25.5 %collective-permute-start.94 = (bf16[2,192,768]{2,1,0:T(8,128)(2,1)S(1)}, bf16[2,192,768]{2,1,0:T(8,128)(2,1)S(1)}, u32[]{:S(2)}, u32[]{:S(2)}) collective-permute-start(bf16[2,192,768]{2,1,0:T(8,128)(2,1)S(1)} %pad_maximum_fusion.31.refs_15_), channel_id=1, source_target_pairs={{0,4},{1,5},{2,6},{3,7},{4,0},{5,1},{6,2},{7,3},{8,12},{9,13},{10,... | collective-permute-start | bytes 1769480 | tf_op jit(solution)/shard_map/ppermute | solution.py:40
  343.8 26.3 %collective-permute-start.105 = (bf16[2,192,768]{2,1,0:T(8,128)(2,1)S(1)}, bf16[2,192,768]{2,1,0:T(8,128)(2,1)S(1)}, u32[]{:S(2)}, u32[]{:S(2)}) collective-permute-start(bf16[2,192,768]{2,1,0:T(8,128)(2,1)S(1)} %pad_maximum_fusion.34.refs_23_), channel_id=1, source_target_pairs={{0,4},{1,5},{2,6},{3,7},{4,0},{5,1},{6,2},{7,3},{8,12},{9,13},{10,... | collective-permute-start | bytes 1769480 | tf_op jit(solution)/shard_map/ppermute | solution.py:40
  345.3 24.8 %collective-permute-start.90 = (bf16[2,192,768]{2,1,0:T(8,128)(2,1)S(1)}, bf16[2,192,768]{2,1,0:T(8,128)(2,1)S(1)}, u32[]{:S(2)}, u32[]{:S(2)}) collective-permute-start(bf16[2,192,768]{2,1,0:T(8,128)(2,1)S(1)} %collective-permute-done.89.refs_13_), channel_id=1, source_target_pairs={{0,1},{1,0},{2,3},{3,2},{4,5},{5,4},{6,7},{7,6},{8,9},{9,8},{10,11... | collective-permute-start | bytes 1769480 | tf_op jit(solution)/shard_map/ppermute | solution.py:40
  346.1 24.1 %collective-permute-start.104 = (bf16[2,192,768]{2,1,0:T(8,128)(2,1)S(1)}, bf16[2,192,768]{2,1,0:T(8,128)(2,1)S(1)}, u32[]{:S(2)}, u32[]{:S(2)}) collective-permute-start(bf16[2,192,768]{2,1,0:T(8,128)(2,1)S(1)} %pad_maximum_fusion.34.refs_23_), channel_id=1, source_target_pairs={{0,1},{1,0},{2,3},{3,2},{4,5},{5,4},{6,7},{7,6},{8,9},{9,8},{10,11... | collective-permute-start | bytes 1769480 | tf_op jit(solution)/shard_map/ppermute | solution.py:40
  381.8 34.0 %collective-permute-start.107 = (f16[384,768]{1,0:T(8,128)(2,1)}, f16[384,768]{1,0:T(8,128)(2,1)}, u32[]{:S(2)}, u32[]{:S(2)}) collective-permute-start(f16[384,768]{1,0:T(8,128)(2,1)} %get-tuple-element.363), channel_id=1, source_target_pairs={{0,4},{1,8},{2,16},{3,24},{4,0},{5,12},{6,20},{7,28},{8,1},{9,13},... | collective-permute-start | bytes 1769480 | tf_op jit(solution)/shard_map/ppermute | solution.py:40
  385.9 28.6 %collective-permute-start.115 = (f16[384,384]{1,0:T(8,128)(2,1)}, f16[384,384]{1,0:T(8,128)(2,1)}, u32[]{:S(2)}, u32[]{:S(2)}) collective-permute-start(f16[384,384]{1,0:T(8,128)(2,1)} %get-tuple-element.398), channel_id=1, source_target_pairs={{0,6},{1,7},{2,4},{3,5},{4,2},{5,3},{6,0},{7,1},{8,14},{9,15},{10,... | collective-permute-start | bytes 884744 | tf_op jit(solution)/shard_map/ppermute | solution.py:40
  386.7 27.9 %collective-permute-start.114 = (f16[384,384]{1,0:T(8,128)(2,1)}, f16[384,384]{1,0:T(8,128)(2,1)}, u32[]{:S(2)}, u32[]{:S(2)}) collective-permute-start(f16[384,384]{1,0:T(8,128)(2,1)} %dynamic-slice_bitcast_fusion.11), channel_id=1, source_target_pairs={{0,4},{1,5},{2,6},{3,7},{4,0},{5,1},{6,2},{7,3},{8,12},{9,13},{10,... | collective-permute-start | bytes 884744 | tf_op jit(solution)/shard_map/ppermute | solution.py:40
  387.8 25.6 %collective-permute-start.111 = (f16[384,384]{1,0:T(8,128)(2,1)}, f16[384,384]{1,0:T(8,128)(2,1)}, u32[]{:S(2)}, u32[]{:S(2)}) collective-permute-start(f16[384,384]{1,0:T(8,128)(2,1)} %get-tuple-element.399), channel_id=1, source_target_pairs={{0,2},{1,3},{2,0},{3,1},{4,6},{5,7},{6,4},{7,5},{8,10},{9,11},{10,... | collective-permute-start | bytes 884744 | tf_op jit(solution)/shard_map/ppermute | solution.py:40
  397.3 28.4 %collective-permute-start.108 = (f16[384,768]{1,0:T(8,128)(2,1)S(1)}, f16[384,768]{1,0:T(8,128)(2,1)S(1)}, u32[]{:S(2)}, u32[]{:S(2)}) collective-permute-start(f16[384,768]{1,0:T(8,128)(2,1)S(1)} %copy-done.61), channel_id=1, source_target_pairs={{0,16},{1,24},{2,0},{3,8},{4,20},{5,28},{6,4},{7,12},{8,17},{9,25}... | collective-permute-start | bytes 1769480 | tf_op jit(solution)/shard_map/ppermute | solution.py:40
  427.0 36.0 %collective-permute-start.110 = (f16[384,768]{1,0:T(8,128)(2,1)S(1)}, f16[384,768]{1,0:T(8,128)(2,1)S(1)}, u32[]{:S(2)}, u32[]{:S(2)}) collective-permute-start(f16[384,768]{1,0:T(8,128)(2,1)S(1)} %get-tuple-element.356), channel_id=1, source_target_pairs={{0,24},{1,16},{2,8},{3,0},{4,28},{5,20},{6,12},{7,4},{8,25},{9,17}... | collective-permute-start | bytes 1769480 | tf_op jit(solution)/shard_map/ppermute | solution.py:40
  429.3 32.7 %collective-permute-start.109 = (f16[384,768]{1,0:T(8,128)(2,1)S(1)}, f16[384,768]{1,0:T(8,128)(2,1)S(1)}, u32[]{:S(2)}, u32[]{:S(2)}) collective-permute-start(f16[384,768]{1,0:T(8,128)(2,1)S(1)} %get-tuple-element.357), channel_id=1, source_target_pairs={{0,8},{1,0},{2,24},{3,16},{4,12},{5,4},{6,28},{7,20},{8,9},{9,1},{... | collective-permute-start | bytes 1769480 | tf_op jit(solution)/shard_map/ppermute | solution.py:40
  432.7 18.5 %collective-permute-start.116 = (f16[384,384]{1,0:T(8,128)(2,1)S(1)}, f16[384,384]{1,0:T(8,128)(2,1)S(1)}, u32[]{:S(2)}, u32[]{:S(2)}) collective-permute-start(f16[384,384]{1,0:T(8,128)(2,1)S(1)} %get-tuple-element.392), channel_id=1, source_target_pairs={{0,5},{1,4},{2,7},{3,6},{4,1},{5,0},{6,3},{7,2},{8,13},{9,12},{10,... | collective-permute-start | bytes 884744 | tf_op jit(solution)/shard_map/ppermute | solution.py:40
  (86 other events, 1760.0 us)

commit v7 on v6

--- a/solution.py
+++ b/solution.py
@@ -1,3 +1,5 @@
+import functools
+
 import jax
 import jax.numpy as jnp
 from jax import lax
@@ -29,7 +31,7 @@
     def index(self, band, lane, major, minor):
         return ((band * self.lanes + lane) * self.majors + major) * 2 + minor
 
-    def send(self, value, where, idle=None):
+    def send(self, value, where, idle=None, arrivals=None):
         stays = [where(*place) == place for place in self.places]
         if all(stays):
             return value
@@ -38,6 +40,8 @@
             target = idle(*place) if stay else where(*place)
             pairs.append((self.index(*place), self.index(*target)))
         received = lax.ppermute(value, AXES, pairs)
+        if arrivals is not None:
+            arrivals.append(received)
         if any(stays):
             device = lax.axis_index("alpha") * self.bands + lax.axis_index("beta")
             received = jnp.where(jnp.array(stays)[device], value, received)
@@ -45,7 +49,7 @@
 
 
 def after(value, *earlier):
-    earlier = [array for array in earlier if array is not None]
+    earlier = jax.tree.leaves(earlier)
     return lax.optimization_barrier((value, *earlier))[0] if earlier else value
 
 
@@ -198,7 +202,7 @@
     return parts
 
 
-def product_kernel(groups, pieces, lanes, base, id_ref, entry_ref, column_ref, count_ref, scale_ref, *refs):
+def product_kernel(groups, pieces, lanes, out_calls, base, id_ref, entry_ref, column_ref, count_ref, scale_ref, *refs):
     couplings, parts = refs[: len(groups) * pieces], refs[len(groups) * pieces : -4]
     out_ref, mirror_ref, coeff_ref, sems = refs[-4:]
     band, lane, major, minor = (id_ref[i] for i in range(4))
@@ -211,18 +215,30 @@
 
     @pl.when(pl.program_id(0) == 0)
     def _():
+        wanted_rows = [
+            (((major * 2 + minor) ^ (2 * i + base)) * lanes + lane) * rows // tile for i in range(out_calls)
+        ]
+        used = [
+            (column_ref[row * sum(groups) + slot], slot < count_ref[row])
+            for row in wanted_rows
+            for slot in range(sum(groups))
+        ]
         copies = []
-        for i, ref in enumerate(parts):
-            turn, flip = i // 2 % lanes, i % 2
+        for i in range(2 * lanes):
+            turn, flip = i // 2, i % 2
             for key in range(majors):
                 alpha = (((band // 2) ^ key) * 2 + (minor ^ flip)) * lanes + lax.rem(lane + lanes - turn, lanes)
-                first = pl.multiple_of(alpha * rows + i // (2 * lanes) * part, part)
-                target = coeff_ref.at[pl.ds(first, part)]
-                copies.append(pltpu.make_async_copy(ref.at[key], target, sems.at[i * majors + key]))
-        for copy in copies:
-            copy.start()
-        for copy in copies:
-            copy.wait()
+                column = alpha * rows // tile
+                needed = functools.reduce(jnp.logical_or, [(one == column) & filled for one, filled in used])
+                for number in range(i, len(parts), 2 * lanes):
+                    first = pl.multiple_of(alpha * rows + number // (2 * lanes) * part, part)
+                    target = coeff_ref.at[pl.ds(first, part)]
+                    source = parts[number].at[key]
+                    copies.append((needed, pltpu.make_async_copy(source, target, sems.at[number * majors + key])))
+        for needed, copy in copies:
+            pl.when(needed)(copy.start)
+        for needed, copy in copies:
+            pl.when(needed)(copy.wait)
 
     def product(number, i, slot):
         first = pl.multiple_of(column_ref[tile_row * sum(groups) + slot] * tile, tile)
@@ -266,7 +282,7 @@
 
     calls = bands // 2
     return pl.pallas_call(
-        lambda *refs: product_kernel(groups, pieces, lanes, base, *refs),
+        lambda *refs: product_kernel(groups, pieces, lanes, calls, base, *refs),
         grid_spec=pltpu.PrefetchScalarGridSpec(
             num_scalar_prefetch=5,
             grid=(calls,),
@@ -304,21 +320,22 @@
 
 def bring_home(grid, run, ids, band, lane, major, minor):
     bands, lanes, majors = grid.bands, grid.lanes, grid.majors
-    received, table, gate = [None] * bands, {}, []
+    received, table, gate, arrivals = [None] * bands, {}, [], []
     for base in range(2):
         sigma, mirrored = run(after(ids, gate), base)
+        strip, part = mirrored.shape[1:]
+        share = strip // lanes
         sigma, mirrored = sigma.astype(jnp.float16), mirrored.astype(jnp.float16)
         gate = [sigma, mirrored]
         if base:
-            sigma, mirrored = after((sigma, mirrored), received[0::2])
-        strip, part = mirrored.shape[1:]
-        share = strip // lanes
+            sigma, mirrored = after((sigma, mirrored), arrivals)
         for i in range(majors):
             key = 2 * i + base
             received[key] = grid.send(
                 sigma[i],
                 lambda z, x, m, n: ((m * 2 + n) ^ key, x, z // 2, z % 2),
                 lambda z, x, m, n: (z, (x + 1) % lanes, m, n),
+                None if base else arrivals,
             )
             for turn in range(lanes):
                 piece = lax.dynamic_slice_in_dim(mirrored[i], (lane ^ turn) * share, share, 0)

time: 478 us -> 467 us (0.977)
  waiting for transfers between devices: 246 us -> 231 us
  starting transfers between devices: 93.1 us -> 105 us
  Pallas kernels: 33 us -> 27.1 us
    ppermute x70, waiting for transfers between devices: 223 us -> 209 us  [send(): received = lax.ppermute(value, AXES, pairs)]
    ppermute x70, starting transfers between devices: 72.3 us -> 84.3 us  [send(): received = lax.ppermute(value, AXES, pairs)]
    pallas_call x4, Pallas kernels: 33 us -> 27.1 us  [products(): pl.pallas_call(lambda *refs: product_kernel(groups, pieces, lanes, calls,...]
  transfers between devices with their start and end apart: 79 -> 79, of which waited for: 29 -> 28; matrix products, arithmetic and copies ran while one was open for 13% -> 13% of each run, Pallas kernels for 3% -> 3%
where the time goes in v7:
time: 467 us; the launch traced here: 459 us
  waiting for transfers between devices  231 us (49%)
  starting transfers between devices  105 us (22%)
  other arithmetic  52.7 us (11%)
  local copies, waits for them, and re-layouts  38.7 us (8%)
  Pallas kernels  27.1 us (6%)
    ppermute x70, waiting for transfers between devices, send(): received = lax.ppermute(value, AXES, pairs)  209 us
    ppermute x70, starting transfers between devices, send(): received = lax.ppermute(value, AXES, pairs)  84.3 us
    pallas_call x4, Pallas kernels, products(): pl.pallas_call(lambda *refs: product_kernel(groups, pieces, lanes, calls,...  27.1 us
    ppermute x9, waiting for transfers between devices, gather_bands(): moving = lax.ppermute(moving, AXES, pairs)  22.4 us
    ppermute x9, starting transfers between devices, gather_bands(): moving = lax.ppermute(moving, AXES, pairs)  20.9 us
  transfers between devices with their start and end apart: 79, of which 28 were waited for; matrix products, arithmetic and copies ran while one was open for 13% of the time, Pallas kernels for 3%

profile of v7, /device:TPU:25, one launch (start us, length us, event | category | flops | bytes accessed | tf_op | source)
XLA Modules:
  0.0 459.3 jit_solution(13374961441300313326)
XLA Ops:
  3.7 166.7 %conditional.2 = (bf16[4,1,192,768]{3,2,1,0:T(8,128)(2,1)S(1)}, bf16[4,1,192,768]{3,2,1,0:T(8,128)(2,1)}, bf16[4,1,208,768]{3,2,1,0:T(8,128)(2,1)}, bf16[4,1,208...) conditional(s32[]{:T(128)} %convert_element_type.71, ...), branch_computations={%region_2.6_spmd, %region_6.12_spmd} | conditional | flops 26185744 | bytes 215436768
  4.0 5.1 %copy.32 = bf16[768,4,768]{2,0,1:T(8,128)(2,1)} copy(bf16[768,4,768]{2,1,0:T(4,128)(2,1)} %get-tuple-element.296) | data formatting | bytes 9437184 | tf_op jit(solution)/shard_map
  10.3 2.6 convert_element_type.51
  29.5 2.2 collective-permute-done.45
  34.9 4.8 %collective-permute-start.41 = (bf16[2,1,192,768]{3,2,1,0:T(8,128)(2,1)}, bf16[2,1,192,768]{3,2,1,0:T(8,128)(2,1)S(1)}, u32[]{:S(2)}, u32[]{:S(2)}) collective-permute-start(bf16[2,1,192,768]{3,2,1,0:T(8,128)(2,1)} %collective-permute-done.40), channel_id=1, source_target_pairs={{0,8},{1,9},{2,10},{3,11},{4,12},{5,13},{6,14},{7,15},{8,0},{9,1},... | collective-permute-start | bytes 1769480 | tf_op jit(solution)/shard_map/cond/branch_1_fun/ppermute | solution.py:99
  39.8 7.7 %collective-permute-done.53 = bf16[768,768]{1,0:T(8,128)(2,1)} collective-permute-done((bf16[768,768]{1,0:T(8,128)(2,1)}, bf16[768,768]{1,0:T(8,128)(2,1)}, u32[]{:S(2)}, u32[]{:S(2)}) %collective-permute-start.53) | collective-permute-done | bytes 1179680 | tf_op jit(solution)/shard_map/cond/branch_1_fun/ppermute | solution.py:42
  49.3 4.0 collective-permute-start.47
  54.0 2.5 collective-permute-start.50
  56.5 5.9 %collective-permute-done.41 = bf16[2,1,192,768]{3,2,1,0:T(8,128)(2,1)S(1)} collective-permute-done((bf16[2,1,192,768]{3,2,1,0:T(8,128)(2,1)}, bf16[2,1,192,768]{3,2,1,0:T(8,128)(2,1)S(1)}, u32[]{:S(2)}, u32[]{:S(2)}) %collective-permute-start.41) | collective-permute-done | bytes 589856 | tf_op jit(solution)/shard_map/cond/branch_1_fun/ppermute | solution.py:99
  64.9 14.3 %collective-permute-done.47 = bf16[2,1,208,768]{3,2,1,0:T(8,128)(2,1)S(1)} collective-permute-done((bf16[2,1,208,768]{3,2,1,0:T(8,128)(2,1)S(1)}, bf16[2,1,208,768]{3,2,1,0:T(8,128)(2,1)S(1)}, u32[]{:S(2)}, u32[]{:S(2)}) %collective-permute-start.47) | collective-permute-done | bytes 639008 | tf_op jit(solution)/shard_map/cond/branch_1_fun/ppermute | solution.py:99
  85.2 4.9 %collective-permute-start.51 = (bf16[1,2,192,768]{3,2,1,0:T(8,128)(2,1)S(1)}, bf16[1,2,192,768]{3,2,1,0:T(8,128)(2,1)S(1)}, u32[]{:S(2)}, u32[]{:S(2)}) collective-permute-start(bf16[1,2,192,768]{3,2,1,0:T(8,128)(2,1)S(1)} %collective-permute-done.50), channel_id=1, source_target_pairs={{0,8},{1,9},{2,10},{3,11},{4,12},{5,13},{6,14},{7,15},{8,0},{9,1},... | collective-permute-start | bytes 1769480 | tf_op jit(solution)/shard_map/cond/branch_1_fun/ppermute | solution.py:99
  92.8 7.0 %collective-permute-done.60 = bf16[192,768]{1,0:T(8,128)(2,1)S(1)} collective-permute-done((bf16[192,768]{1,0:T(8,128)(2,1)S(1)}, bf16[192,768]{1,0:T(8,128)(2,1)S(1)}, u32[]{:S(2)}, u32[]{:S(2)}) %collective-permute-start.60) | collective-permute-done | bytes 294944 | tf_op jit(solution)/shard_map/cond/branch_1_fun/ppermute | solution.py:42
  102.4 14.7 %collective-permute-done.48 = bf16[4,1,208,768]{3,2,1,0:T(8,128)(2,1)S(1)} collective-permute-done((bf16[4,1,208,768]{3,2,1,0:T(8,128)(2,1)S(1)}, bf16[4,1,208,768]{3,2,1,0:T(8,128)(2,1)S(1)}, u32[]{:S(2)}, u32[]{:S(2)}) %collective-permute-start.48) | collective-permute-done | bytes 1277984 | tf_op jit(solution)/shard_map/cond/branch_1_fun/ppermute | solution.py:42
  121.6 7.2 %collective-permute-start.61 = (bf16[2,192,768]{2,1,0:T(8,128)(2,1)S(1)}, bf16[2,192,768]{2,1,0:T(8,128)(2,1)S(1)}, u32[]{:S(2)}, u32[]{:S(2)}) collective-permute-start(bf16[2,192,768]{2,1,0:T(8,128)(2,1)S(1)} %pad_maximum_fusion.21), channel_id=1, source_target_pairs={{0,1},{1,0},{2,3},{3,2},{4,5},{5,4},{6,7},{7,6},{8,9},{9,8},{10,11... | collective-permute-start | bytes 1769480 | tf_op jit(solution)/shard_map/cond/branch_1_fun/ppermute | solution.py:42
  128.8 6.5 %collective-permute-done.69 = bf16[192,768]{1,0:T(8,128)(2,1)S(1)} collective-permute-done((bf16[192,768]{1,0:T(8,128)(2,1)S(1)}, bf16[192,768]{1,0:T(8,128)(2,1)S(1)}, u32[]{:S(2)}, u32[]{:S(2)}) %collective-permute-start.69) | collective-permute-done | bytes 294944 | tf_op jit(solution)/shard_map/cond/branch_1_fun/ppermute | solution.py:42
  140.4 10.1 %collective-permute-done.52 = bf16[1,2,192,768]{3,2,1,0:T(8,128)(2,1)S(1)} collective-permute-done((bf16[1,2,192,768]{3,2,1,0:T(8,128)(2,1)S(1)}, bf16[1,2,192,768]{3,2,1,0:T(8,128)(2,1)S(1)}, u32[]{:S(2)}, u32[]{:S(2)}) %collective-permute-start.52) | collective-permute-done | bytes 589856 | tf_op jit(solution)/shard_map/cond/branch_1_fun/ppermute | solution.py:42
  151.9 3.0 collective-permute-start.68
  154.9 9.7 %collective-permute-done.72 = bf16[2,192,768]{2,1,0:T(8,128)(2,1)} collective-permute-done((bf16[2,192,768]{2,1,0:T(8,128)(2,1)}, bf16[2,192,768]{2,1,0:T(8,128)(2,1)}, u32[]{:S(2)}, u32[]{:S(2)}) %collective-permute-start.72) | collective-permute-done | bytes 589856 | tf_op jit(solution)/shard_map/cond/branch_1_fun/ppermute | solution.py:42
  172.7 6.3 %shard_map.253 = (f32[2,384,768]{2,1,0:T(8,128)S(1)}, f32[2,768,384]{2,1,0:T(8,128)S(1)}) custom-call(s32[4]{0:T(128)S(1)} %pad_add_fusion.refs_0_, s32[16]{0:T(128)S(1)} %copy-done.2, s32[32]{0:T(128)S(1)} %reshape.105.refs_2_, s32[8]{0:T(128)S(1)} %copy-done, f32[1]{0:T(128)} %get-tuple-element.210.refs_4_, ...), custom_call_target="tpu_custom_call" | custom-call | flops 3623878656 | bytes 14155776 | tf_op jit(solution)/shard_map/pallas_call | solution.py:284
  184.8 2.9 collective-permute-start.82
  188.8 8.9 %shard_map.254 = (f32[2,384,768]{2,1,0:T(8,128)S(1)}, f32[2,768,384]{2,1,0:T(8,128)S(1)}) custom-call(s32[4]{0:T(128)S(1)} %pad_add_fusion.refs_0_, s32[16]{0:T(128)S(1)} %copy-done.2, s32[32]{0:T(128)S(1)} %reshape.105.refs_2_, s32[8]{0:T(128)S(1)} %copy-done, f32[1]{0:T(128)} %get-tuple-element.210.refs_4_, ...), custom_call_target="tpu_custom_call" | custom-call | flops 3623878656 | bytes 14155776 | tf_op jit(solution)/shard_map/pallas_call | solution.py:284
  199.1 2.8 convert_element_type.74
  204.5 8.0 %collective-permute-done.78 = f16[384,384]{1,0:T(8,128)(2,1)} collective-permute-done((f16[384,384]{1,0:T(8,128)(2,1)}, f16[384,384]{1,0:T(8,128)(2,1)}, u32[]{:S(2)}, u32[]{:S(2)}) %collective-permute-start.78) | collective-permute-done | bytes 294944 | tf_op jit(solution)/shard_map/ppermute | solution.py:42
  216.9 4.3 collective-permute-start.77
  221.2 2.7 collective-permute-start.76
  226.4 8.2 %collective-permute-done.84 = f16[384,384]{1,0:T(8,128)(2,1)S(1)} collective-permute-done((f16[384,384]{1,0:T(8,128)(2,1)S(1)}, f16[384,384]{1,0:T(8,128)(2,1)S(1)}, u32[]{:S(2)}, u32[]{:S(2)}) %collective-permute-start.84) | collective-permute-done | bytes 294944 | tf_op jit(solution)/shard_map/ppermute | solution.py:42
  234.7 7.1 %collective-permute-done.83 = f16[384,384]{1,0:T(8,128)(2,1)S(1)} collective-permute-done((f16[384,384]{1,0:T(8,128)(2,1)S(1)}, f16[384,384]{1,0:T(8,128)(2,1)S(1)}, u32[]{:S(2)}, u32[]{:S(2)}) %collective-permute-start.83) | collective-permute-done | bytes 294944 | tf_op jit(solution)/shard_map/ppermute | solution.py:42
  242.1 12.6 %collective-permute-done.76 = f16[384,768]{1,0:T(8,128)(2,1)S(1)} collective-permute-done((f16[384,768]{1,0:T(8,128)(2,1)S(1)}, f16[384,768]{1,0:T(8,128)(2,1)S(1)}, u32[]{:S(2)}, u32[]{:S(2)}) %collective-permute-start.76) | collective-permute-done | bytes 589856 | tf_op jit(solution)/shard_map/ppermute | solution.py:42
  254.8 2.3 broadcast_select_fusion.21
  267.5 7.3 %collective-permute-done.85 = bf16[384,768]{1,0:T(8,128)(2,1)} collective-permute-done((bf16[384,768]{1,0:T(8,128)(2,1)}, bf16[384,768]{1,0:T(8,128)(2,1)}, u32[]{:S(2)}, u32[]{:S(2)}) %collective-permute-start.85) | collective-permute-done | bytes 589856 | tf_op jit(solution)/shard_map/ppermute | solution.py:42
  278.8 5.7 %collective-permute-done.86 = bf16[192,768]{1,0:T(8,128)(2,1)S(1)} collective-permute-done((bf16[192,768]{1,0:T(8,128)(2,1)S(1)}, bf16[192,768]{1,0:T(8,128)(2,1)S(1)}, u32[]{:S(2)}, u32[]{:S(2)}) %collective-permute-start.86) | collective-permute-done | bytes 294944 | tf_op jit(solution)/shard_map/ppermute | solution.py:42
  285.4 9.5 %collective-permute-start.92 = (bf16[192,768]{1,0:T(8,128)(2,1)S(1)}, bf16[192,768]{1,0:T(8,128)(2,1)S(1)}, u32[]{:S(2)}, u32[]{:S(2)}) collective-permute-start(bf16[192,768]{1,0:T(8,128)(2,1)S(1)} %get-tuple-element.243), channel_id=1, source_target_pairs={{0,16},{1,24},{2,18},{3,26},{4,20},{5,28},{6,22},{7,30},{8,17},{9,... | collective-permute-start | bytes 884744 | tf_op jit(solution)/shard_map/ppermute | solution.py:42
  295.9 15.8 %collective-permute-done.92 = bf16[192,768]{1,0:T(8,128)(2,1)S(1)} collective-permute-done((bf16[192,768]{1,0:T(8,128)(2,1)S(1)}, bf16[192,768]{1,0:T(8,128)(2,1)S(1)}, u32[]{:S(2)}, u32[]{:S(2)}) %collective-permute-start.92) | collective-permute-done | bytes 294944 | tf_op jit(solution)/shard_map/ppermute | solution.py:42
  316.0 14.5 %collective-permute-done.98 = bf16[192,768]{1,0:T(8,128)(2,1)S(1)} collective-permute-done((bf16[192,768]{1,0:T(8,128)(2,1)S(1)}, bf16[192,768]{1,0:T(8,128)(2,1)S(1)}, u32[]{:S(2)}, u32[]{:S(2)}) %collective-permute-start.98) | collective-permute-done | bytes 294944 | tf_op jit(solution)/shard_map/ppermute | solution.py:42
  331.3 5.7 %collective-permute-done.103 = bf16[192,768]{1,0:T(8,128)(2,1)S(1)} collective-permute-done((bf16[192,768]{1,0:T(8,128)(2,1)S(1)}, bf16[192,768]{1,0:T(8,128)(2,1)S(1)}, u32[]{:S(2)}, u32[]{:S(2)}) %collective-permute-start.103) | collective-permute-done | bytes 294944 | tf_op jit(solution)/shard_map/ppermute | solution.py:42
  338.7 3.2 collective-permute-start.90
  341.9 10.5 %collective-permute-done.100.refs_21_ = bf16[2,192,768]{2,1,0:T(8,128)(2,1)S(1)} collective-permute-done((bf16[2,192,768]{2,1,0:T(8,128)(2,1)S(1)}, bf16[2,192,768]{2,1,0:T(8,128)(2,1)S(1)}, u32[]{:S(2)}, u32[]{:S(2)}) %collective-permute-start.100) | collective-permute-done | bytes 589856 | tf_op jit(solution)/shard_map/ppermute | solution.py:42
  354.5 10.5 %collective-permute-done.105.refs_25_ = bf16[2,192,768]{2,1,0:T(8,128)(2,1)S(1)} collective-permute-done((bf16[2,192,768]{2,1,0:T(8,128)(2,1)S(1)}, bf16[2,192,768]{2,1,0:T(8,128)(2,1)S(1)}, u32[]{:S(2)}, u32[]{:S(2)}) %collective-permute-start.105) | collective-permute-done | bytes 589856 | tf_op jit(solution)/shard_map/ppermute | solution.py:42
  367.9 4.8 %shard_map.255 = (f32[2,384,768]{2,1,0:T(8,128)S(1)}, f32[2,768,384]{2,1,0:T(8,128)S(1)}) custom-call(s32[4]{0:T(128)S(1)} %pad_add_fusion.refs_0_, s32[16]{0:T(128)S(1)} %copy-done.2, s32[32]{0:T(128)S(1)} %reshape.105.refs_2_, s32[8]{0:T(128)S(1)} %copy-done, f32[1]{0:T(128)} %get-tuple-element.241.refs_4_, ...), custom_call_target="tpu_custom_call" | custom-call | flops 3623878656 | bytes 14155776 | tf_op jit(solution)/shard_map/pallas_call | solution.py:284
  374.6 3.6 collective-permute-start.107
  382.6 7.1 %shard_map.256 = (f32[2,384,768]{2,1,0:T(8,128)S(1)}, f32[2,768,384]{2,1,0:T(8,128)S(1)}) custom-call(s32[4]{0:T(128)S(1)} %pad_add_fusion.refs_0_, s32[16]{0:T(128)S(1)} %copy-done.2, s32[32]{0:T(128)S(1)} %reshape.105.refs_2_, s32[8]{0:T(128)S(1)} %copy-done, f32[1]{0:T(128)} %get-tuple-element.241.refs_4_, ...), custom_call_target="tpu_custom_call" | custom-call | flops 3623878656 | bytes 14155776 | tf_op jit(solution)/shard_map/pallas_call | solution.py:284
  390.0 15.2 %collective-permute-done.111 = f16[384,384]{1,0:T(8,128)(2,1)} collective-permute-done((f16[384,384]{1,0:T(8,128)(2,1)}, f16[384,384]{1,0:T(8,128)(2,1)}, u32[]{:S(2)}, u32[]{:S(2)}) %collective-permute-start.111) | collective-permute-done | bytes 294944 | tf_op jit(solution)/shard_map/ppermute | solution.py:42
  410.2 6.4 %collective-permute-start.110 = (f16[384,768]{1,0:T(8,128)(2,1)S(1)}, f16[384,768]{1,0:T(8,128)(2,1)S(1)}, u32[]{:S(2)}, u32[]{:S(2)}) collective-permute-start(f16[384,768]{1,0:T(8,128)(2,1)S(1)} %get-tuple-element.360), channel_id=1, source_target_pairs={{0,24},{1,16},{2,8},{3,0},{4,28},{5,20},{6,12},{7,4},{8,25},{9,17}... | collective-permute-start | bytes 1769480 | tf_op jit(solution)/shard_map/ppermute | solution.py:42
  416.6 2.7 collective-permute-start.109
  420.5 9.6 %collective-permute-done.117 = f16[384,384]{1,0:T(8,128)(2,1)S(1)} collective-permute-done((f16[384,384]{1,0:T(8,128)(2,1)S(1)}, f16[384,384]{1,0:T(8,128)(2,1)S(1)}, u32[]{:S(2)}, u32[]{:S(2)}) %collective-permute-start.117) | collective-permute-done | bytes 294944 | tf_op jit(solution)/shard_map/ppermute | solution.py:42
  430.1 7.8 %collective-permute-done.116 = f16[384,384]{1,0:T(8,128)(2,1)S(1)} collective-permute-done((f16[384,384]{1,0:T(8,128)(2,1)S(1)}, f16[384,384]{1,0:T(8,128)(2,1)S(1)}, u32[]{:S(2)}, u32[]{:S(2)}) %collective-permute-start.116) | collective-permute-done | bytes 294944 | tf_op jit(solution)/shard_map/ppermute | solution.py:42
  438.3 11.5 %collective-permute-done.109 = f16[384,768]{1,0:T(8,128)(2,1)S(1)} collective-permute-done((f16[384,768]{1,0:T(8,128)(2,1)S(1)}, f16[384,768]{1,0:T(8,128)(2,1)S(1)}, u32[]{:S(2)}, u32[]{:S(2)}) %collective-permute-start.109) | collective-permute-done | bytes 589856 | tf_op jit(solution)/shard_map/ppermute | solution.py:42
  455.4 3.7 divide_subtract_fusion
  (366 shorter events, 121.3 us)
Async XLA Ops:
  20.3 27.2 %collective-permute-start.53 = (bf16[768,768]{1,0:T(8,128)(2,1)}, bf16[768,768]{1,0:T(8,128)(2,1)}, u32[]{:S(2)}, u32[]{:S(2)}) collective-permute-start(bf16[768,768]{1,0:T(8,128)(2,1)} %pad_maximum_fusion.17), channel_id=1, source_target_pairs={{0,2},{1,3},{2,0},{3,1},{4,6},{5,7},{6,4},{7,5},{8,10},{9,11},{10,... | collective-permute-start | bytes 3538952 | tf_op jit(solution)/shard_map/cond/branch_1_fun/ppermute | solution.py:42
  31.8 17.5 %collective-permute-start.46 = (bf16[2,1,208,768]{3,2,1,0:T(8,128)(2,1)S(1)}, bf16[2,1,208,768]{3,2,1,0:T(8,128)(2,1)S(1)}, u32[]{:S(2)}, u32[]{:S(2)}) collective-permute-start(bf16[2,1,208,768]{3,2,1,0:T(8,128)(2,1)S(1)} %pad_maximum_fusion.18), channel_id=1, source_target_pairs={{0,1},{1,0},{2,3},{3,2},{4,5},{5,4},{6,7},{7,6},{8,16},{9,17},{10,... | collective-permute-start | bytes 1916936 | tf_op jit(solution)/shard_map/cond/branch_1_fun/ppermute | solution.py:99
  34.7 18.6 %collective-permute-start.49 = (bf16[1,2,192,768]{3,2,1,0:T(8,128)(2,1)S(1)}, bf16[1,2,192,768]{3,2,1,0:T(8,128)(2,1)S(1)}, u32[]{:S(2)}, u32[]{:S(2)}) collective-permute-start(bf16[1,2,192,768]{3,2,1,0:T(8,128)(2,1)S(1)} %maximum_bitcast_fusion.2), channel_id=1, source_target_pairs={{0,8},{1,9},{2,10},{3,11},{4,12},{5,13},{6,14},{7,15},{8,0},{9,1},... | collective-permute-start | bytes 1769480 | tf_op jit(solution)/shard_map/cond/branch_1_fun/ppermute | solution.py:99
  34.9 27.4 %collective-permute-start.41 = (bf16[2,1,192,768]{3,2,1,0:T(8,128)(2,1)}, bf16[2,1,192,768]{3,2,1,0:T(8,128)(2,1)S(1)}, u32[]{:S(2)}, u32[]{:S(2)}) collective-permute-start(bf16[2,1,192,768]{3,2,1,0:T(8,128)(2,1)} %collective-permute-done.40), channel_id=1, source_target_pairs={{0,8},{1,9},{2,10},{3,11},{4,12},{5,13},{6,14},{7,15},{8,0},{9,1},... | collective-permute-start | bytes 1769480 | tf_op jit(solution)/shard_map/cond/branch_1_fun/ppermute | solution.py:99
  49.3 29.9 %collective-permute-start.47 = (bf16[2,1,208,768]{3,2,1,0:T(8,128)(2,1)S(1)}, bf16[2,1,208,768]{3,2,1,0:T(8,128)(2,1)S(1)}, u32[]{:S(2)}, u32[]{:S(2)}) collective-permute-start(bf16[2,1,208,768]{3,2,1,0:T(8,128)(2,1)S(1)} %collective-permute-done.46), channel_id=1, source_target_pairs={{0,8},{1,9},{2,10},{3,11},{4,12},{5,13},{6,14},{7,15},{8,0},{9,1},... | collective-permute-start | bytes 1916936 | tf_op jit(solution)/shard_map/cond/branch_1_fun/ppermute | solution.py:99
  54.0 31.2 %collective-permute-start.50 = (bf16[1,2,192,768]{3,2,1,0:T(8,128)(2,1)S(1)}, bf16[1,2,192,768]{3,2,1,0:T(8,128)(2,1)S(1)}, u32[]{:S(2)}, u32[]{:S(2)}) collective-permute-start(bf16[1,2,192,768]{3,2,1,0:T(8,128)(2,1)S(1)} %broadcast_select_fusion.8), channel_id=1, source_target_pairs={{0,1},{1,0},{2,3},{3,2},{4,5},{5,4},{6,7},{7,6},{8,16},{9,17},{10,... | collective-permute-start | bytes 1769480 | tf_op jit(solution)/shard_map/cond/branch_1_fun/ppermute | solution.py:99
  63.3 27.5 %collective-permute-start.42 = (bf16[4,1,192,768]{3,2,1,0:T(8,128)(2,1)S(1)}, bf16[4,1,192,768]{3,2,1,0:T(8,128)(2,1)S(1)}, u32[]{:S(2)}, u32[]{:S(2)}) collective-permute-start(bf16[4,1,192,768]{3,2,1,0:T(8,128)(2,1)S(1)} %pad_maximum_fusion.16), channel_id=1, source_target_pairs={{0,2},{1,3},{2,0},{3,1},{4,6},{5,7},{6,4},{7,5},{8,10},{9,11},{10,... | collective-permute-start | bytes 3538952 | tf_op jit(solution)/shard_map/cond/branch_1_fun/ppermute | solution.py:42
  63.7 16.8 %collective-permute-start.54 = (bf16[192,768]{1,0:T(8,128)(2,1)S(1)}, bf16[192,768]{1,0:T(8,128)(2,1)S(1)}, u32[]{:S(2)}, u32[]{:S(2)}) collective-permute-start(bf16[192,768]{1,0:T(8,128)(2,1)S(1)} %get-tuple-element.153), channel_id=1, source_target_pairs={{0,4},{1,8},{2,6},{3,10},{4,0},{5,12},{6,2},{7,14},{8,1},{9,13},{1... | collective-permute-start | bytes 884744 | tf_op jit(solution)/shard_map/cond/branch_1_fun/ppermute | solution.py:42
  64.9 20.2 %collective-permute-start.55 = (bf16[192,768]{1,0:T(8,128)(2,1)S(1)}, bf16[192,768]{1,0:T(8,128)(2,1)S(1)}, u32[]{:S(2)}, u32[]{:S(2)}) collective-permute-start(bf16[192,768]{1,0:T(8,128)(2,1)S(1)} %get-tuple-element.154), channel_id=1, source_target_pairs={{0,16},{1,24},{2,18},{3,26},{4,20},{5,28},{6,22},{7,30},{8,17},{9,... | collective-permute-start | bytes 884744 | tf_op jit(solution)/shard_map/cond/branch_1_fun/ppermute | solution.py:42
  80.1 36.9 %collective-permute-start.48 = (bf16[4,1,208,768]{3,2,1,0:T(8,128)(2,1)S(1)}, bf16[4,1,208,768]{3,2,1,0:T(8,128)(2,1)S(1)}, u32[]{:S(2)}, u32[]{:S(2)}) collective-permute-start(bf16[4,1,208,768]{3,2,1,0:T(8,128)(2,1)S(1)} %pad_maximum_fusion.15), channel_id=1, source_target_pairs={{0,2},{1,3},{2,0},{3,1},{4,6},{5,7},{6,4},{7,5},{8,10},{9,11},{10,... | collective-permute-start | bytes 3833864 | tf_op jit(solution)/shard_map/cond/branch_1_fun/ppermute | solution.py:42
  85.2 32.1 %collective-permute-start.51 = (bf16[1,2,192,768]{3,2,1,0:T(8,128)(2,1)S(1)}, bf16[1,2,192,768]{3,2,1,0:T(8,128)(2,1)S(1)}, u32[]{:S(2)}, u32[]{:S(2)}) collective-permute-start(bf16[1,2,192,768]{3,2,1,0:T(8,128)(2,1)S(1)} %collective-permute-done.50), channel_id=1, source_target_pairs={{0,8},{1,9},{2,10},{3,11},{4,12},{5,13},{6,14},{7,15},{8,0},{9,1},... | collective-permute-start | bytes 1769480 | tf_op jit(solution)/shard_map/cond/branch_1_fun/ppermute | solution.py:99
  92.7 29.0 %collective-permute-start.57 = (bf16[2,192,768]{2,1,0:T(8,128)(2,1)S(1)}, bf16[2,192,768]{2,1,0:T(8,128)(2,1)S(1)}, u32[]{:S(2)}, u32[]{:S(2)}) collective-permute-start(bf16[2,192,768]{2,1,0:T(8,128)(2,1)S(1)} %pad_maximum_fusion.20), channel_id=1, source_target_pairs={{0,4},{1,5},{2,6},{3,7},{4,0},{5,1},{6,2},{7,3},{8,12},{9,13},{10,... | collective-permute-start | bytes 1769480 | tf_op jit(solution)/shard_map/cond/branch_1_fun/ppermute | solution.py:42
  99.7 37.8 %collective-permute-start.56 = (bf16[2,192,768]{2,1,0:T(8,128)(2,1)S(1)}, bf16[2,192,768]{2,1,0:T(8,128)(2,1)S(1)}, u32[]{:S(2)}, u32[]{:S(2)}) collective-permute-start(bf16[2,192,768]{2,1,0:T(8,128)(2,1)S(1)} %pad_maximum_fusion.20), channel_id=1, source_target_pairs={{0,1},{1,0},{2,3},{3,2},{4,5},{5,4},{6,7},{7,6},{8,9},{9,8},{10,11... | collective-permute-start | bytes 1769480 | tf_op jit(solution)/shard_map/cond/branch_1_fun/ppermute | solution.py:42
  99.8 20.8 %collective-permute-start.65 = (bf16[192,768]{1,0:T(8,128)(2,1)S(1)}, bf16[192,768]{1,0:T(8,128)(2,1)S(1)}, u32[]{:S(2)}, u32[]{:S(2)}) collective-permute-start(bf16[192,768]{1,0:T(8,128)(2,1)S(1)} %get-tuple-element.160), channel_id=1, source_target_pairs={{0,16},{1,24},{2,18},{3,26},{4,20},{5,28},{6,22},{7,30},{8,17},{9,... | collective-permute-start | bytes 884744 | tf_op jit(solution)/shard_map/cond/branch_1_fun/ppermute | solution.py:42
  117.1 21.6 %collective-permute-start.62 = (bf16[2,192,768]{2,1,0:T(8,128)(2,1)S(1)}, bf16[2,192,768]{2,1,0:T(8,128)(2,1)}, u32[]{:S(2)}, u32[]{:S(2)}) collective-permute-start(bf16[2,192,768]{2,1,0:T(8,128)(2,1)S(1)} %pad_maximum_fusion.21), channel_id=1, source_target_pairs={{0,4},{1,5},{2,6},{3,7},{4,0},{5,1},{6,2},{7,3},{8,12},{9,13},{10,... | collective-permute-start | bytes 1769480 | tf_op jit(solution)/shard_map/cond/branch_1_fun/ppermute | solution.py:42
  117.4 18.0 %collective-permute-start.69 = (bf16[192,768]{1,0:T(8,128)(2,1)S(1)}, bf16[192,768]{1,0:T(8,128)(2,1)S(1)}, u32[]{:S(2)}, u32[]{:S(2)}) collective-permute-start(bf16[192,768]{1,0:T(8,128)(2,1)S(1)} %get-tuple-element.162), channel_id=1, source_target_pairs={{0,4},{1,8},{2,6},{3,10},{4,0},{5,12},{6,2},{7,14},{8,1},{9,13},{1... | collective-permute-start | bytes 884744 | tf_op jit(solution)/shard_map/cond/branch_1_fun/ppermute | solution.py:42
  121.6 17.4 %collective-permute-start.61 = (bf16[2,192,768]{2,1,0:T(8,128)(2,1)S(1)}, bf16[2,192,768]{2,1,0:T(8,128)(2,1)S(1)}, u32[]{:S(2)}, u32[]{:S(2)}) collective-permute-start(bf16[2,192,768]{2,1,0:T(8,128)(2,1)S(1)} %pad_maximum_fusion.21), channel_id=1, source_target_pairs={{0,1},{1,0},{2,3},{3,2},{4,5},{5,4},{6,7},{7,6},{8,9},{9,8},{10,11... | collective-permute-start | bytes 1769480 | tf_op jit(solution)/shard_map/cond/branch_1_fun/ppermute | solution.py:42
  138.7 25.9 %collective-permute-start.72 = (bf16[2,192,768]{2,1,0:T(8,128)(2,1)}, bf16[2,192,768]{2,1,0:T(8,128)(2,1)}, u32[]{:S(2)}, u32[]{:S(2)}) collective-permute-start(bf16[2,192,768]{2,1,0:T(8,128)(2,1)} %pad_maximum_fusion.23), channel_id=1, source_target_pairs={{0,4},{1,5},{2,6},{3,7},{4,0},{5,1},{6,2},{7,3},{8,12},{9,13},{10,... | collective-permute-start | bytes 1769480 | tf_op jit(solution)/shard_map/cond/branch_1_fun/ppermute | solution.py:42
  139.0 29.9 %collective-permute-start.63 = (bf16[2,192,768]{2,1,0:T(8,128)(2,1)}, bf16[2,192,768]{2,1,0:T(8,128)(2,1)}, u32[]{:S(2)}, u32[]{:S(2)}) collective-permute-start(bf16[2,192,768]{2,1,0:T(8,128)(2,1)} %collective-permute-done.62), channel_id=1, source_target_pairs={{0,1},{1,0},{2,3},{3,2},{4,5},{5,4},{6,7},{7,6},{8,9},{9,8},{10,11... | collective-permute-start | bytes 1769480 | tf_op jit(solution)/shard_map/cond/branch_1_fun/ppermute | solution.py:42
  140.4 28.5 %collective-permute-start.66 = (bf16[2,192,768]{2,1,0:T(8,128)(2,1)}, bf16[2,192,768]{2,1,0:T(8,128)(2,1)}, u32[]{:S(2)}, u32[]{:S(2)}) collective-permute-start(bf16[2,192,768]{2,1,0:T(8,128)(2,1)} %pad_maximum_fusion.22), channel_id=1, source_target_pairs={{0,1},{1,0},{2,3},{3,2},{4,5},{5,4},{6,7},{7,6},{8,9},{9,8},{10,11... | collective-permute-start | bytes 1769480 | tf_op jit(solution)/shard_map/cond/branch_1_fun/ppermute | solution.py:42
  150.5 18.4 %collective-permute-start.71 = (bf16[2,192,768]{2,1,0:T(8,128)(2,1)}, bf16[2,192,768]{2,1,0:T(8,128)(2,1)}, u32[]{:S(2)}, u32[]{:S(2)}) collective-permute-start(bf16[2,192,768]{2,1,0:T(8,128)(2,1)} %pad_maximum_fusion.23), channel_id=1, source_target_pairs={{0,1},{1,0},{2,3},{3,2},{4,5},{5,4},{6,7},{7,6},{8,9},{9,8},{10,11... | collective-permute-start | bytes 1769480 | tf_op jit(solution)/shard_map/cond/branch_1_fun/ppermute | solution.py:42
  151.9 17.0 %collective-permute-start.68 = (bf16[2,192,768]{2,1,0:T(8,128)(2,1)}, bf16[2,192,768]{2,1,0:T(8,128)(2,1)}, u32[]{:S(2)}, u32[]{:S(2)}) collective-permute-start(bf16[2,192,768]{2,1,0:T(8,128)(2,1)} %collective-permute-done.67), channel_id=1, source_target_pairs={{0,1},{1,0},{2,3},{3,2},{4,5},{5,4},{6,7},{7,6},{8,9},{9,8},{10,11... | collective-permute-start | bytes 1769480 | tf_op jit(solution)/shard_map/cond/branch_1_fun/ppermute | solution.py:42
  181.4 33.5 %collective-permute-start.74 = (f16[384,768]{1,0:T(8,128)(2,1)}, f16[384,768]{1,0:T(8,128)(2,1)}, u32[]{:S(2)}, u32[]{:S(2)}) collective-permute-start(f16[384,768]{1,0:T(8,128)(2,1)} %get-tuple-element.383), channel_id=1, source_target_pairs={{0,4},{1,8},{2,16},{3,24},{4,0},{5,12},{6,20},{7,28},{8,1},{9,13},... | collective-permute-start | bytes 1769480 | tf_op jit(solution)/shard_map/ppermute | solution.py:42
  181.4 33.5 %collective-permute-start.75 = (f16[384,768]{1,0:T(8,128)(2,1)}, f16[384,768]{1,0:T(8,128)(2,1)}, u32[]{:S(2)}, u32[]{:S(2)}) collective-permute-start(f16[384,768]{1,0:T(8,128)(2,1)} %get-tuple-element.382), channel_id=1, source_target_pairs={{0,16},{1,24},{2,0},{3,8},{4,20},{5,28},{6,4},{7,12},{8,17},{9,25}... | collective-permute-start | bytes 1769480 | tf_op jit(solution)/shard_map/ppermute | solution.py:42
  184.8 29.0 %collective-permute-start.82 = (f16[384,384]{1,0:T(8,128)(2,1)}, f16[384,384]{1,0:T(8,128)(2,1)}, u32[]{:S(2)}, u32[]{:S(2)}) collective-permute-start(f16[384,384]{1,0:T(8,128)(2,1)} %get-tuple-element.426), channel_id=1, source_target_pairs={{0,6},{1,7},{2,4},{3,5},{4,2},{5,3},{6,0},{7,1},{8,14},{9,15},{10,... | collective-permute-start | bytes 884744 | tf_op jit(solution)/shard_map/ppermute | solution.py:42
  188.5 25.3 %collective-permute-start.81 = (f16[384,384]{1,0:T(8,128)(2,1)}, f16[384,384]{1,0:T(8,128)(2,1)}, u32[]{:S(2)}, u32[]{:S(2)}) collective-permute-start(f16[384,384]{1,0:T(8,128)(2,1)} %dynamic-slice_bitcast_fusion.18), channel_id=1, source_target_pairs={{0,4},{1,5},{2,6},{3,7},{4,0},{5,1},{6,2},{7,3},{8,12},{9,13},{10,... | collective-permute-start | bytes 884744 | tf_op jit(solution)/shard_map/ppermute | solution.py:42
  188.8 23.7 %collective-permute-start.78 = (f16[384,384]{1,0:T(8,128)(2,1)}, f16[384,384]{1,0:T(8,128)(2,1)}, u32[]{:S(2)}, u32[]{:S(2)}) collective-permute-start(f16[384,384]{1,0:T(8,128)(2,1)} %get-tuple-element.427), channel_id=1, source_target_pairs={{0,2},{1,3},{2,0},{3,1},{4,6},{5,7},{6,4},{7,5},{8,10},{9,11},{10,... | collective-permute-start | bytes 884744 | tf_op jit(solution)/shard_map/ppermute | solution.py:42
  216.9 40.8 %collective-permute-start.77 = (f16[384,768]{1,0:T(8,128)(2,1)S(1)}, f16[384,768]{1,0:T(8,128)(2,1)S(1)}, u32[]{:S(2)}, u32[]{:S(2)}) collective-permute-start(f16[384,768]{1,0:T(8,128)(2,1)S(1)} %get-tuple-element.378), channel_id=1, source_target_pairs={{0,24},{1,16},{2,8},{3,0},{4,28},{5,20},{6,12},{7,4},{8,25},{9,17}... | collective-permute-start | bytes 1769480 | tf_op jit(solution)/shard_map/ppermute | solution.py:42
  221.2 33.6 %collective-permute-start.76 = (f16[384,768]{1,0:T(8,128)(2,1)S(1)}, f16[384,768]{1,0:T(8,128)(2,1)S(1)}, u32[]{:S(2)}, u32[]{:S(2)}) collective-permute-start(f16[384,768]{1,0:T(8,128)(2,1)S(1)} %get-tuple-element.379), channel_id=1, source_target_pairs={{0,8},{1,0},{2,24},{3,16},{4,12},{5,4},{6,28},{7,20},{8,9},{9,1},{... | collective-permute-start | bytes 1769480 | tf_op jit(solution)/shard_map/ppermute | solution.py:42
  225.0 16.8 %collective-permute-start.83 = (f16[384,384]{1,0:T(8,128)(2,1)S(1)}, f16[384,384]{1,0:T(8,128)(2,1)S(1)}, u32[]{:S(2)}, u32[]{:S(2)}) collective-permute-start(f16[384,384]{1,0:T(8,128)(2,1)S(1)} %get-tuple-element.420), channel_id=1, source_target_pairs={{0,5},{1,4},{2,7},{3,6},{4,1},{5,0},{6,3},{7,2},{8,13},{9,12},{10,... | collective-permute-start | bytes 884744 | tf_op jit(solution)/shard_map/ppermute | solution.py:42
  264.8 20.3 %collective-permute-start.96 = (bf16[384,768]{1,0:T(8,128)(2,1)S(1)}, bf16[384,768]{1,0:T(8,128)(2,1)S(1)}, u32[]{:S(2)}, u32[]{:S(2)}) collective-permute-start(bf16[384,768]{1,0:T(8,128)(2,1)S(1)} %pad_maximum_fusion.32), channel_id=1, source_target_pairs={{0,2},{1,3},{2,0},{3,1},{4,6},{5,7},{6,4},{7,5},{8,10},{9,11},{10,... | collective-permute-start | bytes 1769480 | tf_op jit(solution)/shard_map/ppermute | solution.py:42
  285.4 26.3 %collective-permute-start.92 = (bf16[192,768]{1,0:T(8,128)(2,1)S(1)}, bf16[192,768]{1,0:T(8,128)(2,1)S(1)}, u32[]{:S(2)}, u32[]{:S(2)}) collective-permute-start(bf16[192,768]{1,0:T(8,128)(2,1)S(1)} %get-tuple-element.243), channel_id=1, source_target_pairs={{0,16},{1,24},{2,18},{3,26},{4,20},{5,28},{6,22},{7,30},{8,17},{9,... | collective-permute-start | bytes 884744 | tf_op jit(solution)/shard_map/ppermute | solution.py:42
  311.7 18.8 %collective-permute-start.98 = (bf16[192,768]{1,0:T(8,128)(2,1)S(1)}, bf16[192,768]{1,0:T(8,128)(2,1)S(1)}, u32[]{:S(2)}, u32[]{:S(2)}) collective-permute-start(bf16[192,768]{1,0:T(8,128)(2,1)S(1)} %get-tuple-element.245), channel_id=1, source_target_pairs={{0,16},{1,24},{2,18},{3,26},{4,20},{5,28},{6,22},{7,30},{8,17},{9,... | collective-permute-start | bytes 884744 | tf_op jit(solution)/shard_map/ppermute | solution.py:42
  312.4 18.2 %collective-permute-start.102 = (bf16[192,768]{1,0:T(8,128)(2,1)S(1)}, bf16[192,768]{1,0:T(8,128)(2,1)S(1)}, u32[]{:S(2)}, u32[]{:S(2)}) collective-permute-start(bf16[192,768]{1,0:T(8,128)(2,1)S(1)} %get-tuple-element.246), channel_id=1, source_target_pairs={{0,2},{1,8},{2,0},{3,10},{4,6},{5,12},{6,4},{7,14},{8,1},{9,11},{1... | collective-permute-start | bytes 884744 | tf_op jit(solution)/shard_map/ppermute | solution.py:42
  312.6 25.2 %collective-permute-start.89 = (bf16[2,192,768]{2,1,0:T(8,128)(2,1)S(1)}, bf16[2,192,768]{2,1,0:T(8,128)(2,1)S(1)}, u32[]{:S(2)}, u32[]{:S(2)}) collective-permute-start(bf16[2,192,768]{2,1,0:T(8,128)(2,1)S(1)} %pad_maximum_fusion.30.refs_11_), channel_id=1, source_target_pairs={{0,4},{1,5},{2,6},{3,7},{4,0},{5,1},{6,2},{7,3},{8,12},{9,13},{10,... | collective-permute-start | bytes 1769480 | tf_op jit(solution)/shard_map/ppermute | solution.py:42
  313.4 24.5 %collective-permute-start.88 = (bf16[2,192,768]{2,1,0:T(8,128)(2,1)S(1)}, bf16[2,192,768]{2,1,0:T(8,128)(2,1)S(1)}, u32[]{:S(2)}, u32[]{:S(2)}) collective-permute-start(bf16[2,192,768]{2,1,0:T(8,128)(2,1)S(1)} %pad_maximum_fusion.30.refs_11_), channel_id=1, source_target_pairs={{0,1},{1,0},{2,3},{3,2},{4,5},{5,4},{6,7},{7,6},{8,9},{9,8},{10,11... | collective-permute-start | bytes 1769480 | tf_op jit(solution)/shard_map/ppermute | solution.py:42
  315.4 23.3 %collective-permute-start.94 = (bf16[2,192,768]{2,1,0:T(8,128)(2,1)S(1)}, bf16[2,192,768]{2,1,0:T(8,128)(2,1)S(1)}, u32[]{:S(2)}, u32[]{:S(2)}) collective-permute-start(bf16[2,192,768]{2,1,0:T(8,128)(2,1)S(1)} %pad_maximum_fusion.31.refs_15_), channel_id=1, source_target_pairs={{0,4},{1,5},{2,6},{3,7},{4,0},{5,1},{6,2},{7,3},{8,12},{9,13},{10,... | collective-permute-start | bytes 1769480 | tf_op jit(solution)/shard_map/ppermute | solution.py:42
  337.9 27.2 %collective-permute-start.105 = (bf16[2,192,768]{2,1,0:T(8,128)(2,1)S(1)}, bf16[2,192,768]{2,1,0:T(8,128)(2,1)S(1)}, u32[]{:S(2)}, u32[]{:S(2)}) collective-permute-start(bf16[2,192,768]{2,1,0:T(8,128)(2,1)S(1)} %pad_maximum_fusion.34.refs_23_), channel_id=1, source_target_pairs={{0,4},{1,5},{2,6},{3,7},{4,0},{5,1},{6,2},{7,3},{8,12},{9,13},{10,... | collective-permute-start | bytes 1769480 | tf_op jit(solution)/shard_map/ppermute | solution.py:42
  338.7 27.6 %collective-permute-start.90 = (bf16[2,192,768]{2,1,0:T(8,128)(2,1)S(1)}, bf16[2,192,768]{2,1,0:T(8,128)(2,1)S(1)}, u32[]{:S(2)}, u32[]{:S(2)}) collective-permute-start(bf16[2,192,768]{2,1,0:T(8,128)(2,1)S(1)} %collective-permute-done.89.refs_13_), channel_id=1, source_target_pairs={{0,1},{1,0},{2,3},{3,2},{4,5},{5,4},{6,7},{7,6},{8,9},{9,8},{10,11... | collective-permute-start | bytes 1769480 | tf_op jit(solution)/shard_map/ppermute | solution.py:42
  341.9 24.4 %collective-permute-start.104 = (bf16[2,192,768]{2,1,0:T(8,128)(2,1)S(1)}, bf16[2,192,768]{2,1,0:T(8,128)(2,1)S(1)}, u32[]{:S(2)}, u32[]{:S(2)}) collective-permute-start(bf16[2,192,768]{2,1,0:T(8,128)(2,1)S(1)} %pad_maximum_fusion.34.refs_23_), channel_id=1, source_target_pairs={{0,1},{1,0},{2,3},{3,2},{4,5},{5,4},{6,7},{7,6},{8,9},{9,8},{10,11... | collective-permute-start | bytes 1769480 | tf_op jit(solution)/shard_map/ppermute | solution.py:42
  374.6 32.9 %collective-permute-start.107 = (f16[384,768]{1,0:T(8,128)(2,1)}, f16[384,768]{1,0:T(8,128)(2,1)}, u32[]{:S(2)}, u32[]{:S(2)}) collective-permute-start(f16[384,768]{1,0:T(8,128)(2,1)} %get-tuple-element.365), channel_id=1, source_target_pairs={{0,4},{1,8},{2,16},{3,24},{4,0},{5,12},{6,20},{7,28},{8,1},{9,13},... | collective-permute-start | bytes 1769480 | tf_op jit(solution)/shard_map/ppermute | solution.py:42
  378.2 29.4 %collective-permute-start.108 = (f16[384,768]{1,0:T(8,128)(2,1)}, f16[384,768]{1,0:T(8,128)(2,1)}, u32[]{:S(2)}, u32[]{:S(2)}) collective-permute-start(f16[384,768]{1,0:T(8,128)(2,1)} %get-tuple-element.364), channel_id=1, source_target_pairs={{0,16},{1,24},{2,0},{3,8},{4,20},{5,28},{6,4},{7,12},{8,17},{9,25}... | collective-permute-start | bytes 1769480 | tf_op jit(solution)/shard_map/ppermute | solution.py:42
  379.1 27.2 %collective-permute-start.115 = (f16[384,384]{1,0:T(8,128)(2,1)}, f16[384,384]{1,0:T(8,128)(2,1)}, u32[]{:S(2)}, u32[]{:S(2)}) collective-permute-start(f16[384,384]{1,0:T(8,128)(2,1)} %get-tuple-element.398), channel_id=1, source_target_pairs={{0,6},{1,7},{2,4},{3,5},{4,2},{5,3},{6,0},{7,1},{8,14},{9,15},{10,... | collective-permute-start | bytes 884744 | tf_op jit(solution)/shard_map/ppermute | solution.py:42
  380.7 25.7 %collective-permute-start.114 = (f16[384,384]{1,0:T(8,128)(2,1)}, f16[384,384]{1,0:T(8,128)(2,1)}, u32[]{:S(2)}, u32[]{:S(2)}) collective-permute-start(f16[384,384]{1,0:T(8,128)(2,1)} %dynamic-slice_bitcast_fusion.11), channel_id=1, source_target_pairs={{0,4},{1,5},{2,6},{3,7},{4,0},{5,1},{6,2},{7,3},{8,12},{9,13},{10,... | collective-permute-start | bytes 884744 | tf_op jit(solution)/shard_map/ppermute | solution.py:42
  381.5 23.8 %collective-permute-start.111 = (f16[384,384]{1,0:T(8,128)(2,1)}, f16[384,384]{1,0:T(8,128)(2,1)}, u32[]{:S(2)}, u32[]{:S(2)}) collective-permute-start(f16[384,384]{1,0:T(8,128)(2,1)} %get-tuple-element.399), channel_id=1, source_target_pairs={{0,2},{1,3},{2,0},{3,1},{4,6},{5,7},{6,4},{7,5},{8,10},{9,11},{10,... | collective-permute-start | bytes 884744 | tf_op jit(solution)/shard_map/ppermute | solution.py:42
  410.2 42.2 %collective-permute-start.110 = (f16[384,768]{1,0:T(8,128)(2,1)S(1)}, f16[384,768]{1,0:T(8,128)(2,1)S(1)}, u32[]{:S(2)}, u32[]{:S(2)}) collective-permute-start(f16[384,768]{1,0:T(8,128)(2,1)S(1)} %get-tuple-element.360), channel_id=1, source_target_pairs={{0,24},{1,16},{2,8},{3,0},{4,28},{5,20},{6,12},{7,4},{8,25},{9,17}... | collective-permute-start | bytes 1769480 | tf_op jit(solution)/shard_map/ppermute | solution.py:42
  416.6 33.2 %collective-permute-start.109 = (f16[384,768]{1,0:T(8,128)(2,1)S(1)}, f16[384,768]{1,0:T(8,128)(2,1)S(1)}, u32[]{:S(2)}, u32[]{:S(2)}) collective-permute-start(f16[384,768]{1,0:T(8,128)(2,1)S(1)} %get-tuple-element.361), channel_id=1, source_target_pairs={{0,8},{1,0},{2,24},{3,16},{4,12},{5,4},{6,28},{7,20},{8,9},{9,1},{... | collective-permute-start | bytes 1769480 | tf_op jit(solution)/shard_map/ppermute | solution.py:42
  419.3 18.6 %collective-permute-start.116 = (f16[384,384]{1,0:T(8,128)(2,1)S(1)}, f16[384,384]{1,0:T(8,128)(2,1)S(1)}, u32[]{:S(2)}, u32[]{:S(2)}) collective-permute-start(f16[384,384]{1,0:T(8,128)(2,1)S(1)} %get-tuple-element.392), channel_id=1, source_target_pairs={{0,5},{1,4},{2,7},{3,6},{4,1},{5,0},{6,3},{7,2},{8,13},{9,12},{10,... | collective-permute-start | bytes 884744 | tf_op jit(solution)/shard_map/ppermute | solution.py:42
  (85 other events, 1793.7 us)

commit v8 on v7

--- a/solution.py
+++ b/solution.py
@@ -301,7 +301,7 @@
             jax.ShapeDtypeStruct((calls, rows, strip), jnp.float32),
             jax.ShapeDtypeStruct((calls, strip, rows), jnp.float32),
         ],
-        compiler_params=pltpu.CompilerParams(vmem_limit_bytes=40 << 20),
+        compiler_params=pltpu.CompilerParams(vmem_limit_bytes=32 << 20),
         cost_estimate=pl.CostEstimate(
             flops=2 * calls * sum(groups) * rows * tile * strip,
             bytes_accessed=2 * (calls * sum(groups) * rows * tile + len(parts) * majors * part * strip),

time: 467 us -> 463 us (level)
  waiting for transfers between devices: 231 us -> 236 us
  transfers between devices with their start and end apart: 79 -> 79, of which waited for: 28 -> 29; matrix products, arithmetic and copies ran while one was open for 13% -> 12% of each run, Pallas kernels for 3% -> 3%
where the time goes in v8:
time: 463 us; the launch traced here: 454 us
  waiting for transfers between devices  236 us (51%)
  starting transfers between devices  103 us (22%)
  other arithmetic  48.9 us (11%)
  local copies, waits for them, and re-layouts  36.1 us (8%)
  Pallas kernels  25.6 us (6%)
    ppermute x70, waiting for transfers between devices, send(): received = lax.ppermute(value, AXES, pairs)  213 us
    ppermute x70, starting transfers between devices, send(): received = lax.ppermute(value, AXES, pairs)  82.5 us
    pallas_call x4, Pallas kernels, products(): pl.pallas_call(lambda *refs: product_kernel(groups, pieces, lanes, calls,...  25.6 us
    ppermute x9, waiting for transfers between devices, gather_bands(): moving = lax.ppermute(moving, AXES, pairs)  22.6 us
    ppermute x9, starting transfers between devices, gather_bands(): moving = lax.ppermute(moving, AXES, pairs)  20.9 us
  transfers between devices with their start and end apart: 79, of which 29 were waited for; matrix products, arithmetic and copies ran while one was open for 12% of the time, Pallas kernels for 3%

profile of v8, /device:TPU:25, one launch (start us, length us, event | category | flops | bytes accessed | tf_op | source)
XLA Modules:
  0.0 454.1 jit_solution(9715162292147508283)
XLA Ops:
  3.7 166.9 %conditional.2 = (bf16[4,1,192,768]{3,2,1,0:T(8,128)(2,1)S(1)}, bf16[4,1,192,768]{3,2,1,0:T(8,128)(2,1)}, bf16[4,1,208,768]{3,2,1,0:T(8,128)(2,1)}, bf16[4,1,208...) conditional(s32[]{:T(128)} %convert_element_type.71, ...), branch_computations={%region_2.6_spmd, %region_6.12_spmd} | conditional | flops 26185744 | bytes 215436768
  4.0 5.1 %copy.32 = bf16[768,4,768]{2,0,1:T(8,128)(2,1)} copy(bf16[768,4,768]{2,1,0:T(4,128)(2,1)} %get-tuple-element.296) | data formatting | bytes 9437184 | tf_op jit(solution)/shard_map
  10.3 2.6 convert_element_type.51
  35.1 4.8 %collective-permute-start.41 = (bf16[2,1,192,768]{3,2,1,0:T(8,128)(2,1)}, bf16[2,1,192,768]{3,2,1,0:T(8,128)(2,1)S(1)}, u32[]{:S(2)}, u32[]{:S(2)}) collective-permute-start(bf16[2,1,192,768]{3,2,1,0:T(8,128)(2,1)} %collective-permute-done.40), channel_id=1, source_target_pairs={{0,8},{1,9},{2,10},{3,11},{4,12},{5,13},{6,14},{7,15},{8,0},{9,1},... | collective-permute-start | bytes 1769480 | tf_op jit(solution)/shard_map/cond/branch_1_fun/ppermute | solution.py:99
  40.0 7.7 %collective-permute-done.53 = bf16[768,768]{1,0:T(8,128)(2,1)} collective-permute-done((bf16[768,768]{1,0:T(8,128)(2,1)}, bf16[768,768]{1,0:T(8,128)(2,1)}, u32[]{:S(2)}, u32[]{:S(2)}) %collective-permute-start.53) | collective-permute-done | bytes 1179680 | tf_op jit(solution)/shard_map/cond/branch_1_fun/ppermute | solution.py:42
  49.5 4.0 collective-permute-start.47
  54.3 2.5 collective-permute-start.50
  56.7 5.9 %collective-permute-done.41 = bf16[2,1,192,768]{3,2,1,0:T(8,128)(2,1)S(1)} collective-permute-done((bf16[2,1,192,768]{3,2,1,0:T(8,128)(2,1)}, bf16[2,1,192,768]{3,2,1,0:T(8,128)(2,1)S(1)}, u32[]{:S(2)}, u32[]{:S(2)}) %collective-permute-start.41) | collective-permute-done | bytes 589856 | tf_op jit(solution)/shard_map/cond/branch_1_fun/ppermute | solution.py:99
  65.0 14.4 %collective-permute-done.47 = bf16[2,1,208,768]{3,2,1,0:T(8,128)(2,1)S(1)} collective-permute-done((bf16[2,1,208,768]{3,2,1,0:T(8,128)(2,1)S(1)}, bf16[2,1,208,768]{3,2,1,0:T(8,128)(2,1)S(1)}, u32[]{:S(2)}, u32[]{:S(2)}) %collective-permute-start.47) | collective-permute-done | bytes 639008 | tf_op jit(solution)/shard_map/cond/branch_1_fun/ppermute | solution.py:99
  85.4 4.9 %collective-permute-start.51 = (bf16[1,2,192,768]{3,2,1,0:T(8,128)(2,1)S(1)}, bf16[1,2,192,768]{3,2,1,0:T(8,128)(2,1)S(1)}, u32[]{:S(2)}, u32[]{:S(2)}) collective-permute-start(bf16[1,2,192,768]{3,2,1,0:T(8,128)(2,1)S(1)} %collective-permute-done.50), channel_id=1, source_target_pairs={{0,8},{1,9},{2,10},{3,11},{4,12},{5,13},{6,14},{7,15},{8,0},{9,1},... | collective-permute-start | bytes 1769480 | tf_op jit(solution)/shard_map/cond/branch_1_fun/ppermute | solution.py:99
  92.9 6.9 %collective-permute-done.60 = bf16[192,768]{1,0:T(8,128)(2,1)S(1)} collective-permute-done((bf16[192,768]{1,0:T(8,128)(2,1)S(1)}, bf16[192,768]{1,0:T(8,128)(2,1)S(1)}, u32[]{:S(2)}, u32[]{:S(2)}) %collective-permute-start.60) | collective-permute-done | bytes 294944 | tf_op jit(solution)/shard_map/cond/branch_1_fun/ppermute | solution.py:42
  102.5 14.6 %collective-permute-done.48 = bf16[4,1,208,768]{3,2,1,0:T(8,128)(2,1)S(1)} collective-permute-done((bf16[4,1,208,768]{3,2,1,0:T(8,128)(2,1)S(1)}, bf16[4,1,208,768]{3,2,1,0:T(8,128)(2,1)S(1)}, u32[]{:S(2)}, u32[]{:S(2)}) %collective-permute-start.48) | collective-permute-done | bytes 1277984 | tf_op jit(solution)/shard_map/cond/branch_1_fun/ppermute | solution.py:42
  121.6 7.5 %collective-permute-start.61 = (bf16[2,192,768]{2,1,0:T(8,128)(2,1)S(1)}, bf16[2,192,768]{2,1,0:T(8,128)(2,1)S(1)}, u32[]{:S(2)}, u32[]{:S(2)}) collective-permute-start(bf16[2,192,768]{2,1,0:T(8,128)(2,1)S(1)} %pad_maximum_fusion.21), channel_id=1, source_target_pairs={{0,1},{1,0},{2,3},{3,2},{4,5},{5,4},{6,7},{7,6},{8,9},{9,8},{10,11... | collective-permute-start | bytes 1769480 | tf_op jit(solution)/shard_map/cond/branch_1_fun/ppermute | solution.py:42
  129.1 6.4 %collective-permute-done.69 = bf16[192,768]{1,0:T(8,128)(2,1)S(1)} collective-permute-done((bf16[192,768]{1,0:T(8,128)(2,1)S(1)}, bf16[192,768]{1,0:T(8,128)(2,1)S(1)}, u32[]{:S(2)}, u32[]{:S(2)}) %collective-permute-start.69) | collective-permute-done | bytes 294944 | tf_op jit(solution)/shard_map/cond/branch_1_fun/ppermute | solution.py:42
  140.6 10.2 %collective-permute-done.52 = bf16[1,2,192,768]{3,2,1,0:T(8,128)(2,1)S(1)} collective-permute-done((bf16[1,2,192,768]{3,2,1,0:T(8,128)(2,1)S(1)}, bf16[1,2,192,768]{3,2,1,0:T(8,128)(2,1)S(1)}, u32[]{:S(2)}, u32[]{:S(2)}) %collective-permute-start.52) | collective-permute-done | bytes 589856 | tf_op jit(solution)/shard_map/cond/branch_1_fun/ppermute | solution.py:42
  152.0 3.0 collective-permute-start.68
  155.0 9.7 %collective-permute-done.72 = bf16[2,192,768]{2,1,0:T(8,128)(2,1)} collective-permute-done((bf16[2,192,768]{2,1,0:T(8,128)(2,1)}, bf16[2,192,768]{2,1,0:T(8,128)(2,1)}, u32[]{:S(2)}, u32[]{:S(2)}) %collective-permute-start.72) | collective-permute-done | bytes 589856 | tf_op jit(solution)/shard_map/cond/branch_1_fun/ppermute | solution.py:42
  172.8 7.3 %shard_map.253 = (f32[2,384,768]{2,1,0:T(8,128)S(1)}, f32[2,768,384]{2,1,0:T(8,128)S(1)}) custom-call(s32[4]{0:T(128)S(1)} %pad_add_fusion.refs_0_, s32[16]{0:T(128)S(1)} %copy-done.2, s32[32]{0:T(128)S(1)} %reshape.105.refs_2_, s32[8]{0:T(128)S(1)} %copy-done, f32[1]{0:T(128)} %get-tuple-element.210.refs_4_, ...), custom_call_target="tpu_custom_call" | custom-call | flops 3623878656 | bytes 14155776 | tf_op jit(solution)/shard_map/pallas_call | solution.py:284
  185.8 3.0 collective-permute-start.82
  189.9 8.0 %shard_map.254 = (f32[2,384,768]{2,1,0:T(8,128)S(1)}, f32[2,768,384]{2,1,0:T(8,128)S(1)}) custom-call(s32[4]{0:T(128)S(1)} %pad_add_fusion.refs_0_, s32[16]{0:T(128)S(1)} %copy-done.2, s32[32]{0:T(128)S(1)} %reshape.105.refs_2_, s32[8]{0:T(128)S(1)} %copy-done, f32[1]{0:T(128)} %get-tuple-element.210.refs_4_, ...), custom_call_target="tpu_custom_call" | custom-call | flops 3623878656 | bytes 14155776 | tf_op jit(solution)/shard_map/pallas_call | solution.py:284
  199.3 2.8 convert_element_type.74
  204.7 9.0 %collective-permute-done.78 = f16[384,384]{1,0:T(8,128)(2,1)} collective-permute-done((f16[384,384]{1,0:T(8,128)(2,1)}, f16[384,384]{1,0:T(8,128)(2,1)}, u32[]{:S(2)}, u32[]{:S(2)}) %collective-permute-start.78) | collective-permute-done | bytes 294944 | tf_op jit(solution)/shard_map/ppermute | solution.py:42
  218.0 4.1 collective-permute-start.77
  222.0 2.5 collective-permute-start.76
  227.8 7.2 %collective-permute-done.84 = f16[384,384]{1,0:T(8,128)(2,1)S(1)} collective-permute-done((f16[384,384]{1,0:T(8,128)(2,1)S(1)}, f16[384,384]{1,0:T(8,128)(2,1)S(1)}, u32[]{:S(2)}, u32[]{:S(2)}) %collective-permute-start.84) | collective-permute-done | bytes 294944 | tf_op jit(solution)/shard_map/ppermute | solution.py:42
  235.0 8.6 %collective-permute-done.83 = f16[384,384]{1,0:T(8,128)(2,1)S(1)} collective-permute-done((f16[384,384]{1,0:T(8,128)(2,1)S(1)}, f16[384,384]{1,0:T(8,128)(2,1)S(1)}, u32[]{:S(2)}, u32[]{:S(2)}) %collective-permute-start.83) | collective-permute-done | bytes 294944 | tf_op jit(solution)/shard_map/ppermute | solution.py:42
  244.0 11.4 %collective-permute-done.76 = f16[384,768]{1,0:T(8,128)(2,1)S(1)} collective-permute-done((f16[384,768]{1,0:T(8,128)(2,1)S(1)}, f16[384,768]{1,0:T(8,128)(2,1)S(1)}, u32[]{:S(2)}, u32[]{:S(2)}) %collective-permute-start.76) | collective-permute-done | bytes 589856 | tf_op jit(solution)/shard_map/ppermute | solution.py:42
  255.4 2.3 broadcast_select_fusion.21
  268.2 7.3 %collective-permute-done.85 = bf16[384,768]{1,0:T(8,128)(2,1)} collective-permute-done((bf16[384,768]{1,0:T(8,128)(2,1)}, bf16[384,768]{1,0:T(8,128)(2,1)}, u32[]{:S(2)}, u32[]{:S(2)}) %collective-permute-start.85) | collective-permute-done | bytes 589856 | tf_op jit(solution)/shard_map/ppermute | solution.py:42
  279.6 5.5 %collective-permute-done.86 = bf16[192,768]{1,0:T(8,128)(2,1)S(1)} collective-permute-done((bf16[192,768]{1,0:T(8,128)(2,1)S(1)}, bf16[192,768]{1,0:T(8,128)(2,1)S(1)}, u32[]{:S(2)}, u32[]{:S(2)}) %collective-permute-start.86) | collective-permute-done | bytes 294944 | tf_op jit(solution)/shard_map/ppermute | solution.py:42
  286.2 9.6 %collective-permute-start.92 = (bf16[192,768]{1,0:T(8,128)(2,1)S(1)}, bf16[192,768]{1,0:T(8,128)(2,1)S(1)}, u32[]{:S(2)}, u32[]{:S(2)}) collective-permute-start(bf16[192,768]{1,0:T(8,128)(2,1)S(1)} %get-tuple-element.243), channel_id=1, source_target_pairs={{0,16},{1,24},{2,18},{3,26},{4,20},{5,28},{6,22},{7,30},{8,17},{9,... | collective-permute-start | bytes 884744 | tf_op jit(solution)/shard_map/ppermute | solution.py:42
  296.9 15.6 %collective-permute-done.92 = bf16[192,768]{1,0:T(8,128)(2,1)S(1)} collective-permute-done((bf16[192,768]{1,0:T(8,128)(2,1)S(1)}, bf16[192,768]{1,0:T(8,128)(2,1)S(1)}, u32[]{:S(2)}, u32[]{:S(2)}) %collective-permute-start.92) | collective-permute-done | bytes 294944 | tf_op jit(solution)/shard_map/ppermute | solution.py:42
  315.1 2.4 collective-permute-start.88
  317.6 13.7 %collective-permute-done.98 = bf16[192,768]{1,0:T(8,128)(2,1)S(1)} collective-permute-done((bf16[192,768]{1,0:T(8,128)(2,1)S(1)}, bf16[192,768]{1,0:T(8,128)(2,1)S(1)}, u32[]{:S(2)}, u32[]{:S(2)}) %collective-permute-start.98) | collective-permute-done | bytes 294944 | tf_op jit(solution)/shard_map/ppermute | solution.py:42
  332.1 5.7 %collective-permute-done.103 = bf16[192,768]{1,0:T(8,128)(2,1)S(1)} collective-permute-done((bf16[192,768]{1,0:T(8,128)(2,1)S(1)}, bf16[192,768]{1,0:T(8,128)(2,1)S(1)}, u32[]{:S(2)}, u32[]{:S(2)}) %collective-permute-start.103) | collective-permute-done | bytes 294944 | tf_op jit(solution)/shard_map/ppermute | solution.py:42
  337.8 4.8 %collective-permute-start.100 = (bf16[2,192,768]{2,1,0:T(8,128)(2,1)S(1)}, bf16[2,192,768]{2,1,0:T(8,128)(2,1)S(1)}, u32[]{:S(2)}, u32[]{:S(2)}) collective-permute-start(bf16[2,192,768]{2,1,0:T(8,128)(2,1)S(1)} %pad_maximum_fusion.33.refs_19_), channel_id=1, source_target_pairs={{0,4},{1,5},{2,6},{3,7},{4,0},{5,1},{6,2},{7,3},{8,12},{9,13},{10,... | collective-permute-start | bytes 1769480 | tf_op jit(solution)/shard_map/ppermute | solution.py:42
  343.6 12.9 %collective-permute-done.100.refs_21_ = bf16[2,192,768]{2,1,0:T(8,128)(2,1)S(1)} collective-permute-done((bf16[2,192,768]{2,1,0:T(8,128)(2,1)S(1)}, bf16[2,192,768]{2,1,0:T(8,128)(2,1)S(1)}, u32[]{:S(2)}, u32[]{:S(2)}) %collective-permute-start.100) | collective-permute-done | bytes 589856 | tf_op jit(solution)/shard_map/ppermute | solution.py:42
  357.1 9.6 %collective-permute-done.105.refs_25_ = bf16[2,192,768]{2,1,0:T(8,128)(2,1)S(1)} collective-permute-done((bf16[2,192,768]{2,1,0:T(8,128)(2,1)S(1)}, bf16[2,192,768]{2,1,0:T(8,128)(2,1)S(1)}, u32[]{:S(2)}, u32[]{:S(2)}) %collective-permute-start.105) | collective-permute-done | bytes 589856 | tf_op jit(solution)/shard_map/ppermute | solution.py:42
  368.7 4.9 %shard_map.255 = (f32[2,384,768]{2,1,0:T(8,128)S(1)}, f32[2,768,384]{2,1,0:T(8,128)S(1)}) custom-call(s32[4]{0:T(128)S(1)} %pad_add_fusion.refs_0_, s32[16]{0:T(128)S(1)} %copy-done.2, s32[32]{0:T(128)S(1)} %reshape.105.refs_2_, s32[8]{0:T(128)S(1)} %copy-done, f32[1]{0:T(128)} %get-tuple-element.241.refs_4_, ...), custom_call_target="tpu_custom_call" | custom-call | flops 3623878656 | bytes 14155776 | tf_op jit(solution)/shard_map/pallas_call | solution.py:284
  374.4 3.9 collective-permute-start.107
  381.4 5.4 %shard_map.256 = (f32[2,384,768]{2,1,0:T(8,128)S(1)}, f32[2,768,384]{2,1,0:T(8,128)S(1)}) custom-call(s32[4]{0:T(128)S(1)} %pad_add_fusion.refs_0_, s32[16]{0:T(128)S(1)} %copy-done.2, s32[32]{0:T(128)S(1)} %reshape.105.refs_2_, s32[8]{0:T(128)S(1)} %copy-done, f32[1]{0:T(128)} %get-tuple-element.241.refs_4_, ...), custom_call_target="tpu_custom_call" | custom-call | flops 3623878656 | bytes 14155776 | tf_op jit(solution)/shard_map/pallas_call | solution.py:284
  387.1 17.7 %collective-permute-done.111 = f16[384,384]{1,0:T(8,128)(2,1)S(1)} collective-permute-done((f16[384,384]{1,0:T(8,128)(2,1)S(1)}, f16[384,384]{1,0:T(8,128)(2,1)S(1)}, u32[]{:S(2)}, u32[]{:S(2)}) %collective-permute-start.111) | collective-permute-done | bytes 294944 | tf_op jit(solution)/shard_map/ppermute | solution.py:42
  408.0 4.6 %collective-permute-start.110 = (f16[384,768]{1,0:T(8,128)(2,1)S(1)}, f16[384,768]{1,0:T(8,128)(2,1)S(1)}, u32[]{:S(2)}, u32[]{:S(2)}) collective-permute-start(f16[384,768]{1,0:T(8,128)(2,1)S(1)} %get-tuple-element.360), channel_id=1, source_target_pairs={{0,24},{1,16},{2,8},{3,0},{4,28},{5,20},{6,12},{7,4},{8,25},{9,17}... | collective-permute-start | bytes 1769480 | tf_op jit(solution)/shard_map/ppermute | solution.py:42
  412.6 4.1 collective-permute-start.109
  417.9 9.7 %collective-permute-done.117 = f16[384,384]{1,0:T(8,128)(2,1)S(1)} collective-permute-done((f16[384,384]{1,0:T(8,128)(2,1)S(1)}, f16[384,384]{1,0:T(8,128)(2,1)S(1)}, u32[]{:S(2)}, u32[]{:S(2)}) %collective-permute-start.117) | collective-permute-done | bytes 294944 | tf_op jit(solution)/shard_map/ppermute | solution.py:42
  427.7 7.6 %collective-permute-done.116 = f16[384,384]{1,0:T(8,128)(2,1)S(1)} collective-permute-done((f16[384,384]{1,0:T(8,128)(2,1)S(1)}, f16[384,384]{1,0:T(8,128)(2,1)S(1)}, u32[]{:S(2)}, u32[]{:S(2)}) %collective-permute-start.116) | collective-permute-done | bytes 294944 | tf_op jit(solution)/shard_map/ppermute | solution.py:42
  435.7 10.9 %collective-permute-done.109 = f16[384,768]{1,0:T(8,128)(2,1)S(1)} collective-permute-done((f16[384,768]{1,0:T(8,128)(2,1)S(1)}, f16[384,768]{1,0:T(8,128)(2,1)S(1)}, u32[]{:S(2)}, u32[]{:S(2)}) %collective-permute-start.109) | collective-permute-done | bytes 589856 | tf_op jit(solution)/shard_map/ppermute | solution.py:42
  450.2 3.7 divide_subtract_fusion
  (360 shorter events, 113.4 us)
Async XLA Ops:
  20.5 27.2 %collective-permute-start.53 = (bf16[768,768]{1,0:T(8,128)(2,1)}, bf16[768,768]{1,0:T(8,128)(2,1)}, u32[]{:S(2)}, u32[]{:S(2)}) collective-permute-start(bf16[768,768]{1,0:T(8,128)(2,1)} %pad_maximum_fusion.17), channel_id=1, source_target_pairs={{0,2},{1,3},{2,0},{3,1},{4,6},{5,7},{6,4},{7,5},{8,10},{9,11},{10,... | collective-permute-start | bytes 3538952 | tf_op jit(solution)/shard_map/cond/branch_1_fun/ppermute | solution.py:42
  32.0 17.5 %collective-permute-start.46 = (bf16[2,1,208,768]{3,2,1,0:T(8,128)(2,1)S(1)}, bf16[2,1,208,768]{3,2,1,0:T(8,128)(2,1)S(1)}, u32[]{:S(2)}, u32[]{:S(2)}) collective-permute-start(bf16[2,1,208,768]{3,2,1,0:T(8,128)(2,1)S(1)} %pad_maximum_fusion.18), channel_id=1, source_target_pairs={{0,1},{1,0},{2,3},{3,2},{4,5},{5,4},{6,7},{7,6},{8,16},{9,17},{10,... | collective-permute-start | bytes 1916936 | tf_op jit(solution)/shard_map/cond/branch_1_fun/ppermute | solution.py:99
  34.9 18.6 %collective-permute-start.49 = (bf16[1,2,192,768]{3,2,1,0:T(8,128)(2,1)S(1)}, bf16[1,2,192,768]{3,2,1,0:T(8,128)(2,1)S(1)}, u32[]{:S(2)}, u32[]{:S(2)}) collective-permute-start(bf16[1,2,192,768]{3,2,1,0:T(8,128)(2,1)S(1)} %maximum_bitcast_fusion.2), channel_id=1, source_target_pairs={{0,8},{1,9},{2,10},{3,11},{4,12},{5,13},{6,14},{7,15},{8,0},{9,1},... | collective-permute-start | bytes 1769480 | tf_op jit(solution)/shard_map/cond/branch_1_fun/ppermute | solution.py:99
  35.1 27.4 %collective-permute-start.41 = (bf16[2,1,192,768]{3,2,1,0:T(8,128)(2,1)}, bf16[2,1,192,768]{3,2,1,0:T(8,128)(2,1)S(1)}, u32[]{:S(2)}, u32[]{:S(2)}) collective-permute-start(bf16[2,1,192,768]{3,2,1,0:T(8,128)(2,1)} %collective-permute-done.40), channel_id=1, source_target_pairs={{0,8},{1,9},{2,10},{3,11},{4,12},{5,13},{6,14},{7,15},{8,0},{9,1},... | collective-permute-start | bytes 1769480 | tf_op jit(solution)/shard_map/cond/branch_1_fun/ppermute | solution.py:99
  49.5 29.9 %collective-permute-start.47 = (bf16[2,1,208,768]{3,2,1,0:T(8,128)(2,1)S(1)}, bf16[2,1,208,768]{3,2,1,0:T(8,128)(2,1)S(1)}, u32[]{:S(2)}, u32[]{:S(2)}) collective-permute-start(bf16[2,1,208,768]{3,2,1,0:T(8,128)(2,1)S(1)} %collective-permute-done.46), channel_id=1, source_target_pairs={{0,8},{1,9},{2,10},{3,11},{4,12},{5,13},{6,14},{7,15},{8,0},{9,1},... | collective-permute-start | bytes 1916936 | tf_op jit(solution)/shard_map/cond/branch_1_fun/ppermute | solution.py:99
  54.3 31.1 %collective-permute-start.50 = (bf16[1,2,192,768]{3,2,1,0:T(8,128)(2,1)S(1)}, bf16[1,2,192,768]{3,2,1,0:T(8,128)(2,1)S(1)}, u32[]{:S(2)}, u32[]{:S(2)}) collective-permute-start(bf16[1,2,192,768]{3,2,1,0:T(8,128)(2,1)S(1)} %broadcast_select_fusion.8), channel_id=1, source_target_pairs={{0,1},{1,0},{2,3},{3,2},{4,5},{5,4},{6,7},{7,6},{8,16},{9,17},{10,... | collective-permute-start | bytes 1769480 | tf_op jit(solution)/shard_map/cond/branch_1_fun/ppermute | solution.py:99
  63.4 27.5 %collective-permute-start.42 = (bf16[4,1,192,768]{3,2,1,0:T(8,128)(2,1)S(1)}, bf16[4,1,192,768]{3,2,1,0:T(8,128)(2,1)S(1)}, u32[]{:S(2)}, u32[]{:S(2)}) collective-permute-start(bf16[4,1,192,768]{3,2,1,0:T(8,128)(2,1)S(1)} %pad_maximum_fusion.16), channel_id=1, source_target_pairs={{0,2},{1,3},{2,0},{3,1},{4,6},{5,7},{6,4},{7,5},{8,10},{9,11},{10,... | collective-permute-start | bytes 3538952 | tf_op jit(solution)/shard_map/cond/branch_1_fun/ppermute | solution.py:42
  65.0 20.2 %collective-permute-start.55 = (bf16[192,768]{1,0:T(8,128)(2,1)S(1)}, bf16[192,768]{1,0:T(8,128)(2,1)S(1)}, u32[]{:S(2)}, u32[]{:S(2)}) collective-permute-start(bf16[192,768]{1,0:T(8,128)(2,1)S(1)} %get-tuple-element.154), channel_id=1, source_target_pairs={{0,16},{1,24},{2,18},{3,26},{4,20},{5,28},{6,22},{7,30},{8,17},{9,... | collective-permute-start | bytes 884744 | tf_op jit(solution)/shard_map/cond/branch_1_fun/ppermute | solution.py:42
  80.3 36.8 %collective-permute-start.48 = (bf16[4,1,208,768]{3,2,1,0:T(8,128)(2,1)S(1)}, bf16[4,1,208,768]{3,2,1,0:T(8,128)(2,1)S(1)}, u32[]{:S(2)}, u32[]{:S(2)}) collective-permute-start(bf16[4,1,208,768]{3,2,1,0:T(8,128)(2,1)S(1)} %pad_maximum_fusion.15), channel_id=1, source_target_pairs={{0,2},{1,3},{2,0},{3,1},{4,6},{5,7},{6,4},{7,5},{8,10},{9,11},{10,... | collective-permute-start | bytes 3833864 | tf_op jit(solution)/shard_map/cond/branch_1_fun/ppermute | solution.py:42
  85.4 32.1 %collective-permute-start.51 = (bf16[1,2,192,768]{3,2,1,0:T(8,128)(2,1)S(1)}, bf16[1,2,192,768]{3,2,1,0:T(8,128)(2,1)S(1)}, u32[]{:S(2)}, u32[]{:S(2)}) collective-permute-start(bf16[1,2,192,768]{3,2,1,0:T(8,128)(2,1)S(1)} %collective-permute-done.50), channel_id=1, source_target_pairs={{0,8},{1,9},{2,10},{3,11},{4,12},{5,13},{6,14},{7,15},{8,0},{9,1},... | collective-permute-start | bytes 1769480 | tf_op jit(solution)/shard_map/cond/branch_1_fun/ppermute | solution.py:99
  92.8 28.9 %collective-permute-start.57 = (bf16[2,192,768]{2,1,0:T(8,128)(2,1)S(1)}, bf16[2,192,768]{2,1,0:T(8,128)(2,1)S(1)}, u32[]{:S(2)}, u32[]{:S(2)}) collective-permute-start(bf16[2,192,768]{2,1,0:T(8,128)(2,1)S(1)} %pad_maximum_fusion.20), channel_id=1, source_target_pairs={{0,4},{1,5},{2,6},{3,7},{4,0},{5,1},{6,2},{7,3},{8,12},{9,13},{10,... | collective-permute-start | bytes 1769480 | tf_op jit(solution)/shard_map/cond/branch_1_fun/ppermute | solution.py:42
  99.7 37.9 %collective-permute-start.56 = (bf16[2,192,768]{2,1,0:T(8,128)(2,1)S(1)}, bf16[2,192,768]{2,1,0:T(8,128)(2,1)S(1)}, u32[]{:S(2)}, u32[]{:S(2)}) collective-permute-start(bf16[2,192,768]{2,1,0:T(8,128)(2,1)S(1)} %pad_maximum_fusion.20), channel_id=1, source_target_pairs={{0,1},{1,0},{2,3},{3,2},{4,5},{5,4},{6,7},{7,6},{8,9},{9,8},{10,11... | collective-permute-start | bytes 1769480 | tf_op jit(solution)/shard_map/cond/branch_1_fun/ppermute | solution.py:42
  100.6 20.0 %collective-permute-start.65 = (bf16[192,768]{1,0:T(8,128)(2,1)S(1)}, bf16[192,768]{1,0:T(8,128)(2,1)S(1)}, u32[]{:S(2)}, u32[]{:S(2)}) collective-permute-start(bf16[192,768]{1,0:T(8,128)(2,1)S(1)} %get-tuple-element.160), channel_id=1, source_target_pairs={{0,16},{1,24},{2,18},{3,26},{4,20},{5,28},{6,22},{7,30},{8,17},{9,... | collective-permute-start | bytes 884744 | tf_op jit(solution)/shard_map/cond/branch_1_fun/ppermute | solution.py:42
  117.1 21.7 %collective-permute-start.62 = (bf16[2,192,768]{2,1,0:T(8,128)(2,1)S(1)}, bf16[2,192,768]{2,1,0:T(8,128)(2,1)}, u32[]{:S(2)}, u32[]{:S(2)}) collective-permute-start(bf16[2,192,768]{2,1,0:T(8,128)(2,1)S(1)} %pad_maximum_fusion.21), channel_id=1, source_target_pairs={{0,4},{1,5},{2,6},{3,7},{4,0},{5,1},{6,2},{7,3},{8,12},{9,13},{10,... | collective-permute-start | bytes 1769480 | tf_op jit(solution)/shard_map/cond/branch_1_fun/ppermute | solution.py:42
  117.4 18.1 %collective-permute-start.69 = (bf16[192,768]{1,0:T(8,128)(2,1)S(1)}, bf16[192,768]{1,0:T(8,128)(2,1)S(1)}, u32[]{:S(2)}, u32[]{:S(2)}) collective-permute-start(bf16[192,768]{1,0:T(8,128)(2,1)S(1)} %get-tuple-element.162), channel_id=1, source_target_pairs={{0,4},{1,8},{2,6},{3,10},{4,0},{5,12},{6,2},{7,14},{8,1},{9,13},{1... | collective-permute-start | bytes 884744 | tf_op jit(solution)/shard_map/cond/branch_1_fun/ppermute | solution.py:42
  121.6 17.5 %collective-permute-start.61 = (bf16[2,192,768]{2,1,0:T(8,128)(2,1)S(1)}, bf16[2,192,768]{2,1,0:T(8,128)(2,1)S(1)}, u32[]{:S(2)}, u32[]{:S(2)}) collective-permute-start(bf16[2,192,768]{2,1,0:T(8,128)(2,1)S(1)} %pad_maximum_fusion.21), channel_id=1, source_target_pairs={{0,1},{1,0},{2,3},{3,2},{4,5},{5,4},{6,7},{7,6},{8,9},{9,8},{10,11... | collective-permute-start | bytes 1769480 | tf_op jit(solution)/shard_map/cond/branch_1_fun/ppermute | solution.py:42
  138.8 25.9 %collective-permute-start.72 = (bf16[2,192,768]{2,1,0:T(8,128)(2,1)}, bf16[2,192,768]{2,1,0:T(8,128)(2,1)}, u32[]{:S(2)}, u32[]{:S(2)}) collective-permute-start(bf16[2,192,768]{2,1,0:T(8,128)(2,1)} %pad_maximum_fusion.23), channel_id=1, source_target_pairs={{0,4},{1,5},{2,6},{3,7},{4,0},{5,1},{6,2},{7,3},{8,12},{9,13},{10,... | collective-permute-start | bytes 1769480 | tf_op jit(solution)/shard_map/cond/branch_1_fun/ppermute | solution.py:42
  139.1 29.9 %collective-permute-start.63 = (bf16[2,192,768]{2,1,0:T(8,128)(2,1)}, bf16[2,192,768]{2,1,0:T(8,128)(2,1)}, u32[]{:S(2)}, u32[]{:S(2)}) collective-permute-start(bf16[2,192,768]{2,1,0:T(8,128)(2,1)} %collective-permute-done.62), channel_id=1, source_target_pairs={{0,1},{1,0},{2,3},{3,2},{4,5},{5,4},{6,7},{7,6},{8,9},{9,8},{10,11... | collective-permute-start | bytes 1769480 | tf_op jit(solution)/shard_map/cond/branch_1_fun/ppermute | solution.py:42
  140.5 28.5 %collective-permute-start.66 = (bf16[2,192,768]{2,1,0:T(8,128)(2,1)}, bf16[2,192,768]{2,1,0:T(8,128)(2,1)}, u32[]{:S(2)}, u32[]{:S(2)}) collective-permute-start(bf16[2,192,768]{2,1,0:T(8,128)(2,1)} %pad_maximum_fusion.22), channel_id=1, source_target_pairs={{0,1},{1,0},{2,3},{3,2},{4,5},{5,4},{6,7},{7,6},{8,9},{9,8},{10,11... | collective-permute-start | bytes 1769480 | tf_op jit(solution)/shard_map/cond/branch_1_fun/ppermute | solution.py:42
  150.7 18.3 %collective-permute-start.71 = (bf16[2,192,768]{2,1,0:T(8,128)(2,1)}, bf16[2,192,768]{2,1,0:T(8,128)(2,1)}, u32[]{:S(2)}, u32[]{:S(2)}) collective-permute-start(bf16[2,192,768]{2,1,0:T(8,128)(2,1)} %pad_maximum_fusion.23), channel_id=1, source_target_pairs={{0,1},{1,0},{2,3},{3,2},{4,5},{5,4},{6,7},{7,6},{8,9},{9,8},{10,11... | collective-permute-start | bytes 1769480 | tf_op jit(solution)/shard_map/cond/branch_1_fun/ppermute | solution.py:42
  152.0 17.0 %collective-permute-start.68 = (bf16[2,192,768]{2,1,0:T(8,128)(2,1)}, bf16[2,192,768]{2,1,0:T(8,128)(2,1)}, u32[]{:S(2)}, u32[]{:S(2)}) collective-permute-start(bf16[2,192,768]{2,1,0:T(8,128)(2,1)} %collective-permute-done.67), channel_id=1, source_target_pairs={{0,1},{1,0},{2,3},{3,2},{4,5},{5,4},{6,7},{7,6},{8,9},{9,8},{10,11... | collective-permute-start | bytes 1769480 | tf_op jit(solution)/shard_map/cond/branch_1_fun/ppermute | solution.py:42
  182.5 33.5 %collective-permute-start.74 = (f16[384,768]{1,0:T(8,128)(2,1)}, f16[384,768]{1,0:T(8,128)(2,1)}, u32[]{:S(2)}, u32[]{:S(2)}) collective-permute-start(f16[384,768]{1,0:T(8,128)(2,1)} %get-tuple-element.383), channel_id=1, source_target_pairs={{0,4},{1,8},{2,16},{3,24},{4,0},{5,12},{6,20},{7,28},{8,1},{9,13},... | collective-permute-start | bytes 1769480 | tf_op jit(solution)/shard_map/ppermute | solution.py:42
  182.5 33.5 %collective-permute-start.75 = (f16[384,768]{1,0:T(8,128)(2,1)}, f16[384,768]{1,0:T(8,128)(2,1)}, u32[]{:S(2)}, u32[]{:S(2)}) collective-permute-start(f16[384,768]{1,0:T(8,128)(2,1)} %get-tuple-element.382), channel_id=1, source_target_pairs={{0,16},{1,24},{2,0},{3,8},{4,20},{5,28},{6,4},{7,12},{8,17},{9,25}... | collective-permute-start | bytes 1769480 | tf_op jit(solution)/shard_map/ppermute | solution.py:42
  185.8 29.1 %collective-permute-start.82 = (f16[384,384]{1,0:T(8,128)(2,1)}, f16[384,384]{1,0:T(8,128)(2,1)}, u32[]{:S(2)}, u32[]{:S(2)}) collective-permute-start(f16[384,384]{1,0:T(8,128)(2,1)} %get-tuple-element.426), channel_id=1, source_target_pairs={{0,6},{1,7},{2,4},{3,5},{4,2},{5,3},{6,0},{7,1},{8,14},{9,15},{10,... | collective-permute-start | bytes 884744 | tf_op jit(solution)/shard_map/ppermute | solution.py:42
  189.6 25.3 %collective-permute-start.81 = (f16[384,384]{1,0:T(8,128)(2,1)}, f16[384,384]{1,0:T(8,128)(2,1)}, u32[]{:S(2)}, u32[]{:S(2)}) collective-permute-start(f16[384,384]{1,0:T(8,128)(2,1)} %dynamic-slice_bitcast_fusion.18), channel_id=1, source_target_pairs={{0,4},{1,5},{2,6},{3,7},{4,0},{5,1},{6,2},{7,3},{8,12},{9,13},{10,... | collective-permute-start | bytes 884744 | tf_op jit(solution)/shard_map/ppermute | solution.py:42
  189.9 23.8 %collective-permute-start.78 = (f16[384,384]{1,0:T(8,128)(2,1)}, f16[384,384]{1,0:T(8,128)(2,1)}, u32[]{:S(2)}, u32[]{:S(2)}) collective-permute-start(f16[384,384]{1,0:T(8,128)(2,1)} %get-tuple-element.427), channel_id=1, source_target_pairs={{0,2},{1,3},{2,0},{3,1},{4,6},{5,7},{6,4},{7,5},{8,10},{9,11},{10,... | collective-permute-start | bytes 884744 | tf_op jit(solution)/shard_map/ppermute | solution.py:42
  218.0 40.4 %collective-permute-start.77 = (f16[384,768]{1,0:T(8,128)(2,1)S(1)}, f16[384,768]{1,0:T(8,128)(2,1)S(1)}, u32[]{:S(2)}, u32[]{:S(2)}) collective-permute-start(f16[384,768]{1,0:T(8,128)(2,1)S(1)} %get-tuple-element.378), channel_id=1, source_target_pairs={{0,24},{1,16},{2,8},{3,0},{4,28},{5,20},{6,12},{7,4},{8,25},{9,17}... | collective-permute-start | bytes 1769480 | tf_op jit(solution)/shard_map/ppermute | solution.py:42
  222.0 33.3 %collective-permute-start.76 = (f16[384,768]{1,0:T(8,128)(2,1)S(1)}, f16[384,768]{1,0:T(8,128)(2,1)S(1)}, u32[]{:S(2)}, u32[]{:S(2)}) collective-permute-start(f16[384,768]{1,0:T(8,128)(2,1)S(1)} %get-tuple-element.379), channel_id=1, source_target_pairs={{0,8},{1,0},{2,24},{3,16},{4,12},{5,4},{6,28},{7,20},{8,9},{9,1},{... | collective-permute-start | bytes 1769480 | tf_op jit(solution)/shard_map/ppermute | solution.py:42
  226.1 17.6 %collective-permute-start.83 = (f16[384,384]{1,0:T(8,128)(2,1)S(1)}, f16[384,384]{1,0:T(8,128)(2,1)S(1)}, u32[]{:S(2)}, u32[]{:S(2)}) collective-permute-start(f16[384,384]{1,0:T(8,128)(2,1)S(1)} %get-tuple-element.420), channel_id=1, source_target_pairs={{0,5},{1,4},{2,7},{3,6},{4,1},{5,0},{6,3},{7,2},{8,13},{9,12},{10,... | collective-permute-start | bytes 884744 | tf_op jit(solution)/shard_map/ppermute | solution.py:42
  265.5 20.4 %collective-permute-start.96 = (bf16[384,768]{1,0:T(8,128)(2,1)S(1)}, bf16[384,768]{1,0:T(8,128)(2,1)S(1)}, u32[]{:S(2)}, u32[]{:S(2)}) collective-permute-start(bf16[384,768]{1,0:T(8,128)(2,1)S(1)} %pad_maximum_fusion.32), channel_id=1, source_target_pairs={{0,2},{1,3},{2,0},{3,1},{4,6},{5,7},{6,4},{7,5},{8,10},{9,11},{10,... | collective-permute-start | bytes 1769480 | tf_op jit(solution)/shard_map/ppermute | solution.py:42
  286.2 26.3 %collective-permute-start.92 = (bf16[192,768]{1,0:T(8,128)(2,1)S(1)}, bf16[192,768]{1,0:T(8,128)(2,1)S(1)}, u32[]{:S(2)}, u32[]{:S(2)}) collective-permute-start(bf16[192,768]{1,0:T(8,128)(2,1)S(1)} %get-tuple-element.243), channel_id=1, source_target_pairs={{0,16},{1,24},{2,18},{3,26},{4,20},{5,28},{6,22},{7,30},{8,17},{9,... | collective-permute-start | bytes 884744 | tf_op jit(solution)/shard_map/ppermute | solution.py:42
  312.5 18.8 %collective-permute-start.98 = (bf16[192,768]{1,0:T(8,128)(2,1)S(1)}, bf16[192,768]{1,0:T(8,128)(2,1)S(1)}, u32[]{:S(2)}, u32[]{:S(2)}) collective-permute-start(bf16[192,768]{1,0:T(8,128)(2,1)S(1)} %get-tuple-element.245), channel_id=1, source_target_pairs={{0,16},{1,24},{2,18},{3,26},{4,20},{5,28},{6,22},{7,30},{8,17},{9,... | collective-permute-start | bytes 884744 | tf_op jit(solution)/shard_map/ppermute | solution.py:42
  313.3 18.1 %collective-permute-start.102 = (bf16[192,768]{1,0:T(8,128)(2,1)S(1)}, bf16[192,768]{1,0:T(8,128)(2,1)S(1)}, u32[]{:S(2)}, u32[]{:S(2)}) collective-permute-start(bf16[192,768]{1,0:T(8,128)(2,1)S(1)} %get-tuple-element.246), channel_id=1, source_target_pairs={{0,2},{1,8},{2,0},{3,10},{4,6},{5,12},{6,4},{7,14},{8,1},{9,11},{1... | collective-permute-start | bytes 884744 | tf_op jit(solution)/shard_map/ppermute | solution.py:42
  313.5 29.2 %collective-permute-start.89 = (bf16[2,192,768]{2,1,0:T(8,128)(2,1)S(1)}, bf16[2,192,768]{2,1,0:T(8,128)(2,1)S(1)}, u32[]{:S(2)}, u32[]{:S(2)}) collective-permute-start(bf16[2,192,768]{2,1,0:T(8,128)(2,1)S(1)} %pad_maximum_fusion.30.refs_11_), channel_id=1, source_target_pairs={{0,4},{1,5},{2,6},{3,7},{4,0},{5,1},{6,2},{7,3},{8,12},{9,13},{10,... | collective-permute-start | bytes 1769480 | tf_op jit(solution)/shard_map/ppermute | solution.py:42
  315.1 27.6 %collective-permute-start.88 = (bf16[2,192,768]{2,1,0:T(8,128)(2,1)S(1)}, bf16[2,192,768]{2,1,0:T(8,128)(2,1)S(1)}, u32[]{:S(2)}, u32[]{:S(2)}) collective-permute-start(bf16[2,192,768]{2,1,0:T(8,128)(2,1)S(1)} %pad_maximum_fusion.30.refs_11_), channel_id=1, source_target_pairs={{0,1},{1,0},{2,3},{3,2},{4,5},{5,4},{6,7},{7,6},{8,9},{9,8},{10,11... | collective-permute-start | bytes 1769480 | tf_op jit(solution)/shard_map/ppermute | solution.py:42
  317.6 25.3 %collective-permute-start.94 = (bf16[2,192,768]{2,1,0:T(8,128)(2,1)S(1)}, bf16[2,192,768]{2,1,0:T(8,128)(2,1)S(1)}, u32[]{:S(2)}, u32[]{:S(2)}) collective-permute-start(bf16[2,192,768]{2,1,0:T(8,128)(2,1)S(1)} %pad_maximum_fusion.31.refs_15_), channel_id=1, source_target_pairs={{0,4},{1,5},{2,6},{3,7},{4,0},{5,1},{6,2},{7,3},{8,12},{9,13},{10,... | collective-permute-start | bytes 1769480 | tf_op jit(solution)/shard_map/ppermute | solution.py:42
  337.8 18.7 %collective-permute-start.100 = (bf16[2,192,768]{2,1,0:T(8,128)(2,1)S(1)}, bf16[2,192,768]{2,1,0:T(8,128)(2,1)S(1)}, u32[]{:S(2)}, u32[]{:S(2)}) collective-permute-start(bf16[2,192,768]{2,1,0:T(8,128)(2,1)S(1)} %pad_maximum_fusion.33.refs_19_), channel_id=1, source_target_pairs={{0,4},{1,5},{2,6},{3,7},{4,0},{5,1},{6,2},{7,3},{8,12},{9,13},{10,... | collective-permute-start | bytes 1769480 | tf_op jit(solution)/shard_map/ppermute | solution.py:42
  342.8 23.9 %collective-permute-start.105 = (bf16[2,192,768]{2,1,0:T(8,128)(2,1)S(1)}, bf16[2,192,768]{2,1,0:T(8,128)(2,1)S(1)}, u32[]{:S(2)}, u32[]{:S(2)}) collective-permute-start(bf16[2,192,768]{2,1,0:T(8,128)(2,1)S(1)} %pad_maximum_fusion.34.refs_23_), channel_id=1, source_target_pairs={{0,4},{1,5},{2,6},{3,7},{4,0},{5,1},{6,2},{7,3},{8,12},{9,13},{10,... | collective-permute-start | bytes 1769480 | tf_op jit(solution)/shard_map/ppermute | solution.py:42
  342.8 23.8 %collective-permute-start.90 = (bf16[2,192,768]{2,1,0:T(8,128)(2,1)S(1)}, bf16[2,192,768]{2,1,0:T(8,128)(2,1)S(1)}, u32[]{:S(2)}, u32[]{:S(2)}) collective-permute-start(bf16[2,192,768]{2,1,0:T(8,128)(2,1)S(1)} %collective-permute-done.89.refs_13_), channel_id=1, source_target_pairs={{0,1},{1,0},{2,3},{3,2},{4,5},{5,4},{6,7},{7,6},{8,9},{9,8},{10,11... | collective-permute-start | bytes 1769480 | tf_op jit(solution)/shard_map/ppermute | solution.py:42
  343.5 23.1 %collective-permute-start.104 = (bf16[2,192,768]{2,1,0:T(8,128)(2,1)S(1)}, bf16[2,192,768]{2,1,0:T(8,128)(2,1)S(1)}, u32[]{:S(2)}, u32[]{:S(2)}) collective-permute-start(bf16[2,192,768]{2,1,0:T(8,128)(2,1)S(1)} %pad_maximum_fusion.34.refs_23_), channel_id=1, source_target_pairs={{0,1},{1,0},{2,3},{3,2},{4,5},{5,4},{6,7},{7,6},{8,9},{9,8},{10,11... | collective-permute-start | bytes 1769480 | tf_op jit(solution)/shard_map/ppermute | solution.py:42
  374.4 30.7 %collective-permute-start.107 = (f16[384,768]{1,0:T(8,128)(2,1)S(1)}, f16[384,768]{1,0:T(8,128)(2,1)S(1)}, u32[]{:S(2)}, u32[]{:S(2)}) collective-permute-start(f16[384,768]{1,0:T(8,128)(2,1)S(1)} %get-tuple-element.365), channel_id=1, source_target_pairs={{0,4},{1,8},{2,16},{3,24},{4,0},{5,12},{6,20},{7,28},{8,1},{9,13},... | collective-permute-start | bytes 1769480 | tf_op jit(solution)/shard_map/ppermute | solution.py:42
  378.3 28.1 %collective-permute-start.108 = (f16[384,768]{1,0:T(8,128)(2,1)S(1)}, f16[384,768]{1,0:T(8,128)(2,1)S(1)}, u32[]{:S(2)}, u32[]{:S(2)}) collective-permute-start(f16[384,768]{1,0:T(8,128)(2,1)S(1)} %get-tuple-element.364), channel_id=1, source_target_pairs={{0,16},{1,24},{2,0},{3,8},{4,20},{5,28},{6,4},{7,12},{8,17},{9,25}... | collective-permute-start | bytes 1769480 | tf_op jit(solution)/shard_map/ppermute | solution.py:42
  378.5 26.5 %collective-permute-start.115 = (f16[384,384]{1,0:T(8,128)(2,1)S(1)}, f16[384,384]{1,0:T(8,128)(2,1)S(1)}, u32[]{:S(2)}, u32[]{:S(2)}) collective-permute-start(f16[384,384]{1,0:T(8,128)(2,1)S(1)} %get-tuple-element.398), channel_id=1, source_target_pairs={{0,6},{1,7},{2,4},{3,5},{4,2},{5,3},{6,0},{7,1},{8,14},{9,15},{10,... | collective-permute-start | bytes 884744 | tf_op jit(solution)/shard_map/ppermute | solution.py:42
  380.1 24.9 %collective-permute-start.114 = (f16[384,384]{1,0:T(8,128)(2,1)S(1)}, f16[384,384]{1,0:T(8,128)(2,1)S(1)}, u32[]{:S(2)}, u32[]{:S(2)}) collective-permute-start(f16[384,384]{1,0:T(8,128)(2,1)S(1)} %dynamic-slice_bitcast_fusion.11), channel_id=1, source_target_pairs={{0,4},{1,5},{2,6},{3,7},{4,0},{5,1},{6,2},{7,3},{8,12},{9,13},{10,... | collective-permute-start | bytes 884744 | tf_op jit(solution)/shard_map/ppermute | solution.py:42
  380.2 24.6 %collective-permute-start.111 = (f16[384,384]{1,0:T(8,128)(2,1)S(1)}, f16[384,384]{1,0:T(8,128)(2,1)S(1)}, u32[]{:S(2)}, u32[]{:S(2)}) collective-permute-start(f16[384,384]{1,0:T(8,128)(2,1)S(1)} %get-tuple-element.399), channel_id=1, source_target_pairs={{0,2},{1,3},{2,0},{3,1},{4,6},{5,7},{6,4},{7,5},{8,10},{9,11},{10,... | collective-permute-start | bytes 884744 | tf_op jit(solution)/shard_map/ppermute | solution.py:42
  408.0 40.2 %collective-permute-start.110 = (f16[384,768]{1,0:T(8,128)(2,1)S(1)}, f16[384,768]{1,0:T(8,128)(2,1)S(1)}, u32[]{:S(2)}, u32[]{:S(2)}) collective-permute-start(f16[384,768]{1,0:T(8,128)(2,1)S(1)} %get-tuple-element.360), channel_id=1, source_target_pairs={{0,24},{1,16},{2,8},{3,0},{4,28},{5,20},{6,12},{7,4},{8,25},{9,17}... | collective-permute-start | bytes 1769480 | tf_op jit(solution)/shard_map/ppermute | solution.py:42
  412.6 34.0 %collective-permute-start.109 = (f16[384,768]{1,0:T(8,128)(2,1)S(1)}, f16[384,768]{1,0:T(8,128)(2,1)S(1)}, u32[]{:S(2)}, u32[]{:S(2)}) collective-permute-start(f16[384,768]{1,0:T(8,128)(2,1)S(1)} %get-tuple-element.361), channel_id=1, source_target_pairs={{0,8},{1,0},{2,24},{3,16},{4,12},{5,4},{6,28},{7,20},{8,9},{9,1},{... | collective-permute-start | bytes 1769480 | tf_op jit(solution)/shard_map/ppermute | solution.py:42
  416.7 18.6 %collective-permute-start.116 = (f16[384,384]{1,0:T(8,128)(2,1)S(1)}, f16[384,384]{1,0:T(8,128)(2,1)S(1)}, u32[]{:S(2)}, u32[]{:S(2)}) collective-permute-start(f16[384,384]{1,0:T(8,128)(2,1)S(1)} %get-tuple-element.392), channel_id=1, source_target_pairs={{0,5},{1,4},{2,7},{3,6},{4,1},{5,0},{6,3},{7,2},{8,13},{9,12},{10,... | collective-permute-start | bytes 884744 | tf_op jit(solution)/shard_map/ppermute | solution.py:42
  (82 other events, 1795.6 us)

commit v9 on v8

--- a/solution.py
+++ b/solution.py
@@ -365,9 +365,8 @@
     band, lane = alpha // grid.lanes, alpha % grid.lanes
     major, minor = beta // 2, beta % 2
     ids = jnp.stack([band, lane, major, minor]).astype(jnp.int32)
-    all_rows = (jnp.arange(grid.bands * grid.lanes) * rows // tile).reshape(grid.bands, grid.lanes)
-    many = tile_count[all_rows] > slots // 2
-    busy = jnp.take(many, lane, axis=1)
+    many = jnp.repeat(tile_count, tile // rows).reshape(grid.bands, grid.lanes) > slots // 2
+    busy = lax.dynamic_index_in_dim(many, lane, 1, keepdims=False)
 
     def one_busy(*values):
         return spread_inputs(grid, *values, busy, band, lane, major, minor)

time: 463 us -> 461 us (level)
  starting transfers between devices: 103 us -> 123 us
  waiting for transfers between devices: 236 us -> 217 us
    ppermute x70, starting transfers between devices: 82.5 us -> 102 us  [send(): received = lax.ppermute(value, AXES, pairs)]
    ppermute x70, waiting for transfers between devices: 213 us -> 194 us  [send(): received = lax.ppermute(value, AXES, pairs)]
  transfers between devices with their start and end apart: 79 -> 79, of which waited for: 29 -> 27; matrix products, arithmetic and copies ran while one was open for 12% -> 12% of each run, Pallas kernels for 3% -> 3%
where the time goes in v9:
time: 461 us; the launch traced here: 454 us
  waiting for transfers between devices  217 us (47%)
  starting transfers between devices  123 us (27%)
  other arithmetic  49.5 us (11%)
  local copies, waits for them, and re-layouts  34.6 us (8%)
  Pallas kernels  25 us (5%)
    ppermute x70, waiting for transfers between devices, send(): received = lax.ppermute(value, AXES, pairs)  194 us
    ppermute x70, starting transfers between devices, send(): received = lax.ppermute(value, AXES, pairs)  102 us
    pallas_call x4, Pallas kernels, products(): pl.pallas_call(lambda *refs: product_kernel(groups, pieces, lanes, calls,...  25 us
    ppermute x9, waiting for transfers between devices, gather_bands(): moving = lax.ppermute(moving, AXES, pairs)  22.6 us
    ppermute x9, starting transfers between devices, gather_bands(): moving = lax.ppermute(moving, AXES, pairs)  20.9 us
  transfers between devices with their start and end apart: 79, of which 27 were waited for; matrix products, arithmetic and copies ran while one was open for 12% of the time, Pallas kernels for 3%

profile of v9, /device:TPU:25, one launch (start us, length us, event | category | flops | bytes accessed | tf_op | source)
XLA Modules:
  0.0 453.7 jit_solution(5900991675817449082)
XLA Ops:
  2.9 166.9 %conditional.2 = (bf16[4,1,192,768]{3,2,1,0:T(8,128)(2,1)S(1)}, bf16[4,1,192,768]{3,2,1,0:T(8,128)(2,1)}, bf16[4,1,208,768]{3,2,1,0:T(8,128)(2,1)}, bf16[4,1,208...) conditional(s32[]{:T(128)} %convert_element_type.71, ...), branch_computations={%region_2.6_spmd, %region_6.12_spmd} | conditional | flops 26185744 | bytes 215436768
  3.2 5.1 %copy.32 = bf16[768,4,768]{2,0,1:T(8,128)(2,1)} copy(bf16[768,4,768]{2,1,0:T(4,128)(2,1)} %get-tuple-element.274) | data formatting | bytes 9437184 | tf_op jit(solution)/shard_map
  9.5 2.6 convert_element_type.51
  28.8 2.3 collective-permute-done.45
  34.3 4.8 %collective-permute-start.41 = (bf16[2,1,192,768]{3,2,1,0:T(8,128)(2,1)}, bf16[2,1,192,768]{3,2,1,0:T(8,128)(2,1)S(1)}, u32[]{:S(2)}, u32[]{:S(2)}) collective-permute-start(bf16[2,1,192,768]{3,2,1,0:T(8,128)(2,1)} %collective-permute-done.40), channel_id=1, source_target_pairs={{0,8},{1,9},{2,10},{3,11},{4,12},{5,13},{6,14},{7,15},{8,0},{9,1},... | collective-permute-start | bytes 1769480 | tf_op jit(solution)/shard_map/cond/branch_1_fun/ppermute | solution.py:99
  39.2 7.7 %collective-permute-done.53 = bf16[768,768]{1,0:T(8,128)(2,1)} collective-permute-done((bf16[768,768]{1,0:T(8,128)(2,1)}, bf16[768,768]{1,0:T(8,128)(2,1)}, u32[]{:S(2)}, u32[]{:S(2)}) %collective-permute-start.53) | collective-permute-done | bytes 1179680 | tf_op jit(solution)/shard_map/cond/branch_1_fun/ppermute | solution.py:42
  48.7 4.0 collective-permute-start.47
  53.5 2.5 collective-permute-start.50
  55.9 5.9 %collective-permute-done.41 = bf16[2,1,192,768]{3,2,1,0:T(8,128)(2,1)S(1)} collective-permute-done((bf16[2,1,192,768]{3,2,1,0:T(8,128)(2,1)}, bf16[2,1,192,768]{3,2,1,0:T(8,128)(2,1)S(1)}, u32[]{:S(2)}, u32[]{:S(2)}) %collective-permute-start.41) | collective-permute-done | bytes 589856 | tf_op jit(solution)/shard_map/cond/branch_1_fun/ppermute | solution.py:99
  64.2 14.4 %collective-permute-done.47 = bf16[2,1,208,768]{3,2,1,0:T(8,128)(2,1)S(1)} collective-permute-done((bf16[2,1,208,768]{3,2,1,0:T(8,128)(2,1)S(1)}, bf16[2,1,208,768]{3,2,1,0:T(8,128)(2,1)S(1)}, u32[]{:S(2)}, u32[]{:S(2)}) %collective-permute-start.47) | collective-permute-done | bytes 639008 | tf_op jit(solution)/shard_map/cond/branch_1_fun/ppermute | solution.py:99
  84.6 4.9 %collective-permute-start.51 = (bf16[1,2,192,768]{3,2,1,0:T(8,128)(2,1)S(1)}, bf16[1,2,192,768]{3,2,1,0:T(8,128)(2,1)S(1)}, u32[]{:S(2)}, u32[]{:S(2)}) collective-permute-start(bf16[1,2,192,768]{3,2,1,0:T(8,128)(2,1)S(1)} %collective-permute-done.50), channel_id=1, source_target_pairs={{0,8},{1,9},{2,10},{3,11},{4,12},{5,13},{6,14},{7,15},{8,0},{9,1},... | collective-permute-start | bytes 1769480 | tf_op jit(solution)/shard_map/cond/branch_1_fun/ppermute | solution.py:99
  92.1 6.9 %collective-permute-done.60 = bf16[192,768]{1,0:T(8,128)(2,1)S(1)} collective-permute-done((bf16[192,768]{1,0:T(8,128)(2,1)S(1)}, bf16[192,768]{1,0:T(8,128)(2,1)S(1)}, u32[]{:S(2)}, u32[]{:S(2)}) %collective-permute-start.60) | collective-permute-done | bytes 294944 | tf_op jit(solution)/shard_map/cond/branch_1_fun/ppermute | solution.py:42
  101.7 14.6 %collective-permute-done.48 = bf16[4,1,208,768]{3,2,1,0:T(8,128)(2,1)S(1)} collective-permute-done((bf16[4,1,208,768]{3,2,1,0:T(8,128)(2,1)S(1)}, bf16[4,1,208,768]{3,2,1,0:T(8,128)(2,1)S(1)}, u32[]{:S(2)}, u32[]{:S(2)}) %collective-permute-start.48) | collective-permute-done | bytes 1277984 | tf_op jit(solution)/shard_map/cond/branch_1_fun/ppermute | solution.py:42
  120.8 7.5 %collective-permute-start.61 = (bf16[2,192,768]{2,1,0:T(8,128)(2,1)S(1)}, bf16[2,192,768]{2,1,0:T(8,128)(2,1)S(1)}, u32[]{:S(2)}, u32[]{:S(2)}) collective-permute-start(bf16[2,192,768]{2,1,0:T(8,128)(2,1)S(1)} %pad_maximum_fusion.21), channel_id=1, source_target_pairs={{0,1},{1,0},{2,3},{3,2},{4,5},{5,4},{6,7},{7,6},{8,9},{9,8},{10,11... | collective-permute-start | bytes 1769480 | tf_op jit(solution)/shard_map/cond/branch_1_fun/ppermute | solution.py:42
  128.3 6.4 %collective-permute-done.69 = bf16[192,768]{1,0:T(8,128)(2,1)S(1)} collective-permute-done((bf16[192,768]{1,0:T(8,128)(2,1)S(1)}, bf16[192,768]{1,0:T(8,128)(2,1)S(1)}, u32[]{:S(2)}, u32[]{:S(2)}) %collective-permute-start.69) | collective-permute-done | bytes 294944 | tf_op jit(solution)/shard_map/cond/branch_1_fun/ppermute | solution.py:42
  139.8 10.2 %collective-permute-done.52 = bf16[1,2,192,768]{3,2,1,0:T(8,128)(2,1)S(1)} collective-permute-done((bf16[1,2,192,768]{3,2,1,0:T(8,128)(2,1)S(1)}, bf16[1,2,192,768]{3,2,1,0:T(8,128)(2,1)S(1)}, u32[]{:S(2)}, u32[]{:S(2)}) %collective-permute-start.52) | collective-permute-done | bytes 589856 | tf_op jit(solution)/shard_map/cond/branch_1_fun/ppermute | solution.py:42
  151.2 3.0 collective-permute-start.68
  154.2 9.7 %collective-permute-done.72 = bf16[2,192,768]{2,1,0:T(8,128)(2,1)} collective-permute-done((bf16[2,192,768]{2,1,0:T(8,128)(2,1)}, bf16[2,192,768]{2,1,0:T(8,128)(2,1)}, u32[]{:S(2)}, u32[]{:S(2)}) %collective-permute-start.72) | collective-permute-done | bytes 589856 | tf_op jit(solution)/shard_map/cond/branch_1_fun/ppermute | solution.py:42
  172.0 7.0 %shard_map.253 = (f32[2,384,768]{2,1,0:T(8,128)S(1)}, f32[2,768,384]{2,1,0:T(8,128)S(1)}) custom-call(s32[4]{0:T(128)S(1)} %pad_add_fusion.refs_0_, s32[16]{0:T(128)S(1)} %copy-done.2, s32[32]{0:T(128)S(1)} %reshape.54.refs_2_, s32[8]{0:T(128)S(1)} %copy-done.1, f32[1]{0:T(128)} %get-tuple-element.199.refs_4_, ...), custom_call_target="tpu_custom_call" | custom-call | flops 3623878656 | bytes 14155776 | tf_op jit(solution)/shard_map/pallas_call | solution.py:284
  181.4 4.4 collective-permute-start.75
  187.2 3.0 collective-permute-start.82
  191.3 8.0 %shard_map.254 = (f32[2,384,768]{2,1,0:T(8,128)S(1)}, f32[2,768,384]{2,1,0:T(8,128)S(1)}) custom-call(s32[4]{0:T(128)S(1)} %pad_add_fusion.refs_0_, s32[16]{0:T(128)S(1)} %copy-done.2, s32[32]{0:T(128)S(1)} %reshape.54.refs_2_, s32[8]{0:T(128)S(1)} %copy-done.1, f32[1]{0:T(128)} %get-tuple-element.199.refs_4_, ...), custom_call_target="tpu_custom_call" | custom-call | flops 3623878656 | bytes 14155776 | tf_op jit(solution)/shard_map/pallas_call | solution.py:284
  200.7 2.8 convert_element_type.74
  206.1 6.6 %collective-permute-done.78 = f16[384,384]{1,0:T(8,128)(2,1)} collective-permute-done((f16[384,384]{1,0:T(8,128)(2,1)}, f16[384,384]{1,0:T(8,128)(2,1)}, u32[]{:S(2)}, u32[]{:S(2)}) %collective-permute-start.78) | collective-permute-done | bytes 294944 | tf_op jit(solution)/shard_map/ppermute | solution.py:42
  217.7 4.2 collective-permute-start.77
  221.9 2.8 collective-permute-start.76
  225.2 14.4 %collective-permute-start.83 = (f16[384,384]{1,0:T(8,128)(2,1)S(1)}, f16[384,384]{1,0:T(8,128)(2,1)S(1)}, u32[]{:S(2)}, u32[]{:S(2)}) collective-permute-start(f16[384,384]{1,0:T(8,128)(2,1)S(1)} %get-tuple-element.398), channel_id=1, source_target_pairs={{0,5},{1,4},{2,7},{3,6},{4,1},{5,0},{6,3},{7,2},{8,13},{9,12},{10,... | collective-permute-start | bytes 884744 | tf_op jit(solution)/shard_map/ppermute | solution.py:42
  240.2 5.8 %collective-permute-done.83 = f16[384,384]{1,0:T(8,128)(2,1)S(1)} collective-permute-done((f16[384,384]{1,0:T(8,128)(2,1)S(1)}, f16[384,384]{1,0:T(8,128)(2,1)S(1)}, u32[]{:S(2)}, u32[]{:S(2)}) %collective-permute-start.83) | collective-permute-done | bytes 294944 | tf_op jit(solution)/shard_map/ppermute | solution.py:42
  246.3 9.3 %collective-permute-done.76 = f16[384,768]{1,0:T(8,128)(2,1)S(1)} collective-permute-done((f16[384,768]{1,0:T(8,128)(2,1)S(1)}, f16[384,768]{1,0:T(8,128)(2,1)S(1)}, u32[]{:S(2)}, u32[]{:S(2)}) %collective-permute-start.76) | collective-permute-done | bytes 589856 | tf_op jit(solution)/shard_map/ppermute | solution.py:42
  255.6 2.3 broadcast_select_fusion.21
  268.5 10.2 %collective-permute-done.85 = bf16[384,768]{1,0:T(8,128)(2,1)} collective-permute-done((bf16[384,768]{1,0:T(8,128)(2,1)}, bf16[384,768]{1,0:T(8,128)(2,1)}, u32[]{:S(2)}, u32[]{:S(2)}) %collective-permute-start.85) | collective-permute-done | bytes 589856 | tf_op jit(solution)/shard_map/ppermute | solution.py:42
  282.6 5.4 %collective-permute-done.86 = bf16[192,768]{1,0:T(8,128)(2,1)S(1)} collective-permute-done((bf16[192,768]{1,0:T(8,128)(2,1)S(1)}, bf16[192,768]{1,0:T(8,128)(2,1)S(1)}, u32[]{:S(2)}, u32[]{:S(2)}) %collective-permute-start.86) | collective-permute-done | bytes 294944 | tf_op jit(solution)/shard_map/ppermute | solution.py:42
  290.8 6.2 %collective-permute-done.87 = bf16[192,768]{1,0:T(8,128)(2,1)S(1)} collective-permute-done((bf16[192,768]{1,0:T(8,128)(2,1)S(1)}, bf16[192,768]{1,0:T(8,128)(2,1)S(1)}, u32[]{:S(2)}, u32[]{:S(2)}) %collective-permute-start.87) | collective-permute-done | bytes 294944 | tf_op jit(solution)/shard_map/ppermute | solution.py:42
  298.0 15.2 %collective-permute-done.92 = bf16[192,768]{1,0:T(8,128)(2,1)S(1)} collective-permute-done((bf16[192,768]{1,0:T(8,128)(2,1)S(1)}, bf16[192,768]{1,0:T(8,128)(2,1)S(1)}, u32[]{:S(2)}, u32[]{:S(2)}) %collective-permute-start.92) | collective-permute-done | bytes 294944 | tf_op jit(solution)/shard_map/ppermute | solution.py:42
  318.6 10.4 %collective-permute-done.98 = bf16[192,768]{1,0:T(8,128)(2,1)S(1)} collective-permute-done((bf16[192,768]{1,0:T(8,128)(2,1)S(1)}, bf16[192,768]{1,0:T(8,128)(2,1)S(1)}, u32[]{:S(2)}, u32[]{:S(2)}) %collective-permute-start.98) | collective-permute-done | bytes 294944 | tf_op jit(solution)/shard_map/ppermute | solution.py:42
  329.8 11.7 %collective-permute-done.103 = bf16[192,768]{1,0:T(8,128)(2,1)S(1)} collective-permute-done((bf16[192,768]{1,0:T(8,128)(2,1)S(1)}, bf16[192,768]{1,0:T(8,128)(2,1)S(1)}, u32[]{:S(2)}, u32[]{:S(2)}) %collective-permute-start.103) | collective-permute-done | bytes 294944 | tf_op jit(solution)/shard_map/ppermute | solution.py:42
  343.9 12.9 %collective-permute-done.100.refs_21_ = bf16[2,192,768]{2,1,0:T(8,128)(2,1)S(1)} collective-permute-done((bf16[2,192,768]{2,1,0:T(8,128)(2,1)S(1)}, bf16[2,192,768]{2,1,0:T(8,128)(2,1)S(1)}, u32[]{:S(2)}, u32[]{:S(2)}) %collective-permute-start.100) | collective-permute-done | bytes 589856 | tf_op jit(solution)/shard_map/ppermute | solution.py:42
  357.3 11.1 %collective-permute-done.105.refs_25_ = bf16[2,192,768]{2,1,0:T(8,128)(2,1)S(1)} collective-permute-done((bf16[2,192,768]{2,1,0:T(8,128)(2,1)S(1)}, bf16[2,192,768]{2,1,0:T(8,128)(2,1)S(1)}, u32[]{:S(2)}, u32[]{:S(2)}) %collective-permute-start.105) | collective-permute-done | bytes 589856 | tf_op jit(solution)/shard_map/ppermute | solution.py:42
  370.5 4.7 %shard_map.255 = (f32[2,384,768]{2,1,0:T(8,128)S(1)}, f32[2,768,384]{2,1,0:T(8,128)S(1)}) custom-call(s32[4]{0:T(128)S(1)} %pad_add_fusion.refs_0_, s32[16]{0:T(128)S(1)} %copy-done.2, s32[32]{0:T(128)S(1)} %reshape.54.refs_2_, s32[8]{0:T(128)S(1)} %copy-done.1, f32[1]{0:T(128)} %get-tuple-element.230.refs_4_, ...), custom_call_target="tpu_custom_call" | custom-call | flops 3623878656 | bytes 14155776 | tf_op jit(solution)/shard_map/pallas_call | solution.py:284
  380.1 3.6 collective-permute-start.115
  384.2 5.4 %shard_map.256 = (f32[2,384,768]{2,1,0:T(8,128)S(1)}, f32[2,768,384]{2,1,0:T(8,128)S(1)}) custom-call(s32[4]{0:T(128)S(1)} %pad_add_fusion.refs_0_, s32[16]{0:T(128)S(1)} %copy-done.2, s32[32]{0:T(128)S(1)} %reshape.54.refs_2_, s32[8]{0:T(128)S(1)} %copy-done.1, f32[1]{0:T(128)} %get-tuple-element.230.refs_4_, ...), custom_call_target="tpu_custom_call" | custom-call | flops 3623878656 | bytes 14155776 | tf_op jit(solution)/shard_map/pallas_call | solution.py:284
  389.9 17.0 %collective-permute-done.111 = f16[384,384]{1,0:T(8,128)(2,1)S(1)} collective-permute-done((f16[384,384]{1,0:T(8,128)(2,1)S(1)}, f16[384,384]{1,0:T(8,128)(2,1)S(1)}, u32[]{:S(2)}, u32[]{:S(2)}) %collective-permute-start.111) | collective-permute-done | bytes 294944 | tf_op jit(solution)/shard_map/ppermute | solution.py:42
  409.0 3.3 collective-permute-start.110
  412.3 3.7 collective-permute-start.109
  417.2 14.4 %collective-permute-start.116 = (f16[384,384]{1,0:T(8,128)(2,1)S(1)}, f16[384,384]{1,0:T(8,128)(2,1)S(1)}, u32[]{:S(2)}, u32[]{:S(2)}) collective-permute-start(f16[384,384]{1,0:T(8,128)(2,1)S(1)} %get-tuple-element.370), channel_id=1, source_target_pairs={{0,5},{1,4},{2,7},{3,6},{4,1},{5,0},{6,3},{7,2},{8,13},{9,12},{10,... | collective-permute-start | bytes 884744 | tf_op jit(solution)/shard_map/ppermute | solution.py:42
  432.2 7.0 %collective-permute-done.116 = f16[384,384]{1,0:T(8,128)(2,1)S(1)} collective-permute-done((f16[384,384]{1,0:T(8,128)(2,1)S(1)}, f16[384,384]{1,0:T(8,128)(2,1)S(1)}, u32[]{:S(2)}, u32[]{:S(2)}) %collective-permute-start.116) | collective-permute-done | bytes 294944 | tf_op jit(solution)/shard_map/ppermute | solution.py:42
  439.5 6.7 %collective-permute-done.109 = f16[384,768]{1,0:T(8,128)(2,1)S(1)} collective-permute-done((f16[384,768]{1,0:T(8,128)(2,1)S(1)}, f16[384,768]{1,0:T(8,128)(2,1)S(1)}, u32[]{:S(2)}, u32[]{:S(2)}) %collective-permute-start.109) | collective-permute-done | bytes 589856 | tf_op jit(solution)/shard_map/ppermute | solution.py:42
  449.8 3.7 divide_subtract_fusion
  (356 shorter events, 113.6 us)
Async XLA Ops:
  19.7 27.2 %collective-permute-start.53 = (bf16[768,768]{1,0:T(8,128)(2,1)}, bf16[768,768]{1,0:T(8,128)(2,1)}, u32[]{:S(2)}, u32[]{:S(2)}) collective-permute-start(bf16[768,768]{1,0:T(8,128)(2,1)} %pad_maximum_fusion.17), channel_id=1, source_target_pairs={{0,2},{1,3},{2,0},{3,1},{4,6},{5,7},{6,4},{7,5},{8,10},{9,11},{10,... | collective-permute-start | bytes 3538952 | tf_op jit(solution)/shard_map/cond/branch_1_fun/ppermute | solution.py:42
  31.2 17.5 %collective-permute-start.46 = (bf16[2,1,208,768]{3,2,1,0:T(8,128)(2,1)S(1)}, bf16[2,1,208,768]{3,2,1,0:T(8,128)(2,1)S(1)}, u32[]{:S(2)}, u32[]{:S(2)}) collective-permute-start(bf16[2,1,208,768]{3,2,1,0:T(8,128)(2,1)S(1)} %pad_maximum_fusion.18), channel_id=1, source_target_pairs={{0,1},{1,0},{2,3},{3,2},{4,5},{5,4},{6,7},{7,6},{8,16},{9,17},{10,... | collective-permute-start | bytes 1916936 | tf_op jit(solution)/shard_map/cond/branch_1_fun/ppermute | solution.py:99
  34.1 18.6 %collective-permute-start.49 = (bf16[1,2,192,768]{3,2,1,0:T(8,128)(2,1)S(1)}, bf16[1,2,192,768]{3,2,1,0:T(8,128)(2,1)S(1)}, u32[]{:S(2)}, u32[]{:S(2)}) collective-permute-start(bf16[1,2,192,768]{3,2,1,0:T(8,128)(2,1)S(1)} %maximum_bitcast_fusion.2), channel_id=1, source_target_pairs={{0,8},{1,9},{2,10},{3,11},{4,12},{5,13},{6,14},{7,15},{8,0},{9,1},... | collective-permute-start | bytes 1769480 | tf_op jit(solution)/shard_map/cond/branch_1_fun/ppermute | solution.py:99
  34.3 27.4 %collective-permute-start.41 = (bf16[2,1,192,768]{3,2,1,0:T(8,128)(2,1)}, bf16[2,1,192,768]{3,2,1,0:T(8,128)(2,1)S(1)}, u32[]{:S(2)}, u32[]{:S(2)}) collective-permute-start(bf16[2,1,192,768]{3,2,1,0:T(8,128)(2,1)} %collective-permute-done.40), channel_id=1, source_target_pairs={{0,8},{1,9},{2,10},{3,11},{4,12},{5,13},{6,14},{7,15},{8,0},{9,1},... | collective-permute-start | bytes 1769480 | tf_op jit(solution)/shard_map/cond/branch_1_fun/ppermute | solution.py:99
  48.7 29.9 %collective-permute-start.47 = (bf16[2,1,208,768]{3,2,1,0:T(8,128)(2,1)S(1)}, bf16[2,1,208,768]{3,2,1,0:T(8,128)(2,1)S(1)}, u32[]{:S(2)}, u32[]{:S(2)}) collective-permute-start(bf16[2,1,208,768]{3,2,1,0:T(8,128)(2,1)S(1)} %collective-permute-done.46), channel_id=1, source_target_pairs={{0,8},{1,9},{2,10},{3,11},{4,12},{5,13},{6,14},{7,15},{8,0},{9,1},... | collective-permute-start | bytes 1916936 | tf_op jit(solution)/shard_map/cond/branch_1_fun/ppermute | solution.py:99
  53.5 31.1 %collective-permute-start.50 = (bf16[1,2,192,768]{3,2,1,0:T(8,128)(2,1)S(1)}, bf16[1,2,192,768]{3,2,1,0:T(8,128)(2,1)S(1)}, u32[]{:S(2)}, u32[]{:S(2)}) collective-permute-start(bf16[1,2,192,768]{3,2,1,0:T(8,128)(2,1)S(1)} %broadcast_select_fusion.8), channel_id=1, source_target_pairs={{0,1},{1,0},{2,3},{3,2},{4,5},{5,4},{6,7},{7,6},{8,16},{9,17},{10,... | collective-permute-start | bytes 1769480 | tf_op jit(solution)/shard_map/cond/branch_1_fun/ppermute | solution.py:99
  62.6 27.5 %collective-permute-start.42 = (bf16[4,1,192,768]{3,2,1,0:T(8,128)(2,1)S(1)}, bf16[4,1,192,768]{3,2,1,0:T(8,128)(2,1)S(1)}, u32[]{:S(2)}, u32[]{:S(2)}) collective-permute-start(bf16[4,1,192,768]{3,2,1,0:T(8,128)(2,1)S(1)} %pad_maximum_fusion.16), channel_id=1, source_target_pairs={{0,2},{1,3},{2,0},{3,1},{4,6},{5,7},{6,4},{7,5},{8,10},{9,11},{10,... | collective-permute-start | bytes 3538952 | tf_op jit(solution)/shard_map/cond/branch_1_fun/ppermute | solution.py:42
  63.0 16.9 %collective-permute-start.54 = (bf16[192,768]{1,0:T(8,128)(2,1)S(1)}, bf16[192,768]{1,0:T(8,128)(2,1)S(1)}, u32[]{:S(2)}, u32[]{:S(2)}) collective-permute-start(bf16[192,768]{1,0:T(8,128)(2,1)S(1)} %get-tuple-element.142), channel_id=1, source_target_pairs={{0,4},{1,8},{2,6},{3,10},{4,0},{5,12},{6,2},{7,14},{8,1},{9,13},{1... | collective-permute-start | bytes 884744 | tf_op jit(solution)/shard_map/cond/branch_1_fun/ppermute | solution.py:42
  64.2 20.2 %collective-permute-start.55 = (bf16[192,768]{1,0:T(8,128)(2,1)S(1)}, bf16[192,768]{1,0:T(8,128)(2,1)S(1)}, u32[]{:S(2)}, u32[]{:S(2)}) collective-permute-start(bf16[192,768]{1,0:T(8,128)(2,1)S(1)} %get-tuple-element.143), channel_id=1, source_target_pairs={{0,16},{1,24},{2,18},{3,26},{4,20},{5,28},{6,22},{7,30},{8,17},{9,... | collective-permute-start | bytes 884744 | tf_op jit(solution)/shard_map/cond/branch_1_fun/ppermute | solution.py:42
  79.5 36.8 %collective-permute-start.48 = (bf16[4,1,208,768]{3,2,1,0:T(8,128)(2,1)S(1)}, bf16[4,1,208,768]{3,2,1,0:T(8,128)(2,1)S(1)}, u32[]{:S(2)}, u32[]{:S(2)}) collective-permute-start(bf16[4,1,208,768]{3,2,1,0:T(8,128)(2,1)S(1)} %pad_maximum_fusion.15), channel_id=1, source_target_pairs={{0,2},{1,3},{2,0},{3,1},{4,6},{5,7},{6,4},{7,5},{8,10},{9,11},{10,... | collective-permute-start | bytes 3833864 | tf_op jit(solution)/shard_map/cond/branch_1_fun/ppermute | solution.py:42
  84.6 32.1 %collective-permute-start.51 = (bf16[1,2,192,768]{3,2,1,0:T(8,128)(2,1)S(1)}, bf16[1,2,192,768]{3,2,1,0:T(8,128)(2,1)S(1)}, u32[]{:S(2)}, u32[]{:S(2)}) collective-permute-start(bf16[1,2,192,768]{3,2,1,0:T(8,128)(2,1)S(1)} %collective-permute-done.50), channel_id=1, source_target_pairs={{0,8},{1,9},{2,10},{3,11},{4,12},{5,13},{6,14},{7,15},{8,0},{9,1},... | collective-permute-start | bytes 1769480 | tf_op jit(solution)/shard_map/cond/branch_1_fun/ppermute | solution.py:99
  92.0 28.9 %collective-permute-start.57 = (bf16[2,192,768]{2,1,0:T(8,128)(2,1)S(1)}, bf16[2,192,768]{2,1,0:T(8,128)(2,1)S(1)}, u32[]{:S(2)}, u32[]{:S(2)}) collective-permute-start(bf16[2,192,768]{2,1,0:T(8,128)(2,1)S(1)} %pad_maximum_fusion.20), channel_id=1, source_target_pairs={{0,4},{1,5},{2,6},{3,7},{4,0},{5,1},{6,2},{7,3},{8,12},{9,13},{10,... | collective-permute-start | bytes 1769480 | tf_op jit(solution)/shard_map/cond/branch_1_fun/ppermute | solution.py:42
  98.9 37.9 %collective-permute-start.56 = (bf16[2,192,768]{2,1,0:T(8,128)(2,1)S(1)}, bf16[2,192,768]{2,1,0:T(8,128)(2,1)S(1)}, u32[]{:S(2)}, u32[]{:S(2)}) collective-permute-start(bf16[2,192,768]{2,1,0:T(8,128)(2,1)S(1)} %pad_maximum_fusion.20), channel_id=1, source_target_pairs={{0,1},{1,0},{2,3},{3,2},{4,5},{5,4},{6,7},{7,6},{8,9},{9,8},{10,11... | collective-permute-start | bytes 1769480 | tf_op jit(solution)/shard_map/cond/branch_1_fun/ppermute | solution.py:42
  99.8 20.0 %collective-permute-start.65 = (bf16[192,768]{1,0:T(8,128)(2,1)S(1)}, bf16[192,768]{1,0:T(8,128)(2,1)S(1)}, u32[]{:S(2)}, u32[]{:S(2)}) collective-permute-start(bf16[192,768]{1,0:T(8,128)(2,1)S(1)} %get-tuple-element.149), channel_id=1, source_target_pairs={{0,16},{1,24},{2,18},{3,26},{4,20},{5,28},{6,22},{7,30},{8,17},{9,... | collective-permute-start | bytes 884744 | tf_op jit(solution)/shard_map/cond/branch_1_fun/ppermute | solution.py:42
  116.3 21.7 %collective-permute-start.62 = (bf16[2,192,768]{2,1,0:T(8,128)(2,1)S(1)}, bf16[2,192,768]{2,1,0:T(8,128)(2,1)}, u32[]{:S(2)}, u32[]{:S(2)}) collective-permute-start(bf16[2,192,768]{2,1,0:T(8,128)(2,1)S(1)} %pad_maximum_fusion.21), channel_id=1, source_target_pairs={{0,4},{1,5},{2,6},{3,7},{4,0},{5,1},{6,2},{7,3},{8,12},{9,13},{10,... | collective-permute-start | bytes 1769480 | tf_op jit(solution)/shard_map/cond/branch_1_fun/ppermute | solution.py:42
  116.6 18.1 %collective-permute-start.69 = (bf16[192,768]{1,0:T(8,128)(2,1)S(1)}, bf16[192,768]{1,0:T(8,128)(2,1)S(1)}, u32[]{:S(2)}, u32[]{:S(2)}) collective-permute-start(bf16[192,768]{1,0:T(8,128)(2,1)S(1)} %get-tuple-element.151), channel_id=1, source_target_pairs={{0,4},{1,8},{2,6},{3,10},{4,0},{5,12},{6,2},{7,14},{8,1},{9,13},{1... | collective-permute-start | bytes 884744 | tf_op jit(solution)/shard_map/cond/branch_1_fun/ppermute | solution.py:42
  120.8 17.5 %collective-permute-start.61 = (bf16[2,192,768]{2,1,0:T(8,128)(2,1)S(1)}, bf16[2,192,768]{2,1,0:T(8,128)(2,1)S(1)}, u32[]{:S(2)}, u32[]{:S(2)}) collective-permute-start(bf16[2,192,768]{2,1,0:T(8,128)(2,1)S(1)} %pad_maximum_fusion.21), channel_id=1, source_target_pairs={{0,1},{1,0},{2,3},{3,2},{4,5},{5,4},{6,7},{7,6},{8,9},{9,8},{10,11... | collective-permute-start | bytes 1769480 | tf_op jit(solution)/shard_map/cond/branch_1_fun/ppermute | solution.py:42
  138.0 25.9 %collective-permute-start.72 = (bf16[2,192,768]{2,1,0:T(8,128)(2,1)}, bf16[2,192,768]{2,1,0:T(8,128)(2,1)}, u32[]{:S(2)}, u32[]{:S(2)}) collective-permute-start(bf16[2,192,768]{2,1,0:T(8,128)(2,1)} %pad_maximum_fusion.23), channel_id=1, source_target_pairs={{0,4},{1,5},{2,6},{3,7},{4,0},{5,1},{6,2},{7,3},{8,12},{9,13},{10,... | collective-permute-start | bytes 1769480 | tf_op jit(solution)/shard_map/cond/branch_1_fun/ppermute | solution.py:42
  138.3 29.9 %collective-permute-start.63 = (bf16[2,192,768]{2,1,0:T(8,128)(2,1)}, bf16[2,192,768]{2,1,0:T(8,128)(2,1)}, u32[]{:S(2)}, u32[]{:S(2)}) collective-permute-start(bf16[2,192,768]{2,1,0:T(8,128)(2,1)} %collective-permute-done.62), channel_id=1, source_target_pairs={{0,1},{1,0},{2,3},{3,2},{4,5},{5,4},{6,7},{7,6},{8,9},{9,8},{10,11... | collective-permute-start | bytes 1769480 | tf_op jit(solution)/shard_map/cond/branch_1_fun/ppermute | solution.py:42
  139.7 28.5 %collective-permute-start.66 = (bf16[2,192,768]{2,1,0:T(8,128)(2,1)}, bf16[2,192,768]{2,1,0:T(8,128)(2,1)}, u32[]{:S(2)}, u32[]{:S(2)}) collective-permute-start(bf16[2,192,768]{2,1,0:T(8,128)(2,1)} %pad_maximum_fusion.22), channel_id=1, source_target_pairs={{0,1},{1,0},{2,3},{3,2},{4,5},{5,4},{6,7},{7,6},{8,9},{9,8},{10,11... | collective-permute-start | bytes 1769480 | tf_op jit(solution)/shard_map/cond/branch_1_fun/ppermute | solution.py:42
  149.9 18.3 %collective-permute-start.71 = (bf16[2,192,768]{2,1,0:T(8,128)(2,1)}, bf16[2,192,768]{2,1,0:T(8,128)(2,1)}, u32[]{:S(2)}, u32[]{:S(2)}) collective-permute-start(bf16[2,192,768]{2,1,0:T(8,128)(2,1)} %pad_maximum_fusion.23), channel_id=1, source_target_pairs={{0,1},{1,0},{2,3},{3,2},{4,5},{5,4},{6,7},{7,6},{8,9},{9,8},{10,11... | collective-permute-start | bytes 1769480 | tf_op jit(solution)/shard_map/cond/branch_1_fun/ppermute | solution.py:42
  151.2 17.0 %collective-permute-start.68 = (bf16[2,192,768]{2,1,0:T(8,128)(2,1)}, bf16[2,192,768]{2,1,0:T(8,128)(2,1)}, u32[]{:S(2)}, u32[]{:S(2)}) collective-permute-start(bf16[2,192,768]{2,1,0:T(8,128)(2,1)} %collective-permute-done.67), channel_id=1, source_target_pairs={{0,1},{1,0},{2,3},{3,2},{4,5},{5,4},{6,7},{7,6},{8,9},{9,8},{10,11... | collective-permute-start | bytes 1769480 | tf_op jit(solution)/shard_map/cond/branch_1_fun/ppermute | solution.py:42
  181.4 33.8 %collective-permute-start.74 = (f16[384,768]{1,0:T(8,128)(2,1)}, f16[384,768]{1,0:T(8,128)(2,1)}, u32[]{:S(2)}, u32[]{:S(2)}) collective-permute-start(f16[384,768]{1,0:T(8,128)(2,1)} %get-tuple-element.361), channel_id=1, source_target_pairs={{0,4},{1,8},{2,16},{3,24},{4,0},{5,12},{6,20},{7,28},{8,1},{9,13},... | collective-permute-start | bytes 1769480 | tf_op jit(solution)/shard_map/ppermute | solution.py:42
  181.4 33.8 %collective-permute-start.75 = (f16[384,768]{1,0:T(8,128)(2,1)}, f16[384,768]{1,0:T(8,128)(2,1)}, u32[]{:S(2)}, u32[]{:S(2)}) collective-permute-start(f16[384,768]{1,0:T(8,128)(2,1)} %get-tuple-element.360), channel_id=1, source_target_pairs={{0,16},{1,24},{2,0},{3,8},{4,20},{5,28},{6,4},{7,12},{8,17},{9,25}... | collective-permute-start | bytes 1769480 | tf_op jit(solution)/shard_map/ppermute | solution.py:42
  187.2 26.7 %collective-permute-start.82 = (f16[384,384]{1,0:T(8,128)(2,1)}, f16[384,384]{1,0:T(8,128)(2,1)}, u32[]{:S(2)}, u32[]{:S(2)}) collective-permute-start(f16[384,384]{1,0:T(8,128)(2,1)} %get-tuple-element.404), channel_id=1, source_target_pairs={{0,6},{1,7},{2,4},{3,5},{4,2},{5,3},{6,0},{7,1},{8,14},{9,15},{10,... | collective-permute-start | bytes 884744 | tf_op jit(solution)/shard_map/ppermute | solution.py:42
  191.0 22.9 %collective-permute-start.81 = (f16[384,384]{1,0:T(8,128)(2,1)}, f16[384,384]{1,0:T(8,128)(2,1)}, u32[]{:S(2)}, u32[]{:S(2)}) collective-permute-start(f16[384,384]{1,0:T(8,128)(2,1)} %dynamic-slice_bitcast_fusion.18), channel_id=1, source_target_pairs={{0,4},{1,5},{2,6},{3,7},{4,0},{5,1},{6,2},{7,3},{8,12},{9,13},{10,... | collective-permute-start | bytes 884744 | tf_op jit(solution)/shard_map/ppermute | solution.py:42
  191.0 21.7 %collective-permute-start.78 = (f16[384,384]{1,0:T(8,128)(2,1)}, f16[384,384]{1,0:T(8,128)(2,1)}, u32[]{:S(2)}, u32[]{:S(2)}) collective-permute-start(f16[384,384]{1,0:T(8,128)(2,1)} %get-tuple-element.405), channel_id=1, source_target_pairs={{0,2},{1,3},{2,0},{3,1},{4,6},{5,7},{6,4},{7,5},{8,10},{9,11},{10,... | collective-permute-start | bytes 884744 | tf_op jit(solution)/shard_map/ppermute | solution.py:42
  215.8 23.8 %collective-permute-start.79 = (f16[384,384]{1,0:T(8,128)(2,1)S(1)}, f16[384,384]{1,0:T(8,128)(2,1)S(1)}, u32[]{:S(2)}, u32[]{:S(2)}) collective-permute-start(f16[384,384]{1,0:T(8,128)(2,1)S(1)} %get-tuple-element.399), channel_id=1, source_target_pairs={{0,1},{1,0},{2,3},{3,2},{4,5},{5,4},{6,7},{7,6},{8,9},{9,8},{10,11... | collective-permute-start | bytes 884744 | tf_op jit(solution)/shard_map/ppermute | solution.py:42
  217.7 40.9 %collective-permute-start.77 = (f16[384,768]{1,0:T(8,128)(2,1)S(1)}, f16[384,768]{1,0:T(8,128)(2,1)S(1)}, u32[]{:S(2)}, u32[]{:S(2)}) collective-permute-start(f16[384,768]{1,0:T(8,128)(2,1)S(1)} %get-tuple-element.356), channel_id=1, source_target_pairs={{0,24},{1,16},{2,8},{3,0},{4,28},{5,20},{6,12},{7,4},{8,25},{9,17}... | collective-permute-start | bytes 1769480 | tf_op jit(solution)/shard_map/ppermute | solution.py:42
  221.9 33.7 %collective-permute-start.76 = (f16[384,768]{1,0:T(8,128)(2,1)S(1)}, f16[384,768]{1,0:T(8,128)(2,1)S(1)}, u32[]{:S(2)}, u32[]{:S(2)}) collective-permute-start(f16[384,768]{1,0:T(8,128)(2,1)S(1)} %get-tuple-element.357), channel_id=1, source_target_pairs={{0,8},{1,0},{2,24},{3,16},{4,12},{5,4},{6,28},{7,20},{8,9},{9,1},{... | collective-permute-start | bytes 1769480 | tf_op jit(solution)/shard_map/ppermute | solution.py:42
  225.2 20.8 %collective-permute-start.83 = (f16[384,384]{1,0:T(8,128)(2,1)S(1)}, f16[384,384]{1,0:T(8,128)(2,1)S(1)}, u32[]{:S(2)}, u32[]{:S(2)}) collective-permute-start(f16[384,384]{1,0:T(8,128)(2,1)S(1)} %get-tuple-element.398), channel_id=1, source_target_pairs={{0,5},{1,4},{2,7},{3,6},{4,1},{5,0},{6,3},{7,2},{8,13},{9,12},{10,... | collective-permute-start | bytes 884744 | tf_op jit(solution)/shard_map/ppermute | solution.py:42
  265.8 24.7 %collective-permute-start.96 = (bf16[384,768]{1,0:T(8,128)(2,1)S(1)}, bf16[384,768]{1,0:T(8,128)(2,1)S(1)}, u32[]{:S(2)}, u32[]{:S(2)}) collective-permute-start(bf16[384,768]{1,0:T(8,128)(2,1)S(1)} %pad_maximum_fusion.32), channel_id=1, source_target_pairs={{0,2},{1,3},{2,0},{3,1},{4,6},{5,7},{6,4},{7,5},{8,10},{9,11},{10,... | collective-permute-start | bytes 1769480 | tf_op jit(solution)/shard_map/ppermute | solution.py:42
  296.9 16.3 %collective-permute-start.92 = (bf16[192,768]{1,0:T(8,128)(2,1)S(1)}, bf16[192,768]{1,0:T(8,128)(2,1)S(1)}, u32[]{:S(2)}, u32[]{:S(2)}) collective-permute-start(bf16[192,768]{1,0:T(8,128)(2,1)S(1)} %get-tuple-element.232), channel_id=1, source_target_pairs={{0,16},{1,24},{2,18},{3,26},{4,20},{5,28},{6,22},{7,30},{8,17},{9,... | collective-permute-start | bytes 884744 | tf_op jit(solution)/shard_map/ppermute | solution.py:42
  314.6 27.0 %collective-permute-start.89 = (bf16[2,192,768]{2,1,0:T(8,128)(2,1)S(1)}, bf16[2,192,768]{2,1,0:T(8,128)(2,1)S(1)}, u32[]{:S(2)}, u32[]{:S(2)}) collective-permute-start(bf16[2,192,768]{2,1,0:T(8,128)(2,1)S(1)} %pad_maximum_fusion.30.refs_11_), channel_id=1, source_target_pairs={{0,4},{1,5},{2,6},{3,7},{4,0},{5,1},{6,2},{7,3},{8,12},{9,13},{10,... | collective-permute-start | bytes 1769480 | tf_op jit(solution)/shard_map/ppermute | solution.py:42
  316.9 24.8 %collective-permute-start.88 = (bf16[2,192,768]{2,1,0:T(8,128)(2,1)S(1)}, bf16[2,192,768]{2,1,0:T(8,128)(2,1)S(1)}, u32[]{:S(2)}, u32[]{:S(2)}) collective-permute-start(bf16[2,192,768]{2,1,0:T(8,128)(2,1)S(1)} %pad_maximum_fusion.30.refs_11_), channel_id=1, source_target_pairs={{0,1},{1,0},{2,3},{3,2},{4,5},{5,4},{6,7},{7,6},{8,9},{9,8},{10,11... | collective-permute-start | bytes 1769480 | tf_op jit(solution)/shard_map/ppermute | solution.py:42
  317.0 26.1 %collective-permute-start.94 = (bf16[2,192,768]{2,1,0:T(8,128)(2,1)S(1)}, bf16[2,192,768]{2,1,0:T(8,128)(2,1)S(1)}, u32[]{:S(2)}, u32[]{:S(2)}) collective-permute-start(bf16[2,192,768]{2,1,0:T(8,128)(2,1)S(1)} %pad_maximum_fusion.31.refs_15_), channel_id=1, source_target_pairs={{0,4},{1,5},{2,6},{3,7},{4,0},{5,1},{6,2},{7,3},{8,12},{9,13},{10,... | collective-permute-start | bytes 1769480 | tf_op jit(solution)/shard_map/ppermute | solution.py:42
  341.7 26.7 %collective-permute-start.105 = (bf16[2,192,768]{2,1,0:T(8,128)(2,1)S(1)}, bf16[2,192,768]{2,1,0:T(8,128)(2,1)S(1)}, u32[]{:S(2)}, u32[]{:S(2)}) collective-permute-start(bf16[2,192,768]{2,1,0:T(8,128)(2,1)S(1)} %pad_maximum_fusion.34.refs_23_), channel_id=1, source_target_pairs={{0,4},{1,5},{2,6},{3,7},{4,0},{5,1},{6,2},{7,3},{8,12},{9,13},{10,... | collective-permute-start | bytes 1769480 | tf_op jit(solution)/shard_map/ppermute | solution.py:42
  343.1 25.3 %collective-permute-start.90 = (bf16[2,192,768]{2,1,0:T(8,128)(2,1)S(1)}, bf16[2,192,768]{2,1,0:T(8,128)(2,1)S(1)}, u32[]{:S(2)}, u32[]{:S(2)}) collective-permute-start(bf16[2,192,768]{2,1,0:T(8,128)(2,1)S(1)} %collective-permute-done.89.refs_13_), channel_id=1, source_target_pairs={{0,1},{1,0},{2,3},{3,2},{4,5},{5,4},{6,7},{7,6},{8,9},{9,8},{10,11... | collective-permute-start | bytes 1769480 | tf_op jit(solution)/shard_map/ppermute | solution.py:42
  343.8 24.6 %collective-permute-start.104 = (bf16[2,192,768]{2,1,0:T(8,128)(2,1)S(1)}, bf16[2,192,768]{2,1,0:T(8,128)(2,1)S(1)}, u32[]{:S(2)}, u32[]{:S(2)}) collective-permute-start(bf16[2,192,768]{2,1,0:T(8,128)(2,1)S(1)} %pad_maximum_fusion.34.refs_23_), channel_id=1, source_target_pairs={{0,1},{1,0},{2,3},{3,2},{4,5},{5,4},{6,7},{7,6},{8,9},{9,8},{10,11... | collective-permute-start | bytes 1769480 | tf_op jit(solution)/shard_map/ppermute | solution.py:42
  376.0 31.3 %collective-permute-start.107 = (f16[384,768]{1,0:T(8,128)(2,1)S(1)}, f16[384,768]{1,0:T(8,128)(2,1)S(1)}, u32[]{:S(2)}, u32[]{:S(2)}) collective-permute-start(f16[384,768]{1,0:T(8,128)(2,1)S(1)} %get-tuple-element.343), channel_id=1, source_target_pairs={{0,4},{1,8},{2,16},{3,24},{4,0},{5,12},{6,20},{7,28},{8,1},{9,13},... | collective-permute-start | bytes 1769480 | tf_op jit(solution)/shard_map/ppermute | solution.py:42
  378.1 29.2 %collective-permute-start.108 = (f16[384,768]{1,0:T(8,128)(2,1)S(1)}, f16[384,768]{1,0:T(8,128)(2,1)S(1)}, u32[]{:S(2)}, u32[]{:S(2)}) collective-permute-start(f16[384,768]{1,0:T(8,128)(2,1)S(1)} %get-tuple-element.342), channel_id=1, source_target_pairs={{0,16},{1,24},{2,0},{3,8},{4,20},{5,28},{6,4},{7,12},{8,17},{9,25}... | collective-permute-start | bytes 1769480 | tf_op jit(solution)/shard_map/ppermute | solution.py:42
  380.1 27.0 %collective-permute-start.115 = (f16[384,384]{1,0:T(8,128)(2,1)S(1)}, f16[384,384]{1,0:T(8,128)(2,1)S(1)}, u32[]{:S(2)}, u32[]{:S(2)}) collective-permute-start(f16[384,384]{1,0:T(8,128)(2,1)S(1)} %get-tuple-element.376), channel_id=1, source_target_pairs={{0,6},{1,7},{2,4},{3,5},{4,2},{5,3},{6,0},{7,1},{8,14},{9,15},{10,... | collective-permute-start | bytes 884744 | tf_op jit(solution)/shard_map/ppermute | solution.py:42
  383.8 23.3 %collective-permute-start.114 = (f16[384,384]{1,0:T(8,128)(2,1)S(1)}, f16[384,384]{1,0:T(8,128)(2,1)S(1)}, u32[]{:S(2)}, u32[]{:S(2)}) collective-permute-start(f16[384,384]{1,0:T(8,128)(2,1)S(1)} %dynamic-slice_bitcast_fusion.11), channel_id=1, source_target_pairs={{0,4},{1,5},{2,6},{3,7},{4,0},{5,1},{6,2},{7,3},{8,12},{9,13},{10,... | collective-permute-start | bytes 884744 | tf_op jit(solution)/shard_map/ppermute | solution.py:42
  383.9 23.1 %collective-permute-start.111 = (f16[384,384]{1,0:T(8,128)(2,1)S(1)}, f16[384,384]{1,0:T(8,128)(2,1)S(1)}, u32[]{:S(2)}, u32[]{:S(2)}) collective-permute-start(f16[384,384]{1,0:T(8,128)(2,1)S(1)} %get-tuple-element.377), channel_id=1, source_target_pairs={{0,2},{1,3},{2,0},{3,1},{4,6},{5,7},{6,4},{7,5},{8,10},{9,11},{10,... | collective-permute-start | bytes 884744 | tf_op jit(solution)/shard_map/ppermute | solution.py:42
  407.9 23.7 %collective-permute-start.112 = (f16[384,384]{1,0:T(8,128)(2,1)S(1)}, f16[384,384]{1,0:T(8,128)(2,1)S(1)}, u32[]{:S(2)}, u32[]{:S(2)}) collective-permute-start(f16[384,384]{1,0:T(8,128)(2,1)S(1)} %get-tuple-element.371), channel_id=1, source_target_pairs={{0,1},{1,0},{2,3},{3,2},{4,5},{5,4},{6,7},{7,6},{8,9},{9,8},{10,11... | collective-permute-start | bytes 884744 | tf_op jit(solution)/shard_map/ppermute | solution.py:42
  409.0 38.8 %collective-permute-start.110 = (f16[384,768]{1,0:T(8,128)(2,1)S(1)}, f16[384,768]{1,0:T(8,128)(2,1)S(1)}, u32[]{:S(2)}, u32[]{:S(2)}) collective-permute-start(f16[384,768]{1,0:T(8,128)(2,1)S(1)} %get-tuple-element.338), channel_id=1, source_target_pairs={{0,24},{1,16},{2,8},{3,0},{4,28},{5,20},{6,12},{7,4},{8,25},{9,17}... | collective-permute-start | bytes 1769480 | tf_op jit(solution)/shard_map/ppermute | solution.py:42
  412.3 33.8 %collective-permute-start.109 = (f16[384,768]{1,0:T(8,128)(2,1)S(1)}, f16[384,768]{1,0:T(8,128)(2,1)S(1)}, u32[]{:S(2)}, u32[]{:S(2)}) collective-permute-start(f16[384,768]{1,0:T(8,128)(2,1)S(1)} %get-tuple-element.339), channel_id=1, source_target_pairs={{0,8},{1,0},{2,24},{3,16},{4,12},{5,4},{6,28},{7,20},{8,9},{9,1},{... | collective-permute-start | bytes 1769480 | tf_op jit(solution)/shard_map/ppermute | solution.py:42
  417.2 21.9 %collective-permute-start.116 = (f16[384,384]{1,0:T(8,128)(2,1)S(1)}, f16[384,384]{1,0:T(8,128)(2,1)S(1)}, u32[]{:S(2)}, u32[]{:S(2)}) collective-permute-start(f16[384,384]{1,0:T(8,128)(2,1)S(1)} %get-tuple-element.370), channel_id=1, source_target_pairs={{0,5},{1,4},{2,7},{3,6},{4,1},{5,0},{6,3},{7,2},{8,13},{9,12},{10,... | collective-permute-start | bytes 884744 | tf_op jit(solution)/shard_map/ppermute | solution.py:42
  (82 other events, 1805.2 us)
